TPU v7x, 128 devices: a whole 4x4x4 slice. The times are simulated.
128 devices in a mesh: grp: 2 (over x_hi), seq: 8 (over y, core), tp: 8 (over x_lo, z).
Axes of the slice: x: 4 (x_hi: 2, x_lo: 2; x = x_hi * 2 + x_lo), y: 4, z: 4, core: 2. Of those that a mesh axis runs over, the one named last changes fastest.
Arguments:
- tokens: bfloat16 [2, 8, 256, 4096], P('grp', 'seq', 'tp'), may hold values from -6 to 6
- text_gaps: int32 [8, 5], P('seq'), may hold values from 1 to 128, 256 in all within a row
- image_runs: int32 [8, 4], P('seq'), may hold values from 1 to 64, 128 in all within a row
- gains: bfloat16 [2, 4096], P('grp'), may hold values from 0.099609375 to 1.8984375
- w_qkv: bfloat16 [2, 4096, 3, 4096], P('grp', None, None, 'tp')
- w_out: bfloat16 [2, 4096, 4096], P('grp', None, 'tp'), may hold values from -0.09375 to 0.09375
- cotangent: bfloat16 [2, 8, 256, 4096], P('grp', 'seq', 'tp'), may hold values from -1.5 to 1.5
Outputs:
- layer_out: bfloat16 [2, 8, 256, 4096], P('grp', 'seq', 'tp')
- tokens_grad: bfloat16 [2, 8, 256, 4096], P('grp', 'seq', 'tp')
- gain_grad: float32 [2, 4096], P('grp')
- qkv_weight_grad: float32 [2, 4096, 3, 4096], P('grp', 'seq', None, 'tp')
- out_weight_grad: float32 [2, 4096, 4096], P('grp', 'seq', 'tp')
Inputs may be any that keep to these rules, and one draw needn't show every extreme that they name: `text_gaps`: the text runs of a sequence add up to 256; some run has exactly 128 tokens. `image_runs`: the image runs of a sequence add up to 128; some run has exactly 64 tokens.
All inputs are finite; a program needn't handle non-finite values.
Results may differ from a plain program's by a relative error of at most 0.034.
The roundings to bfloat16 on the way count: a program that leaves them out, or rounds other values in their place, can miss the bound.
Values may be sent and summed in bfloat16 or wider, within the bound.
No kernel may reach another device: no remote copies, remote signals or barrier semaphores. Data moves between devices by JAX's collectives and lax.ppermute only.
A program may use at most 128 MiB of HBM per device.

v0:
```python
import jax
import jax.numpy as jnp
from jax import lax
from jax.sharding import PartitionSpec as P

HS = 128
LI = 128


far_place = 1073741824


def swapped(value, axis, stride):
    return lax.ppermute(value, axis, [(i, i ^ 1 << stride) for i in range(lax.axis_size(axis))])


def place_tokens(text_gaps, image_runs, slot_count, image_count):
    text_ends = jnp.cumsum(text_gaps)
    image_ends = jnp.cumsum(image_runs)
    run_count = image_runs.shape[0]
    slot_ids = jnp.arange(slot_count, dtype=jnp.int32)
    run_ids = jnp.arange(run_count + 1, dtype=jnp.int32)
    image_before = jnp.concatenate([jnp.zeros((1,), jnp.int32), image_ends])
    text_run = jnp.sum((slot_ids[:, None] >= text_ends[None, :]).astype(jnp.int32), axis=1)
    text_shift = jnp.sum(
        jnp.where(run_ids[None, :] == text_run[:, None], image_before[None, :], 0), axis=1
    )
    image_run = jnp.sum((slot_ids[:, None] >= image_ends[None, :]).astype(jnp.int32), axis=1)
    image_shift = jnp.sum(
        jnp.where(run_ids[None, :] == image_run[:, None], text_ends[None, :], 0), axis=1
    )
    text_place = slot_ids + text_shift
    image_place = jnp.where(slot_ids < image_count, slot_ids + image_shift, far_place)
    return (text_place, image_place)


def attend_rows(queries, query_place, all_keys, key_place, scale):
    scores = (
        jnp.einsum("qhd,khd->hqk", queries, all_keys, preferred_element_type=jnp.float32) * scale
    )
    allowed = key_place[None, :] <= query_place[:, None]
    scores = jnp.where(allowed[None], scores, -1e30)
    row_max = jnp.max(scores, axis=2, keepdims=True)
    weights = jnp.exp(scores - row_max)
    row_sum = jnp.sum(weights, axis=2, keepdims=True)
    return weights / row_sum


def contract_rows(left, right):
    return lax.dot_general(
        left, right, (((0,), (0,)), ((), ())), preferred_element_type=jnp.float32
    )


def per_device(tokens, text_gaps, image_runs, gains, w_qkv, w_out, cotangent):
    f32 = jnp.float32
    bf16 = jnp.bfloat16
    scale = HS ** (-0.5)
    group_index = lax.axis_index("grp")
    tp_index = lax.axis_index("tp")
    x_rows = tokens[0, 0]
    row_count = x_rows.shape[0]
    width = x_rows.shape[1]
    weights_in = w_qkv[0]
    head_cols = weights_in.shape[2]
    head_count = head_cols // HS
    flat_w = weights_in.reshape(width, 3 * head_cols)
    out_w = w_out[0]
    gain_row = gains[0].astype(f32)
    slot_count = row_count * lax.axis_size("tp")
    text_place, image_place = place_tokens(text_gaps[0], image_runs[0], slot_count, LI)
    own_place = jnp.where(group_index == 0, text_place, image_place)
    other_place = jnp.where(group_index == 0, image_place, text_place)
    key_place = jnp.concatenate([own_place, other_place], axis=0)
    valid_all = (own_place < far_place).astype(f32)
    valid_rows = lax.dynamic_slice_in_dim(valid_all, tp_index * row_count, row_count, 0)[:, None]
    x_float = x_rows.astype(f32)
    inv_rms = lax.rsqrt(jnp.mean(x_float * x_float, axis=1, keepdims=True) + 1e-05)
    normed = (x_float * inv_rms * gain_row).astype(bf16)
    normed_full = lax.all_gather(normed, "tp", axis=0, tiled=True)
    qkv = jnp.dot(normed_full, flat_w, preferred_element_type=f32).astype(bf16)
    qkv = qkv.reshape(slot_count, 3, head_count, HS)
    own_q = qkv[:, 0]
    own_k = qkv[:, 1]
    own_v = qkv[:, 2]
    other_k, other_v = swapped((own_k, own_v), "grp", 0)
    all_keys = jnp.concatenate([own_k, other_k], axis=0)
    all_values = jnp.concatenate([own_v, other_v], axis=0)
    block = min(slot_count, 512)
    blocks = slot_count // block
    query_blocks = own_q.reshape(blocks, block, head_count, HS)
    place_blocks = own_place.reshape(blocks, block)

    def forward_block(pieces):
        queries, query_place = pieces
        attn = attend_rows(queries, query_place, all_keys, key_place, scale)
        return jnp.einsum(
            "hqk,khd->qhd", attn.astype(bf16), all_values, preferred_element_type=f32
        ).astype(bf16)

    mixed = lax.map(forward_block, (query_blocks, place_blocks))
    mixed_flat = mixed.reshape(slot_count, head_cols)
    summed = lax.psum(
        lax.dot_general(
            mixed_flat, out_w, (((1,), (1,)), ((), ())), preferred_element_type=f32
        ).astype(jnp.bfloat16),
        "tp",
    ).astype(jnp.float32)
    proj_rows = lax.dynamic_slice_in_dim(summed, tp_index * row_count, row_count, 0)
    layer_out = ((x_float + proj_rows) * valid_rows).astype(bf16)
    grad_rows = cotangent[0, 0] * valid_rows.astype(bf16)
    grad_full = lax.all_gather(grad_rows, "tp", axis=0, tiled=True)
    grad_mixed = jnp.dot(grad_full, out_w, preferred_element_type=f32).astype(bf16)
    grad_blocks = grad_mixed.reshape(blocks, block, head_count, HS)

    def backward_block(carried, pieces):
        key_acc, value_acc = carried
        queries, query_place, grad_block, mixed_block = pieces
        attn = attend_rows(queries, query_place, all_keys, key_place, scale)
        attn_b = attn.astype(bf16)
        value_acc = value_acc + jnp.einsum(
            "hqk,qhd->khd", attn_b, grad_block, preferred_element_type=f32
        )
        weight_grad = jnp.einsum("qhd,khd->hqk", grad_block, all_values, preferred_element_type=f32)
        row_dot = jnp.einsum("qhd,qhd->hq", grad_block, mixed_block, preferred_element_type=f32)[
            :, :, None
        ]
        score_grad = (attn * (weight_grad - row_dot)).astype(bf16)
        query_grad = (
            jnp.einsum("hqk,khd->qhd", score_grad, all_keys, preferred_element_type=f32) * scale
        )
        key_acc = (
            key_acc
            + jnp.einsum("hqk,qhd->khd", score_grad, queries, preferred_element_type=f32) * scale
        )
        return ((key_acc, value_acc), query_grad)

    empty_keys = jnp.zeros((2 * slot_count, head_count, HS), f32)
    (key_grad, value_grad), query_grad = lax.scan(
        backward_block, (empty_keys, empty_keys), (query_blocks, place_blocks, grad_blocks, mixed)
    )
    query_grad = query_grad.reshape(slot_count, head_count, HS)
    back_key, back_value = swapped((key_grad[slot_count:], value_grad[slot_count:]), "grp", 0)
    own_key = key_grad[:slot_count] + back_key
    own_value = value_grad[:slot_count] + back_value
    qkv_grad = (
        jnp.stack([query_grad, own_key, own_value], axis=1)
        .astype(bf16)
        .reshape(slot_count, 3 * head_cols)
    )
    summed_grad = lax.psum(
        lax.dot_general(
            qkv_grad, flat_w, (((1,), (1,)), ((), ())), preferred_element_type=f32
        ).astype(jnp.bfloat16),
        "tp",
    ).astype(jnp.float32)
    normed_grad = lax.dynamic_slice_in_dim(summed_grad, tp_index * row_count, row_count, 0)
    gain_term = jnp.sum(normed_grad * x_float * inv_rms, axis=0)
    gain_grad = lax.psum(gain_term, ("seq", "tp"))
    scaled = gain_row * normed_grad
    x_grad = (
        grad_rows.astype(f32)
        + inv_rms * scaled
        - x_float
        * (inv_rms * inv_rms * inv_rms)
        * jnp.mean(scaled * x_float, axis=1, keepdims=True)
    )
    tokens_grad = x_grad.astype(bf16)
    seq_count = lax.axis_size("seq")
    share_rows = width // seq_count
    shares = lax.psum_scatter(
        jnp.concatenate(
            [contract_rows(normed_full, qkv_grad), contract_rows(grad_full, mixed_flat)], axis=1
        ).astype(jnp.bfloat16),
        "seq",
        scatter_dimension=0,
        tiled=True,
    ).astype(jnp.float32)
    qkv_share = shares[:, : 3 * head_cols]
    out_share = shares[:, 3 * head_cols :]
    return (
        layer_out.reshape(1, 1, row_count, width),
        tokens_grad.reshape(1, 1, row_count, width),
        gain_grad.reshape(1, width),
        qkv_share.reshape(1, share_rows, 3, head_cols),
        out_share.reshape(1, share_rows, head_cols),
    )


def solution(mesh):
    in_specs = (
        P("grp", "seq", "tp", None),
        P("seq", None),
        P("seq", None),
        P("grp", None),
        P("grp", None, None, "tp"),
        P("grp", None, "tp"),
        P("grp", "seq", "tp", None),
    )
    out_specs = (
        P("grp", "seq", "tp", None),
        P("grp", "seq", "tp", None),
        P("grp", None),
        P("grp", "seq", None, "tp"),
        P("grp", "seq", "tp"),
    )
    return jax.shard_map(
        per_device, mesh=mesh, in_specs=in_specs, out_specs=out_specs, check_vma=False
    )
```

profile of v0, /device:TPU:0, one launch (start us, length us, event | category | flops | bytes accessed | tf_op | source)
XLA Modules:
  0.0 545.5 jit_solution(13011465269947178676)
XLA Ops:
  7.2 0.8 reduce-window.16
  8.0 0.8 reduce-window.17
  8.9 0.1 convert_reduce_fusion.1
  9.0 1.1 fusion.18
  10.1 0.7 mul.154
  11.0 0.1 select_reduce_fusion.1
  11.2 1.8 fusion.20
  13.0 1.7 bitcast_multiply_fusion
  14.8 16.9 %copy.33 = bf16[1,4096,3,512]{1,3,2,0:T(8,128)(2,1)} copy(bf16[1,4096,3,512]{3,1,2,0:T(8,128)(2,1)} %param.11) | data formatting | bytes 25165824 | tf_op args[4]
  31.8 0.1 broadcast_compare_fusion
  31.9 25.6 %all-gather.3.cloned.1.call-done = bf16[256,4096]{1,0:T(8,128)(2,1)} async-done(((bf16[32,4096]{1,0:T(8,128)(2,1)}), bf16[256,4096]{1,0:T(8,128)(2,1)}) %all-gather.3.cloned.1.call-update) | async-done | bytes 2097168 | tf_op jit(solution)/shard_map/all_gather | solution.py:80
  57.5 8.7 %convolution_convert_fusion.4 = bf16[256,1536]{1,0:T(8,128)(2,1)S(1)} fusion(bf16[256,4096]{1,0:T(8,128)(2,1)} %all-gather.3.cloned.1.call-done, bf16[4096,1536]{0,1:T(8,128)(2,1)} %bitcast.84), kind=kOutput, calls=%fused_computation.9 | convolution fusion | flops 3221618688 | bytes 15466496 | tf_op jit(solution)/shard_map/dot_general | solution.py:81
  66.1 0.2 reshape.156
  66.3 0.3 fusion.43
  66.6 2.8 collective-permute-start.1
  69.4 31.2 %all-gather.5.cloned.1.call-done = bf16[256,4096]{1,0:T(8,128)(2,1)} async-done(((bf16[32,4096]{1,0:T(8,128)(2,1)}), bf16[256,4096]{1,0:T(8,128)(2,1)}) %all-gather.5.cloned.1.call-update) | async-done | bytes 2097168 | tf_op jit(solution)/shard_map/all_gather | solution.py:112
  100.6 4.1 fusion.7
  104.7 0.2 copy.41
  105.0 0.2 copy.50
  105.2 0.2 copy.53
  105.4 1.8 collective-permute-start
  107.2 2.2 fusion.44
  109.4 2.1 convolution_bitcast_fusion
  111.5 1.8 collective-permute-done
  113.3 0.6 multiply_reduce_fusion
  113.9 0.5 multiply_convert_fusion
  114.5 0.3 fusion.5
  114.9 1.8 collective-permute-start.3
  116.8 1.8 collective-permute-start.2
  118.5 2.6 convolution_convert_fusion.3
  121.2 0.5 fusion.6
  121.7 9.7 %collective-permute-done.3 = f32[256,4,128]{0,2,1:T(8,128)S(1)} collective-permute-done((f32[256,4,128]{0,2,1:T(8,128)S(1)}, f32[256,4,128]{0,2,1:T(8,128)S(1)}, u32[]{:S(2)}, u32[]{:S(2)}) %collective-permute-start.3) | collective-permute-done | bytes 524320 | tf_op jit(solution)/shard_map/ppermute | solution.py:14
  131.4 0.1 fusion.27
  131.5 5.9 %collective-permute-done.2 = f32[256,4,128]{0,2,1:T(8,128)S(1)} collective-permute-done((f32[256,4,128]{0,2,1:T(8,128)S(1)}, f32[256,4,128]{0,2,1:T(8,128)S(1)}, u32[]{:S(2)}, u32[]{:S(2)}) %collective-permute-start.2) | collective-permute-done | bytes 524320 | tf_op jit(solution)/shard_map/ppermute | solution.py:14
  137.4 0.1 fusion.28
  137.5 0.1 maximum_convert_fusion
  137.6 4.7 convolution_convert_fusion.2
  142.4 4.8 convolution_convert_fusion.1
  147.2 5.2 convolution_convert_fusion
  152.4 9.6 %pad_maximum_fusion = bf16[4096,2048]{0,1:T(8,128)(2,1)} fusion(bf16[4096,512]{0,1:T(8,128)(2,1)} %convolution_convert_fusion.1, bf16[4096,1536]{0,1:T(8,128)(2,1)S(1)} %convolution_convert_fusion), kind=kLoop, calls=%fused_computation.1 | loop fusion | flops 33554432 | bytes 33554432 | tf_op jit(solution)/shard_map/concatenate | solution.py:172
  162.0 85.3 %all-reduce.3.cloned.1.call-done = (bf16[256,4096]{1,0:T(8,128)(2,1)}, bf16[256,4096]{1,0:T(8,128)(2,1)}) async-done(((bf16[256,4096]{1,0:T(8,128)(2,1)}, bf16[256,4096]{1,0:T(8,128)(2,1)}), (bf16[256,4096]{1,0:T(8,128)(2,1)}, bf16[256,4096]{1,0:T(8,128)(2,1)})) %all-reduce.3.cloned.1.call-update) | async-done | bytes 4194320 | tf_op jit(solution)/shard_map/psum | solution.py:103
  247.3 1.2 fusion.26
  248.5 279.2 %psum.23 = f32[1,4096]{1,0:T(1,128)} all-reduce(f32[1,4096]{1,0:T(1,128)S(1)} %bitcast.102), channel_id=1, replica_groups=mesh['grp'=2,'seq'=8,'tp'=8] {'seq','tp'}, use_global_device_ids=true, to_apply=%region_13.14 | all-reduce | flops 4096 | bytes 32768 | tf_op jit(solution)/shard_map/psum | solution.py:159
  527.7 2.1 fusion.31
  529.8 3.5 slice.43
  533.3 3.7 copy.42
  537.0 0.6 convert_element_type.108
  537.7 1.3 copy.43
  (40 shorter events, 0.8 us)
Async XLA Ops:
  7.2 50.3 %all-gather.3.cloned.1.call-start = ((), (), s32[]{:S(2)}) async-start(), calls=%async_computation.1 | async-start | bytes 2359296 | tf_op jit(solution)/shard_map/all_gather | solution.py:80
  13.0 87.6 %all-gather.5.cloned.1.call-start = ((), (), s32[]{:S(2)}) async-start(), calls=%async_computation.2 | async-start | bytes 2359296 | tf_op jit(solution)/shard_map/all_gather | solution.py:112
  14.8 232.5 %all-reduce.3.cloned.1.call-start = ((), (), s32[]{:S(2)}) async-start(), calls=%async_computation.4 | async-start | bytes 8388608 | tf_op jit(solution)/shard_map/psum | solution.py:103
  66.6 40.6 %collective-permute-start.1 = (bf16[256,4,128]{2,0,1:T(8,128)(2,1)S(1)}, bf16[256,4,128]{2,0,1:T(8,128)(2,1)S(1)}, u32[]{:S(2)}, u32[]{:S(2)}) collective-permute-start(bf16[256,4,128]{2,0,1:T(8,128)(2,1)S(1)} %bitcast.96), channel_id=1, source_target_pairs={{0,64},{64,0},{1,65},{65,1},{2,66},{66,2},{3,67},{67,3},{4,68},{68... | collective-permute-start | bytes 786440 | tf_op jit(solution)/shard_map/ppermute | solution.py:14
  105.4 8.0 %collective-permute-start = (bf16[256,4,128]{0,2,1:T(8,128)(2,1)S(1)}, bf16[256,4,128]{0,2,1:T(8,128)(2,1)S(1)}, u32[]{:S(2)}, u32[]{:S(2)}) collective-permute-start(bf16[256,4,128]{0,2,1:T(8,128)(2,1)S(1)} %bitcast.99), channel_id=1, source_target_pairs={{0,64},{64,0},{1,65},{65,1},{2,66},{66,2},{3,67},{67,3},{4,68},{68... | collective-permute-start | bytes 786440 | tf_op jit(solution)/shard_map/ppermute | solution.py:14
  109.4 3.9 copy-start.4
  113.9 23.7 %slice-start = ((s8[12582912]{0:T(1024)(128)(4,1)}), s8[4194304]{0:T(1024)(128)(4,1)S(1)}, s32[]{:S(2)}) async-start(s8[12582912]{0:T(1024)(128)(4,1)} %bitcast.85), calls=%async_computation.5 | async-start | bytes 8388608
  113.9 23.7 %slice-start.1 = ((s8[12582912]{0:T(1024)(128)(4,1)}), s8[4194304]{0:T(1024)(128)(4,1)S(1)}, s32[]{:S(2)}) async-start(s8[12582912]{0:T(1024)(128)(4,1)} %bitcast.85), calls=%async_computation.6 | async-start | bytes 8388608
  114.5 4.1 copy-start.1
  114.9 16.4 %collective-permute-start.3 = (f32[256,4,128]{0,2,1:T(8,128)S(1)}, f32[256,4,128]{0,2,1:T(8,128)S(1)}, u32[]{:S(2)}, u32[]{:S(2)}) collective-permute-start(f32[256,4,128]{0,2,1:T(8,128)S(1)} %slice.42), channel_id=1, source_target_pairs={{0,64},{64,0},{1,65},{65,1},{2,66},{66,2},{3,67},{67,3},{4,68},{68... | collective-permute-start | bytes 1572872 | tf_op jit(solution)/shard_map/ppermute | solution.py:14
  116.8 20.6 %collective-permute-start.2 = (f32[256,4,128]{0,2,1:T(8,128)S(1)}, f32[256,4,128]{0,2,1:T(8,128)S(1)}, u32[]{:S(2)}, u32[]{:S(2)}) collective-permute-start(f32[256,4,128]{0,2,1:T(8,128)S(1)} %slice.40), channel_id=1, source_target_pairs={{0,64},{64,0},{1,65},{65,1},{2,66},{66,2},{3,67},{67,3},{4,68},{68... | collective-permute-start | bytes 1572872 | tf_op jit(solution)/shard_map/ppermute | solution.py:14
  118.5 19.1 %slice-start.2 = ((s8[12582912]{0:T(1024)(128)(4,1)}), s8[4194304]{0:T(1024)(128)(4,1)S(1)}, s32[]{:S(2)}) async-start(s8[12582912]{0:T(1024)(128)(4,1)} %bitcast.85), calls=%async_computation.7 | async-start | bytes 8388608
  142.3 387.4 %reduce-scatter.2.cloned.1.call-start = ((), (), s32[]{:S(2)}) async-start(), calls=%async_computation.3 | async-start | bytes 18874368 | tf_op jit(solution)/shard_map/reduce_scatter | solution.py:171
  162.0 85.3 %copy-start.2 = (bf16[1,1,32,4096]{3,2,1,0:T(8,128)(2,1)S(1)}, bf16[1,1,32,4096]{3,2,1,0:T(8,128)(2,1)}, u32[]{:S(2)}) copy-start(bf16[1,1,32,4096]{3,2,1,0:T(8,128)(2,1)} %param.7) | copy-start | bytes 786436
  162.0 365.7 %copy-start.3 = (bf16[1,1,32,4096]{3,2,1,0:T(8,128)(2,1)S(1)}, bf16[1,1,32,4096]{3,2,1,0:T(8,128)(2,1)}, u32[]{:S(2)}) copy-start(bf16[1,1,32,4096]{3,2,1,0:T(8,128)(2,1)} %param.13) | copy-start | bytes 786436
  533.3 3.7 copy-start
Sparse Core Ops, SparseCore 0:
  13.1 44.3 all-gather.2
  59.7 40.8 all-gather.4
  142.5 104.7 all-reduce.2
  249.6 90.4 reduce-scatter.1
where the time goes:
time: 547 us; the launch traced here: 546 us
  blocking collectives  279 us (51%)
  waiting for transfers between devices  159 us (29%)
  matrix products  36.3 us (7%)
  local copies, waits for them, and re-layouts  26.7 us (5%)
  other arithmetic  21.4 us (4%)
  between operations  14 us (3%)
  starting transfers between devices  8.37 us (2%)
    psum x1, blocking collectives, per_device(): gain_grad = lax.psum(gain_term, ('seq', 'tp'))  279 us
    psum x1, waiting for transfers between devices, per_device(): lax.psum(lax.dot_general(mixed_flat, out_w, (((1,), (1,)), ((), ())), pre...  85.3 us
    all_gather x1, waiting for transfers between devices, per_device(): grad_full = lax.all_gather(grad_rows, 'tp', axis=0, tiled=True)  31.2 us
    all_gather x1, waiting for transfers between devices, per_device(): normed_full = lax.all_gather(normed, 'tp', axis=0, tiled=True)  25.6 us
    unnamed x22, local copies, waits for them, and re-layouts  22.4 us
    ppermute x4, waiting for transfers between devices, swapped(): lax.ppermute(value, axis, [(i, i ^ 1 << stride) for i in range(lax.axis_s...  17.4 us
  transfers between devices with their start and end apart: 8, of which 6 were waited for; matrix products, arithmetic and copies ran while one was open for 12% of the time, Pallas kernels for 0%

commit v1 on v0

v1 whole, which is shorter than its diff:
```python
import jax
import jax.numpy as jnp
from jax import lax
from jax.sharding import PartitionSpec as P

HS = 128
LI = 128


far_place = 1073741824
f32 = jnp.float32
bf16 = jnp.bfloat16


def z_shift(k):
    return [(i, (i // 4) * 4 + (i + k) % 4) for i in range(8)]


X_SWAP = [(i, i ^ 4) for i in range(8)]


def y_shift(k):
    return [(i, (i + 2 * k) % 8) for i in range(8)]


CORE_SWAP = [(i, i ^ 1) for i in range(8)]
STEPS = (1, 3, 2)


def place_tokens(text_gaps, image_runs, slot_count, image_count):
    text_ends = jnp.cumsum(text_gaps)
    image_ends = jnp.cumsum(image_runs)
    run_count = image_runs.shape[0]
    slot_ids = jnp.arange(slot_count, dtype=jnp.int32)
    run_ids = jnp.arange(run_count + 1, dtype=jnp.int32)
    image_before = jnp.concatenate([jnp.zeros((1,), jnp.int32), image_ends])
    text_run = jnp.sum((slot_ids[:, None] >= text_ends[None, :]).astype(jnp.int32), axis=1)
    text_shift = jnp.sum(
        jnp.where(run_ids[None, :] == text_run[:, None], image_before[None, :], 0), axis=1
    )
    image_run = jnp.sum((slot_ids[:, None] >= image_ends[None, :]).astype(jnp.int32), axis=1)
    image_shift = jnp.sum(
        jnp.where(run_ids[None, :] == image_run[:, None], text_ends[None, :], 0), axis=1
    )
    text_place = slot_ids + text_shift
    image_place = jnp.where(slot_ids < image_count, slot_ids + image_shift, far_place)
    return (text_place, image_place)


def block_at(blocks, index):
    return lax.dynamic_index_in_dim(blocks, index, 0, keepdims=False)


def gather_blocks(rows, x_index, z_index):
    half = rows.shape[1] // 2
    left, right = rows[:, :half], rows[:, half:]
    right_pair = jnp.stack([right, lax.ppermute(right, "tp", X_SWAP)])
    left_four = [left] + [lax.ppermute(left, "tp", z_shift(k)) for k in STEPS]
    right_four = [right_pair] + [lax.ppermute(right_pair, "tp", z_shift(k)) for k in STEPS]
    left_other = lax.ppermute(jnp.stack(left_four), "tp", X_SWAP)
    found = []
    for slot, k in enumerate((0,) + STEPS):
        z_from = (z_index + 4 - k) % 4
        own, other = x_index * 4 + z_from, (1 - x_index) * 4 + z_from
        found.append((own, 0, left_four[slot]))
        found.append((other, 0, left_other[slot]))
        found.append((own, 1, right_four[slot][0]))
        found.append((other, 1, right_four[slot][1]))
    return found


def scatter_left(part, x_index, z_index):
    blocks = part.reshape((2, 4) + part.shape[1:])

    def column(z):
        return lax.dynamic_index_in_dim(blocks, z, 1, keepdims=False)

    total = column(z_index).astype(f32)
    for k in STEPS:
        total = total + lax.ppermute(column((z_index + k) % 4), "tp", z_shift(k)).astype(f32)
    sent = block_at(total, 1 - x_index).astype(bf16)
    return block_at(total, x_index) + lax.ppermute(sent, "tp", X_SWAP).astype(f32)


def scatter_right(part, x_index, z_index):
    blocks = part.reshape((2, 4) + part.shape[1:])
    came = lax.ppermute(block_at(blocks, 1 - x_index), "tp", X_SWAP)
    pair = block_at(blocks, x_index).astype(f32) + came.astype(f32)
    pair_b = pair.astype(bf16)
    total = block_at(pair, z_index)
    for k in STEPS:
        sent = block_at(pair_b, (z_index + k) % 4)
        total = total + lax.ppermute(sent, "tp", z_shift(k)).astype(f32)
    return total


def attend_rows(queries, query_place, all_keys, key_place, scale):
    scores = (
        jnp.einsum("qhd,khd->hqk", queries, all_keys, preferred_element_type=jnp.float32) * scale
    )
    allowed = key_place[None, :] <= query_place[:, None]
    scores = jnp.where(allowed[None], scores, -1e30)
    row_max = jnp.max(scores, axis=2, keepdims=True)
    weights = jnp.exp(scores - row_max)
    row_sum = jnp.sum(weights, axis=2, keepdims=True)
    return weights / row_sum


def dot_rows(left, right):
    return lax.dot_general(left, right, (((1,), (1,)), ((), ())), preferred_element_type=f32)


def dot_tokens(left, right):
    return lax.dot_general(left, right, (((0,), (0,)), ((), ())), preferred_element_type=f32)


def per_device(tokens, text_gaps, image_runs, gains, w_qkv, w_out, cotangent):
    scale = HS ** (-0.5)
    group_index = lax.axis_index("grp")
    tp_index = lax.axis_index("tp")
    seq_index = lax.axis_index("seq")
    x_index, z_index = tp_index // 4, tp_index % 4
    y_index, core = seq_index // 2, seq_index % 2
    x_rows = tokens[0, 0]
    row_count, width = x_rows.shape
    w_parts = jnp.transpose(w_qkv[0], (1, 0, 2))
    head_cols = w_parts.shape[2]
    head_count = head_cols // HS
    out_w = w_out[0]
    gain_row = gains[0].astype(f32)
    slot_count = row_count * 8
    text_place, image_place = place_tokens(text_gaps[0], image_runs[0], slot_count, LI)
    own_place = jnp.where(group_index == 0, text_place, image_place)
    other_place = jnp.where(group_index == 0, image_place, text_place)
    key_place = jnp.concatenate([own_place, other_place], axis=0)
    valid_all = (own_place < far_place).astype(f32)
    valid_rows = lax.dynamic_slice_in_dim(valid_all, tp_index * row_count, row_count, 0)[:, None]

    grad_rows = cotangent[0, 0] * valid_rows.astype(bf16)
    grad_full = lax.all_gather(grad_rows, "tp", axis=0, tiled=True)
    x_float = x_rows.astype(f32)
    inv_rms = lax.rsqrt(jnp.mean(x_float * x_float, axis=1, keepdims=True) + 1e-05)
    normed = (x_float * inv_rms * gain_row).astype(bf16)
    half = width // 2
    normed_full = jnp.zeros((slot_count, width), bf16)
    for index, side, block in gather_blocks(normed, x_index, z_index):
        normed_full = lax.dynamic_update_slice(
            normed_full, block, (index * row_count, side * half)
        )

    pair_rows = width // 4
    chunks = [lax.dynamic_slice_in_dim(normed_full, y_index * pair_rows, pair_rows, 1)]
    for k in STEPS:
        sent = lax.dynamic_slice_in_dim(normed_full, (y_index + k) % 4 * pair_rows, pair_rows, 1)
        chunks.append(lax.ppermute(sent, "seq", y_shift(k)))

    def project(part):
        return jnp.dot(normed_full, w_parts[part], preferred_element_type=f32).astype(bf16)

    own_kv = jnp.stack([project(1), project(2)])
    other_kv = lax.ppermute(own_kv, "grp", [(0, 1), (1, 0)])
    own_q = project(0).reshape(slot_count, head_count, HS)
    all_kv = jnp.concatenate([own_kv, other_kv], axis=1)
    all_keys = all_kv[0].reshape(2 * slot_count, head_count, HS)
    all_values = all_kv[1].reshape(2 * slot_count, head_count, HS)
    attn = attend_rows(own_q, own_place, all_keys, key_place, scale)
    attn_b = attn.astype(bf16)
    mixed = jnp.einsum("hqk,khd->qhd", attn_b, all_values, preferred_element_type=f32).astype(bf16)
    mixed_flat = mixed.reshape(slot_count, head_cols)
    proj_rows = lax.psum_scatter(
        dot_rows(mixed_flat, out_w).astype(bf16), "tp", scatter_dimension=0, tiled=True
    ).astype(f32)
    layer_out = ((x_float + proj_rows) * valid_rows).astype(bf16)
    grad_mixed = jnp.dot(grad_full, out_w, preferred_element_type=f32).astype(bf16)
    out_share = lax.psum_scatter(
        dot_tokens(grad_full, mixed_flat).astype(bf16), "seq", scatter_dimension=0, tiled=True
    ).astype(f32)

    grad_heads = grad_mixed.reshape(slot_count, head_count, HS)
    value_grad = jnp.einsum("hqk,qhd->khd", attn_b, grad_heads, preferred_element_type=f32)
    weight_grad = jnp.einsum("qhd,khd->hqk", grad_heads, all_values, preferred_element_type=f32)
    row_dot = jnp.einsum("qhd,qhd->hq", grad_heads, mixed, preferred_element_type=f32)[:, :, None]
    score_grad = (attn * (weight_grad - row_dot)).astype(bf16)
    query_grad = jnp.einsum("hqk,khd->qhd", score_grad, all_keys, preferred_element_type=f32) * scale
    key_grad = jnp.einsum("hqk,qhd->khd", score_grad, own_q, preferred_element_type=f32) * scale
    kv_grad = jnp.stack([key_grad, value_grad]).reshape(2, 2 * slot_count, head_cols)
    back = lax.ppermute(kv_grad[:, slot_count:].astype(bf16), "grp", [(0, 1), (1, 0)])
    own_kv_grad = (kv_grad[:, :slot_count] + back.astype(f32)).astype(bf16)
    own_q_grad = query_grad.astype(bf16).reshape(slot_count, head_cols)

    def normed_part(rows):
        part = dot_rows(own_q_grad, w_parts[0][rows])
        part = part + dot_rows(own_kv_grad[0], w_parts[1][rows])
        part = part + dot_rows(own_kv_grad[1], w_parts[2][rows])
        return part.astype(bf16)

    halves = [normed_part(slice(0, half)), normed_part(slice(half, width))]
    inv_gain = 1.0 / gain_row
    gain_term = jnp.concatenate(
        [
            jnp.sum(part.astype(f32) * normed_full[:, cols].astype(f32), axis=0)
            for part, cols in zip(halves, (slice(0, half), slice(half, width)))
        ]
    )
    gain_grad = gain_term * inv_gain
    for axis, flip in (("tp", 1), ("tp", 2), ("tp", 4), ("seq", 1), ("seq", 2), ("seq", 4)):
        gain_grad = gain_grad + lax.ppermute(gain_grad, axis, [(i, i ^ flip) for i in range(8)])
    part_shape = (8, row_count, half)
    normed_grad = jnp.concatenate(
        [
            scatter_left(halves[0].reshape(part_shape), x_index, z_index),
            scatter_right(halves[1].reshape(part_shape), x_index, z_index),
        ],
        axis=1,
    )
    scaled = gain_row * normed_grad
    x_grad = (
        grad_rows.astype(f32)
        + inv_rms * scaled
        - x_float
        * (inv_rms * inv_rms * inv_rms)
        * jnp.mean(scaled * x_float, axis=1, keepdims=True)
    )
    tokens_grad = x_grad.astype(bf16)

    q_grads = [own_q_grad] + [lax.ppermute(own_q_grad, "seq", y_shift(k)) for k in STEPS]
    kv_grads = [own_kv_grad] + [lax.ppermute(own_kv_grad, "seq", y_shift(k)) for k in STEPS]
    share = []
    for part in range(3):
        right = [q_grads[i] if part == 0 else kv_grads[i][part - 1] for i in range(4)]
        share.append(dot_tokens(jnp.concatenate(chunks, axis=0), jnp.concatenate(right, axis=0)))
    share = jnp.stack(share).reshape(3, 2, pair_rows // 2, head_cols)
    mine = lax.dynamic_index_in_dim(share, core, 1, keepdims=False)
    sent = lax.dynamic_index_in_dim(share, 1 - core, 1, keepdims=False).astype(bf16)
    qkv_share = mine + lax.ppermute(sent, "seq", CORE_SWAP).astype(f32)
    return (
        layer_out.reshape(1, 1, row_count, width),
        tokens_grad.reshape(1, 1, row_count, width),
        gain_grad.reshape(1, width),
        jnp.transpose(qkv_share, (1, 0, 2))[None],
        out_share[None],
    )


def solution(mesh):
    in_specs = (
        P("grp", "seq", "tp", None),
        P("seq", None),
        P("seq", None),
        P("grp", None),
        P("grp", None, None, "tp"),
        P("grp", None, "tp"),
        P("grp", "seq", "tp", None),
    )
    out_specs = (
        P("grp", "seq", "tp", None),
        P("grp", "seq", "tp", None),
        P("grp", None),
        P("grp", "seq", None, "tp"),
        P("grp", "seq", "tp"),
    )
    return jax.shard_map(
        per_device, mesh=mesh, in_specs=in_specs, out_specs=out_specs, check_vma=False
    )
```

time: 547 us -> 248 us (0.45)
  blocking collectives: 279 us -> 0 us
  waiting for transfers between devices: 159 us -> 94 us
  starting transfers between devices: 8.37 us -> 45.3 us
  matrix products: 36.3 us -> 51 us
  local copies, waits for them, and re-layouts: 26.7 us -> 15.1 us
    psum x1 -> x0, blocking collectives: 279 us -> none  [per_device(): gain_grad = lax.psum(gain_term, ('seq', 'tp'))]
    psum x1 -> x0, waiting for transfers between devices: 85.3 us -> none  [per_device(): lax.psum(lax.dot_general(mixed_flat, out_w, (((1,), (1,)), ((), ())), pre...]
    ppermute x4 -> x34, waiting for transfers between devices: 17.4 us -> 93.9 us  [the longest x6 17.9 us: per_device(): lax.ppermute(gain_grad, axis, [(i, i ^ flip) for i in range(8)])]
    ppermute x4 -> x34, starting transfers between devices: 8.21 us -> 45.1 us  [the longest x3 5.99 us: gather_blocks(): left_four = [left] + [lax.ppermute(left, 'tp', z_shift(k)) for k in STEPS]]
    all_gather x1, waiting for transfers between devices: 31.2 us -> 0.02 us  [per_device(): grad_full = lax.all_gather(grad_rows, 'tp', axis=0, tiled=True)]
    all_gather x1 -> x0, waiting for transfers between devices: 25.6 us -> none  [per_device(): normed_full = lax.all_gather(normed, 'tp', axis=0, tiled=True)]
    unnamed x22 -> x61, local copies, waits for them, and re-layouts: 22.4 us -> 3.44 us
    dot_general x10 -> x19, matrix products: 30.1 us -> 43.4 us  [the longest x7 19.5 us: dot_rows(): lax.dot_general(left, right, (((1,), (1,)), ((), ())), preferred_element_...]
  transfers between devices with their start and end apart: 8 -> 37, of which waited for: 6 -> 17; matrix products, arithmetic and copies ran while one was open for 12% -> 27% of each run, Pallas kernels for 0% -> 0%
where the time goes in v1:
time: 248 us; the launch traced here: 247 us
  waiting for transfers between devices  94 us (38%)
  matrix products  51 us (21%)
  starting transfers between devices  45.3 us (18%)
  other arithmetic  26.5 us (11%)
  local copies, waits for them, and re-layouts  15.1 us (6%)
  between operations  14.7 us (6%)
    dot_general x7, matrix products, dot_rows(): lax.dot_general(left, right, (((1,), (1,)), ((), ())), preferred_element_...  19.5 us
    ppermute x6, waiting for transfers between devices, per_device(): lax.ppermute(gain_grad, axis, [(i, i ^ flip) for i in range(8)])  17.9 us
    ppermute x1, waiting for transfers between devices, per_device(): lax.ppermute(kv_grad[:, slot_count:].astype(bf16), 'grp', [(0, 1), (1, 0)])  15.2 us
    ppermute x3, waiting for transfers between devices, per_device(): lax.ppermute(own_q_grad, 'seq', y_shift(k))  14 us
    dot_general x4, matrix products, dot_tokens(): lax.dot_general(left, right, (((0,), (0,)), ((), ())), preferred_element_...  11.5 us
    ppermute x1, waiting for transfers between devices, gather_blocks(): left_other = lax.ppermute(jnp.stack(left_four), 'tp', X_SWAP)  10.8 us
    ppermute x3, waiting for transfers between devices, gather_blocks(): lax.ppermute(right_pair, 'tp', z_shift(k))  9.92 us
    ppermute x1, waiting for transfers between devices, per_device(): other_kv = lax.ppermute(own_kv, 'grp', [(0, 1), (1, 0)])  8.87 us
  transfers between devices with their start and end apart: 37, of which 17 were waited for; matrix products, arithmetic and copies ran while one was open for 27% of the time, Pallas kernels for 0%

profile of v1, /device:TPU:0, one launch (start us, length us, event | category | flops | bytes accessed | tf_op | source)
XLA Modules:
  0.0 246.6 jit_solution(7012900752223143396)
XLA Ops:
  14.4 4.0 %collective-permute-start.2 = (bf16[32,2048]{1,0:T(8,128)(2,1)S(1)}, bf16[32,2048]{1,0:T(8,128)(2,1)S(1)}, u32[]{:S(2)}, u32[]{:S(2)}) collective-permute-start(bf16[32,2048]{1,0:T(8,128)(2,1)S(1)} %get-tuple-element.41), channel_id=1, source_target_pairs={{0,2},{1,3},{2,0},{3,1},{4,6},{5,7},{6,4},{7,5},{8,10},{9,11},{10,... | collective-permute-start | bytes 393224 | tf_op jit(solution)/shard_map/ppermute | solution.py:58
  22.7 2.7 %collective-permute-done.1 = bf16[32,2048]{1,0:T(8,128)(2,1)S(1)} collective-permute-done((bf16[32,2048]{1,0:T(8,128)(2,1)S(1)}, bf16[32,2048]{1,0:T(8,128)(2,1)S(1)}, u32[]{:S(2)}, u32[]{:S(2)}) %collective-permute-start.1) | collective-permute-done | bytes 131104 | tf_op jit(solution)/shard_map/ppermute | solution.py:58
  32.6 2.3 collective-permute-start.6
  36.2 10.8 %collective-permute-done.3 = bf16[4,32,2048]{2,1,0:T(8,128)(2,1)S(1)} collective-permute-done((bf16[4,32,2048]{2,1,0:T(8,128)(2,1)S(1)}, bf16[4,32,2048]{2,1,0:T(8,128)(2,1)S(1)}, u32[]{:S(2)}, u32[]{:S(2)}) %collective-permute-start.3) | collective-permute-done | bytes 524320 | tf_op jit(solution)/shard_map/ppermute | solution.py:60
  49.4 8.1 %collective-permute-done.6 = bf16[2,32,2048]{2,1,0:T(8,128)(2,1)S(1)} collective-permute-done((bf16[2,32,2048]{2,1,0:T(8,128)(2,1)S(1)}, bf16[2,32,2048]{2,1,0:T(8,128)(2,1)S(1)}, u32[]{:S(2)}, u32[]{:S(2)}) %collective-permute-start.6) | collective-permute-done | bytes 262176 | tf_op jit(solution)/shard_map/ppermute | solution.py:59
  57.7 1.8 collective-permute-done.7
  59.5 4.2 %fusion.21 = bf16[1,256,512]{2,1,0:T(8,128)(2,1)S(1)} fusion(bf16[256,4096]{1,0:T(8,128)(2,1)S(1)} %fusion.80, bf16[3,4096,512]{2,1,0:T(8,128)(2,1)} %bitcast.259), kind=kOutput, calls=%fused_computation.48 | convolution fusion | flops 1073872896 | bytes 6553600 | tf_op jit(solution)/shard_map/dot_general | solution.py:158
  65.1 3.3 %collective-permute-start.8 = (bf16[2,256,512]{2,1,0:T(8,128)(2,1)S(1)}, bf16[2,256,512]{2,1,0:T(8,128)(2,1)}, u32[]{:S(2)}, u32[]{:S(2)}) collective-permute-start(bf16[2,256,512]{2,1,0:T(8,128)(2,1)S(1)} %pad_maximum_fusion.5), channel_id=1, source_target_pairs={{0,64},{64,0},{1,65},{65,1},{2,66},{66,2},{3,67},{67,3},{4,68},{68... | collective-permute-start | bytes 1572872 | tf_op jit(solution)/shard_map/ppermute | solution.py:161
  68.5 1.9 fusion.20
  71.5 8.9 %collective-permute-done.8 = bf16[2,256,512]{2,1,0:T(8,128)(2,1)} collective-permute-done((bf16[2,256,512]{2,1,0:T(8,128)(2,1)S(1)}, bf16[2,256,512]{2,1,0:T(8,128)(2,1)}, u32[]{:S(2)}, u32[]{:S(2)}) %collective-permute-start.8) | collective-permute-done | bytes 524320 | tf_op jit(solution)/shard_map/ppermute | solution.py:161
  84.7 2.8 %fusion.98 = (f32[4,256]{1,0:T(4,128)}, f32[4,256,512]{2,1,0:T(8,128)}) fusion(pred[256,512]{1,0:T(8,128)(4,1)S(1)} %broadcast_compare_fusion, bf16[256,4,128]{0,2,1:T(8,128)(2,1)S(1)} %bitcast.285, bf16[512,4,128]{0,2,1:T(8,128)(2,1)S(1)} %bitcast.280), kind=kOutput, calls=%fused_computation.201 | convolution fusion | flops 136315392 | bytes 3018752 | tf_op jit(solution)/shard_map/sub | solution.py:104
  87.5 1.8 fusion.54
  89.3 4.8 %fusion.15 = bf16[256,512]{1,0:T(8,128)(2,1)} fusion(bf16[256,4096]{1,0:T(8,128)(2,1)} %all-gather.2.cloned.1.call-done, bf16[1,4096,512]{2,1,0:T(8,128)(2,1)} %param.12), kind=kOutput, calls=%fused_computation.43 | convolution fusion | flops 1073872896 | bytes 6553600 | tf_op jit(solution)/shard_map/dot_general | solution.py:174
  96.0 2.1 copy.52
  99.8 4.9 %convolution_convert_fusion.1 = bf16[256,4096]{1,0:T(8,128)(2,1)} fusion(bf16[256,512]{0,1:T(8,128)(2,1)S(1)} %bitcast.270, bf16[1,4096,512]{2,1,0:T(8,128)(2,1)} %param.12), kind=kOutput, calls=%fused_computation.3 | convolution fusion | flops 1074790400 | bytes 6553600 | tf_op jit(solution)/shard_map/dot_general | solution.py:110
  106.9 3.1 %collective-permute-start.26 = (bf16[256,1024]{1,0:T(8,128)(2,1)}, bf16[256,1024]{1,0:T(8,128)(2,1)}, u32[]{:S(2)}, u32[]{:S(2)}) collective-permute-start(bf16[256,1024]{1,0:T(8,128)(2,1)} %get-tuple-element.18), channel_id=1, source_target_pairs={{0,32},{8,40},{16,48},{24,56},{32,0},{40,8},{48,16},{56,24},{1,33}... | collective-permute-start | bytes 1572872 | tf_op jit(solution)/shard_map/ppermute | solution.py:155
  113.5 2.2 multiply_convert_fusion
  116.9 1.7 collective-permute-start.9
  119.1 3.3 %convolution_convert_fusion = bf16[4096,512]{1,0:T(8,128)(2,1)} fusion(bf16[256,4096]{1,0:T(8,128)(2,1)S(1)} %copy-done.3, bf16[256,512]{0,1:T(8,128)(2,1)S(1)} %bitcast.271), kind=kOutput, calls=%fused_computation.2 | convolution fusion | flops 1075838976 | bytes 6553600 | tf_op jit(solution)/shard_map/dot_general | solution.py:114
  122.4 2.4 fusion.10
  124.8 2.4 fusion.11
  127.1 15.2 %collective-permute-done.9 = bf16[2,256,512]{1,2,0:T(8,128)(2,1)} collective-permute-done((bf16[2,256,512]{1,2,0:T(8,128)(2,1)}, bf16[2,256,512]{1,2,0:T(8,128)(2,1)}, u32[]{:S(2)}, u32[]{:S(2)}) %collective-permute-start.9) | collective-permute-done | bytes 524320 | tf_op jit(solution)/shard_map/ppermute | solution.py:187
  143.6 2.4 convolution_add_fusion.1
  146.0 2.4 fusion.9
  148.4 2.5 %convolution_add_fusion.3 = f32[256,2048]{1,0:T(8,128)S(1)} fusion(f32[256,2048]{1,0:T(8,128)S(1)} %fusion.11, bf16[3,4096,512]{2,1,0:T(8,128)(2,1)} %bitcast.264, bf16[2,256,512]{1,2,0:T(8,128)(2,1)S(1)} %fusion.25), kind=kOutput, calls=%fused_computation.19 | convolution fusion | flops 537395200 | bytes 6553600 | tf_op jit(solution)/shard_map/dot_general | solution.py:110
  150.9 2.6 %multiply_reduce_fusion.1 = (f32[2048]{0:T(1024)S(1)}, f32[2048]{0:T(1024)S(1)}, bf16[256,2048]{1,0:T(8,128)(2,1)S(1)}) fusion(bf16[256,4096]{1,0:T(8,128)(2,1)S(1)} %copy-done.2, bf16[256,2048]{1,0:T(8,128)(2,1)S(1)} %fusion.9, f32[256,2048]{1,0:T(8,128)S(1)} %convolution_add_fusion.3, bf16[3,4096,512]{2,1,0:T(8,128)(2,1)} %bitcast.265, ...), kind=kOutput, calls=%fused_computation.34 | convolution fusion | flops 542109696 | bytes 8667136 | tf_op jit(solution)/shard_map/dot_general | solution.py:110
  153.7 3.7 %collective-permute-done.18 = f32[4096]{0:T(1024)S(1)} collective-permute-done((f32[4096]{0:T(1024)S(1)}, f32[4096]{0:T(1024)S(1)}, u32[]{:S(2)}, u32[]{:S(2)}) %collective-permute-start.18) | collective-permute-done | bytes 16416 | tf_op jit(solution)/shard_map/ppermute | solution.py:207
  158.3 2.6 %collective-permute-start.28 = (bf16[256,512]{0,1:T(8,128)(2,1)S(1)}, bf16[256,512]{0,1:T(8,128)(2,1)}, u32[]{:S(2)}, u32[]{:S(2)}) collective-permute-start(bf16[256,512]{0,1:T(8,128)(2,1)S(1)} %bitcast.275), channel_id=1, source_target_pairs={{0,48},{8,56},{16,0},{24,8},{32,16},{40,24},{48,32},{56,40},{1,49}... | collective-permute-start | bytes 786440 | tf_op jit(solution)/shard_map/ppermute | solution.py:226
  160.9 1.7 collective-permute-done.19
  162.9 5.5 %collective-permute-done.29 = bf16[256,512]{0,1:T(8,128)(2,1)} collective-permute-done((bf16[256,512]{0,1:T(8,128)(2,1)S(1)}, bf16[256,512]{0,1:T(8,128)(2,1)}, u32[]{:S(2)}, u32[]{:S(2)}) %collective-permute-start.29) | collective-permute-done | bytes 262176 | tf_op jit(solution)/shard_map/ppermute | solution.py:226
  168.5 8.5 %collective-permute-done.28 = bf16[256,512]{0,1:T(8,128)(2,1)} collective-permute-done((bf16[256,512]{0,1:T(8,128)(2,1)S(1)}, bf16[256,512]{0,1:T(8,128)(2,1)}, u32[]{:S(2)}, u32[]{:S(2)}) %collective-permute-start.28) | collective-permute-done | bytes 262176 | tf_op jit(solution)/shard_map/ppermute | solution.py:226
  177.0 2.9 %fusion.27 = f32[1024,512]{1,0:T(8,128)S(1)} fusion(bf16[256,512]{0,1:T(8,128)(2,1)} %collective-permute-done.29, bf16[256,512]{0,1:T(8,128)(2,1)} %collective-permute-done.28, bf16[256,512]{0,1:T(8,128)(2,1)} %collective-permute-done.27, bf16[256,512]{0,1:T(8,128)(2,1)S(1)} %bitcast.277, bf16[256,1024]{1,0:T(8,128)(2,1)} %collective-permute-done.26, ...), kind=kOutput, calls=%fused_computation.56 | convolution fusion | flops 1086324736 | bytes 5242880 | tf_op jit(solution)/shard_map/dot_general | solution.py:114
  181.5 3.3 %collective-permute-start.11 = (bf16[2,32,2048]{2,1,0:T(8,128)(2,1)S(1)}, bf16[2,32,2048]{2,1,0:T(8,128)(2,1)S(1)}, u32[]{:S(2)}, u32[]{:S(2)}) collective-permute-start(bf16[2,32,2048]{2,1,0:T(8,128)(2,1)S(1)} %get-tuple-element.21), channel_id=1, source_target_pairs={{0,3},{1,0},{2,1},{3,2},{4,7},{5,4},{6,5},{7,6},{8,11},{9,8},{10,9... | collective-permute-start | bytes 786440 | tf_op jit(solution)/shard_map/ppermute | solution.py:80
  185.7 8.9 %collective-permute-done.22 = f32[4096]{0:T(1024)S(1)} collective-permute-done((f32[4096]{0:T(1024)S(1)}, f32[4096]{0:T(1024)S(1)}, u32[]{:S(2)}, u32[]{:S(2)}) %collective-permute-start.22) | collective-permute-done | bytes 16416 | tf_op jit(solution)/shard_map/ppermute | solution.py:207
  194.6 2.0 collective-permute-start.23
  196.6 3.6 %collective-permute-done.23 = f32[4096]{0:T(1024)S(1)} collective-permute-done((f32[4096]{0:T(1024)S(1)}, f32[4096]{0:T(1024)S(1)}, u32[]{:S(2)}, u32[]{:S(2)}) %collective-permute-start.23) | collective-permute-done | bytes 16416 | tf_op jit(solution)/shard_map/ppermute | solution.py:207
  200.2 3.1 %collective-permute-start.31 = (bf16[2,256,512]{1,2,0:T(8,128)(2,1)S(1)}, bf16[2,256,512]{1,2,0:T(8,128)(2,1)S(1)}, u32[]{:S(2)}, u32[]{:S(2)}) collective-permute-start(bf16[2,256,512]{1,2,0:T(8,128)(2,1)S(1)} %fusion.25), channel_id=1, source_target_pairs={{0,48},{8,56},{16,0},{24,8},{32,16},{40,24},{48,32},{56,40},{1,49}... | collective-permute-start | bytes 1572872 | tf_op jit(solution)/shard_map/ppermute | solution.py:227
  204.4 1.9 collective-permute-start.13
  206.4 5.0 %collective-permute-done.31 = bf16[2,256,512]{1,2,0:T(8,128)(2,1)S(1)} collective-permute-done((bf16[2,256,512]{1,2,0:T(8,128)(2,1)S(1)}, bf16[2,256,512]{1,2,0:T(8,128)(2,1)S(1)}, u32[]{:S(2)}, u32[]{:S(2)}) %collective-permute-start.31) | collective-permute-done | bytes 524320 | tf_op jit(solution)/shard_map/ppermute | solution.py:227
  211.4 2.9 %collective-permute-done.30 = bf16[2,256,512]{1,2,0:T(8,128)(2,1)S(1)} collective-permute-done((bf16[2,256,512]{1,2,0:T(8,128)(2,1)S(1)}, bf16[2,256,512]{1,2,0:T(8,128)(2,1)S(1)}, u32[]{:S(2)}, u32[]{:S(2)}) %collective-permute-start.30) | collective-permute-done | bytes 524320 | tf_op jit(solution)/shard_map/ppermute | solution.py:227
  214.4 2.7 %fusion.43 = f32[1024,512]{1,0:T(8,128)S(1)} fusion(bf16[256,512]{0,1:T(8,128)(2,1)S(1)} %get-tuple-element.31, bf16[256,512]{0,1:T(8,128)(2,1)S(1)} %get-tuple-element.29, bf16[256,512]{0,1:T(8,128)(2,1)S(1)} %get-tuple-element.27, bf16[256,512]{0,1:T(8,128)(2,1)S(1)} %get-tuple-element.25, bf16[256,1024]{1,0:T(8,128)(2,1)} %collective-permute-done.26, ...), kind=kOutput, calls=%fused_computation.72 | convolution fusion | flops 1086324736 | bytes 5242880 | tf_op jit(solution)/shard_map/dot_general | solution.py:114
  217.1 2.7 %fusion.35 = f32[1024,512]{1,0:T(8,128)S(1)} fusion(bf16[256,512]{0,1:T(8,128)(2,1)S(1)} %get-tuple-element.30, bf16[256,512]{0,1:T(8,128)(2,1)S(1)} %get-tuple-element.28, bf16[256,512]{0,1:T(8,128)(2,1)S(1)} %get-tuple-element.26, bf16[256,512]{0,1:T(8,128)(2,1)S(1)} %get-tuple-element.24, bf16[256,1024]{1,0:T(8,128)(2,1)} %collective-permute-done.26, ...), kind=kOutput, calls=%fused_computation.64 | convolution fusion | flops 1086324736 | bytes 5242880 | tf_op jit(solution)/shard_map/dot_general | solution.py:114
  222.4 3.7 %collective-permute-start.16 = (bf16[32,2048]{1,0:T(8,128)(2,1)S(1)}, bf16[32,2048]{1,0:T(8,128)(2,1)S(1)}, u32[]{:S(2)}, u32[]{:S(2)}) collective-permute-start(bf16[32,2048]{1,0:T(8,128)(2,1)S(1)} %get-tuple-element.34), channel_id=1, source_target_pairs={{0,3},{1,0},{2,1},{3,2},{4,7},{5,4},{6,5},{7,6},{8,11},{9,8},{10,9... | collective-permute-start | bytes 393224 | tf_op jit(solution)/shard_map/ppermute | solution.py:93
  226.2 3.3 %collective-permute-done.17 = bf16[32,2048]{1,0:T(8,128)(2,1)S(1)} collective-permute-done((bf16[32,2048]{1,0:T(8,128)(2,1)S(1)}, bf16[32,2048]{1,0:T(8,128)(2,1)S(1)}, u32[]{:S(2)}, u32[]{:S(2)}) %collective-permute-start.17) | collective-permute-done | bytes 131104 | tf_op jit(solution)/shard_map/ppermute | solution.py:93
  230.4 2.3 collective-permute-done.15
  232.8 2.2 fusion.7
  235.0 1.9 fusion.64
  237.9 2.1 bitcast_convert_fusion
  (185 shorter events, 50.6 us)
Async XLA Ops:
  7.2 14.7 %copy-start.11 = (bf16[1,1,32,4096]{3,2,1,0:T(8,128)(2,1)S(1)}, bf16[1,1,32,4096]{3,2,1,0:T(8,128)(2,1)}, u32[]{:S(2)}) copy-start(bf16[1,1,32,4096]{3,2,1,0:T(8,128)(2,1)} %param.13) | copy-start | bytes 786436
  7.2 82.1 %all-gather.2.cloned.1.call-start = ((), (), s32[]{:S(2)}) async-start(), calls=%async_computation.3 | async-start | bytes 2359296 | tf_op jit(solution)/shard_map/all_gather | solution.py:140
  12.3 10.4 %copy-start.25 = (bf16[32]{0:T(256)(128)(2,1)}, bf16[32]{0:T(256)(128)(2,1)S(1)}, u32[]{:S(2)}) copy-start(bf16[32]{0:T(256)(128)(2,1)S(1)} %get-tuple-element.49) | copy-start | bytes 196
  14.4 8.4 %collective-permute-start.2 = (bf16[32,2048]{1,0:T(8,128)(2,1)S(1)}, bf16[32,2048]{1,0:T(8,128)(2,1)S(1)}, u32[]{:S(2)}, u32[]{:S(2)}) collective-permute-start(bf16[32,2048]{1,0:T(8,128)(2,1)S(1)} %get-tuple-element.41), channel_id=1, source_target_pairs={{0,2},{1,3},{2,0},{3,1},{4,6},{5,7},{6,4},{7,5},{8,10},{9,11},{10,... | collective-permute-start | bytes 393224 | tf_op jit(solution)/shard_map/ppermute | solution.py:58
  18.3 7.1 %collective-permute-start.1 = (bf16[32,2048]{1,0:T(8,128)(2,1)S(1)}, bf16[32,2048]{1,0:T(8,128)(2,1)S(1)}, u32[]{:S(2)}, u32[]{:S(2)}) collective-permute-start(bf16[32,2048]{1,0:T(8,128)(2,1)S(1)} %get-tuple-element.41), channel_id=1, source_target_pairs={{0,3},{1,0},{2,1},{3,2},{4,7},{5,4},{6,5},{7,6},{8,11},{9,8},{10,9... | collective-permute-start | bytes 393224 | tf_op jit(solution)/shard_map/ppermute | solution.py:58
  19.0 6.4 %collective-permute-start = (bf16[32,2048]{1,0:T(8,128)(2,1)S(1)}, bf16[32,2048]{1,0:T(8,128)(2,1)S(1)}, u32[]{:S(2)}, u32[]{:S(2)}) collective-permute-start(bf16[32,2048]{1,0:T(8,128)(2,1)S(1)} %get-tuple-element.41), channel_id=1, source_target_pairs={{0,1},{1,2},{2,3},{3,0},{4,5},{5,6},{6,7},{7,4},{8,9},{9,10},{10,1... | collective-permute-start | bytes 393224 | tf_op jit(solution)/shard_map/ppermute | solution.py:58
  20.3 10.4 %collective-permute-start.4 = (bf16[32,2048]{1,0:T(8,128)(2,1)}, bf16[32,2048]{1,0:T(8,128)(2,1)}, u32[]{:S(2)}, u32[]{:S(2)}) collective-permute-start(bf16[32,2048]{1,0:T(8,128)(2,1)} %get-tuple-element.40), channel_id=1, source_target_pairs={{0,4},{1,5},{2,6},{3,7},{4,0},{5,1},{6,2},{7,3},{8,12},{9,13},{10,... | collective-permute-start | bytes 393224 | tf_op jit(solution)/shard_map/ppermute | solution.py:57
  22.7 212.3 %reduce-scatter.3.cloned.1.call-start = ((), (), s32[]{:S(2)}) async-start(), calls=%async_computation.2 | async-start | bytes 2359296 | tf_op jit(solution)/shard_map/reduce_scatter | solution.py:170
  27.1 19.9 %collective-permute-start.3 = (bf16[4,32,2048]{2,1,0:T(8,128)(2,1)S(1)}, bf16[4,32,2048]{2,1,0:T(8,128)(2,1)S(1)}, u32[]{:S(2)}, u32[]{:S(2)}) collective-permute-start(bf16[4,32,2048]{2,1,0:T(8,128)(2,1)S(1)} %pad_maximum_fusion.4), channel_id=1, source_target_pairs={{0,4},{1,5},{2,6},{3,7},{4,0},{5,1},{6,2},{7,3},{8,12},{9,13},{10,... | collective-permute-start | bytes 1572872 | tf_op jit(solution)/shard_map/ppermute | solution.py:60
  30.0 19.4 %copy-start.16 = (bf16[32,2048]{1,0:T(8,128)(2,1)S(1)}, bf16[32,2048]{1,0:T(8,128)(2,1)}, u32[]{:S(2)}) copy-start(bf16[32,2048]{1,0:T(8,128)(2,1)} %copy-done.15) | copy-start | bytes 393220
  30.0 27.6 %copy-start.14 = (bf16[32,2048]{1,0:T(8,128)(2,1)S(1)}, bf16[32,2048]{1,0:T(8,128)(2,1)}, u32[]{:S(2)}) copy-start(bf16[32,2048]{1,0:T(8,128)(2,1)} %copy-done.13) | copy-start | bytes 393220
  31.7 17.6 %collective-permute-start.5 = (bf16[2,32,2048]{2,1,0:T(8,128)(2,1)S(1)}, bf16[2,32,2048]{2,1,0:T(8,128)(2,1)S(1)}, u32[]{:S(2)}, u32[]{:S(2)}) collective-permute-start(bf16[2,32,2048]{2,1,0:T(8,128)(2,1)S(1)} %pad_maximum_fusion.6), channel_id=1, source_target_pairs={{0,1},{1,2},{2,3},{3,0},{4,5},{5,6},{6,7},{7,4},{8,9},{9,10},{10,1... | collective-permute-start | bytes 786440 | tf_op jit(solution)/shard_map/ppermute | solution.py:59
  32.6 24.9 %collective-permute-start.6 = (bf16[2,32,2048]{2,1,0:T(8,128)(2,1)S(1)}, bf16[2,32,2048]{2,1,0:T(8,128)(2,1)S(1)}, u32[]{:S(2)}, u32[]{:S(2)}) collective-permute-start(bf16[2,32,2048]{2,1,0:T(8,128)(2,1)S(1)} %pad_maximum_fusion.6), channel_id=1, source_target_pairs={{0,3},{1,0},{2,1},{3,2},{4,7},{5,4},{6,5},{7,6},{8,11},{9,8},{10,9... | collective-permute-start | bytes 786440 | tf_op jit(solution)/shard_map/ppermute | solution.py:59
  35.0 24.5 %collective-permute-start.7 = (bf16[2,32,2048]{2,1,0:T(8,128)(2,1)S(1)}, bf16[2,32,2048]{2,1,0:T(8,128)(2,1)S(1)}, u32[]{:S(2)}, u32[]{:S(2)}) collective-permute-start(bf16[2,32,2048]{2,1,0:T(8,128)(2,1)S(1)} %pad_maximum_fusion.6), channel_id=1, source_target_pairs={{0,2},{1,3},{2,0},{3,1},{4,6},{5,7},{6,4},{7,5},{8,10},{9,11},{10,... | collective-permute-start | bytes 786440 | tf_op jit(solution)/shard_map/ppermute | solution.py:59
  47.0 16.7 %copy-start = (bf16[1,4096,3,512]{3,1,2,0:T(8,128)(2,1)S(1)}, bf16[1,4096,3,512]{3,1,2,0:T(8,128)(2,1)}, u32[]{:S(2)}) copy-start(bf16[1,4096,3,512]{3,1,2,0:T(8,128)(2,1)} %param.11) | copy-start | bytes 37748740
  59.5 45.9 %copy-start.1 = (bf16[256,4096]{1,0:T(8,128)(2,1)}, bf16[256,4096]{1,0:T(8,128)(2,1)S(1)}, u32[]{:S(2)}) copy-start(bf16[256,4096]{1,0:T(8,128)(2,1)S(1)} %fusion.80) | copy-start | bytes 6291460
  63.7 4.6 %copy-start.20 = (s32[256]{0:T(256)S(1)}, s32[256]{0:T(256)}, u32[]{:S(2)}) copy-start(s32[256]{0:T(256)} %get-tuple-element.14) | copy-start | bytes 3076
  65.1 15.3 %collective-permute-start.8 = (bf16[2,256,512]{2,1,0:T(8,128)(2,1)S(1)}, bf16[2,256,512]{2,1,0:T(8,128)(2,1)}, u32[]{:S(2)}, u32[]{:S(2)}) collective-permute-start(bf16[2,256,512]{2,1,0:T(8,128)(2,1)S(1)} %pad_maximum_fusion.5), channel_id=1, source_target_pairs={{0,64},{64,0},{1,65},{65,1},{2,66},{66,2},{3,67},{67,3},{4,68},{68... | collective-permute-start | bytes 1572872 | tf_op jit(solution)/shard_map/ppermute | solution.py:161
  71.5 13.1 %copy-start.9 = (bf16[256,512]{0,1:T(8,128)(2,1)}, bf16[256,512]{0,1:T(8,128)(2,1)S(1)}, u32[]{:S(2)}) copy-start(bf16[256,512]{0,1:T(8,128)(2,1)S(1)} %copy.54) | copy-start | bytes 786436
  104.7 133.2 %reduce-scatter.5.cloned.1.call-start = ((), (), s32[]{:S(2)}) async-start(), calls=%async_computation.4 | async-start | bytes 4718592 | tf_op jit(solution)/shard_map/reduce_scatter | solution.py:175
  106.8 6.6 %copy-start.8 = (bf16[512,4,128]{2,1,0:T(4,128)(2,1)S(1)}, bf16[512,4,128]{2,1,0:T(4,128)(2,1)}, u32[]{:S(2)}) copy-start(bf16[512,4,128]{2,1,0:T(4,128)(2,1)} %reshape_squeeze.6) | copy-start | bytes 1572868
  106.9 6.6 %copy-start.27 = (f32[4,256]{1,0:T(4,128)S(1)}, f32[4,256]{1,0:T(4,128)}, u32[]{:S(2)}) copy-start(f32[4,256]{1,0:T(4,128)} %get-tuple-element.44) | copy-start | bytes 12292
  106.9 51.4 %collective-permute-start.26 = (bf16[256,1024]{1,0:T(8,128)(2,1)}, bf16[256,1024]{1,0:T(8,128)(2,1)}, u32[]{:S(2)}, u32[]{:S(2)}) collective-permute-start(bf16[256,1024]{1,0:T(8,128)(2,1)} %get-tuple-element.18), channel_id=1, source_target_pairs={{0,32},{8,40},{16,48},{24,56},{32,0},{40,8},{48,16},{56,24},{1,33}... | collective-permute-start | bytes 1572872 | tf_op jit(solution)/shard_map/ppermute | solution.py:155
  110.0 52.7 %collective-permute-start.25 = (bf16[256,1024]{1,0:T(8,128)(2,1)}, bf16[256,1024]{1,0:T(8,128)(2,1)}, u32[]{:S(2)}, u32[]{:S(2)}) collective-permute-start(bf16[256,1024]{1,0:T(8,128)(2,1)} %get-tuple-element.16), channel_id=1, source_target_pairs={{0,48},{8,56},{16,0},{24,8},{32,16},{40,24},{48,32},{56,40},{1,49}... | collective-permute-start | bytes 1572872 | tf_op jit(solution)/shard_map/ppermute | solution.py:155
  111.1 51.8 %collective-permute-start.24 = (bf16[256,1024]{1,0:T(8,128)(2,1)}, bf16[256,1024]{1,0:T(8,128)(2,1)}, u32[]{:S(2)}, u32[]{:S(2)}) collective-permute-start(bf16[256,1024]{1,0:T(8,128)(2,1)} %get-tuple-element.17), channel_id=1, source_target_pairs={{0,16},{8,24},{16,32},{24,40},{32,48},{40,56},{48,0},{56,8},{1,17}... | collective-permute-start | bytes 1572872 | tf_op jit(solution)/shard_map/ppermute | solution.py:155
  116.9 25.5 %collective-permute-start.9 = (bf16[2,256,512]{1,2,0:T(8,128)(2,1)}, bf16[2,256,512]{1,2,0:T(8,128)(2,1)}, u32[]{:S(2)}, u32[]{:S(2)}) collective-permute-start(bf16[2,256,512]{1,2,0:T(8,128)(2,1)} %fusion.26), channel_id=1, source_target_pairs={{0,64},{64,0},{1,65},{65,1},{2,66},{66,2},{3,67},{67,3},{4,68},{68... | collective-permute-start | bytes 1572872 | tf_op jit(solution)/shard_map/ppermute | solution.py:187
  150.9 26.1 %copy-start.18 = (bf16[256,1024]{1,0:T(8,128)(2,1)S(1)}, bf16[256,1024]{1,0:T(8,128)(2,1)}, u32[]{:S(2)}) copy-start(bf16[256,1024]{1,0:T(8,128)(2,1)} %get-tuple-element.15) | copy-start | bytes 1572868
  153.6 3.8 %collective-permute-start.18 = (f32[4096]{0:T(1024)S(1)}, f32[4096]{0:T(1024)S(1)}, u32[]{:S(2)}, u32[]{:S(2)}) collective-permute-start(f32[4096]{0:T(1024)S(1)} %maximum_multiply_fusion.2), channel_id=1, source_target_pairs={{0,1},{1,0},{2,3},{3,2},{4,5},{5,4},{6,7},{7,6},{8,9},{9,8},{10,11... | collective-permute-start | bytes 49160 | tf_op jit(solution)/shard_map/ppermute | solution.py:207
  157.4 5.2 %collective-permute-start.19 = (f32[4096]{0:T(1024)S(1)}, f32[4096]{0:T(1024)S(1)}, u32[]{:S(2)}, u32[]{:S(2)}) collective-permute-start(f32[4096]{0:T(1024)S(1)} %add.319), channel_id=1, source_target_pairs={{0,2},{1,3},{2,0},{3,1},{4,6},{5,7},{6,4},{7,5},{8,10},{9,11},{10,... | collective-permute-start | bytes 49160 | tf_op jit(solution)/shard_map/ppermute | solution.py:207
  158.3 10.2 %collective-permute-start.29 = (bf16[256,512]{0,1:T(8,128)(2,1)S(1)}, bf16[256,512]{0,1:T(8,128)(2,1)}, u32[]{:S(2)}, u32[]{:S(2)}) collective-permute-start(bf16[256,512]{0,1:T(8,128)(2,1)S(1)} %bitcast.274), channel_id=1, source_target_pairs={{0,32},{8,40},{16,48},{24,56},{32,0},{40,8},{48,16},{56,24},{1,33}... | collective-permute-start | bytes 786440 | tf_op jit(solution)/shard_map/ppermute | solution.py:226
  158.3 18.7 %collective-permute-start.28 = (bf16[256,512]{0,1:T(8,128)(2,1)S(1)}, bf16[256,512]{0,1:T(8,128)(2,1)}, u32[]{:S(2)}, u32[]{:S(2)}) collective-permute-start(bf16[256,512]{0,1:T(8,128)(2,1)S(1)} %bitcast.275), channel_id=1, source_target_pairs={{0,48},{8,56},{16,0},{24,8},{32,16},{40,24},{48,32},{56,40},{1,49}... | collective-permute-start | bytes 786440 | tf_op jit(solution)/shard_map/ppermute | solution.py:226
  162.6 14.3 %collective-permute-start.27 = (bf16[256,512]{0,1:T(8,128)(2,1)S(1)}, bf16[256,512]{0,1:T(8,128)(2,1)}, u32[]{:S(2)}, u32[]{:S(2)}) collective-permute-start(bf16[256,512]{0,1:T(8,128)(2,1)S(1)} %bitcast.276), channel_id=1, source_target_pairs={{0,16},{8,24},{16,32},{24,40},{32,48},{40,56},{48,0},{56,8},{1,17}... | collective-permute-start | bytes 786440 | tf_op jit(solution)/shard_map/ppermute | solution.py:226
  162.7 17.3 %collective-permute-start.20 = (f32[4096]{0:T(1024)S(1)}, f32[4096]{0:T(1024)S(1)}, u32[]{:S(2)}, u32[]{:S(2)}) collective-permute-start(f32[4096]{0:T(1024)S(1)} %add.320), channel_id=1, source_target_pairs={{0,4},{1,5},{2,6},{3,7},{4,0},{5,1},{6,2},{7,3},{8,12},{9,13},{10,... | collective-permute-start | bytes 49160 | tf_op jit(solution)/shard_map/ppermute | solution.py:207
  179.9 26.4 %collective-permute-start.32 = (bf16[2,256,512]{1,2,0:T(8,128)(2,1)S(1)}, bf16[2,256,512]{1,2,0:T(8,128)(2,1)S(1)}, u32[]{:S(2)}, u32[]{:S(2)}) collective-permute-start(bf16[2,256,512]{1,2,0:T(8,128)(2,1)S(1)} %fusion.25), channel_id=1, source_target_pairs={{0,32},{8,40},{16,48},{24,56},{32,0},{40,8},{48,16},{56,24},{1,33}... | collective-permute-start | bytes 1572872 | tf_op jit(solution)/shard_map/ppermute | solution.py:227
  180.0 4.9 %collective-permute-start.21 = (f32[4096]{0:T(1024)S(1)}, f32[4096]{0:T(1024)S(1)}, u32[]{:S(2)}, u32[]{:S(2)}) collective-permute-start(f32[4096]{0:T(1024)S(1)} %add.321), channel_id=1, source_target_pairs={{0,8},{8,0},{16,24},{24,16},{32,40},{40,32},{48,56},{56,48},{1,9},... | collective-permute-start | bytes 49160 | tf_op jit(solution)/shard_map/ppermute | solution.py:207
  180.2 23.8 %collective-permute-start.12 = (bf16[2,32,2048]{2,1,0:T(8,128)(2,1)S(1)}, bf16[2,32,2048]{2,1,0:T(8,128)(2,1)S(1)}, u32[]{:S(2)}, u32[]{:S(2)}) collective-permute-start(bf16[2,32,2048]{2,1,0:T(8,128)(2,1)S(1)} %get-tuple-element.20), channel_id=1, source_target_pairs={{0,2},{1,3},{2,0},{3,1},{4,6},{5,7},{6,4},{7,5},{8,10},{9,11},{10,... | collective-permute-start | bytes 786440 | tf_op jit(solution)/shard_map/ppermute | solution.py:80
  181.5 22.4 %collective-permute-start.11 = (bf16[2,32,2048]{2,1,0:T(8,128)(2,1)S(1)}, bf16[2,32,2048]{2,1,0:T(8,128)(2,1)S(1)}, u32[]{:S(2)}, u32[]{:S(2)}) collective-permute-start(bf16[2,32,2048]{2,1,0:T(8,128)(2,1)S(1)} %get-tuple-element.21), channel_id=1, source_target_pairs={{0,3},{1,0},{2,1},{3,2},{4,7},{5,4},{6,5},{7,6},{8,11},{9,8},{10,9... | collective-permute-start | bytes 786440 | tf_op jit(solution)/shard_map/ppermute | solution.py:80
  184.9 19.3 %collective-permute-start.10 = (bf16[2,32,2048]{2,1,0:T(8,128)(2,1)S(1)}, bf16[2,32,2048]{2,1,0:T(8,128)(2,1)S(1)}, u32[]{:S(2)}, u32[]{:S(2)}) collective-permute-start(bf16[2,32,2048]{2,1,0:T(8,128)(2,1)S(1)} %get-tuple-element.19), channel_id=1, source_target_pairs={{0,1},{1,2},{2,3},{3,0},{4,5},{5,6},{6,7},{7,4},{8,9},{9,10},{10,1... | collective-permute-start | bytes 786440 | tf_op jit(solution)/shard_map/ppermute | solution.py:80
  184.9 9.7 %collective-permute-start.22 = (f32[4096]{0:T(1024)S(1)}, f32[4096]{0:T(1024)S(1)}, u32[]{:S(2)}, u32[]{:S(2)}) collective-permute-start(f32[4096]{0:T(1024)S(1)} %add.322), channel_id=1, source_target_pairs={{0,16},{8,24},{16,0},{24,8},{32,48},{40,56},{48,32},{56,40},{1,17}... | collective-permute-start | bytes 49160 | tf_op jit(solution)/shard_map/ppermute | solution.py:207
  194.6 5.6 %collective-permute-start.23 = (f32[4096]{0:T(1024)S(1)}, f32[4096]{0:T(1024)S(1)}, u32[]{:S(2)}, u32[]{:S(2)}) collective-permute-start(f32[4096]{0:T(1024)S(1)} %add.323), channel_id=1, source_target_pairs={{0,32},{8,40},{16,48},{24,56},{32,0},{40,8},{48,16},{56,24},{1,33}... | collective-permute-start | bytes 49160 | tf_op jit(solution)/shard_map/ppermute | solution.py:207
  200.2 11.2 %collective-permute-start.31 = (bf16[2,256,512]{1,2,0:T(8,128)(2,1)S(1)}, bf16[2,256,512]{1,2,0:T(8,128)(2,1)S(1)}, u32[]{:S(2)}, u32[]{:S(2)}) collective-permute-start(bf16[2,256,512]{1,2,0:T(8,128)(2,1)S(1)} %fusion.25), channel_id=1, source_target_pairs={{0,48},{8,56},{16,0},{24,8},{32,16},{40,24},{48,32},{56,40},{1,49}... | collective-permute-start | bytes 1572872 | tf_op jit(solution)/shard_map/ppermute | solution.py:227
  203.9 10.4 %collective-permute-start.30 = (bf16[2,256,512]{1,2,0:T(8,128)(2,1)S(1)}, bf16[2,256,512]{1,2,0:T(8,128)(2,1)S(1)}, u32[]{:S(2)}, u32[]{:S(2)}) collective-permute-start(bf16[2,256,512]{1,2,0:T(8,128)(2,1)S(1)} %fusion.25), channel_id=1, source_target_pairs={{0,16},{8,24},{16,32},{24,40},{32,48},{40,56},{48,0},{56,8},{1,17}... | collective-permute-start | bytes 1572872 | tf_op jit(solution)/shard_map/ppermute | solution.py:227
  204.0 17.5 %collective-permute-start.14 = (bf16[4,32,2048]{2,1,0:T(8,128)(2,1)S(1)}, bf16[4,32,2048]{2,1,0:T(8,128)(2,1)S(1)}, u32[]{:S(2)}, u32[]{:S(2)}) collective-permute-start(bf16[4,32,2048]{2,1,0:T(8,128)(2,1)S(1)} %dynamic-slice_bitcast_fusion), channel_id=1, source_target_pairs={{0,4},{1,5},{2,6},{3,7},{4,0},{5,1},{6,2},{7,3},{8,12},{9,13},{10,... | collective-permute-start | bytes 1572872 | tf_op jit(solution)/shard_map/ppermute | solution.py:87
  204.4 21.8 %collective-permute-start.13 = (bf16[32,2048]{1,0:T(8,128)(2,1)S(1)}, bf16[32,2048]{1,0:T(8,128)(2,1)S(1)}, u32[]{:S(2)}, u32[]{:S(2)}) collective-permute-start(bf16[32,2048]{1,0:T(8,128)(2,1)S(1)} %fusion.79), channel_id=1, source_target_pairs={{0,4},{1,5},{2,6},{3,7},{4,0},{5,1},{6,2},{7,3},{8,12},{9,13},{10,... | collective-permute-start | bytes 393224 | tf_op jit(solution)/shard_map/ppermute | solution.py:82
  221.3 11.5 %collective-permute-start.33 = (bf16[3,512,512]{2,1,0:T(8,128)(2,1)S(1)}, bf16[3,512,512]{2,1,0:T(8,128)(2,1)S(1)}, u32[]{:S(2)}, u32[]{:S(2)}) collective-permute-start(bf16[3,512,512]{2,1,0:T(8,128)(2,1)S(1)} %fusion.13), channel_id=1, source_target_pairs={{0,8},{8,0},{16,24},{24,16},{32,40},{40,32},{48,56},{56,48},{1,9},... | collective-permute-start | bytes 4718600 | tf_op jit(solution)/shard_map/ppermute | solution.py:235
  221.6 7.9 %collective-permute-start.17 = (bf16[32,2048]{1,0:T(8,128)(2,1)S(1)}, bf16[32,2048]{1,0:T(8,128)(2,1)S(1)}, u32[]{:S(2)}, u32[]{:S(2)}) collective-permute-start(bf16[32,2048]{1,0:T(8,128)(2,1)S(1)} %get-tuple-element.33), channel_id=1, source_target_pairs={{0,2},{1,3},{2,0},{3,1},{4,6},{5,7},{6,4},{7,5},{8,10},{9,11},{10,... | collective-permute-start | bytes 393224 | tf_op jit(solution)/shard_map/ppermute | solution.py:93
  222.4 8.0 %collective-permute-start.16 = (bf16[32,2048]{1,0:T(8,128)(2,1)S(1)}, bf16[32,2048]{1,0:T(8,128)(2,1)S(1)}, u32[]{:S(2)}, u32[]{:S(2)}) collective-permute-start(bf16[32,2048]{1,0:T(8,128)(2,1)S(1)} %get-tuple-element.34), channel_id=1, source_target_pairs={{0,3},{1,0},{2,1},{3,2},{4,7},{5,4},{6,5},{7,6},{8,11},{9,8},{10,9... | collective-permute-start | bytes 393224 | tf_op jit(solution)/shard_map/ppermute | solution.py:93
  226.2 6.5 %collective-permute-start.15 = (bf16[32,2048]{1,0:T(8,128)(2,1)S(1)}, bf16[32,2048]{1,0:T(8,128)(2,1)S(1)}, u32[]{:S(2)}, u32[]{:S(2)}) collective-permute-start(bf16[32,2048]{1,0:T(8,128)(2,1)S(1)} %get-tuple-element.32), channel_id=1, source_target_pairs={{0,1},{1,2},{2,3},{3,0},{4,5},{5,6},{6,7},{7,4},{8,9},{9,10},{10,1... | collective-permute-start | bytes 393224 | tf_op jit(solution)/shard_map/ppermute | solution.py:93
  (19 other events, 47.7 us)
Sparse Core Ops, SparseCore 0:
  22.8 47.9 all-gather.1
  104.8 45.7 reduce-scatter.2
  153.0 50.1 reduce-scatter.4

commit v2 on v1

v2 whole, which is shorter than its diff:
```python
import functools

import jax
import jax.numpy as jnp
from jax import lax
from jax.experimental import pallas as pl
from jax.experimental.pallas import tpu as pltpu
from jax.sharding import PartitionSpec as P

HS = 128
LI = 128
HEADS = 4
SLOTS = 256
ROWS = 32
WIDTH = 4096
HALF = 2048
COLS = 512
FAR = 1073741824
f32 = jnp.float32
bf16 = jnp.bfloat16
VMEM_LIMIT = 40 * 1024 * 1024

STEPS = (0, 1, 3, 2)


def z_shift(k):
    return [(i, (i // 4) * 4 + (i + k) % 4) for i in range(8)]


X_SWAP = [(i, i ^ 4) for i in range(8)]


def y_shift(k):
    return [(i, (i + 2 * k) % 8) for i in range(8)]


CORE_SWAP = [(i, i ^ 1) for i in range(8)]
GRP_SWAP = [(0, 1), (1, 0)]


def sds(shape, dtype):
    return jax.ShapeDtypeStruct(shape, dtype)


def call(kernel, out_shape, flops=0, nbytes=0, **kwargs):
    return pl.pallas_call(
        kernel,
        out_shape=out_shape,
        compiler_params=pltpu.CompilerParams(vmem_limit_bytes=VMEM_LIMIT),
        cost_estimate=pl.CostEstimate(flops=flops, bytes_accessed=nbytes, transcendentals=0),
        **kwargs,
    )


def whole(shape):
    return pl.BlockSpec(shape, lambda *_: (0,) * len(shape))


SMEM = pl.BlockSpec(memory_space=pltpu.SMEM)


def dot(left, right):
    return jnp.dot(left, right, preferred_element_type=f32)


def dot_rows(left, right):
    return lax.dot_general(left, right, (((1,), (1,)), ((), ())), preferred_element_type=f32)


def dot_tokens(left, right):
    return lax.dot_general(left, right, (((0,), (0,)), ((), ())), preferred_element_type=f32)


def norm_kernel(valid, x, gain, cot, n_left, n_right, c_left, c_right, inv):
    x_float = x[...].astype(f32)
    scale = lax.rsqrt(jnp.mean(x_float * x_float, axis=1, keepdims=True) + 1e-05)
    normed = (x_float * scale * gain[...].astype(f32)).astype(bf16)
    n_left[...] = normed[:, :HALF]
    n_right[...] = normed[:, HALF:]
    grad = (cot[...].astype(f32) * valid[0]).astype(bf16)
    c_left[...] = grad[:, :HALF]
    c_right[...] = grad[:, HALF:]
    inv[...] = jnp.broadcast_to(scale, (ROWS, 128))


def norm_rows(valid, x, gain, cot):
    part = sds((ROWS, HALF), bf16)
    return call(
        norm_kernel,
        [part, part, part, part, sds((ROWS, 128), f32)],
        nbytes=4 * ROWS * WIDTH * 2,
        in_specs=[SMEM] + [pl.BlockSpec(memory_space=pltpu.VMEM)] * 3,
        name="norm_rows",
    )(valid, x, gain, cot)


def gather_blocks(left, right):
    right_pair = jnp.stack([right, lax.ppermute(right, "tp", X_SWAP)])
    left_four = [left] + [lax.ppermute(left, "tp", z_shift(k)) for k in STEPS[1:]]
    right_four = [right_pair] + [lax.ppermute(right_pair, "tp", z_shift(k)) for k in STEPS[1:]]
    left_own = jnp.stack(left_four)
    left_other = lax.ppermute(left_own, "tp", X_SWAP)
    return [left_own, left_other] + right_four


def place_pieces(pieces, whole_ref):
    left_own, left_other = pieces[:2]
    for slot in range(4):
        rows = pl.ds(slot * ROWS, ROWS)
        other = pl.ds((4 + slot) * ROWS, ROWS)
        whole_ref[rows, :HALF] = left_own[slot]
        whole_ref[other, :HALF] = left_other[slot]
        whole_ref[rows, HALF:] = pieces[2 + slot][0]
        whole_ref[other, HALF:] = pieces[2 + slot][1]


PIECE_SHAPES = [(4, ROWS, HALF)] * 2 + [(2, ROWS, HALF)] * 4


def scatter_left(own, sends):
    total = own.astype(f32)
    for k, sent in zip(STEPS[1:], sends):
        total = total + lax.ppermute(sent, "tp", z_shift(-k)).astype(f32)
    return total[0] + lax.ppermute(total[1].astype(bf16), "tp", X_SWAP).astype(f32)


def scatter_right(own, sent):
    four = own.astype(f32) + lax.ppermute(sent, "tp", X_SWAP).astype(f32)
    total = four[0]
    for slot in range(1, 4):
        came = lax.ppermute(four[slot].astype(bf16), "tp", z_shift(-STEPS[slot]))
        total = total + came.astype(f32)
    return total


def gather_dot_kernel(*refs):
    pieces, weight, full, out = refs[:6], refs[6], refs[7], refs[8]
    first = functools.reduce(
        jnp.logical_and, [pl.program_id(i) == 0 for i in range(2)]
    )

    @pl.when(first)
    def _():
        place_pieces(pieces, full)

    out[0] = dot(full[...], weight[0]).astype(bf16)


def gather_dot(pieces, weights, parts):
    count = len(parts)
    block = 256
    low = parts[0]
    return call(
        gather_dot_kernel,
        [sds((SLOTS, WIDTH), bf16), sds((count, SLOTS, COLS), bf16)],
        flops=2 * count * SLOTS * WIDTH * COLS,
        nbytes=count * WIDTH * COLS * 2 + 2 * SLOTS * WIDTH * 2,
        grid=(count, COLS // block),
        in_specs=[whole(s) for s in PIECE_SHAPES]
        + [pl.BlockSpec((1, WIDTH, block), lambda p, j: (p + low, 0, j))],
        out_specs=[
            whole((SLOTS, WIDTH)),
            pl.BlockSpec((1, SLOTS, block), lambda p, j: (p, 0, j)),
        ],
        name="gather_dot",
    )(*pieces, weights)


def one_dot_kernel(full, weight, out):
    out[...] = dot(full[...], weight[0]).astype(bf16)


def one_dot(full, weights, part):
    block = 256
    return call(
        one_dot_kernel,
        sds((SLOTS, COLS), bf16),
        flops=2 * SLOTS * WIDTH * COLS,
        nbytes=WIDTH * COLS * 2 + SLOTS * WIDTH * 2,
        grid=(COLS // block,),
        in_specs=[
            whole((SLOTS, WIDTH)),
            pl.BlockSpec((1, WIDTH, block), lambda j: (part, 0, j)),
        ],
        out_specs=pl.BlockSpec((SLOTS, block), lambda j: (0, j)),
        name="one_dot",
    )(full, weights)


def back_kernel(count, left_half, with_gain, *refs):
    lefts, weight = refs[:count], refs[count]
    refs = refs[count + 1:]
    total = dot_rows(lefts[0][...], weight[0])
    for part in range(1, count):
        total = total + dot_rows(lefts[part][...], weight[part])
    rounded = total.astype(bf16)
    if with_gain:
        normed, refs = refs[0], refs[1:]
        refs[-1][...] = jnp.sum(
            rounded.astype(f32) * normed[...].astype(f32), axis=0, keepdims=True
        )
    for xbit in range(2):
        for slot in range(4):
            start = (xbit * 4 + slot) * ROWS
            block = rounded[start:start + ROWS]
            if left_half:
                refs[slot][xbit] = block
            else:
                refs[xbit][slot] = block


def back_dot(lefts, weights, left_half, normed=None):
    count = len(lefts)
    block = 512
    first = 0 if left_half else HALF // block
    with_gain = normed is not None
    operands = list(lefts) + [weights]
    in_specs = [whole((SLOTS, COLS))] * count + [
        pl.BlockSpec((count, block, COLS), lambda j: (0, j + first, 0))
    ]
    if with_gain:
        operands.append(normed)
        in_specs.append(pl.BlockSpec((SLOTS, block), lambda j: (0, j + first)))
    lead, outs = (2, 4) if left_half else (4, 2)
    out_shape = [sds((lead, ROWS, HALF), bf16)] * outs
    out_specs = [pl.BlockSpec((lead, ROWS, block), lambda j: (0, 0, j))] * outs
    if with_gain:
        out_shape = out_shape + [sds((1, HALF), f32)]
        out_specs = out_specs + [pl.BlockSpec((1, block), lambda j: (0, j))]
    return call(
        functools.partial(back_kernel, count, left_half, with_gain),
        out_shape,
        flops=2 * count * SLOTS * HALF * COLS,
        nbytes=count * HALF * COLS * 2 + 2 * SLOTS * HALF * 2,
        grid=(HALF // block,),
        in_specs=in_specs,
        out_specs=out_specs,
        name="back_dot",
    )(*operands)


def slot_of(row, x_index, z_index):
    block = row // ROWS
    xbit = block // 4
    slot = block - xbit * 4
    back = jnp.where(slot == 2, 3, jnp.where(slot == 3, 2, slot))
    x_from = jnp.where(xbit == 0, x_index, 1 - x_index)
    z_from = z_index - back
    z_from = jnp.where(z_from < 0, z_from + 4, z_from)
    return (x_from * 4 + z_from) * ROWS + (row - block * ROWS)


def places(meta, rows, is_text):
    slot = slot_of(rows, meta[10], meta[11])
    text = slot
    end = jnp.int32(0)
    for run in range(4):
        end = end + meta[run]
        text = text + jnp.where(slot >= end, meta[5 + run], 0)
    image = slot + meta[0]
    end = jnp.int32(0)
    for run in range(3):
        end = end + meta[5 + run]
        image = image + jnp.where(slot >= end, meta[run + 1], 0)
    image = jnp.where(slot < LI, image, FAR)
    return jnp.where(is_text, text, image)


def admitted(meta):
    group = meta[9]
    query = places(meta, lax.broadcasted_iota(jnp.int32, (SLOTS, 1), 0), group == 0)
    key_row = lax.broadcasted_iota(jnp.int32, (1, SLOTS), 1)
    own = places(meta, key_row, group == 0)
    other = places(meta, key_row, group != 0)
    return own <= query, other <= query


def head_attn(query, own_key, other_key, own_ok, other_ok):
    scale = HS ** (-0.5)
    own = jnp.where(own_ok, dot_rows(query, own_key) * scale, -1e30)
    other = jnp.where(other_ok, dot_rows(query, other_key) * scale, -1e30)
    row_max = jnp.maximum(
        jnp.max(own, axis=1, keepdims=True), jnp.max(other, axis=1, keepdims=True)
    )
    own = jnp.exp(own - row_max)
    other = jnp.exp(other - row_max)
    row_sum = jnp.sum(own, axis=1, keepdims=True) + jnp.sum(other, axis=1, keepdims=True)
    share = 1.0 / row_sum
    return own * share, other * share


def forward_kernel(meta, query, own_kv, other_kv, mixed):
    own_ok, other_ok = admitted(meta)
    for head in range(HEADS):
        cols = slice(head * HS, (head + 1) * HS)
        own, other = head_attn(
            query[:, cols], own_kv[0, :, cols], other_kv[0, :, cols], own_ok, other_ok
        )
        total = dot(own.astype(bf16), own_kv[1, :, cols])
        total = total + dot(other.astype(bf16), other_kv[1, :, cols])
        mixed[:, cols] = total.astype(bf16)


def backward_kernel(meta, query, own_kv, other_kv, mixed, grad, q_grad, own_grad, other_grad):
    scale = HS ** (-0.5)
    own_ok, other_ok = admitted(meta)
    for head in range(HEADS):
        cols = slice(head * HS, (head + 1) * HS)
        q, g = query[:, cols], grad[:, cols]
        row_dot = jnp.sum(g.astype(f32) * mixed[:, cols].astype(f32), axis=1, keepdims=True)
        attns = head_attn(q, own_kv[0, :, cols], other_kv[0, :, cols], own_ok, other_ok)
        dq = None
        for attn, kv, kv_grad in zip(attns, (own_kv, other_kv), (own_grad, other_grad)):
            value_grad = dot_tokens(attn.astype(bf16), g)
            weight_grad = dot_rows(g, kv[1, :, cols])
            score_grad = (attn * (weight_grad - row_dot)).astype(bf16)
            part = dot(score_grad, kv[0, :, cols])
            dq = part if dq is None else dq + part
            key_grad = dot_tokens(score_grad, q) * scale
            kv_grad[0, :, cols] = key_grad.astype(kv_grad.dtype)
            kv_grad[1, :, cols] = value_grad.astype(kv_grad.dtype)
        q_grad[:, cols] = (dq * scale).astype(bf16)


ATTN_FLOPS = 2 * HEADS * SLOTS * 2 * SLOTS * HS
VMEM = pl.BlockSpec(memory_space=pltpu.VMEM)


def attend_forward(meta, query, own_kv, other_kv):
    return call(
        forward_kernel,
        sds((SLOTS, COLS), bf16),
        flops=4 * ATTN_FLOPS,
        nbytes=6 * SLOTS * COLS * 2,
        in_specs=[SMEM] + [VMEM] * 3,
        out_specs=VMEM,
        name="attend_forward",
    )(meta, query, own_kv, other_kv)


def attend_backward(meta, query, own_kv, other_kv, mixed, grad):
    kv = (2, SLOTS, COLS)
    return call(
        backward_kernel,
        [sds((SLOTS, COLS), bf16), sds(kv, f32), sds(kv, bf16)],
        flops=8 * ATTN_FLOPS,
        nbytes=12 * SLOTS * COLS * 2,
        in_specs=[SMEM] + [VMEM] * 5,
        out_specs=[VMEM] * 3,
        name="attend_backward",
    )(meta, query, own_kv, other_kv, mixed, grad)


def out_kernel(order, grad, mixed, sent, kept):
    share = dot_tokens(grad[...], mixed[...]).astype(bf16)

    @pl.when(pl.program_id(0) < 4)
    def _():
        sent[0] = share

    @pl.when(pl.program_id(0) >= 4)
    def _():
        kept[0] = share


def out_weight_parts(order, grad_full, mixed):
    return call(
        out_kernel,
        [sds((4, COLS, COLS), bf16)] * 2,
        flops=2 * SLOTS * WIDTH * COLS,
        nbytes=SLOTS * WIDTH * 2 + WIDTH * COLS * 2,
        grid_spec=pltpu.PrefetchScalarGridSpec(
            num_scalar_prefetch=1,
            grid=(8,),
            in_specs=[
                pl.BlockSpec((SLOTS, COLS), lambda i, order: (0, order[i])),
                pl.BlockSpec((SLOTS, COLS), lambda i, order: (0, 0)),
            ],
            out_specs=[
                pl.BlockSpec((1, COLS, COLS), lambda i, order: (jnp.minimum(i, 3), 0, 0)),
                pl.BlockSpec((1, COLS, COLS), lambda i, order: (jnp.maximum(i - 4, 0), 0, 0)),
            ],
        ),
        name="out_weight_parts",
    )(order, grad_full, mixed)


def share_kernel(core, *refs):
    chunks, grads, sent, mine = refs[:4], refs[4:8], refs[8], refs[9]
    total = dot_tokens(chunks[0][...], grads[0][0])
    for chunk, grad in zip(chunks[1:], grads[1:]):
        total = total + dot_tokens(chunk[...], grad[0])

    @pl.when(pl.program_id(0) == 0)
    def _():
        sent[0] = total.astype(bf16)

    @pl.when(pl.program_id(0) == 1)
    def _():
        mine[0] = total


def qkv_weight_parts(core, chunks, grads):
    count = grads[0].shape[0]
    return call(
        share_kernel,
        [sds((count, COLS, COLS), bf16), sds((count, COLS, COLS), f32)],
        flops=2 * count * 4 * SLOTS * 2 * COLS * COLS,
        nbytes=8 * SLOTS * COLS * 2 * (count + 1) + count * COLS * COLS * 6,
        grid_spec=pltpu.PrefetchScalarGridSpec(
            num_scalar_prefetch=1,
            grid=(2, count),
            in_specs=[
                pl.BlockSpec((SLOTS, COLS), lambda i, p, core: (0, jnp.abs(core[0] - 1 + i)))
            ]
            * 4
            + [pl.BlockSpec((1, SLOTS, COLS), lambda i, p, core: (p, 0, 0))] * 4,
            out_specs=[
                pl.BlockSpec(
                    (1, COLS, COLS),
                    lambda i, p, core: (jnp.where(i == 0, p, count - 1), 0, 0),
                ),
                pl.BlockSpec(
                    (1, COLS, COLS), lambda i, p, core: (jnp.where(i == 0, 0, p), 0, 0)
                ),
            ],
        ),
        name="qkv_weight_parts",
    )(core, *chunks, *grads)


def per_device(tokens, text_gaps, image_runs, gains, w_qkv, w_out, cotangent):
    group = lax.axis_index("grp")
    tp_index = lax.axis_index("tp")
    seq_index = lax.axis_index("seq")
    x_index, z_index = tp_index // 4, tp_index % 4
    y_index, core = seq_index // 2, seq_index % 2
    x_rows = tokens[0, 0]
    w_parts = jnp.transpose(w_qkv[0], (1, 0, 2))
    gain_row = gains.astype(f32)
    valid = jnp.where((group == 0) | (tp_index * ROWS < LI), 1.0, 0.0).astype(f32)
    meta = jnp.concatenate(
        [text_gaps[0], image_runs[0], jnp.stack([group, x_index, z_index]).astype(jnp.int32)]
    )

    n_left, n_right, c_left, c_right, inv = norm_rows(
        valid.reshape(1), x_rows, gains, cotangent[0, 0]
    )
    inv_rms = inv[:, :1]
    pieces = gather_blocks(n_left, n_right)
    grad_pieces = gather_blocks(c_left, c_right)
    normed_full, own_kv = gather_dot(pieces, w_parts, (1, 2))
    other_kv = lax.ppermute(own_kv, "grp", GRP_SWAP)
    query = one_dot(normed_full, w_parts, 0)

    chunks = []
    for k in STEPS:
        sent = lax.dynamic_slice_in_dim(normed_full, (y_index + k) % 4 * 1024, 1024, 1)
        chunks.append(lax.ppermute(sent, "seq", y_shift(k)) if k else sent)

    mixed = attend_forward(meta, query, own_kv, other_kv)
    grad_full, grad_mixed = gather_dot(grad_pieces, w_out, (0,))

    def summed(lefts, weights, normed=None):
        left = back_dot(lefts, weights, True, normed)
        right = back_dot(lefts, weights, False, normed)
        total_left = scatter_left(left[0], left[1:4])
        total_right = scatter_right(right[0], right[1])
        return jnp.concatenate([total_left, total_right], axis=1), left[4:], right[2:]

    x_float = x_rows.astype(f32)
    proj_rows, _, _ = summed([mixed], w_out)
    layer_out = ((x_float + proj_rows) * valid).astype(bf16)

    q_grad, own_part, other_part = attend_backward(
        meta, query, own_kv, other_kv, mixed, grad_mixed[0]
    )
    back = lax.ppermute(other_part, "grp", GRP_SWAP)
    q_grads = [q_grad] + [lax.ppermute(q_grad, "seq", y_shift(k)) for k in STEPS[1:]]
    kv_grad = (own_part + back.astype(f32)).astype(bf16)
    kv_grads = [kv_grad] + [lax.ppermute(kv_grad, "seq", y_shift(k)) for k in STEPS[1:]]

    back_y = jnp.stack([(y_index - k) % 4 for k in STEPS]) * 2
    order = jnp.concatenate([back_y + 1 - core, back_y + core]).astype(jnp.int32)
    out_sent, out_kept = out_weight_parts(order, grad_full, mixed)
    out_came = lax.ppermute(out_sent, "seq", CORE_SWAP)
    out_share = out_kept[0].astype(f32) + out_came[0].astype(f32)
    for slot in range(1, 4):
        term = (out_kept[slot].astype(f32) + out_came[slot].astype(f32)).astype(bf16)
        out_share = out_share + lax.ppermute(term, "seq", y_shift(-STEPS[slot])).astype(f32)

    normed_grad, gain_left, gain_right = summed(
        [q_grad, kv_grad[0], kv_grad[1]], w_parts, normed_full
    )
    gain_grad = jnp.concatenate([gain_left[0], gain_right[0]], axis=1) / gain_row
    for axis, flip in (("tp", 1), ("tp", 2), ("tp", 4), ("seq", 1), ("seq", 2), ("seq", 4)):
        gain_grad = gain_grad + lax.ppermute(gain_grad, axis, [(i, i ^ flip) for i in range(8)])
    scaled = gain_row * normed_grad
    x_grad = (
        cotangent[0, 0].astype(f32) * valid
        + inv_rms * scaled
        - x_float
        * (inv_rms * inv_rms * inv_rms)
        * jnp.mean(scaled * x_float, axis=1, keepdims=True)
    )
    tokens_grad = x_grad.astype(bf16)

    core_ref = core.reshape(1).astype(jnp.int32)
    q_sent, q_mine = qkv_weight_parts(core_ref, chunks, [g[None] for g in q_grads])
    q_share = q_mine + lax.ppermute(q_sent, "seq", CORE_SWAP).astype(f32)
    kv_sent, kv_mine = qkv_weight_parts(core_ref, chunks, kv_grads)
    kv_share = kv_mine + lax.ppermute(kv_sent, "seq", CORE_SWAP).astype(f32)
    qkv_share = jnp.concatenate([q_share, kv_share], axis=0)
    return (
        layer_out[None, None],
        tokens_grad[None, None],
        gain_grad,
        jnp.transpose(qkv_share, (1, 0, 2))[None],
        out_share[None],
    )


def solution(mesh):
    in_specs = (
        P("grp", "seq", "tp", None),
        P("seq", None),
        P("seq", None),
        P("grp", None),
        P("grp", None, None, "tp"),
        P("grp", None, "tp"),
        P("grp", "seq", "tp", None),
    )
    out_specs = (
        P("grp", "seq", "tp", None),
        P("grp", "seq", "tp", None),
        P("grp", None),
        P("grp", "seq", None, "tp"),
        P("grp", "seq", "tp"),
    )
    return jax.shard_map(
        per_device, mesh=mesh, in_specs=in_specs, out_specs=out_specs, check_vma=False
    )
```

time: 248 us -> 240 us (0.968)
  matrix products: 51 us -> 0 us
  Pallas kernels: 0 us -> 42.9 us
  starting transfers between devices: 45.3 us -> 73.9 us
  other arithmetic: 26.5 us -> 8.7 us
  between operations: 14.7 us -> 1.26 us
  waiting for transfers between devices: 94 us -> 106 us
  local copies, waits for them, and re-layouts: 15.1 us -> 5.66 us
    dot_general x20 -> x0, matrix products: 48.2 us -> none  [the longest x7 19.5 us: dot_rows(): lax.dot_general(left, right, (((1,), (1,)), ((), ())), preferred_element_...]
    pallas_call x0 -> x13, Pallas kernels: none -> 42.9 us  [the longest x4 13 us: back_dot(): call(functools.partial(back_kernel, count, left_half, with_gain), out_sha...]
    ppermute x24 -> x41, starting transfers between devices: 35.1 us -> 55.7 us  [the longest x6 10.6 us: gather_blocks(): lax.ppermute(left, 'tp', z_shift(k))]
    ppermute x24 -> x41, waiting for transfers between devices: 66.1 us -> 82.8 us  [the longest x3 19.4 us: per_device(): lax.ppermute(term, 'seq', y_shift(-STEPS[slot])).astype(f32)]
    ppermute x6, waiting for transfers between devices: 17.9 us -> 8.18 us  [per_device(): lax.ppermute(gain_grad, axis, [(i, i ^ flip) for i in range(8)])]
    ppermute x3 -> x6, waiting for transfers between devices: 9.92 us -> 15.1 us  [gather_blocks(): lax.ppermute(right_pair, 'tp', z_shift(k))]
    another operation x6 -> x4, other arithmetic: 4.99 us -> 0.44 us
    ppermute x6, starting transfers between devices: 4.06 us -> 8.42 us  [per_device(): lax.ppermute(gain_grad, axis, [(i, i ^ flip) for i in range(8)])]
  transfers between devices with their start and end apart: 37 -> 55, of which waited for: 17 -> 22; matrix products, arithmetic and copies ran while one was open for 27% -> 3% of each run, Pallas kernels for 0% -> 15%
where the time goes in v2:
time: 240 us; the launch traced here: 239 us
  waiting for transfers between devices  106 us (44%)
  starting transfers between devices  73.9 us (31%)
  Pallas kernels  42.9 us (18%)
  other arithmetic  8.7 us (4%)
  local copies, waits for them, and re-layouts  5.66 us (2%)
    ppermute x3, waiting for transfers between devices, per_device(): lax.ppermute(term, 'seq', y_shift(-STEPS[slot])).astype(f32)  19.4 us
    ppermute x3, waiting for transfers between devices, per_device(): chunks.append(lax.ppermute(sent, 'seq', y_shift(k)) if k else sent)  16.1 us
    ppermute x6, waiting for transfers between devices, gather_blocks(): lax.ppermute(right_pair, 'tp', z_shift(k))  15.1 us
    ppermute x2, waiting for transfers between devices, scatter_left(): lax.ppermute(total[1].astype(bf16), 'tp', X_SWAP).astype(f32)  14.2 us
    pallas_call x4, Pallas kernels, back_dot(): call(functools.partial(back_kernel, count, left_half, with_gain), out_sha...  13 us
    ppermute x6, waiting for transfers between devices, scatter_left(): total = total + lax.ppermute(sent, 'tp', z_shift(-k)).astype(f32)  10.8 us
    ppermute x6, starting transfers between devices, gather_blocks(): lax.ppermute(left, 'tp', z_shift(k))  10.6 us
    ppermute x6, starting transfers between devices, scatter_right(): came = lax.ppermute(four[slot].astype(bf16), 'tp', z_shift(-STEPS[slot]))  9.31 us
  transfers between devices with their start and end apart: 55, of which 22 were waited for; matrix products, arithmetic and copies ran while one was open for 3% of the time, Pallas kernels for 15%

profile of v2, /device:TPU:0, one launch (start us, length us, event | category | flops | bytes accessed | tf_op | source)
XLA Modules:
  0.0 238.5 jit_solution(8484258825842926091)
XLA Ops:
  3.5 4.0 %collective-permute-start.2 = (bf16[32,2048]{1,0:T(8,128)(2,1)S(1)}, bf16[32,2048]{1,0:T(8,128)(2,1)S(1)}, u32[]{:S(2)}, u32[]{:S(2)}) collective-permute-start(bf16[32,2048]{1,0:T(8,128)(2,1)S(1)} %get-tuple-element.37), channel_id=1, source_target_pairs={{0,2},{1,3},{2,0},{3,1},{4,6},{5,7},{6,4},{7,5},{8,10},{9,11},{10,... | collective-permute-start | bytes 393224 | tf_op jit(solution)/shard_map/ppermute | solution.py:99
  11.4 3.2 %collective-permute-done.1 = bf16[32,2048]{1,0:T(8,128)(2,1)S(1)} collective-permute-done((bf16[32,2048]{1,0:T(8,128)(2,1)S(1)}, bf16[32,2048]{1,0:T(8,128)(2,1)S(1)}, u32[]{:S(2)}, u32[]{:S(2)}) %collective-permute-start.1) | collective-permute-done | bytes 131104 | tf_op jit(solution)/shard_map/ppermute | solution.py:99
  14.7 1.6 collective-permute-start.3
  16.3 2.5 %collective-permute-start.19 = (bf16[32,2048]{1,0:T(8,128)(2,1)S(1)}, bf16[32,2048]{1,0:T(8,128)(2,1)S(1)}, u32[]{:S(2)}, u32[]{:S(2)}) collective-permute-start(bf16[32,2048]{1,0:T(8,128)(2,1)S(1)} %get-tuple-element.48), channel_id=1, source_target_pairs={{0,2},{1,3},{2,0},{3,1},{4,6},{5,7},{6,4},{7,5},{8,10},{9,11},{10,... | collective-permute-start | bytes 393224 | tf_op jit(solution)/shard_map/ppermute | solution.py:99
  21.9 1.9 collective-permute-done.19
  23.7 3.0 %collective-permute-start.6 = (bf16[2,32,2048]{2,1,0:T(8,128)(2,1)S(1)}, bf16[2,32,2048]{2,1,0:T(8,128)(2,1)S(1)}, u32[]{:S(2)}, u32[]{:S(2)}) collective-permute-start(bf16[2,32,2048]{2,1,0:T(8,128)(2,1)S(1)} %pad_maximum_fusion.2.refs_2_), channel_id=1, source_target_pairs={{0,3},{1,0},{2,1},{3,2},{4,7},{5,4},{6,5},{7,6},{8,11},{9,8},{10,9... | collective-permute-start | bytes 786440 | tf_op jit(solution)/shard_map/ppermute | solution.py:100
  28.1 8.8 %collective-permute-done.5.refs_3_ = bf16[2,32,2048]{2,1,0:T(8,128)(2,1)S(1)} collective-permute-done((bf16[2,32,2048]{2,1,0:T(8,128)(2,1)S(1)}, bf16[2,32,2048]{2,1,0:T(8,128)(2,1)S(1)}, u32[]{:S(2)}, u32[]{:S(2)}) %collective-permute-start.5) | collective-permute-done | bytes 262176 | tf_op jit(solution)/shard_map/ppermute | solution.py:100
  37.5 6.4 %gather_dot.2 = (bf16[256,4096]{1,0:T(8,128)(2,1)S(1)}, bf16[2,256,512]{2,1,0:T(8,128)(2,1)}) custom-call(bf16[4,32,2048]{2,1,0:T(8,128)(2,1)S(1)} %pad_maximum_fusion.refs_0_, bf16[4,32,2048]{2,1,0:T(8,128)(2,1)S(1)} %collective-permute-done.3.refs_1_, bf16[2,32,2048]{2,1,0:T(8,128)(2,1)S(1)} %pad_maximum_fusion.2.refs_2_, ...), custom_call_target="tpu_custom_call" | custom-call | flops 2147483648 | bytes 12582912 | tf_op jit(solution)/shard_map/gather_dot/pallas_call | solution.py:153
  43.9 3.0 %collective-permute-start.8 = (bf16[2,256,512]{2,1,0:T(8,128)(2,1)}, bf16[2,256,512]{2,1,0:T(8,128)(2,1)}, u32[]{:S(2)}, u32[]{:S(2)}) collective-permute-start(bf16[2,256,512]{2,1,0:T(8,128)(2,1)} %get-tuple-element.40.own_kv), channel_id=1, source_target_pairs={{0,64},{64,0},{1,65},{65,1},{2,66},{66,2},{3,67},{67,3},{4,68},{68... | collective-permute-start | bytes 1572872 | tf_op jit(solution)/shard_map/ppermute | solution.py:453
  47.1 3.2 %collective-permute-start.23 = (bf16[2,32,2048]{2,1,0:T(8,128)(2,1)S(1)}, bf16[2,32,2048]{2,1,0:T(8,128)(2,1)}, u32[]{:S(2)}, u32[]{:S(2)}) collective-permute-start(bf16[2,32,2048]{2,1,0:T(8,128)(2,1)S(1)} %pad_maximum_fusion.3.refs_2_), channel_id=1, source_target_pairs={{0,3},{1,0},{2,1},{3,2},{4,7},{5,4},{6,5},{7,6},{8,11},{9,8},{10,9... | collective-permute-start | bytes 786440 | tf_op jit(solution)/shard_map/ppermute | solution.py:100
  50.8 3.2 %one_dot.1.query = bf16[256,512]{1,0:T(8,128)(2,1)S(1)} custom-call(bf16[256,4096]{1,0:T(8,128)(2,1)S(1)} %get-tuple-element.39.full.refs_4_, bf16[3,4096,512]{2,1,0:T(8,128)(2,1)} %bitcast.121), custom_call_target="tpu_custom_call" | custom-call | flops 1073741824 | bytes 6291456 | tf_op jit(solution)/shard_map/one_dot/pallas_call | solution.py:175
  54.1 3.5 %collective-permute-done.22.refs_3_ = bf16[2,32,2048]{2,1,0:T(8,128)(2,1)} collective-permute-done((bf16[2,32,2048]{2,1,0:T(8,128)(2,1)S(1)}, bf16[2,32,2048]{2,1,0:T(8,128)(2,1)}, u32[]{:S(2)}, u32[]{:S(2)}) %collective-permute-start.22) | collective-permute-done | bytes 262176 | tf_op jit(solution)/shard_map/ppermute | solution.py:100
  57.5 1.6 collective-permute-done.23.refs_4_
  60.3 2.9 %gather_dot.3 = (bf16[256,4096]{1,0:T(8,128)(2,1)S(1)}, bf16[1,256,512]{2,1,0:T(8,128)(2,1)S(1)}) custom-call(bf16[4,32,2048]{2,1,0:T(8,128)(2,1)S(1)} %pad_maximum_fusion.1.refs_0_, bf16[4,32,2048]{2,1,0:T(8,128)(2,1)S(1)} %collective-permute-done.20.refs_1_, bf16[2,32,2048]{2,1,0:T(8,128)(2,1)S(1)} %pad_maximum_fusion.3.refs_2_, ...), custom_call_target="tpu_custom_call" | custom-call | flops 1073741824 | bytes 8388608 | tf_op jit(solution)/shard_map/gather_dot/pallas_call | solution.py:153
  64.6 3.1 %attend_forward.1.refs_0_.mixed = bf16[256,512]{1,0:T(8,128)(2,1)S(1)} custom-call(s32[12]{0:T(128)S(1)} %concatenate.36.meta, bf16[256,512]{1,0:T(8,128)(2,1)S(1)} %one_dot.1.query, bf16[2,256,512]{2,1,0:T(8,128)(2,1)} %get-tuple-element.40.own_kv, bf16[2,256,512]{2,1,0:T(8,128)(2,1)} %collective-permute-done.8.other_kv), custom_call_target="tpu_custom_call" | custom-call | flops 536870912 | bytes 1572864 | tf_op jit(solution)/shard_map/attend_forward/pallas_call | solution.py:330
  67.7 4.9 %attend_backward.1 = (bf16[256,512]{1,0:T(8,128)(2,1)S(1)}, f32[2,256,512]{2,1,0:T(8,128)S(1)}, bf16[2,256,512]{2,1,0:T(8,128)(2,1)S(1)}) custom-call(s32[12]{0:T(128)S(1)} %concatenate.36.meta, bf16[256,512]{1,0:T(8,128)(2,1)S(1)} %one_dot.1.query, bf16[2,256,512]{2,1,0:T(8,128)(2,1)} %get-tuple-element.40.own_kv, ...), custom_call_target="tpu_custom_call" | custom-call | flops 1073741824 | bytes 3145728 | tf_op jit(solution)/shard_map/attend_backward/pallas_call | solution.py:343
  74.9 1.6 collective-permute-start.40
  78.6 3.3 %collective-permute-start.10 = (bf16[2,32,2048]{2,1,0:T(8,128)(2,1)S(1)}, bf16[2,32,2048]{2,1,0:T(8,128)(2,1)S(1)}, u32[]{:S(2)}, u32[]{:S(2)}) collective-permute-start(bf16[2,32,2048]{2,1,0:T(8,128)(2,1)S(1)} %get-tuple-element.43), channel_id=1, source_target_pairs={{0,1},{1,2},{2,3},{3,0},{4,5},{5,6},{6,7},{7,4},{8,9},{9,10},{10,1... | collective-permute-start | bytes 786440 | tf_op jit(solution)/shard_map/ppermute | solution.py:123
  82.2 3.6 %collective-permute-done.25 = bf16[2,256,512]{2,1,0:T(8,128)(2,1)} collective-permute-done((bf16[2,256,512]{2,1,0:T(8,128)(2,1)S(1)}, bf16[2,256,512]{2,1,0:T(8,128)(2,1)}, u32[]{:S(2)}, u32[]{:S(2)}) %collective-permute-start.25) | collective-permute-done | bytes 524320 | tf_op jit(solution)/shard_map/ppermute | solution.py:478
  87.1 5.0 %back_dot.7 = (bf16[4,32,2048]{2,1,0:T(8,128)(2,1)S(1)}, bf16[4,32,2048]{2,1,0:T(8,128)(2,1)S(1)}, f32[1,2048]{1,0:T(1,128)S(1)}) custom-call(bf16[256,512]{1,0:T(8,128)(2,1)S(1)} %get-tuple-element.51.refs_0_, bf16[256,512]{1,0:T(8,128)(2,1)S(1)} %get-tuple-element.88.refs_1_, bf16[256,512]{1,0:T(8,128)(2,1)S(1)} %get-tuple-element.87.refs_2_, ...), custom_call_target="tpu_custom_call" | custom-call | flops 1610612736 | bytes 8388608 | tf_op jit(solution)/shard_map/back_dot/pallas_call | solution.py:230
  92.1 5.1 %back_dot.6 = (bf16[2,32,2048]{2,1,0:T(8,128)(2,1)S(1)}, bf16[2,32,2048]{2,1,0:T(8,128)(2,1)S(1)}, bf16[2,32,2048]{2,1,0:T(8,128)(2,1)S(1)}, bf16[2,32,2048]{2,1,0:T(8,128)(2,1)S(1)}, f32[1,2048]{1,0:T(1,128)S(1)}) custom-call(bf16[256,512]{1,0:T(8,128)(2,1)S(1)} %get-tuple-element.51.refs_0_, bf16[256,512]{1,0:T(8,128)(2,1)S(1)} %get-tuple-element.88.refs_1_, ...), custom_call_target="tpu_custom_call" | custom-call | flops 1610612736 | bytes 8388608 | tf_op jit(solution)/shard_map/back_dot/pallas_call | solution.py:230
  98.2 3.8 %out_weight_parts.1 = (bf16[4,512,512]{2,1,0:T(8,128)(2,1)S(1)}, bf16[4,512,512]{2,1,0:T(8,128)(2,1)S(1)}) custom-call(s32[8]{0:T(128)S(1)} %pad_add_fusion.order, bf16[256,4096]{1,0:T(8,128)(2,1)S(1)} %copy-done.11, bf16[256,512]{1,0:T(8,128)(2,1)S(1)} %attend_forward.1.refs_0_.mixed), custom_call_target="tpu_custom_call" | custom-call | flops 1073741824 | bytes 6291456 | tf_op jit(solution)/shard_map/out_weight_parts/pallas_call | solution.py:367
  102.0 3.1 %collective-permute-start.41 = (bf16[256,1024]{1,0:T(8,128)(2,1)S(1)}, bf16[256,1024]{1,0:T(8,128)(2,1)S(1)}, u32[]{:S(2)}, u32[]{:S(2)}) collective-permute-start(bf16[256,1024]{1,0:T(8,128)(2,1)S(1)} %get-tuple-element.77), channel_id=1, source_target_pairs={{0,48},{8,56},{16,0},{24,8},{32,16},{40,24},{48,32},{56,40},{1,49}... | collective-permute-start | bytes 1572872 | tf_op jit(solution)/shard_map/ppermute | solution.py:459
  108.3 1.9 collective-permute-start.35
  110.3 2.3 collective-permute-start.44
  112.6 16.1 %collective-permute-done.41.refs_2_ = bf16[256,1024]{1,0:T(8,128)(2,1)S(1)} collective-permute-done((bf16[256,1024]{1,0:T(8,128)(2,1)S(1)}, bf16[256,1024]{1,0:T(8,128)(2,1)S(1)}, u32[]{:S(2)}, u32[]{:S(2)}) %collective-permute-start.41) | collective-permute-done | bytes 524320 | tf_op jit(solution)/shard_map/ppermute | solution.py:459
  129.1 1.9 collective-permute-start.12
  131.7 4.9 %collective-permute-done.45 = bf16[256,512]{1,0:T(8,128)(2,1)S(1)} collective-permute-done((bf16[256,512]{1,0:T(8,128)(2,1)S(1)}, bf16[256,512]{1,0:T(8,128)(2,1)S(1)}, u32[]{:S(2)}, u32[]{:S(2)}) %collective-permute-start.45) | collective-permute-done | bytes 262176 | tf_op jit(solution)/shard_map/ppermute | solution.py:479
  136.6 1.9 qkv_weight_parts.2
  138.5 2.6 %collective-permute-done.36 = f32[1,4096]{1,0:T(1,128)S(1)} collective-permute-done((f32[1,4096]{1,0:T(1,128)S(1)}, f32[1,4096]{1,0:T(1,128)S(1)}, u32[]{:S(2)}, u32[]{:S(2)}) %collective-permute-start.36) | collective-permute-done | bytes 16416 | tf_op jit(solution)/shard_map/ppermute | solution.py:497
  142.3 4.6 %collective-permute-start.38 = (f32[1,4096]{1,0:T(1,128)S(1)}, f32[1,4096]{1,0:T(1,128)S(1)}, u32[]{:S(2)}, u32[]{:S(2)}) collective-permute-start(f32[1,4096]{1,0:T(1,128)S(1)} %add.195), channel_id=1, source_target_pairs={{0,16},{8,24},{16,0},{24,8},{32,48},{40,56},{48,32},{56,40},{1,17}... | collective-permute-start | bytes 49160 | tf_op jit(solution)/shard_map/ppermute | solution.py:497
  149.4 2.1 collective-permute-start.14
  152.3 4.6 %collective-permute-done.39 = f32[1,4096]{1,0:T(1,128)S(1)} collective-permute-done((f32[1,4096]{1,0:T(1,128)S(1)}, f32[1,4096]{1,0:T(1,128)S(1)}, u32[]{:S(2)}, u32[]{:S(2)}) %collective-permute-start.39) | collective-permute-done | bytes 16416 | tf_op jit(solution)/shard_map/ppermute | solution.py:497
  160.1 1.8 collective-permute-start.26
  162.0 6.2 %collective-permute-done.28 = bf16[2,32,2048]{2,1,0:T(8,128)(2,1)S(1)} collective-permute-done((bf16[2,32,2048]{2,1,0:T(8,128)(2,1)S(1)}, bf16[2,32,2048]{2,1,0:T(8,128)(2,1)S(1)}, u32[]{:S(2)}, u32[]{:S(2)}) %collective-permute-start.28) | collective-permute-done | bytes 262176 | tf_op jit(solution)/shard_map/ppermute | solution.py:123
  168.8 4.5 %collective-permute-done.27 = bf16[2,32,2048]{2,1,0:T(8,128)(2,1)S(1)} collective-permute-done((bf16[2,32,2048]{2,1,0:T(8,128)(2,1)S(1)}, bf16[2,32,2048]{2,1,0:T(8,128)(2,1)S(1)}, u32[]{:S(2)}, u32[]{:S(2)}) %collective-permute-start.27) | collective-permute-done | bytes 262176 | tf_op jit(solution)/shard_map/ppermute | solution.py:123
  173.6 2.1 collective-permute-start.29
  175.8 14.2 %collective-permute-done.29 = bf16[32,2048]{1,0:T(8,128)(2,1)S(1)} collective-permute-done((bf16[32,2048]{1,0:T(8,128)(2,1)S(1)}, bf16[32,2048]{1,0:T(8,128)(2,1)S(1)}, u32[]{:S(2)}, u32[]{:S(2)}) %collective-permute-start.29) | collective-permute-done | bytes 131104 | tf_op jit(solution)/shard_map/ppermute | solution.py:124
  190.0 2.4 %collective-permute-start.49 = (bf16[2,256,512]{2,1,0:T(8,128)(2,1)S(1)}, bf16[2,256,512]{2,1,0:T(8,128)(2,1)S(1)}, u32[]{:S(2)}, u32[]{:S(2)}) collective-permute-start(bf16[2,256,512]{2,1,0:T(8,128)(2,1)S(1)} %add_convert_fusion.3.refs_4_), channel_id=1, source_target_pairs={{0,32},{8,40},{16,48},{24,56},{32,0},{40,8},{48,16},{56,24},{1,33}... | collective-permute-start | bytes 1572872 | tf_op jit(solution)/shard_map/ppermute | solution.py:481
  192.7 1.6 collective-permute-start.33
  194.3 3.2 %collective-permute-start.31 = (bf16[32,2048]{1,0:T(8,128)(2,1)S(1)}, bf16[32,2048]{1,0:T(8,128)(2,1)S(1)}, u32[]{:S(2)}, u32[]{:S(2)}) collective-permute-start(bf16[32,2048]{1,0:T(8,128)(2,1)S(1)} %get-tuple-element.84), channel_id=1, source_target_pairs={{0,3},{1,0},{2,1},{3,2},{4,7},{5,4},{6,5},{7,6},{8,11},{9,8},{10,9... | collective-permute-start | bytes 393224 | tf_op jit(solution)/shard_map/ppermute | solution.py:131
  197.5 7.1 %collective-permute-done.49.refs_7_ = bf16[2,256,512]{2,1,0:T(8,128)(2,1)S(1)} collective-permute-done((bf16[2,256,512]{2,1,0:T(8,128)(2,1)S(1)}, bf16[2,256,512]{2,1,0:T(8,128)(2,1)S(1)}, u32[]{:S(2)}, u32[]{:S(2)}) %collective-permute-start.49) | collective-permute-done | bytes 524320 | tf_op jit(solution)/shard_map/ppermute | solution.py:481
  204.6 3.6 %qkv_weight_parts.3 = (bf16[2,512,512]{2,1,0:T(8,128)(2,1)S(1)}, f32[2,512,512]{2,1,0:T(8,128)S(1)}) custom-call(s32[1]{0:T(128)} %bitcast.43.core, bf16[256,1024]{1,0:T(8,128)(2,1)S(1)} %get-tuple-element.79.refs_0_, bf16[256,1024]{1,0:T(8,128)(2,1)S(1)} %collective-permute-done.40.refs_1_, bf16[256,1024]{1,0:T(8,128)(2,1)S(1)} %collective-permute-done.41.refs_2_, ...), custom_call_target="tpu_custom_call" | custom-call | flops 2147483648 | bytes 9437184 | tf_op jit(solution)/shard_map/qkv_weight_parts/pallas_call | solution.py:405
  210.1 2.2 collective-permute-start.54
  212.3 3.2 %collective-permute-start.52 = (bf16[512,512]{1,0:T(8,128)(2,1)S(1)}, bf16[512,512]{1,0:T(8,128)(2,1)S(1)}, u32[]{:S(2)}, u32[]{:S(2)}) collective-permute-start(bf16[512,512]{1,0:T(8,128)(2,1)S(1)} %get-tuple-element.73), channel_id=1, source_target_pairs={{0,48},{8,56},{16,0},{24,8},{32,16},{40,24},{48,32},{56,40},{1,49}... | collective-permute-start | bytes 1572872 | tf_op jit(solution)/shard_map/ppermute | solution.py:490
  215.9 2.0 maximum_bitcast_fusion
  217.9 8.6 %collective-permute-done.54 = bf16[512,512]{1,0:T(8,128)(2,1)S(1)} collective-permute-done((bf16[512,512]{1,0:T(8,128)(2,1)S(1)}, bf16[512,512]{1,0:T(8,128)(2,1)S(1)}, u32[]{:S(2)}, u32[]{:S(2)}) %collective-permute-start.54) | collective-permute-done | bytes 524320 | tf_op jit(solution)/shard_map/ppermute | solution.py:490
  226.4 10.8 %collective-permute-done.53 = bf16[512,512]{1,0:T(8,128)(2,1)S(1)} collective-permute-done((bf16[512,512]{1,0:T(8,128)(2,1)S(1)}, bf16[512,512]{1,0:T(8,128)(2,1)S(1)}, u32[]{:S(2)}, u32[]{:S(2)}) %collective-permute-start.53) | collective-permute-done | bytes 524320 | tf_op jit(solution)/shard_map/ppermute | solution.py:490
  (143 shorter events, 38.6 us)
Async XLA Ops:
  3.5 7.9 %collective-permute-start.2 = (bf16[32,2048]{1,0:T(8,128)(2,1)S(1)}, bf16[32,2048]{1,0:T(8,128)(2,1)S(1)}, u32[]{:S(2)}, u32[]{:S(2)}) collective-permute-start(bf16[32,2048]{1,0:T(8,128)(2,1)S(1)} %get-tuple-element.37), channel_id=1, source_target_pairs={{0,2},{1,3},{2,0},{3,1},{4,6},{5,7},{6,4},{7,5},{8,10},{9,11},{10,... | collective-permute-start | bytes 393224 | tf_op jit(solution)/shard_map/ppermute | solution.py:99
  9.6 11.2 %collective-permute-start.4 = (bf16[32,2048]{1,0:T(8,128)(2,1)S(1)}, bf16[32,2048]{1,0:T(8,128)(2,1)S(1)}, u32[]{:S(2)}, u32[]{:S(2)}) collective-permute-start(bf16[32,2048]{1,0:T(8,128)(2,1)S(1)} %get-tuple-element.38), channel_id=1, source_target_pairs={{0,4},{1,5},{2,6},{3,7},{4,0},{5,1},{6,2},{7,3},{8,12},{9,13},{10,... | collective-permute-start | bytes 393224 | tf_op jit(solution)/shard_map/ppermute | solution.py:98
  14.7 22.8 %collective-permute-start.3 = (bf16[4,32,2048]{2,1,0:T(8,128)(2,1)S(1)}, bf16[4,32,2048]{2,1,0:T(8,128)(2,1)S(1)}, u32[]{:S(2)}, u32[]{:S(2)}) collective-permute-start(bf16[4,32,2048]{2,1,0:T(8,128)(2,1)S(1)} %pad_maximum_fusion.refs_0_), channel_id=1, source_target_pairs={{0,4},{1,5},{2,6},{3,7},{4,0},{5,1},{6,2},{7,3},{8,12},{9,13},{10,... | collective-permute-start | bytes 1572872 | tf_op jit(solution)/shard_map/ppermute | solution.py:102
  16.3 7.5 %collective-permute-start.19 = (bf16[32,2048]{1,0:T(8,128)(2,1)S(1)}, bf16[32,2048]{1,0:T(8,128)(2,1)S(1)}, u32[]{:S(2)}, u32[]{:S(2)}) collective-permute-start(bf16[32,2048]{1,0:T(8,128)(2,1)S(1)} %get-tuple-element.48), channel_id=1, source_target_pairs={{0,2},{1,3},{2,0},{3,1},{4,6},{5,7},{6,4},{7,5},{8,10},{9,11},{10,... | collective-permute-start | bytes 393224 | tf_op jit(solution)/shard_map/ppermute | solution.py:99
  18.7 8.2 %collective-permute-start.18 = (bf16[32,2048]{1,0:T(8,128)(2,1)S(1)}, bf16[32,2048]{1,0:T(8,128)(2,1)S(1)}, u32[]{:S(2)}, u32[]{:S(2)}) collective-permute-start(bf16[32,2048]{1,0:T(8,128)(2,1)S(1)} %get-tuple-element.48), channel_id=1, source_target_pairs={{0,3},{1,0},{2,1},{3,2},{4,7},{5,4},{6,5},{7,6},{8,11},{9,8},{10,9... | collective-permute-start | bytes 393224 | tf_op jit(solution)/shard_map/ppermute | solution.py:99
  19.9 7.6 %collective-permute-start.17 = (bf16[32,2048]{1,0:T(8,128)(2,1)S(1)}, bf16[32,2048]{1,0:T(8,128)(2,1)S(1)}, u32[]{:S(2)}, u32[]{:S(2)}) collective-permute-start(bf16[32,2048]{1,0:T(8,128)(2,1)S(1)} %get-tuple-element.48), channel_id=1, source_target_pairs={{0,1},{1,2},{2,3},{3,0},{4,5},{5,6},{6,7},{7,4},{8,9},{9,10},{10,1... | collective-permute-start | bytes 393224 | tf_op jit(solution)/shard_map/ppermute | solution.py:99
  20.8 16.2 %collective-permute-start.5 = (bf16[2,32,2048]{2,1,0:T(8,128)(2,1)S(1)}, bf16[2,32,2048]{2,1,0:T(8,128)(2,1)S(1)}, u32[]{:S(2)}, u32[]{:S(2)}) collective-permute-start(bf16[2,32,2048]{2,1,0:T(8,128)(2,1)S(1)} %pad_maximum_fusion.2.refs_2_), channel_id=1, source_target_pairs={{0,1},{1,2},{2,3},{3,0},{4,5},{5,6},{6,7},{7,4},{8,9},{9,10},{10,1... | collective-permute-start | bytes 786440 | tf_op jit(solution)/shard_map/ppermute | solution.py:100
  23.7 13.8 %collective-permute-start.6 = (bf16[2,32,2048]{2,1,0:T(8,128)(2,1)S(1)}, bf16[2,32,2048]{2,1,0:T(8,128)(2,1)S(1)}, u32[]{:S(2)}, u32[]{:S(2)}) collective-permute-start(bf16[2,32,2048]{2,1,0:T(8,128)(2,1)S(1)} %pad_maximum_fusion.2.refs_2_), channel_id=1, source_target_pairs={{0,3},{1,0},{2,1},{3,2},{4,7},{5,4},{6,5},{7,6},{8,11},{9,8},{10,9... | collective-permute-start | bytes 786440 | tf_op jit(solution)/shard_map/ppermute | solution.py:100
  26.9 10.6 %collective-permute-start.7 = (bf16[2,32,2048]{2,1,0:T(8,128)(2,1)S(1)}, bf16[2,32,2048]{2,1,0:T(8,128)(2,1)S(1)}, u32[]{:S(2)}, u32[]{:S(2)}) collective-permute-start(bf16[2,32,2048]{2,1,0:T(8,128)(2,1)S(1)} %pad_maximum_fusion.2.refs_2_), channel_id=1, source_target_pairs={{0,2},{1,3},{2,0},{3,1},{4,6},{5,7},{6,4},{7,5},{8,10},{9,11},{10,... | collective-permute-start | bytes 786440 | tf_op jit(solution)/shard_map/ppermute | solution.py:100
  27.5 19.4 %collective-permute-start.21 = (bf16[32,2048]{1,0:T(8,128)(2,1)S(1)}, bf16[32,2048]{1,0:T(8,128)(2,1)S(1)}, u32[]{:S(2)}, u32[]{:S(2)}) collective-permute-start(bf16[32,2048]{1,0:T(8,128)(2,1)S(1)} %get-tuple-element.49), channel_id=1, source_target_pairs={{0,4},{1,5},{2,6},{3,7},{4,0},{5,1},{6,2},{7,3},{8,12},{9,13},{10,... | collective-permute-start | bytes 393224 | tf_op jit(solution)/shard_map/ppermute | solution.py:98
  37.0 23.4 %collective-permute-start.20 = (bf16[4,32,2048]{2,1,0:T(8,128)(2,1)S(1)}, bf16[4,32,2048]{2,1,0:T(8,128)(2,1)S(1)}, u32[]{:S(2)}, u32[]{:S(2)}) collective-permute-start(bf16[4,32,2048]{2,1,0:T(8,128)(2,1)S(1)} %pad_maximum_fusion.1.refs_0_), channel_id=1, source_target_pairs={{0,4},{1,5},{2,6},{3,7},{4,0},{5,1},{6,2},{7,3},{8,12},{9,13},{10,... | collective-permute-start | bytes 1572872 | tf_op jit(solution)/shard_map/ppermute | solution.py:102
  43.9 20.7 %collective-permute-start.8 = (bf16[2,256,512]{2,1,0:T(8,128)(2,1)}, bf16[2,256,512]{2,1,0:T(8,128)(2,1)}, u32[]{:S(2)}, u32[]{:S(2)}) collective-permute-start(bf16[2,256,512]{2,1,0:T(8,128)(2,1)} %get-tuple-element.40.own_kv), channel_id=1, source_target_pairs={{0,64},{64,0},{1,65},{65,1},{2,66},{66,2},{3,67},{67,3},{4,68},{68... | collective-permute-start | bytes 1572872 | tf_op jit(solution)/shard_map/ppermute | solution.py:453
  47.0 10.6 %collective-permute-start.22 = (bf16[2,32,2048]{2,1,0:T(8,128)(2,1)S(1)}, bf16[2,32,2048]{2,1,0:T(8,128)(2,1)}, u32[]{:S(2)}, u32[]{:S(2)}) collective-permute-start(bf16[2,32,2048]{2,1,0:T(8,128)(2,1)S(1)} %pad_maximum_fusion.3.refs_2_), channel_id=1, source_target_pairs={{0,1},{1,2},{2,3},{3,0},{4,5},{5,6},{6,7},{7,4},{8,9},{9,10},{10,1... | collective-permute-start | bytes 786440 | tf_op jit(solution)/shard_map/ppermute | solution.py:100
  47.1 12.1 %collective-permute-start.23 = (bf16[2,32,2048]{2,1,0:T(8,128)(2,1)S(1)}, bf16[2,32,2048]{2,1,0:T(8,128)(2,1)}, u32[]{:S(2)}, u32[]{:S(2)}) collective-permute-start(bf16[2,32,2048]{2,1,0:T(8,128)(2,1)S(1)} %pad_maximum_fusion.3.refs_2_), channel_id=1, source_target_pairs={{0,3},{1,0},{2,1},{3,2},{4,7},{5,4},{6,5},{7,6},{8,11},{9,8},{10,9... | collective-permute-start | bytes 786440 | tf_op jit(solution)/shard_map/ppermute | solution.py:100
  50.3 10.1 %collective-permute-start.24 = (bf16[2,32,2048]{2,1,0:T(8,128)(2,1)S(1)}, bf16[2,32,2048]{2,1,0:T(8,128)(2,1)}, u32[]{:S(2)}, u32[]{:S(2)}) collective-permute-start(bf16[2,32,2048]{2,1,0:T(8,128)(2,1)S(1)} %pad_maximum_fusion.3.refs_2_), channel_id=1, source_target_pairs={{0,2},{1,3},{2,0},{3,1},{4,6},{5,7},{6,4},{7,5},{8,10},{9,11},{10,... | collective-permute-start | bytes 786440 | tf_op jit(solution)/shard_map/ppermute | solution.py:100
  73.6 12.3 %collective-permute-start.25 = (bf16[2,256,512]{2,1,0:T(8,128)(2,1)S(1)}, bf16[2,256,512]{2,1,0:T(8,128)(2,1)}, u32[]{:S(2)}, u32[]{:S(2)}) collective-permute-start(bf16[2,256,512]{2,1,0:T(8,128)(2,1)S(1)} %get-tuple-element.53), channel_id=1, source_target_pairs={{0,64},{64,0},{1,65},{65,1},{2,66},{66,2},{3,67},{67,3},{4,68},{68... | collective-permute-start | bytes 1572872 | tf_op jit(solution)/shard_map/ppermute | solution.py:478
  74.9 35.4 %collective-permute-start.40 = (bf16[256,1024]{1,0:T(8,128)(2,1)S(1)}, bf16[256,1024]{1,0:T(8,128)(2,1)S(1)}, u32[]{:S(2)}, u32[]{:S(2)}) collective-permute-start(bf16[256,1024]{1,0:T(8,128)(2,1)S(1)} %get-tuple-element.78), channel_id=1, source_target_pairs={{0,16},{8,24},{16,32},{24,40},{32,48},{40,56},{48,0},{56,8},{1,17}... | collective-permute-start | bytes 1572872 | tf_op jit(solution)/shard_map/ppermute | solution.py:459
  78.3 28.3 %collective-permute-start.11 = (bf16[2,32,2048]{2,1,0:T(8,128)(2,1)S(1)}, bf16[2,32,2048]{2,1,0:T(8,128)(2,1)S(1)}, u32[]{:S(2)}, u32[]{:S(2)}) collective-permute-start(bf16[2,32,2048]{2,1,0:T(8,128)(2,1)S(1)} %get-tuple-element.44), channel_id=1, source_target_pairs={{0,2},{1,3},{2,0},{3,1},{4,6},{5,7},{6,4},{7,5},{8,10},{9,11},{10,... | collective-permute-start | bytes 786440 | tf_op jit(solution)/shard_map/ppermute | solution.py:123
  78.6 28.7 %collective-permute-start.10 = (bf16[2,32,2048]{2,1,0:T(8,128)(2,1)S(1)}, bf16[2,32,2048]{2,1,0:T(8,128)(2,1)S(1)}, u32[]{:S(2)}, u32[]{:S(2)}) collective-permute-start(bf16[2,32,2048]{2,1,0:T(8,128)(2,1)S(1)} %get-tuple-element.43), channel_id=1, source_target_pairs={{0,1},{1,2},{2,3},{3,0},{4,5},{5,6},{6,7},{7,4},{8,9},{9,10},{10,1... | collective-permute-start | bytes 786440 | tf_op jit(solution)/shard_map/ppermute | solution.py:123
  81.9 26.4 %collective-permute-start.9 = (bf16[2,32,2048]{2,1,0:T(8,128)(2,1)S(1)}, bf16[2,32,2048]{2,1,0:T(8,128)(2,1)S(1)}, u32[]{:S(2)}, u32[]{:S(2)}) collective-permute-start(bf16[2,32,2048]{2,1,0:T(8,128)(2,1)S(1)} %get-tuple-element.42), channel_id=1, source_target_pairs={{0,3},{1,0},{2,1},{3,2},{4,7},{5,4},{6,5},{7,6},{8,11},{9,8},{10,9... | collective-permute-start | bytes 786440 | tf_op jit(solution)/shard_map/ppermute | solution.py:123
  102.0 26.7 %collective-permute-start.41 = (bf16[256,1024]{1,0:T(8,128)(2,1)S(1)}, bf16[256,1024]{1,0:T(8,128)(2,1)S(1)}, u32[]{:S(2)}, u32[]{:S(2)}) collective-permute-start(bf16[256,1024]{1,0:T(8,128)(2,1)S(1)} %get-tuple-element.77), channel_id=1, source_target_pairs={{0,48},{8,56},{16,0},{24,8},{32,16},{40,24},{48,32},{56,40},{1,49}... | collective-permute-start | bytes 1572872 | tf_op jit(solution)/shard_map/ppermute | solution.py:459
  106.6 22.4 %collective-permute-start.42 = (bf16[256,1024]{1,0:T(8,128)(2,1)S(1)}, bf16[256,1024]{1,0:T(8,128)(2,1)S(1)}, u32[]{:S(2)}, u32[]{:S(2)}) collective-permute-start(bf16[256,1024]{1,0:T(8,128)(2,1)S(1)} %get-tuple-element.76), channel_id=1, source_target_pairs={{0,32},{8,40},{16,48},{24,56},{32,0},{40,8},{48,16},{56,24},{1,33}... | collective-permute-start | bytes 1572872 | tf_op jit(solution)/shard_map/ppermute | solution.py:459
  107.3 21.7 %collective-permute-start.43 = (bf16[256,512]{1,0:T(8,128)(2,1)S(1)}, bf16[256,512]{1,0:T(8,128)(2,1)S(1)}, u32[]{:S(2)}, u32[]{:S(2)}) collective-permute-start(bf16[256,512]{1,0:T(8,128)(2,1)S(1)} %get-tuple-element.51.refs_0_), channel_id=1, source_target_pairs={{0,16},{8,24},{16,32},{24,40},{32,48},{40,56},{48,0},{56,8},{1,17}... | collective-permute-start | bytes 786440 | tf_op jit(solution)/shard_map/ppermute | solution.py:479
  108.3 20.4 %collective-permute-start.35 = (f32[1,4096]{1,0:T(1,128)S(1)}, f32[1,4096]{1,0:T(1,128)S(1)}, u32[]{:S(2)}, u32[]{:S(2)}) collective-permute-start(f32[1,4096]{1,0:T(1,128)S(1)} %add.192), channel_id=1, source_target_pairs={{0,2},{1,3},{2,0},{3,1},{4,6},{5,7},{6,4},{7,5},{8,10},{9,11},{10,... | collective-permute-start | bytes 49160 | tf_op jit(solution)/shard_map/ppermute | solution.py:497
  110.3 21.2 %collective-permute-start.44 = (bf16[256,512]{1,0:T(8,128)(2,1)S(1)}, bf16[256,512]{1,0:T(8,128)(2,1)S(1)}, u32[]{:S(2)}, u32[]{:S(2)}) collective-permute-start(bf16[256,512]{1,0:T(8,128)(2,1)S(1)} %get-tuple-element.51.refs_0_), channel_id=1, source_target_pairs={{0,48},{8,56},{16,0},{24,8},{32,16},{40,24},{48,32},{56,40},{1,49}... | collective-permute-start | bytes 786440 | tf_op jit(solution)/shard_map/ppermute | solution.py:479
  128.7 7.9 %collective-permute-start.45 = (bf16[256,512]{1,0:T(8,128)(2,1)S(1)}, bf16[256,512]{1,0:T(8,128)(2,1)S(1)}, u32[]{:S(2)}, u32[]{:S(2)}) collective-permute-start(bf16[256,512]{1,0:T(8,128)(2,1)S(1)} %get-tuple-element.51.refs_0_), channel_id=1, source_target_pairs={{0,32},{8,40},{16,48},{24,56},{32,0},{40,8},{48,16},{56,24},{1,33}... | collective-permute-start | bytes 786440 | tf_op jit(solution)/shard_map/ppermute | solution.py:479
  128.7 12.4 %collective-permute-start.13 = (bf16[4,32,2048]{2,1,0:T(8,128)(2,1)S(1)}, bf16[4,32,2048]{2,1,0:T(8,128)(2,1)S(1)}, u32[]{:S(2)}, u32[]{:S(2)}) collective-permute-start(bf16[4,32,2048]{2,1,0:T(8,128)(2,1)S(1)} %get-tuple-element.46), channel_id=1, source_target_pairs={{0,4},{1,5},{2,6},{3,7},{4,0},{5,1},{6,2},{7,3},{8,12},{9,13},{10,... | collective-permute-start | bytes 1572872 | tf_op jit(solution)/shard_map/ppermute | solution.py:128
  129.0 80.6 %collective-permute-start.51 = (bf16[4,512,512]{2,1,0:T(8,128)(2,1)S(1)}, bf16[4,512,512]{2,1,0:T(8,128)(2,1)S(1)}, u32[]{:S(2)}, u32[]{:S(2)}) collective-permute-start(bf16[4,512,512]{2,1,0:T(8,128)(2,1)S(1)} %get-tuple-element.68), channel_id=1, source_target_pairs={{0,8},{8,0},{16,24},{24,16},{32,40},{40,32},{48,56},{56,48},{1,9},... | collective-permute-start | bytes 6291464 | tf_op jit(solution)/shard_map/ppermute | solution.py:486
  129.1 22.5 %collective-permute-start.12 = (bf16[32,2048]{1,0:T(8,128)(2,1)S(1)}, bf16[32,2048]{1,0:T(8,128)(2,1)S(1)}, u32[]{:S(2)}, u32[]{:S(2)}) collective-permute-start(bf16[32,2048]{1,0:T(8,128)(2,1)S(1)} %fusion.25), channel_id=1, source_target_pairs={{0,4},{1,5},{2,6},{3,7},{4,0},{5,1},{6,2},{7,3},{8,12},{9,13},{10,... | collective-permute-start | bytes 393224 | tf_op jit(solution)/shard_map/ppermute | solution.py:124
  131.5 9.5 %collective-permute-start.36 = (f32[1,4096]{1,0:T(1,128)S(1)}, f32[1,4096]{1,0:T(1,128)S(1)}, u32[]{:S(2)}, u32[]{:S(2)}) collective-permute-start(f32[1,4096]{1,0:T(1,128)S(1)} %add.193), channel_id=1, source_target_pairs={{0,4},{1,5},{2,6},{3,7},{4,0},{5,1},{6,2},{7,3},{8,12},{9,13},{10,... | collective-permute-start | bytes 49160 | tf_op jit(solution)/shard_map/ppermute | solution.py:497
  147.0 10.5 %collective-permute-start.16 = (bf16[32,2048]{1,0:T(8,128)(2,1)S(1)}, bf16[32,2048]{1,0:T(8,128)(2,1)S(1)}, u32[]{:S(2)}, u32[]{:S(2)}) collective-permute-start(bf16[32,2048]{1,0:T(8,128)(2,1)S(1)} %get-tuple-element.90), channel_id=1, source_target_pairs={{0,2},{1,3},{2,0},{3,1},{4,6},{5,7},{6,4},{7,5},{8,10},{9,11},{10,... | collective-permute-start | bytes 393224 | tf_op jit(solution)/shard_map/ppermute | solution.py:131
  148.3 10.4 %collective-permute-start.15 = (bf16[32,2048]{1,0:T(8,128)(2,1)S(1)}, bf16[32,2048]{1,0:T(8,128)(2,1)S(1)}, u32[]{:S(2)}, u32[]{:S(2)}) collective-permute-start(bf16[32,2048]{1,0:T(8,128)(2,1)S(1)} %get-tuple-element.91), channel_id=1, source_target_pairs={{0,1},{1,2},{2,3},{3,0},{4,5},{5,6},{6,7},{7,4},{8,9},{9,10},{10,1... | collective-permute-start | bytes 393224 | tf_op jit(solution)/shard_map/ppermute | solution.py:131
  149.4 10.7 %collective-permute-start.14 = (bf16[32,2048]{1,0:T(8,128)(2,1)S(1)}, bf16[32,2048]{1,0:T(8,128)(2,1)S(1)}, u32[]{:S(2)}, u32[]{:S(2)}) collective-permute-start(bf16[32,2048]{1,0:T(8,128)(2,1)S(1)} %get-tuple-element.89), channel_id=1, source_target_pairs={{0,3},{1,0},{2,1},{3,2},{4,7},{5,4},{6,5},{7,6},{8,11},{9,8},{10,9... | collective-permute-start | bytes 393224 | tf_op jit(solution)/shard_map/ppermute | solution.py:131
  156.9 16.7 %collective-permute-start.46 = (bf16[1,512,512]{2,1,0:T(8,128)(2,1)S(1)}, bf16[1,512,512]{2,1,0:T(8,128)(2,1)S(1)}, u32[]{:S(2)}, u32[]{:S(2)}) collective-permute-start(bf16[1,512,512]{2,1,0:T(8,128)(2,1)S(1)} %get-tuple-element.63), channel_id=1, source_target_pairs={{0,8},{8,0},{16,24},{24,16},{32,40},{40,32},{48,56},{56,48},{1,9},... | collective-permute-start | bytes 1572872 | tf_op jit(solution)/shard_map/ppermute | solution.py:510
  157.5 10.7 %collective-permute-start.28 = (bf16[2,32,2048]{2,1,0:T(8,128)(2,1)S(1)}, bf16[2,32,2048]{2,1,0:T(8,128)(2,1)S(1)}, u32[]{:S(2)}, u32[]{:S(2)}) collective-permute-start(bf16[2,32,2048]{2,1,0:T(8,128)(2,1)S(1)} %get-tuple-element.57), channel_id=1, source_target_pairs={{0,2},{1,3},{2,0},{3,1},{4,6},{5,7},{6,4},{7,5},{8,10},{9,11},{10,... | collective-permute-start | bytes 786440 | tf_op jit(solution)/shard_map/ppermute | solution.py:123
  158.6 14.7 %collective-permute-start.27 = (bf16[2,32,2048]{2,1,0:T(8,128)(2,1)S(1)}, bf16[2,32,2048]{2,1,0:T(8,128)(2,1)S(1)}, u32[]{:S(2)}, u32[]{:S(2)}) collective-permute-start(bf16[2,32,2048]{2,1,0:T(8,128)(2,1)S(1)} %get-tuple-element.56), channel_id=1, source_target_pairs={{0,1},{1,2},{2,3},{3,0},{4,5},{5,6},{6,7},{7,4},{8,9},{9,10},{10,1... | collective-permute-start | bytes 786440 | tf_op jit(solution)/shard_map/ppermute | solution.py:123
  160.1 13.3 %collective-permute-start.26 = (bf16[2,32,2048]{2,1,0:T(8,128)(2,1)S(1)}, bf16[2,32,2048]{2,1,0:T(8,128)(2,1)S(1)}, u32[]{:S(2)}, u32[]{:S(2)}) collective-permute-start(bf16[2,32,2048]{2,1,0:T(8,128)(2,1)S(1)} %get-tuple-element.55), channel_id=1, source_target_pairs={{0,3},{1,0},{2,1},{3,2},{4,7},{5,4},{6,5},{7,6},{8,11},{9,8},{10,9... | collective-permute-start | bytes 786440 | tf_op jit(solution)/shard_map/ppermute | solution.py:123
  168.2 26.1 %collective-permute-start.47 = (bf16[2,256,512]{2,1,0:T(8,128)(2,1)S(1)}, bf16[2,256,512]{2,1,0:T(8,128)(2,1)S(1)}, u32[]{:S(2)}, u32[]{:S(2)}) collective-permute-start(bf16[2,256,512]{2,1,0:T(8,128)(2,1)S(1)} %add_convert_fusion.3.refs_4_), channel_id=1, source_target_pairs={{0,16},{8,24},{16,32},{24,40},{32,48},{40,56},{48,0},{56,8},{1,17}... | collective-permute-start | bytes 1572872 | tf_op jit(solution)/shard_map/ppermute | solution.py:481
  173.3 20.9 %collective-permute-start.48 = (bf16[2,256,512]{2,1,0:T(8,128)(2,1)S(1)}, bf16[2,256,512]{2,1,0:T(8,128)(2,1)S(1)}, u32[]{:S(2)}, u32[]{:S(2)}) collective-permute-start(bf16[2,256,512]{2,1,0:T(8,128)(2,1)S(1)} %add_convert_fusion.3.refs_4_), channel_id=1, source_target_pairs={{0,48},{8,56},{16,0},{24,8},{32,16},{40,24},{48,32},{56,40},{1,49}... | collective-permute-start | bytes 1572872 | tf_op jit(solution)/shard_map/ppermute | solution.py:481
  173.4 19.1 %collective-permute-start.30 = (bf16[4,32,2048]{2,1,0:T(8,128)(2,1)S(1)}, bf16[4,32,2048]{2,1,0:T(8,128)(2,1)S(1)}, u32[]{:S(2)}, u32[]{:S(2)}) collective-permute-start(bf16[4,32,2048]{2,1,0:T(8,128)(2,1)S(1)} %get-tuple-element.59), channel_id=1, source_target_pairs={{0,4},{1,5},{2,6},{3,7},{4,0},{5,1},{6,2},{7,3},{8,12},{9,13},{10,... | collective-permute-start | bytes 1572872 | tf_op jit(solution)/shard_map/ppermute | solution.py:128
  173.6 16.5 %collective-permute-start.29 = (bf16[32,2048]{1,0:T(8,128)(2,1)S(1)}, bf16[32,2048]{1,0:T(8,128)(2,1)S(1)}, u32[]{:S(2)}, u32[]{:S(2)}) collective-permute-start(bf16[32,2048]{1,0:T(8,128)(2,1)S(1)} %fusion.26), channel_id=1, source_target_pairs={{0,4},{1,5},{2,6},{3,7},{4,0},{5,1},{6,2},{7,3},{8,12},{9,13},{10,... | collective-permute-start | bytes 393224 | tf_op jit(solution)/shard_map/ppermute | solution.py:124
  190.0 14.5 %collective-permute-start.49 = (bf16[2,256,512]{2,1,0:T(8,128)(2,1)S(1)}, bf16[2,256,512]{2,1,0:T(8,128)(2,1)S(1)}, u32[]{:S(2)}, u32[]{:S(2)}) collective-permute-start(bf16[2,256,512]{2,1,0:T(8,128)(2,1)S(1)} %add_convert_fusion.3.refs_4_), channel_id=1, source_target_pairs={{0,32},{8,40},{16,48},{24,56},{32,0},{40,8},{48,16},{56,24},{1,33}... | collective-permute-start | bytes 1572872 | tf_op jit(solution)/shard_map/ppermute | solution.py:481
  192.7 15.5 %collective-permute-start.33 = (bf16[32,2048]{1,0:T(8,128)(2,1)S(1)}, bf16[32,2048]{1,0:T(8,128)(2,1)S(1)}, u32[]{:S(2)}, u32[]{:S(2)}) collective-permute-start(bf16[32,2048]{1,0:T(8,128)(2,1)S(1)} %get-tuple-element.85), channel_id=1, source_target_pairs={{0,2},{1,3},{2,0},{3,1},{4,6},{5,7},{6,4},{7,5},{8,10},{9,11},{10,... | collective-permute-start | bytes 393224 | tf_op jit(solution)/shard_map/ppermute | solution.py:131
  194.3 14.0 %collective-permute-start.32 = (bf16[32,2048]{1,0:T(8,128)(2,1)S(1)}, bf16[32,2048]{1,0:T(8,128)(2,1)S(1)}, u32[]{:S(2)}, u32[]{:S(2)}) collective-permute-start(bf16[32,2048]{1,0:T(8,128)(2,1)S(1)} %get-tuple-element.86), channel_id=1, source_target_pairs={{0,1},{1,2},{2,3},{3,0},{4,5},{5,6},{6,7},{7,4},{8,9},{9,10},{10,1... | collective-permute-start | bytes 393224 | tf_op jit(solution)/shard_map/ppermute | solution.py:131
  194.3 14.0 %collective-permute-start.31 = (bf16[32,2048]{1,0:T(8,128)(2,1)S(1)}, bf16[32,2048]{1,0:T(8,128)(2,1)S(1)}, u32[]{:S(2)}, u32[]{:S(2)}) collective-permute-start(bf16[32,2048]{1,0:T(8,128)(2,1)S(1)} %get-tuple-element.84), channel_id=1, source_target_pairs={{0,3},{1,0},{2,1},{3,2},{4,7},{5,4},{6,5},{7,6},{8,11},{9,8},{10,9... | collective-permute-start | bytes 393224 | tf_op jit(solution)/shard_map/ppermute | solution.py:131
  210.1 16.4 %collective-permute-start.54 = (bf16[512,512]{1,0:T(8,128)(2,1)S(1)}, bf16[512,512]{1,0:T(8,128)(2,1)S(1)}, u32[]{:S(2)}, u32[]{:S(2)}) collective-permute-start(bf16[512,512]{1,0:T(8,128)(2,1)S(1)} %get-tuple-element.74), channel_id=1, source_target_pairs={{0,32},{8,40},{16,48},{24,56},{32,0},{40,8},{48,16},{56,24},{1,33}... | collective-permute-start | bytes 1572872 | tf_op jit(solution)/shard_map/ppermute | solution.py:490
  212.3 24.9 %collective-permute-start.53 = (bf16[512,512]{1,0:T(8,128)(2,1)S(1)}, bf16[512,512]{1,0:T(8,128)(2,1)S(1)}, u32[]{:S(2)}, u32[]{:S(2)}) collective-permute-start(bf16[512,512]{1,0:T(8,128)(2,1)S(1)} %get-tuple-element.75), channel_id=1, source_target_pairs={{0,16},{8,24},{16,32},{24,40},{32,48},{40,56},{48,0},{56,8},{1,17}... | collective-permute-start | bytes 1572872 | tf_op jit(solution)/shard_map/ppermute | solution.py:490
  212.3 24.9 %collective-permute-start.52 = (bf16[512,512]{1,0:T(8,128)(2,1)S(1)}, bf16[512,512]{1,0:T(8,128)(2,1)S(1)}, u32[]{:S(2)}, u32[]{:S(2)}) collective-permute-start(bf16[512,512]{1,0:T(8,128)(2,1)S(1)} %get-tuple-element.73), channel_id=1, source_target_pairs={{0,48},{8,56},{16,0},{24,8},{32,16},{40,24},{48,32},{56,40},{1,49}... | collective-permute-start | bytes 1572872 | tf_op jit(solution)/shard_map/ppermute | solution.py:490
  (21 other events, 134.3 us)

commit v3 on v2

v3 whole, which is shorter than its diff:
```python
import functools

import jax
import jax.numpy as jnp
from jax import lax
from jax.experimental import pallas as pl
from jax.experimental.pallas import tpu as pltpu
from jax.sharding import PartitionSpec as P

HS = 128
LI = 128
HEADS = 4
SLOTS = 256
ROWS = 32
WIDTH = 4096
HALF = 2048
COLS = 512
FAR = 1073741824
f32 = jnp.float32
bf16 = jnp.bfloat16
VMEM_LIMIT = 40 * 1024 * 1024

STEPS = (0, 1, 3, 2)


def z_shift(k):
    return [(i, (i // 4) * 4 + (i + k) % 4) for i in range(8)]


X_SWAP = [(i, i ^ 4) for i in range(8)]


def y_shift(k):
    return [(i, (i + 2 * k) % 8) for i in range(8)]


CORE_SWAP = [(i, i ^ 1) for i in range(8)]
GRP_SWAP = [(0, 1), (1, 0)]


def sds(shape, dtype):
    return jax.ShapeDtypeStruct(shape, dtype)


def call(kernel, out_shape, flops=0, nbytes=0, **kwargs):
    return pl.pallas_call(
        kernel,
        out_shape=out_shape,
        compiler_params=pltpu.CompilerParams(vmem_limit_bytes=VMEM_LIMIT),
        cost_estimate=pl.CostEstimate(flops=flops, bytes_accessed=nbytes, transcendentals=0),
        **kwargs,
    )


def whole(shape):
    return pl.BlockSpec(shape, lambda *_: (0,) * len(shape))


SMEM = pl.BlockSpec(memory_space=pltpu.SMEM)
VMEM = pl.BlockSpec(memory_space=pltpu.VMEM)
ANY = pl.BlockSpec(memory_space=pl.ANY)


def dot(left, right):
    return jnp.dot(left, right, preferred_element_type=f32)


def dot_rows(left, right):
    return lax.dot_general(left, right, (((1,), (1,)), ((), ())), preferred_element_type=f32)


def dot_tokens(left, right):
    return lax.dot_general(left, right, (((0,), (0,)), ((), ())), preferred_element_type=f32)


def norm_kernel(valid, x, gain, cot, n_left, n_right, grad, inv):
    x_float = x[...].astype(f32)
    scale = lax.rsqrt(jnp.mean(x_float * x_float, axis=1, keepdims=True) + 1e-05)
    normed = (x_float * scale * gain[...].astype(f32)).astype(bf16)
    n_left[...] = normed[:, :HALF]
    n_right[...] = normed[:, HALF:]
    grad[...] = (cot[...].astype(f32) * valid[0]).astype(bf16)
    inv[...] = jnp.broadcast_to(scale, (ROWS, 128))


def norm_rows(valid, x, gain, cot):
    part = sds((ROWS, HALF), bf16)
    return call(
        norm_kernel,
        [part, part, sds((ROWS, WIDTH), bf16), sds((ROWS, 128), f32)],
        nbytes=4 * ROWS * WIDTH * 2,
        in_specs=[SMEM] + [VMEM] * 3,
        name="norm_rows",
    )(valid, x, gain, cot)


def gather_blocks(left, right):
    right_pair = jnp.stack([right, lax.ppermute(right, "tp", X_SWAP)])
    left_four = [left] + [lax.ppermute(left, "tp", z_shift(k)) for k in STEPS[1:]]
    right_four = [right_pair] + [lax.ppermute(right_pair, "tp", z_shift(k)) for k in STEPS[1:]]
    left_own = jnp.stack(left_four)
    left_other = lax.ppermute(left_own, "tp", X_SWAP)
    return [left_own, left_other] + right_four


def place_pieces(pieces, whole_ref):
    left_own, left_other = pieces[:2]
    for slot in range(4):
        rows = pl.ds(slot * ROWS, ROWS)
        other = pl.ds((4 + slot) * ROWS, ROWS)
        whole_ref[rows, :HALF] = left_own[slot]
        whole_ref[other, :HALF] = left_other[slot]
        whole_ref[rows, HALF:] = pieces[2 + slot][0]
        whole_ref[other, HALF:] = pieces[2 + slot][1]


PIECE_SHAPES = [(4, ROWS, HALF)] * 2 + [(2, ROWS, HALF)] * 4


def sum_z_kernel(own, c1, c2, c3, *refs):
    kept, sent = refs[-2:]
    total = own[...].astype(f32)
    for came in (c1, c2, c3):
        total = total + came[...].astype(f32)
    kept[...] = total[0]
    sent[...] = total[1].astype(bf16)


def sum_z(own, came, after=()):
    shape = own.shape[1:]
    return call(
        sum_z_kernel,
        [sds(shape, f32), sds(shape, bf16)],
        nbytes=11 * shape[0] * shape[1] * 2,
        in_specs=[VMEM] * 4 + [ANY] * len(after),
        out_specs=[VMEM] * 2,
        name="sum_z",
    )(own, *came, *after)


def sum_left_kernel(own, c1, c2, c3, *refs):
    kept, sent, gain = refs[-3:]
    for part in range(2):
        total = own[part].astype(f32)
        for came in (c1, c2, c3):
            total = total + came[part].astype(f32)
        kept[pl.ds(part * 16, 16)] = total
        total = own[2 + part].astype(f32)
        for came in (c1, c2, c3):
            total = total + came[2 + part].astype(f32)
        sent[part] = total.astype(bf16)
    left, right = gain_from(own[4])
    for came in (c1, c2, c3):
        more_left, more_right = gain_from(came[4])
        left, right = left + more_left, right + more_right
    sent[2] = gain_rows_of(left, right)
    gain[0:1] = left
    gain[1:2] = right


def sum_left(own, came, after=()):
    return call(
        sum_left_kernel,
        [sds((ROWS, HALF), f32), sds((3, 16, HALF), bf16), sds((2, HALF), f32)],
        nbytes=11 * ROWS * HALF * 2,
        in_specs=[VMEM] * 4 + [ANY] * len(after),
        out_specs=[VMEM] * 3,
        name="sum_left",
    )(own, *came, *after)


def sum_gain_kernel(own, came, gain, out):
    left, right = gain_from(came[2])
    out[:, :HALF] = (own[0:1] + left) / gain[:, :HALF].astype(f32)
    out[:, HALF:] = (own[1:2] + right) / gain[:, HALF:].astype(f32)


def sum_gain(own, came, gain):
    return call(
        sum_gain_kernel,
        sds((1, WIDTH), f32),
        nbytes=10 * WIDTH * 2,
        in_specs=[VMEM] * 3,
        out_specs=VMEM,
        name="sum_gain",
    )(own, came, gain)


def sum_x_kernel(own, came, *refs):
    kept, sends = refs[-4], refs[-3:]
    kept[...] = own[0].astype(f32) + came[0].astype(f32)
    for slot, sent in enumerate(sends, 1):
        sent[...] = (own[slot].astype(f32) + came[slot].astype(f32)).astype(bf16)


def sum_x(own, came, after=()):
    shape = own.shape[1:]
    return call(
        sum_x_kernel,
        [sds(shape, f32)] + [sds(shape, bf16)] * 3,
        nbytes=13 * shape[0] * shape[1] * 2,
        in_specs=[VMEM] * 2 + [ANY] * len(after),
        out_specs=[VMEM] * 4,
        name="sum_x",
    )(own, came, *after)


def sum_keys_kernel(own, came, *refs):
    refs[-1][...] = (own[...] + came[...].astype(f32)).astype(bf16)


def sum_keys(own, came, after=()):
    return call(
        sum_keys_kernel,
        sds(came.shape, bf16),
        nbytes=8 * came.size,
        in_specs=[VMEM] * 2 + [ANY] * len(after),
        out_specs=VMEM,
        name="sum_keys",
    )(own, came, *after)


def rows_kernel(x, grad, gain, inv, l_kept, l_came, r_kept, r1, r2, r3, *refs):
    out = refs[-1]
    left = l_kept[...] + l_came[0:2].reshape(ROWS, HALF).astype(f32)
    right = r_kept[...]
    for came in (r1, r2, r3):
        right = right + came[...].astype(f32)
    scale = inv[:, :1]
    halves = []
    dots = jnp.zeros((ROWS, 1), f32)
    for part, cols in ((left, slice(0, HALF)), (right, slice(HALF, WIDTH))):
        scaled = gain[:, cols].astype(f32) * part
        rows = x[:, cols].astype(f32)
        dots = dots + jnp.sum(scaled * rows, axis=1, keepdims=True)
        halves.append((scaled, rows, cols))
    mean = dots * (1.0 / WIDTH)
    for scaled, rows, cols in halves:
        total = grad[:, cols].astype(f32) + scale * scaled - rows * (scale * scale * scale) * mean
        out[:, cols] = total.astype(bf16)


def token_rows(x, grad, gain, inv, left, right, after=()):
    return call(
        rows_kernel,
        sds((ROWS, WIDTH), bf16),
        nbytes=6 * ROWS * WIDTH * 2,
        in_specs=[VMEM] * 10 + [ANY] * len(after),
        out_specs=VMEM,
        name="token_rows",
    )(x, grad, gain, inv, *left, *right, *after)


def first_step():
    return jnp.logical_and(pl.program_id(0) == 0, pl.program_id(1) == 0)


def key_value_kernel(*refs):
    pieces, weight, grad, grad_other = refs[:6], refs[6], refs[7], refs[8]
    full, out, pair = refs[9:]

    @pl.when(first_step())
    def _():
        place_pieces(pieces, full)
        pair[0] = grad[...]
        pair[1] = grad_other[...]

    out[0] = dot(full[...], weight[0]).astype(bf16)


def key_value(pieces, weights, grad, grad_other):
    block = 256
    return call(
        key_value_kernel,
        [
            sds((SLOTS, WIDTH), bf16),
            sds((2, SLOTS, COLS), bf16),
            sds((2, ROWS, WIDTH), bf16),
        ],
        flops=4 * SLOTS * WIDTH * COLS,
        nbytes=2 * WIDTH * COLS * 2 + 2 * SLOTS * WIDTH * 2,
        grid=(2, COLS // block),
        in_specs=[whole(s) for s in PIECE_SHAPES]
        + [pl.BlockSpec((1, WIDTH, block), lambda p, j: (p + 1, 0, j))]
        + [whole((ROWS, WIDTH))] * 2,
        out_specs=[
            whole((SLOTS, WIDTH)),
            pl.BlockSpec((1, SLOTS, block), lambda p, j: (p, 0, j)),
            whole((2, ROWS, WIDTH)),
        ],
        name="key_value",
    )(*pieces, weights, grad, grad_other)


def grad_mixed_kernel(p0, p1, p2, p3, weight, *refs):
    full, out = refs[-2:]

    @pl.when(pl.program_id(0) == 0)
    def _():
        for slot, pair in enumerate((p0, p1, p2, p3)):
            full[pl.ds(slot * ROWS, ROWS)] = pair[0]
            full[pl.ds((4 + slot) * ROWS, ROWS)] = pair[1]

    out[...] = dot(full[...], weight[0]).astype(bf16)


def grad_mixed_of(pairs, weights, after):
    block = 256
    return call(
        grad_mixed_kernel,
        [sds((SLOTS, WIDTH), bf16), sds((SLOTS, COLS), bf16)],
        flops=2 * SLOTS * WIDTH * COLS,
        nbytes=WIDTH * COLS * 2 + 2 * SLOTS * WIDTH * 2,
        grid=(COLS // block,),
        in_specs=[whole((2, ROWS, WIDTH))] * 4
        + [pl.BlockSpec((1, WIDTH, block), lambda j: (0, 0, j))]
        + [ANY] * len(after),
        out_specs=[whole((SLOTS, WIDTH)), pl.BlockSpec((SLOTS, block), lambda j: (0, j))],
        name="grad_mixed",
    )(*pairs, weights, *after)


def one_dot_kernel(full, weight, out):
    out[...] = dot(full[...], weight[0]).astype(bf16)


def one_dot(full, weights, part):
    block = 256
    return call(
        one_dot_kernel,
        sds((SLOTS, COLS), bf16),
        flops=2 * SLOTS * WIDTH * COLS,
        nbytes=WIDTH * COLS * 2 + SLOTS * WIDTH * 2,
        grid=(COLS // block,),
        in_specs=[
            whole((SLOTS, WIDTH)),
            pl.BlockSpec((1, WIDTH, block), lambda j: (part, 0, j)),
        ],
        out_specs=pl.BlockSpec((SLOTS, block), lambda j: (0, j)),
        name="one_dot",
    )(full, weights)


def gain_rows_of(left, right):
    row = lax.broadcasted_iota(jnp.int32, (16, left.shape[1]), 0)
    rows = jnp.zeros((16, left.shape[1]), f32)
    for first, part in ((0, left), (2, right)):
        high = part.astype(bf16).astype(f32)
        rows = jnp.where(row == first, high, rows)
        rows = jnp.where(row == first + 1, part - high, rows)
    return rows.astype(bf16)


def gain_from(rows):
    rows = rows.astype(f32)
    return rows[0:1] + rows[1:2], rows[2:3] + rows[3:4]


def back_total(lefts, weight, normed):
    total = dot_rows(lefts[0][...], weight[0])
    for part in range(1, 3):
        total = total + dot_rows(lefts[part][...], weight[part])
    rounded = total.astype(bf16)
    gain = jnp.sum(rounded.astype(f32) * normed[...].astype(f32), axis=0, keepdims=True)
    return rounded, gain


def back_right_kernel(l0, l1, l2, weight, normed, *refs):
    own, sent, gain = refs[-3:]
    rounded, gain[...] = back_total((l0, l1, l2), weight, normed)
    for xbit, out in enumerate((own, sent)):
        for slot in range(4):
            start = (xbit * 4 + slot) * ROWS
            out[slot] = rounded[start:start + ROWS]


def back_left_kernel(l0, l1, l2, weight, normed, gain_right, *refs):
    rounded, gain = back_total((l0, l1, l2), weight, normed)
    gains = gain_rows_of(gain, gain_right[...])
    for slot, out in enumerate(refs[-4:]):
        for xbit in range(2):
            start = (xbit * 4 + slot) * ROWS
            out[2 * xbit] = rounded[start:start + 16]
            out[2 * xbit + 1] = rounded[start + 16:start + ROWS]
        out[4] = gains


def back_dot(kernel, first, lefts, weights, normed, extra, out_shape, after, name):
    block = 512
    return call(
        kernel,
        out_shape,
        flops=2 * 3 * SLOTS * HALF * COLS,
        nbytes=3 * HALF * COLS * 2 + 2 * SLOTS * HALF * 2,
        grid=(HALF // block,),
        in_specs=[whole((SLOTS, COLS))] * 3
        + [
            pl.BlockSpec((3, block, COLS), lambda j: (0, j + first, 0)),
            pl.BlockSpec((SLOTS, block), lambda j: (0, j + first)),
        ]
        + [pl.BlockSpec((1, block), lambda j: (0, j))] * len(extra)
        + [ANY] * len(after),
        out_specs=[
            pl.BlockSpec(v.shape[:-1] + (block,), lambda j, n=len(v.shape): (0,) * (n - 1) + (j,))
            for v in out_shape
        ],
        name=name,
    )(*lefts, weights, normed, *extra, *after)


def back_right(lefts, weights, normed, after=()):
    out = [sds((4, ROWS, HALF), bf16)] * 2 + [sds((1, HALF), f32)]
    return back_dot(
        back_right_kernel, HALF // 512, lefts, weights, normed, [], out, after, "back_right"
    )


def back_left(lefts, weights, normed, gain_right, after=()):
    out = [sds((5, 16, HALF), bf16)] * 4
    return back_dot(
        back_left_kernel, 0, lefts, weights, normed, [gain_right], out, after, "back_left"
    )


def proj_kernel(left, weight, *refs):
    rounded = dot_rows(left[...], weight[0]).astype(bf16)
    for slot in range(4):
        for xbit in range(2):
            start = (xbit * 4 + slot) * ROWS
            refs[slot][xbit] = rounded[start:start + ROWS]


def proj_parts(mixed, weights):
    block = 512
    return call(
        proj_kernel,
        [sds((2, ROWS, WIDTH), bf16)] * 4,
        flops=2 * SLOTS * WIDTH * COLS,
        nbytes=WIDTH * COLS * 2 + SLOTS * WIDTH * 2,
        grid=(WIDTH // block,),
        in_specs=[whole((SLOTS, COLS)), pl.BlockSpec((1, block, COLS), lambda j: (0, j, 0))],
        out_specs=[pl.BlockSpec((2, ROWS, block), lambda j: (0, 0, j))] * 4,
        name="proj_parts",
    )(mixed, weights)


def slot_of(row, x_index, z_index):
    block = row // ROWS
    xbit = block // 4
    slot = block - xbit * 4
    back = jnp.where(slot == 2, 3, jnp.where(slot == 3, 2, slot))
    x_from = jnp.where(xbit == 0, x_index, 1 - x_index)
    z_from = z_index - back
    z_from = jnp.where(z_from < 0, z_from + 4, z_from)
    return (x_from * 4 + z_from) * ROWS + (row - block * ROWS)


def places(meta, rows, is_text):
    slot = slot_of(rows, meta[10], meta[11])
    text = slot
    end = jnp.int32(0)
    for run in range(4):
        end = end + meta[run]
        text = text + jnp.where(slot >= end, meta[5 + run], 0)
    image = slot + meta[0]
    end = jnp.int32(0)
    for run in range(3):
        end = end + meta[5 + run]
        image = image + jnp.where(slot >= end, meta[run + 1], 0)
    image = jnp.where(slot < LI, image, FAR)
    return jnp.where(is_text, text, image)


def admitted(meta):
    group = meta[9]
    query = places(meta, lax.broadcasted_iota(jnp.int32, (SLOTS, 1), 0), group == 0)
    key_row = lax.broadcasted_iota(jnp.int32, (1, SLOTS), 1)
    own = places(meta, key_row, group == 0)
    other = places(meta, key_row, group != 0)
    return own <= query, other <= query


def head_attn(query, own_key, other_key, own_ok, other_ok):
    scale = HS ** (-0.5)
    own = jnp.where(own_ok, dot_rows(query, own_key) * scale, -1e30)
    other = jnp.where(other_ok, dot_rows(query, other_key) * scale, -1e30)
    row_max = jnp.maximum(
        jnp.max(own, axis=1, keepdims=True), jnp.max(other, axis=1, keepdims=True)
    )
    own = jnp.exp(own - row_max)
    other = jnp.exp(other - row_max)
    row_sum = jnp.sum(own, axis=1, keepdims=True) + jnp.sum(other, axis=1, keepdims=True)
    share = 1.0 / row_sum
    return own * share, other * share


def forward_kernel(meta, query, own_kv, other_kv, mixed):
    own_ok, other_ok = admitted(meta)
    for head in range(HEADS):
        cols = slice(head * HS, (head + 1) * HS)
        own, other = head_attn(
            query[:, cols], own_kv[0, :, cols], other_kv[0, :, cols], own_ok, other_ok
        )
        total = dot(own.astype(bf16), own_kv[1, :, cols])
        total = total + dot(other.astype(bf16), other_kv[1, :, cols])
        mixed[:, cols] = total.astype(bf16)


def backward_kernel(meta, query, own_kv, other_kv, mixed, grad, *refs):
    pair, own_grad, other_grad = refs[-3:]
    pair[0] = mixed[...]
    scale = HS ** (-0.5)
    own_ok, other_ok = admitted(meta)
    for head in range(HEADS):
        cols = slice(head * HS, (head + 1) * HS)
        q, g = query[:, cols], grad[:, cols]
        row_dot = jnp.sum(g.astype(f32) * mixed[:, cols].astype(f32), axis=1, keepdims=True)
        attns = head_attn(q, own_kv[0, :, cols], other_kv[0, :, cols], own_ok, other_ok)
        dq = None
        for attn, kv, kv_grad in zip(attns, (own_kv, other_kv), (own_grad, other_grad)):
            value_grad = dot_tokens(attn.astype(bf16), g)
            weight_grad = dot_rows(g, kv[1, :, cols])
            score_grad = (attn * (weight_grad - row_dot)).astype(bf16)
            part = dot(score_grad, kv[0, :, cols])
            dq = part if dq is None else dq + part
            key_grad = dot_tokens(score_grad, q) * scale
            kv_grad[0, :, cols] = key_grad.astype(kv_grad.dtype)
            kv_grad[1, :, cols] = value_grad.astype(kv_grad.dtype)
        pair[1, :, cols] = (dq * scale).astype(bf16)


ATTN_FLOPS = 2 * HEADS * SLOTS * 2 * SLOTS * HS


def attend_forward(meta, query, own_kv, other_kv):
    return call(
        forward_kernel,
        sds((SLOTS, COLS), bf16),
        flops=4 * ATTN_FLOPS,
        nbytes=6 * SLOTS * COLS * 2,
        in_specs=[SMEM] + [VMEM] * 3,
        out_specs=VMEM,
        name="attend_forward",
    )(meta, query, own_kv, other_kv)


def attend_backward(meta, query, own_kv, other_kv, mixed, grad, after):
    kv = (2, SLOTS, COLS)
    return call(
        backward_kernel,
        [sds(kv, bf16), sds(kv, f32), sds(kv, bf16)],
        flops=8 * ATTN_FLOPS,
        nbytes=12 * SLOTS * COLS * 2,
        in_specs=[SMEM] + [VMEM] * 5 + [ANY] * len(after),
        out_specs=[VMEM] * 3,
        name="attend_backward",
    )(meta, query, own_kv, other_kv, mixed, grad, *after)


def share_kernel(count, *refs):
    refs = refs[1:]
    grads = refs[3 * count:3 * count + 4]
    sent, mine = refs[-2:]

    def share(part, own, came, other):
        total = dot_tokens(own[...], grads[0][part])
        for k in range(3):
            total = total + dot_tokens(came[k], grads[k + 1][part, :SLOTS // 2])
            total = total + dot_tokens(other[k], grads[k + 1][part, SLOTS // 2:])

        @pl.when(pl.program_id(0) == 0)
        def _():
            sent[part] = total.astype(bf16)

        @pl.when(pl.program_id(0) == 1)
        def _():
            mine[part] = total

    for part in range(2):
        first = 3 * (part if count == 2 else 0)
        share(part, *refs[first:first + 3])


def weight_shares(core, chunks, grads, after=()):
    count = len(chunks)
    flat = [ref for triple in chunks for ref in triple]

    def column(i, core):
        return jnp.abs(core[0] - 1 + i)

    triple = [
        pl.BlockSpec((SLOTS, COLS), lambda i, core: (0, column(i, core))),
        pl.BlockSpec((3, SLOTS // 2, COLS), lambda i, core: (0, 0, column(i, core))),
        pl.BlockSpec((3, SLOTS // 2, COLS), lambda i, core: (0, 0, column(i, core))),
    ]
    return call(
        functools.partial(share_kernel, count),
        [sds((2, COLS, COLS), bf16), sds((2, COLS, COLS), f32)],
        flops=4 * 4 * SLOTS * 2 * COLS * COLS,
        nbytes=8 * SLOTS * COLS * 2 * (count + 2) + 2 * COLS * COLS * 6,
        grid_spec=pltpu.PrefetchScalarGridSpec(
            num_scalar_prefetch=1,
            grid=(2,),
            in_specs=triple * count + [whole((2, SLOTS, COLS))] * 4 + [ANY] * len(after),
            out_specs=[whole((2, COLS, COLS))] * 2,
        ),
        name="weight_shares",
    )(core, *flat, *grads, *after)


def chunks_over_y(full, y_index):
    sent = [
        lax.dynamic_slice(full, (0, (y_index + k) % 4 * 1024), (SLOTS // 2, 1024))
        for k in STEPS[1:]
    ]
    came = jnp.stack([lax.ppermute(v, "seq", y_shift(k)) for v, k in zip(sent, STEPS[1:])])
    other = lax.ppermute(came, "tp", X_SWAP)
    own = lax.dynamic_slice_in_dim(full, y_index * 1024, 1024, 1)
    return own, came, other


def per_device(tokens, text_gaps, image_runs, gains, w_qkv, w_out, cotangent):
    group = lax.axis_index("grp")
    tp_index = lax.axis_index("tp")
    seq_index = lax.axis_index("seq")
    x_index, z_index = tp_index // 4, tp_index % 4
    y_index, core = seq_index // 2, seq_index % 2
    x_rows = tokens[0, 0]
    w_parts = jnp.transpose(w_qkv[0], (1, 0, 2))
    valid = jnp.where((group == 0) | (tp_index * ROWS < LI), 1.0, 0.0).astype(f32)
    meta = jnp.concatenate(
        [text_gaps[0], image_runs[0], jnp.stack([group, x_index, z_index]).astype(jnp.int32)]
    )

    n_left, n_right, grad_rows, inv = norm_rows(valid.reshape(1), x_rows, gains, cotangent[0, 0])
    pieces = gather_blocks(n_left, n_right)
    grad_other = lax.ppermute(grad_rows, "tp", X_SWAP)
    normed_full, own_kv, grad_pair = key_value(pieces, w_parts, grad_rows, grad_other)
    other_kv = lax.ppermute(own_kv, "grp", GRP_SWAP)
    grad_pairs = [grad_pair] + [lax.ppermute(grad_pair, "tp", z_shift(k)) for k in STEPS[1:]]
    query = one_dot(normed_full, w_parts, 0)
    normed_chunks = chunks_over_y(normed_full, y_index)

    mixed = attend_forward(meta, query, own_kv, other_kv)
    proj = proj_parts(mixed, w_out)
    grad_full, grad_mixed = grad_mixed_of(grad_pairs, w_out, [proj[0]])
    grad_chunks = chunks_over_y(grad_full, y_index)
    pair, own_part, other_part = attend_backward(
        meta, query, own_kv, other_kv, mixed, grad_mixed, [normed_chunks[2]]
    )
    back = lax.ppermute(other_part, "grp", GRP_SWAP)

    proj_came = [lax.ppermute(proj[i], "tp", z_shift(-STEPS[i])) for i in range(1, 4)]
    pairs = [pair] + [lax.ppermute(pair, "seq", y_shift(k)) for k in STEPS[1:]]
    kv_grad = sum_keys(own_part, back, [grad_chunks[1]])
    kv_grads = [kv_grad] + [lax.ppermute(kv_grad, "seq", y_shift(k)) for k in STEPS[1:]]

    lefts = [pair[1], kv_grad[0], kv_grad[1]]
    right = back_right(lefts, w_parts, normed_full)
    proj_kept, proj_sent = sum_z(proj[0], proj_came)
    right_x = lax.ppermute(right[1], "tp", X_SWAP)
    left = back_left(lefts, w_parts, normed_full, right[2], [proj_sent])
    left_came = [lax.ppermute(left[i], "tp", z_shift(-STEPS[i])) for i in range(1, 4)]
    proj_x = lax.ppermute(proj_sent, "tp", X_SWAP)
    right_kept, *right_sends = sum_x(right[0], right_x, pairs[1:3] + [proj_x])
    right_came = [
        lax.ppermute(sent, "tp", z_shift(-k)) for sent, k in zip(right_sends, STEPS[1:])
    ]
    left_kept, left_sent, gain_kept = sum_left(left[0], left_came, pairs[3:])
    left_x = lax.ppermute(left_sent, "tp", X_SWAP)
    layer_out = ((x_rows.astype(f32) + proj_kept + proj_x.astype(f32)) * valid).astype(bf16)

    core_ref = core.reshape(1).astype(jnp.int32)
    pair_sent, pair_mine = weight_shares(
        core_ref, [grad_chunks, normed_chunks], pairs, kv_grads[1:3]
    )
    tokens_grad = token_rows(
        x_rows, grad_rows, gains, inv, (left_kept, left_x), (right_kept, *right_came), kv_grads[3:]
    )
    kv_sent, kv_mine = weight_shares(core_ref, [normed_chunks], kv_grads)
    gain_grad = sum_gain(gain_kept, left_x, gains)
    for flip in (2, 4, 1):
        gain_grad = gain_grad + lax.ppermute(gain_grad, "seq", [(i, i ^ flip) for i in range(8)])
    pair_share = pair_mine + lax.ppermute(pair_sent, "seq", CORE_SWAP).astype(f32)
    kv_share = kv_mine + lax.ppermute(kv_sent, "seq", CORE_SWAP).astype(f32)
    out_share = pair_share[0]
    qkv_share = jnp.concatenate([pair_share[1:], kv_share], axis=0)
    return (
        layer_out[None, None],
        tokens_grad[None, None],
        gain_grad,
        jnp.transpose(qkv_share, (1, 0, 2))[None],
        out_share[None],
    )


def solution(mesh):
    in_specs = (
        P("grp", "seq", "tp", None),
        P("seq", None),
        P("seq", None),
        P("grp", None),
        P("grp", None, None, "tp"),
        P("grp", None, "tp"),
        P("grp", "seq", "tp", None),
    )
    out_specs = (
        P("grp", "seq", "tp", None),
        P("grp", "seq", "tp", None),
        P("grp", None),
        P("grp", "seq", None, "tp"),
        P("grp", "seq", "tp"),
    )
    return jax.shard_map(
        per_device, mesh=mesh, in_specs=in_specs, out_specs=out_specs, check_vma=False
    )
```

time: 240 us -> 197 us (0.82)
  waiting for transfers between devices: 106 us -> 49.2 us
  local copies, waits for them, and re-layouts: 5.66 us -> 18.9 us
  Pallas kernels: 42.9 us -> 49.5 us
  starting transfers between devices: 73.9 us -> 70.2 us
  other arithmetic: 8.7 us -> 5.55 us
    ppermute x33 -> x31, waiting for transfers between devices: 74 us -> 45.6 us  [the longest x1 11.8 us: per_device(): grad_other = lax.ppermute(grad_rows, 'tp', X_SWAP)]
    ppermute x6 -> x3, waiting for transfers between devices: 15.1 us -> 0.01 us  [gather_blocks(): lax.ppermute(right_pair, 'tp', z_shift(k))]
    unnamed x28 -> x88, local copies, waits for them, and re-layouts: 5.23 us -> 16.3 us
    ppermute x3, waiting for transfers between devices: 7.07 us -> 0.01 us  [per_device(): lax.ppermute(kv_grad, 'seq', y_shift(k))]
    pallas_call x11 -> x15, Pallas kernels: 36.6 us -> 43.2 us  [the longest x2 12.3 us: weight_shares(): call(functools.partial(share_kernel, count), [sds((2, COLS, COLS), bf16),...]
    ppermute x6 -> x3, starting transfers between devices: 10.6 us -> 6.06 us  [gather_blocks(): lax.ppermute(left, 'tp', z_shift(k))]
    ppermute x1, waiting for transfers between devices: 3.63 us -> 0.01 us  [per_device(): back = lax.ppermute(other_part, 'grp', GRP_SWAP)]
    ppermute x6 -> x3, starting transfers between devices: 7.79 us -> 4.56 us  [gather_blocks(): lax.ppermute(right_pair, 'tp', z_shift(k))]
  transfers between devices with their start and end apart: 55 -> 45, of which waited for: 22 -> 13; matrix products, arithmetic and copies ran while one was open for 3% -> 3% of each run, Pallas kernels for 15% -> 22%
where the time goes in v3:
time: 197 us; the launch traced here: 195 us
  starting transfers between devices  70.2 us (36%)
  Pallas kernels  49.5 us (25%)
  waiting for transfers between devices  49.2 us (25%)
  local copies, waits for them, and re-layouts  18.9 us (10%)
  other arithmetic  5.55 us (3%)
    unnamed x88, local copies, waits for them, and re-layouts  16.3 us
    pallas_call x2, Pallas kernels, weight_shares(): call(functools.partial(share_kernel, count), [sds((2, COLS, COLS), bf16),...  12.3 us
    ppermute x1, waiting for transfers between devices, per_device(): grad_other = lax.ppermute(grad_rows, 'tp', X_SWAP)  11.8 us
    ppermute x6, starting transfers between devices, chunks_over_y(): lax.ppermute(v, 'seq', y_shift(k))  11.4 us
    ppermute x1, waiting for transfers between devices, per_device(): left_x = lax.ppermute(left_sent, 'tp', X_SWAP)  10.8 us
    pallas_call x2, Pallas kernels, back_dot(): call(kernel, out_shape, flops=2 * 3 * SLOTS * HALF * COLS, nbytes=3 * HAL...  10.6 us
    ppermute x3, waiting for transfers between devices, per_device(): lax.ppermute(left[i], 'tp', z_shift(-STEPS[i]))  9.04 us
    ppermute x3, starting transfers between devices, per_device(): lax.ppermute(grad_pair, 'tp', z_shift(k))  8.47 us
  transfers between devices with their start and end apart: 45, of which 13 were waited for; matrix products, arithmetic and copies ran while one was open for 3% of the time, Pallas kernels for 22%

profile of v3, /device:TPU:0, one launch (start us, length us, event | category | flops | bytes accessed | tf_op | source)
XLA Modules:
  0.0 194.6 jit_solution(15625817919059114282)
XLA Ops:
  3.5 4.0 %collective-permute-start.2 = (bf16[32,2048]{1,0:T(8,128)(2,1)S(1)}, bf16[32,2048]{1,0:T(8,128)(2,1)S(1)}, u32[]{:S(2)}, u32[]{:S(2)}) collective-permute-start(bf16[32,2048]{1,0:T(8,128)(2,1)S(1)} %get-tuple-element.41), channel_id=1, source_target_pairs={{0,2},{1,3},{2,0},{3,1},{4,6},{5,7},{6,4},{7,5},{8,10},{9,11},{10,... | collective-permute-start | bytes 393224 | tf_op jit(solution)/shard_map/ppermute | solution.py:99
  8.3 1.3 collective-permute-start
  9.6 1.5 collective-permute-start.4
  11.4 3.2 %collective-permute-done.1 = bf16[32,2048]{1,0:T(8,128)(2,1)S(1)} collective-permute-done((bf16[32,2048]{1,0:T(8,128)(2,1)S(1)}, bf16[32,2048]{1,0:T(8,128)(2,1)S(1)}, u32[]{:S(2)}, u32[]{:S(2)}) %collective-permute-start.1) | collective-permute-done | bytes 131104 | tf_op jit(solution)/shard_map/ppermute | solution.py:99
  14.7 1.6 collective-permute-start.3
  17.9 2.3 %collective-permute-start.6 = (bf16[2,32,2048]{2,1,0:T(8,128)(2,1)S(1)}, bf16[2,32,2048]{2,1,0:T(8,128)(2,1)S(1)}, u32[]{:S(2)}, u32[]{:S(2)}) collective-permute-start(bf16[2,32,2048]{2,1,0:T(8,128)(2,1)S(1)} %pad_maximum_fusion.3.refs_2_), channel_id=1, source_target_pairs={{0,3},{1,0},{2,1},{3,2},{4,7},{5,4},{6,5},{7,6},{8,11},{9,8},{10,9... | collective-permute-start | bytes 786440 | tf_op jit(solution)/shard_map/ppermute | solution.py:100
  20.1 1.3 collective-permute-start.7
  21.4 11.8 %collective-permute-done.8.refs_8_ = bf16[32,4096]{1,0:T(8,128)(2,1)S(1)} collective-permute-done((bf16[32,4096]{1,0:T(8,128)(2,1)S(1)}, bf16[32,4096]{1,0:T(8,128)(2,1)S(1)}, u32[]{:S(2)}, u32[]{:S(2)}) %collective-permute-start.8) | collective-permute-done | bytes 262176 | tf_op jit(solution)/shard_map/ppermute | solution.py:637
  40.0 6.4 %key_value.1 = (bf16[256,4096]{1,0:T(8,128)(2,1)S(1)}, bf16[2,256,512]{2,1,0:T(8,128)(2,1)}, bf16[2,32,4096]{2,1,0:T(8,128)(2,1)}) custom-call(bf16[4,32,2048]{2,1,0:T(8,128)(2,1)S(1)} %pad_maximum_fusion.2.refs_0_, bf16[4,32,2048]{2,1,0:T(8,128)(2,1)S(1)} %copy-done.25, bf16[2,32,2048]{2,1,0:T(8,128)(2,1)S(1)} %pad_maximum_fusion.3.refs_2_, ...), custom_call_target="tpu_custom_call" | custom-call | flops 2147483648 | bytes 12582912 | tf_op jit(solution)/shard_map/key_value/pallas_call | solution.py:273
  46.5 3.3 %collective-permute-start.19 = (bf16[128,1024]{1,0:T(8,128)(2,1)S(1)}, bf16[128,1024]{1,0:T(8,128)(2,1)}, u32[]{:S(2)}, u32[]{:S(2)}) collective-permute-start(bf16[128,1024]{1,0:T(8,128)(2,1)S(1)} %get-tuple-element.83), channel_id=1, source_target_pairs={{0,32},{8,40},{16,48},{24,56},{32,0},{40,8},{48,16},{56,24},{1,33}... | collective-permute-start | bytes 786440 | tf_op jit(solution)/shard_map/ppermute | solution.py:616
  50.9 3.0 %collective-permute-start.9 = (bf16[2,256,512]{2,1,0:T(8,128)(2,1)}, bf16[2,256,512]{2,1,0:T(8,128)(2,1)}, u32[]{:S(2)}, u32[]{:S(2)}) collective-permute-start(bf16[2,256,512]{2,1,0:T(8,128)(2,1)} %get-tuple-element.45.own_kv), channel_id=1, source_target_pairs={{0,64},{64,0},{1,65},{65,1},{2,66},{66,2},{3,67},{67,3},{4,68},{68... | collective-permute-start | bytes 1572872 | tf_op jit(solution)/shard_map/ppermute | solution.py:639
  56.0 3.9 %collective-permute-start.15 = (bf16[2,32,4096]{2,1,0:T(8,128)(2,1)}, bf16[2,32,4096]{2,1,0:T(8,128)(2,1)S(1)}, u32[]{:S(2)}, u32[]{:S(2)}) collective-permute-start(bf16[2,32,4096]{2,1,0:T(8,128)(2,1)} %get-tuple-element.53.p0), channel_id=1, source_target_pairs={{0,3},{1,0},{2,1},{3,2},{4,7},{5,4},{6,5},{7,6},{8,11},{9,8},{10,9... | collective-permute-start | bytes 1572872 | tf_op jit(solution)/shard_map/ppermute | solution.py:640
  61.1 3.5 %collective-permute-start.16 = (bf16[2,32,4096]{2,1,0:T(8,128)(2,1)}, bf16[2,32,4096]{2,1,0:T(8,128)(2,1)}, u32[]{:S(2)}, u32[]{:S(2)}) collective-permute-start(bf16[2,32,4096]{2,1,0:T(8,128)(2,1)} %get-tuple-element.53.p0), channel_id=1, source_target_pairs={{0,2},{1,3},{2,0},{3,1},{4,6},{5,7},{6,4},{7,5},{8,10},{9,11},{10,... | collective-permute-start | bytes 1572872 | tf_op jit(solution)/shard_map/ppermute | solution.py:640
  64.7 1.2 pad_maximum_fusion.refs_5_.refs_2_
  65.9 1.6 collective-permute-start.20
  67.5 3.2 %one_dot.1.query = bf16[256,512]{1,0:T(8,128)(2,1)S(1)} custom-call(bf16[256,4096]{1,0:T(8,128)(2,1)S(1)} %get-tuple-element.44.full.normed, bf16[3,4096,512]{2,1,0:T(8,128)(2,1)} %bitcast.44), custom_call_target="tpu_custom_call" | custom-call | flops 1073741824 | bytes 6291456 | tf_op jit(solution)/shard_map/one_dot/pallas_call | solution.py:329
  70.7 3.1 %attend_forward.1.left.mixed = bf16[256,512]{1,0:T(8,128)(2,1)S(1)} custom-call(s32[12]{0:T(128)S(1)} %concatenate.6.meta, bf16[256,512]{1,0:T(8,128)(2,1)S(1)} %one_dot.1.query, bf16[2,256,512]{2,1,0:T(8,128)(2,1)} %get-tuple-element.45.own_kv, bf16[2,256,512]{2,1,0:T(8,128)(2,1)} %collective-permute-done.9.other_kv), custom_call_target="tpu_custom_call" | custom-call | flops 536870912 | bytes 1572864 | tf_op jit(solution)/shard_map/attend_forward/pallas_call | solution.py:536
  73.8 2.9 %proj_parts.1 = (bf16[2,32,4096]{2,1,0:T(8,128)(2,1)S(1)}, bf16[2,32,4096]{2,1,0:T(8,128)(2,1)S(1)}, bf16[2,32,4096]{2,1,0:T(8,128)(2,1)S(1)}, bf16[2,32,4096]{2,1,0:T(8,128)(2,1)S(1)}) custom-call(bf16[256,512]{1,0:T(8,128)(2,1)S(1)} %attend_forward.1.left.mixed, bf16[1,4096,512]{2,1,0:T(8,128)(2,1)S(1)} %copy-done), custom_call_target="tpu_custom_call" | custom-call | flops 1073741824 | bytes 6291456 | tf_op jit(solution)/shard_map/proj_parts/pallas_call | solution.py:435
  76.7 3.6 %collective-permute-done.15.p2 = bf16[2,32,4096]{2,1,0:T(8,128)(2,1)S(1)} collective-permute-done((bf16[2,32,4096]{2,1,0:T(8,128)(2,1)}, bf16[2,32,4096]{2,1,0:T(8,128)(2,1)S(1)}, u32[]{:S(2)}, u32[]{:S(2)}) %collective-permute-start.15) | collective-permute-done | bytes 524320 | tf_op jit(solution)/shard_map/ppermute | solution.py:640
  81.3 3.0 %grad_mixed.1 = (bf16[256,4096]{1,0:T(8,128)(2,1)S(1)}, bf16[256,512]{1,0:T(8,128)(2,1)S(1)}) custom-call(bf16[2,32,4096]{2,1,0:T(8,128)(2,1)} %get-tuple-element.53.p0, bf16[2,32,4096]{2,1,0:T(8,128)(2,1)S(1)} %collective-permute-done.14.p1, bf16[2,32,4096]{2,1,0:T(8,128)(2,1)S(1)} %collective-permute-done.15.p2, ...), custom_call_target="tpu_custom_call" | custom-call | flops 1073741824 | bytes 8388608 | tf_op jit(solution)/shard_map/grad_mixed/pallas_call | solution.py:309
  84.4 2.3 %collective-permute-start.24 = (bf16[128,1024]{1,0:T(8,128)(2,1)S(1)}, bf16[128,1024]{1,0:T(8,128)(2,1)S(1)}, u32[]{:S(2)}, u32[]{:S(2)}) collective-permute-start(bf16[128,1024]{1,0:T(8,128)(2,1)S(1)} %get-tuple-element.80), channel_id=1, source_target_pairs={{0,32},{8,40},{16,48},{24,56},{32,0},{40,8},{48,16},{56,24},{1,33}... | collective-permute-start | bytes 786440 | tf_op jit(solution)/shard_map/ppermute | solution.py:616
  86.6 1.1 collective-permute-start.23
  87.8 3.5 %collective-permute-start.10 = (bf16[2,32,4096]{2,1,0:T(8,128)(2,1)S(1)}, bf16[2,32,4096]{2,1,0:T(8,128)(2,1)S(1)}, u32[]{:S(2)}, u32[]{:S(2)}) collective-permute-start(bf16[2,32,4096]{2,1,0:T(8,128)(2,1)S(1)} %get-tuple-element.47), channel_id=1, source_target_pairs={{0,3},{1,0},{2,1},{3,2},{4,7},{5,4},{6,5},{7,6},{8,11},{9,8},{10,9... | collective-permute-start | bytes 1572872 | tf_op jit(solution)/shard_map/ppermute | solution.py:653
  92.8 2.7 %collective-permute-start.22 = (bf16[128,1024]{1,0:T(8,128)(2,1)S(1)}, bf16[128,1024]{1,0:T(8,128)(2,1)S(1)}, u32[]{:S(2)}, u32[]{:S(2)}) collective-permute-start(bf16[128,1024]{1,0:T(8,128)(2,1)S(1)} %get-tuple-element.79), channel_id=1, source_target_pairs={{0,16},{8,24},{16,32},{24,40},{32,48},{40,56},{48,0},{56,8},{1,17}... | collective-permute-start | bytes 786440 | tf_op jit(solution)/shard_map/ppermute | solution.py:616
  95.5 4.9 %attend_backward.1 = (bf16[2,256,512]{2,1,0:T(8,128)(2,1)S(1)}, f32[2,256,512]{2,1,0:T(8,128)S(1)}, bf16[2,256,512]{2,1,0:T(8,128)(2,1)S(1)}) custom-call(s32[12]{0:T(128)S(1)} %concatenate.6.meta, bf16[256,512]{1,0:T(8,128)(2,1)S(1)} %one_dot.1.query, bf16[2,256,512]{2,1,0:T(8,128)(2,1)} %get-tuple-element.45.own_kv, ...), custom_call_target="tpu_custom_call" | custom-call | flops 1073741824 | bytes 3145728 | tf_op jit(solution)/shard_map/attend_backward/pallas_call | solution.py:549
  100.5 3.1 %collective-permute-start.21 = (bf16[2,256,512]{2,1,0:T(8,128)(2,1)S(1)}, bf16[2,256,512]{2,1,0:T(8,128)(2,1)S(1)}, u32[]{:S(2)}, u32[]{:S(2)}) collective-permute-start(bf16[2,256,512]{2,1,0:T(8,128)(2,1)S(1)} %get-tuple-element.57), channel_id=1, source_target_pairs={{0,64},{64,0},{1,65},{65,1},{2,66},{66,2},{3,67},{67,3},{4,68},{68... | collective-permute-start | bytes 1572872 | tf_op jit(solution)/shard_map/ppermute | solution.py:651
  103.7 2.9 %collective-permute-start.28 = (bf16[2,256,512]{2,1,0:T(8,128)(2,1)S(1)}, bf16[2,256,512]{2,1,0:T(8,128)(2,1)S(1)}, u32[]{:S(2)}, u32[]{:S(2)}) collective-permute-start(bf16[2,256,512]{2,1,0:T(8,128)(2,1)S(1)} %get-tuple-element.55.refs_7_), channel_id=1, source_target_pairs={{0,32},{8,40},{16,48},{24,56},{32,0},{40,8},{48,16},{56,24},{1,33}... | collective-permute-start | bytes 1572872 | tf_op jit(solution)/shard_map/ppermute | solution.py:654
  106.6 3.3 %collective-permute-done.10.c1 = bf16[2,32,4096]{2,1,0:T(8,128)(2,1)S(1)} collective-permute-done((bf16[2,32,4096]{2,1,0:T(8,128)(2,1)S(1)}, bf16[2,32,4096]{2,1,0:T(8,128)(2,1)S(1)}, u32[]{:S(2)}, u32[]{:S(2)}) %collective-permute-start.10) | collective-permute-done | bytes 524320 | tf_op jit(solution)/shard_map/ppermute | solution.py:653
  110.2 3.1 %collective-permute-done.11.c2 = bf16[2,32,4096]{2,1,0:T(8,128)(2,1)S(1)} collective-permute-done((bf16[2,32,4096]{2,1,0:T(8,128)(2,1)S(1)}, bf16[2,32,4096]{2,1,0:T(8,128)(2,1)S(1)}, u32[]{:S(2)}, u32[]{:S(2)}) %collective-permute-start.11) | collective-permute-done | bytes 524320 | tf_op jit(solution)/shard_map/ppermute | solution.py:653
  113.9 1.6 collective-permute-start.13
  115.6 5.6 %back_right.1 = (bf16[4,32,2048]{2,1,0:T(8,128)(2,1)S(1)}, bf16[4,32,2048]{2,1,0:T(8,128)(2,1)}, f32[1,2048]{1,0:T(1,128)S(1)}) custom-call(bf16[256,512]{1,0:T(8,128)(2,1)S(1)} %slice_bitcast_fusion.2.l0, bf16[256,512]{1,0:T(8,128)(2,1)S(1)} %get-tuple-element.86.l1, bf16[256,512]{1,0:T(8,128)(2,1)S(1)} %get-tuple-element.85.l2, ...), custom_call_target="tpu_custom_call" | custom-call | flops 1610612736 | bytes 8388608 | tf_op jit(solution)/shard_map/back_right/pallas_call | solution.py:390
  122.1 5.0 %back_left.1 = (bf16[5,16,2048]{2,1,0:T(8,128)(2,1)S(1)}, bf16[5,16,2048]{2,1,0:T(8,128)(2,1)S(1)}, bf16[5,16,2048]{2,1,0:T(8,128)(2,1)S(1)}, bf16[5,16,2048]{2,1,0:T(8,128)(2,1)S(1)}) custom-call(bf16[256,512]{1,0:T(8,128)(2,1)S(1)} %slice_bitcast_fusion.2.l0, bf16[256,512]{1,0:T(8,128)(2,1)S(1)} %get-tuple-element.86.l1, ...), custom_call_target="tpu_custom_call" | custom-call | flops 1610612736 | bytes 8388608 | tf_op jit(solution)/shard_map/back_left/pallas_call | solution.py:390
  127.1 3.3 %collective-permute-start.25 = (bf16[5,16,2048]{2,1,0:T(8,128)(2,1)S(1)}, bf16[5,16,2048]{2,1,0:T(8,128)(2,1)S(1)}, u32[]{:S(2)}, u32[]{:S(2)}) collective-permute-start(bf16[5,16,2048]{2,1,0:T(8,128)(2,1)S(1)} %get-tuple-element.61), channel_id=1, source_target_pairs={{0,3},{1,0},{2,1},{3,2},{4,7},{5,4},{6,5},{7,6},{8,11},{9,8},{10,9... | collective-permute-start | bytes 983048 | tf_op jit(solution)/shard_map/ppermute | solution.py:663
  130.4 1.7 collective-permute-start.27
  132.7 2.4 %collective-permute-done.25.c1 = bf16[5,16,2048]{2,1,0:T(8,128)(2,1)S(1)} collective-permute-done((bf16[5,16,2048]{2,1,0:T(8,128)(2,1)S(1)}, bf16[5,16,2048]{2,1,0:T(8,128)(2,1)S(1)}, u32[]{:S(2)}, u32[]{:S(2)}) %collective-permute-start.25) | collective-permute-done | bytes 327712 | tf_op jit(solution)/shard_map/ppermute | solution.py:663
  135.5 6.7 %collective-permute-done.26.c2 = bf16[5,16,2048]{2,1,0:T(8,128)(2,1)S(1)} collective-permute-done((bf16[5,16,2048]{2,1,0:T(8,128)(2,1)S(1)}, bf16[5,16,2048]{2,1,0:T(8,128)(2,1)S(1)}, u32[]{:S(2)}, u32[]{:S(2)}) %collective-permute-start.26) | collective-permute-done | bytes 327712 | tf_op jit(solution)/shard_map/ppermute | solution.py:663
  142.2 3.2 %collective-permute-start.42 = (bf16[2,256,512]{2,1,0:T(8,128)(2,1)S(1)}, bf16[2,256,512]{2,1,0:T(8,128)(2,1)}, u32[]{:S(2)}, u32[]{:S(2)}) collective-permute-start(bf16[2,256,512]{2,1,0:T(8,128)(2,1)S(1)} %sum_keys.1.refs_4_), channel_id=1, source_target_pairs={{0,48},{8,56},{16,0},{24,8},{32,16},{40,24},{48,32},{56,40},{1,49}... | collective-permute-start | bytes 1572872 | tf_op jit(solution)/shard_map/ppermute | solution.py:656
  147.7 10.8 %collective-permute-done.29.l_came.came = bf16[3,16,2048]{2,1,0:T(8,128)(2,1)S(1)} collective-permute-done((bf16[3,16,2048]{2,1,0:T(8,128)(2,1)S(1)}, bf16[3,16,2048]{2,1,0:T(8,128)(2,1)S(1)}, u32[]{:S(2)}, u32[]{:S(2)}) %collective-permute-start.29) | collective-permute-done | bytes 196640 | tf_op jit(solution)/shard_map/ppermute | solution.py:670
  159.2 1.9 collective-permute-start.36
  165.6 1.3 sum_x.1
  166.9 1.3 collective-permute-done.37
  169.0 1.3 collective-permute-start.34
  170.3 2.5 %collective-permute-start.35 = (bf16[32,2048]{1,0:T(8,128)(2,1)S(1)}, bf16[32,2048]{1,0:T(8,128)(2,1)S(1)}, u32[]{:S(2)}, u32[]{:S(2)}) collective-permute-start(bf16[32,2048]{1,0:T(8,128)(2,1)S(1)} %get-tuple-element.71), channel_id=1, source_target_pairs={{0,2},{1,3},{2,0},{3,1},{4,6},{5,7},{6,4},{7,5},{8,10},{9,11},{10,... | collective-permute-start | bytes 393224 | tf_op jit(solution)/shard_map/ppermute | solution.py:667
  172.8 2.1 %collective-permute-start.38 = (f32[1,4096]{1,0:T(1,128)S(1)}, f32[1,4096]{1,0:T(1,128)S(1)}, u32[]{:S(2)}, u32[]{:S(2)}) collective-permute-start(f32[1,4096]{1,0:T(1,128)S(1)} %add.82), channel_id=1, source_target_pairs={{0,32},{8,40},{16,48},{24,56},{32,0},{40,8},{48,16},{56,24},{1,33}... | collective-permute-start | bytes 49160 | tf_op jit(solution)/shard_map/ppermute | solution.py:683
  174.9 6.0 %weight_shares.2 = (bf16[2,512,512]{2,1,0:T(8,128)(2,1)S(1)}, f32[2,512,512]{2,1,0:T(8,128)S(1)}) custom-call(s32[1]{0:T(128)} %bitcast.28.refs_0_, bf16[256,1024]{1,0:T(8,128)(2,1)S(1)} %constant_dynamic-slice_fusion.1.refs_1_, bf16[3,128,1024]{2,1,0:T(8,128)(2,1)S(1)} %pad_maximum_fusion.1.refs_0_.refs_2_, ...), custom_call_target="tpu_custom_call" | custom-call | flops 2147483648 | bytes 11534336 | tf_op jit(solution)/shard_map/weight_shares/pallas_call | solution.py:596
  181.6 6.3 %weight_shares.3 = (bf16[2,512,512]{2,1,0:T(8,128)(2,1)S(1)}, f32[2,512,512]{2,1,0:T(8,128)S(1)}) custom-call(s32[1]{0:T(128)} %bitcast.28.refs_0_, bf16[256,1024]{1,0:T(8,128)(2,1)S(1)} %constant_dynamic-slice_fusion.refs_4_.refs_1_, bf16[3,128,1024]{2,1,0:T(8,128)(2,1)S(1)} %copy-done.9, bf16[3,128,1024]{2,1,0:T(8,128)(2,1)S(1)} %copy-done.40, ...), custom_call_target="tpu_custom_call" | custom-call | flops 2147483648 | bytes 9437184 | tf_op jit(solution)/shard_map/weight_shares/pallas_call | solution.py:596
  191.1 1.1 fusion.1
  192.6 2.0 %maximum_bitcast_fusion = f32[1,512,3,512]{3,1,2,0:T(8,128)} fusion(f32[2,512,512]{2,1,0:T(8,128)S(1)} %convert_add_fusion, f32[1,512,512]{2,1,0:T(8,128)S(1)} %get-tuple-element.78), kind=kLoop, calls=%fused_computation | loop fusion | flops 786432 | bytes 6291456 | tf_op jit(solution)/shard_map/broadcast_in_dim | solution.py:692
  (166 shorter events, 34.8 us)
Async XLA Ops:
  3.5 43.0 %copy-start.5 = (bf16[32,4096]{1,0:T(8,128)(2,1)}, bf16[32,4096]{1,0:T(8,128)(2,1)S(1)}, u32[]{:S(2)}) copy-start(bf16[32,4096]{1,0:T(8,128)(2,1)S(1)} %get-tuple-element.43.refs_7_.grad) | copy-start | bytes 786436
  3.5 7.9 %collective-permute-start.2 = (bf16[32,2048]{1,0:T(8,128)(2,1)S(1)}, bf16[32,2048]{1,0:T(8,128)(2,1)S(1)}, u32[]{:S(2)}, u32[]{:S(2)}) collective-permute-start(bf16[32,2048]{1,0:T(8,128)(2,1)S(1)} %get-tuple-element.41), channel_id=1, source_target_pairs={{0,2},{1,3},{2,0},{3,1},{4,6},{5,7},{6,4},{7,5},{8,10},{9,11},{10,... | collective-permute-start | bytes 393224 | tf_op jit(solution)/shard_map/ppermute | solution.py:99
  7.5 7.1 %collective-permute-start.1 = (bf16[32,2048]{1,0:T(8,128)(2,1)S(1)}, bf16[32,2048]{1,0:T(8,128)(2,1)S(1)}, u32[]{:S(2)}, u32[]{:S(2)}) collective-permute-start(bf16[32,2048]{1,0:T(8,128)(2,1)S(1)} %get-tuple-element.41), channel_id=1, source_target_pairs={{0,3},{1,0},{2,1},{3,2},{4,7},{5,4},{6,5},{7,6},{8,11},{9,8},{10,9... | collective-permute-start | bytes 393224 | tf_op jit(solution)/shard_map/ppermute | solution.py:99
  8.3 6.4 %collective-permute-start = (bf16[32,2048]{1,0:T(8,128)(2,1)S(1)}, bf16[32,2048]{1,0:T(8,128)(2,1)S(1)}, u32[]{:S(2)}, u32[]{:S(2)}) collective-permute-start(bf16[32,2048]{1,0:T(8,128)(2,1)S(1)} %get-tuple-element.41), channel_id=1, source_target_pairs={{0,1},{1,2},{2,3},{3,0},{4,5},{5,6},{6,7},{7,4},{8,9},{9,10},{10,1... | collective-permute-start | bytes 393224 | tf_op jit(solution)/shard_map/ppermute | solution.py:99
  9.6 7.2 %collective-permute-start.4 = (bf16[32,2048]{1,0:T(8,128)(2,1)S(1)}, bf16[32,2048]{1,0:T(8,128)(2,1)S(1)}, u32[]{:S(2)}, u32[]{:S(2)}) collective-permute-start(bf16[32,2048]{1,0:T(8,128)(2,1)S(1)} %get-tuple-element.42), channel_id=1, source_target_pairs={{0,4},{1,5},{2,6},{3,7},{4,0},{5,1},{6,2},{7,3},{8,12},{9,13},{10,... | collective-permute-start | bytes 393224 | tf_op jit(solution)/shard_map/ppermute | solution.py:98
  14.7 20.7 %collective-permute-start.3 = (bf16[4,32,2048]{2,1,0:T(8,128)(2,1)S(1)}, bf16[4,32,2048]{2,1,0:T(8,128)(2,1)S(1)}, u32[]{:S(2)}, u32[]{:S(2)}) collective-permute-start(bf16[4,32,2048]{2,1,0:T(8,128)(2,1)S(1)} %pad_maximum_fusion.2.refs_0_), channel_id=1, source_target_pairs={{0,4},{1,5},{2,6},{3,7},{4,0},{5,1},{6,2},{7,3},{8,12},{9,13},{10,... | collective-permute-start | bytes 1572872 | tf_op jit(solution)/shard_map/ppermute | solution.py:102
  16.3 17.0 %collective-permute-start.8 = (bf16[32,4096]{1,0:T(8,128)(2,1)S(1)}, bf16[32,4096]{1,0:T(8,128)(2,1)S(1)}, u32[]{:S(2)}, u32[]{:S(2)}) collective-permute-start(bf16[32,4096]{1,0:T(8,128)(2,1)S(1)} %get-tuple-element.43.refs_7_.grad), channel_id=1, source_target_pairs={{0,4},{1,5},{2,6},{3,7},{4,0},{5,1},{6,2},{7,3},{8,12},{9,13},{10,... | collective-permute-start | bytes 786440 | tf_op jit(solution)/shard_map/ppermute | solution.py:637
  16.8 16.4 %collective-permute-start.5 = (bf16[2,32,2048]{2,1,0:T(8,128)(2,1)S(1)}, bf16[2,32,2048]{2,1,0:T(8,128)(2,1)S(1)}, u32[]{:S(2)}, u32[]{:S(2)}) collective-permute-start(bf16[2,32,2048]{2,1,0:T(8,128)(2,1)S(1)} %pad_maximum_fusion.3.refs_2_), channel_id=1, source_target_pairs={{0,1},{1,2},{2,3},{3,0},{4,5},{5,6},{6,7},{7,4},{8,9},{9,10},{10,1... | collective-permute-start | bytes 786440 | tf_op jit(solution)/shard_map/ppermute | solution.py:100
  17.9 16.1 %collective-permute-start.6 = (bf16[2,32,2048]{2,1,0:T(8,128)(2,1)S(1)}, bf16[2,32,2048]{2,1,0:T(8,128)(2,1)S(1)}, u32[]{:S(2)}, u32[]{:S(2)}) collective-permute-start(bf16[2,32,2048]{2,1,0:T(8,128)(2,1)S(1)} %pad_maximum_fusion.3.refs_2_), channel_id=1, source_target_pairs={{0,3},{1,0},{2,1},{3,2},{4,7},{5,4},{6,5},{7,6},{8,11},{9,8},{10,9... | collective-permute-start | bytes 786440 | tf_op jit(solution)/shard_map/ppermute | solution.py:100
  20.1 14.5 %collective-permute-start.7 = (bf16[2,32,2048]{2,1,0:T(8,128)(2,1)S(1)}, bf16[2,32,2048]{2,1,0:T(8,128)(2,1)S(1)}, u32[]{:S(2)}, u32[]{:S(2)}) collective-permute-start(bf16[2,32,2048]{2,1,0:T(8,128)(2,1)S(1)} %pad_maximum_fusion.3.refs_2_), channel_id=1, source_target_pairs={{0,2},{1,3},{2,0},{3,1},{4,6},{5,7},{6,4},{7,5},{8,10},{9,11},{10,... | collective-permute-start | bytes 786440 | tf_op jit(solution)/shard_map/ppermute | solution.py:100
  46.5 9.4 %collective-permute-start.19 = (bf16[128,1024]{1,0:T(8,128)(2,1)S(1)}, bf16[128,1024]{1,0:T(8,128)(2,1)}, u32[]{:S(2)}, u32[]{:S(2)}) collective-permute-start(bf16[128,1024]{1,0:T(8,128)(2,1)S(1)} %get-tuple-element.83), channel_id=1, source_target_pairs={{0,32},{8,40},{16,48},{24,56},{32,0},{40,8},{48,16},{56,24},{1,33}... | collective-permute-start | bytes 786440 | tf_op jit(solution)/shard_map/ppermute | solution.py:616
  49.8 10.6 %collective-permute-start.18 = (bf16[128,1024]{1,0:T(8,128)(2,1)S(1)}, bf16[128,1024]{1,0:T(8,128)(2,1)S(1)}, u32[]{:S(2)}, u32[]{:S(2)}) collective-permute-start(bf16[128,1024]{1,0:T(8,128)(2,1)S(1)} %get-tuple-element.84), channel_id=1, source_target_pairs={{0,48},{8,56},{16,0},{24,8},{32,16},{40,24},{48,32},{56,40},{1,49}... | collective-permute-start | bytes 786440 | tf_op jit(solution)/shard_map/ppermute | solution.py:616
  50.9 19.8 %collective-permute-start.9 = (bf16[2,256,512]{2,1,0:T(8,128)(2,1)}, bf16[2,256,512]{2,1,0:T(8,128)(2,1)}, u32[]{:S(2)}, u32[]{:S(2)}) collective-permute-start(bf16[2,256,512]{2,1,0:T(8,128)(2,1)} %get-tuple-element.45.own_kv), channel_id=1, source_target_pairs={{0,64},{64,0},{1,65},{65,1},{2,66},{66,2},{3,67},{67,3},{4,68},{68... | collective-permute-start | bytes 1572872 | tf_op jit(solution)/shard_map/ppermute | solution.py:639
  53.9 10.8 %collective-permute-start.17 = (bf16[128,1024]{1,0:T(8,128)(2,1)S(1)}, bf16[128,1024]{1,0:T(8,128)(2,1)}, u32[]{:S(2)}, u32[]{:S(2)}) collective-permute-start(bf16[128,1024]{1,0:T(8,128)(2,1)S(1)} %get-tuple-element.82), channel_id=1, source_target_pairs={{0,16},{8,24},{16,32},{24,40},{32,48},{40,56},{48,0},{56,8},{1,17}... | collective-permute-start | bytes 786440 | tf_op jit(solution)/shard_map/ppermute | solution.py:616
  54.9 21.8 %collective-permute-start.14 = (bf16[2,32,4096]{2,1,0:T(8,128)(2,1)}, bf16[2,32,4096]{2,1,0:T(8,128)(2,1)S(1)}, u32[]{:S(2)}, u32[]{:S(2)}) collective-permute-start(bf16[2,32,4096]{2,1,0:T(8,128)(2,1)} %get-tuple-element.53.p0), channel_id=1, source_target_pairs={{0,1},{1,2},{2,3},{3,0},{4,5},{5,6},{6,7},{7,4},{8,9},{9,10},{10,1... | collective-permute-start | bytes 1572872 | tf_op jit(solution)/shard_map/ppermute | solution.py:640
  56.0 24.3 %collective-permute-start.15 = (bf16[2,32,4096]{2,1,0:T(8,128)(2,1)}, bf16[2,32,4096]{2,1,0:T(8,128)(2,1)S(1)}, u32[]{:S(2)}, u32[]{:S(2)}) collective-permute-start(bf16[2,32,4096]{2,1,0:T(8,128)(2,1)} %get-tuple-element.53.p0), channel_id=1, source_target_pairs={{0,3},{1,0},{2,1},{3,2},{4,7},{5,4},{6,5},{7,6},{8,11},{9,8},{10,9... | collective-permute-start | bytes 1572872 | tf_op jit(solution)/shard_map/ppermute | solution.py:640
  61.1 20.2 %collective-permute-start.16 = (bf16[2,32,4096]{2,1,0:T(8,128)(2,1)}, bf16[2,32,4096]{2,1,0:T(8,128)(2,1)}, u32[]{:S(2)}, u32[]{:S(2)}) collective-permute-start(bf16[2,32,4096]{2,1,0:T(8,128)(2,1)} %get-tuple-element.53.p0), channel_id=1, source_target_pairs={{0,2},{1,3},{2,0},{3,1},{4,6},{5,7},{6,4},{7,5},{8,10},{9,11},{10,... | collective-permute-start | bytes 1572872 | tf_op jit(solution)/shard_map/ppermute | solution.py:640
  65.9 26.9 %collective-permute-start.20 = (bf16[3,128,1024]{2,1,0:T(8,128)(2,1)S(1)}, bf16[3,128,1024]{2,1,0:T(8,128)(2,1)S(1)}, u32[]{:S(2)}, u32[]{:S(2)}) collective-permute-start(bf16[3,128,1024]{2,1,0:T(8,128)(2,1)S(1)} %pad_maximum_fusion.refs_5_.refs_2_), channel_id=1, source_target_pairs={{0,4},{1,5},{2,6},{3,7},{4,0},{5,1},{6,2},{7,3},{8,12},{9,13},{10,... | collective-permute-start | bytes 2359304 | tf_op jit(solution)/shard_map/ppermute | solution.py:617
  84.4 8.0 %collective-permute-start.24 = (bf16[128,1024]{1,0:T(8,128)(2,1)S(1)}, bf16[128,1024]{1,0:T(8,128)(2,1)S(1)}, u32[]{:S(2)}, u32[]{:S(2)}) collective-permute-start(bf16[128,1024]{1,0:T(8,128)(2,1)S(1)} %get-tuple-element.80), channel_id=1, source_target_pairs={{0,32},{8,40},{16,48},{24,56},{32,0},{40,8},{48,16},{56,24},{1,33}... | collective-permute-start | bytes 786440 | tf_op jit(solution)/shard_map/ppermute | solution.py:616
  86.6 13.8 %collective-permute-start.23 = (bf16[128,1024]{1,0:T(8,128)(2,1)S(1)}, bf16[128,1024]{1,0:T(8,128)(2,1)S(1)}, u32[]{:S(2)}, u32[]{:S(2)}) collective-permute-start(bf16[128,1024]{1,0:T(8,128)(2,1)S(1)} %get-tuple-element.81), channel_id=1, source_target_pairs={{0,48},{8,56},{16,0},{24,8},{32,16},{40,24},{48,32},{56,40},{1,49}... | collective-permute-start | bytes 786440 | tf_op jit(solution)/shard_map/ppermute | solution.py:616
  87.8 22.1 %collective-permute-start.10 = (bf16[2,32,4096]{2,1,0:T(8,128)(2,1)S(1)}, bf16[2,32,4096]{2,1,0:T(8,128)(2,1)S(1)}, u32[]{:S(2)}, u32[]{:S(2)}) collective-permute-start(bf16[2,32,4096]{2,1,0:T(8,128)(2,1)S(1)} %get-tuple-element.47), channel_id=1, source_target_pairs={{0,3},{1,0},{2,1},{3,2},{4,7},{5,4},{6,5},{7,6},{8,11},{9,8},{10,9... | collective-permute-start | bytes 1572872 | tf_op jit(solution)/shard_map/ppermute | solution.py:653
  91.3 22.0 %collective-permute-start.11 = (bf16[2,32,4096]{2,1,0:T(8,128)(2,1)S(1)}, bf16[2,32,4096]{2,1,0:T(8,128)(2,1)S(1)}, u32[]{:S(2)}, u32[]{:S(2)}) collective-permute-start(bf16[2,32,4096]{2,1,0:T(8,128)(2,1)S(1)} %get-tuple-element.48), channel_id=1, source_target_pairs={{0,1},{1,2},{2,3},{3,0},{4,5},{5,6},{6,7},{7,4},{8,9},{9,10},{10,1... | collective-permute-start | bytes 1572872 | tf_op jit(solution)/shard_map/ppermute | solution.py:653
  92.3 21.3 %collective-permute-start.12 = (bf16[2,32,4096]{2,1,0:T(8,128)(2,1)S(1)}, bf16[2,32,4096]{2,1,0:T(8,128)(2,1)S(1)}, u32[]{:S(2)}, u32[]{:S(2)}) collective-permute-start(bf16[2,32,4096]{2,1,0:T(8,128)(2,1)S(1)} %get-tuple-element.49), channel_id=1, source_target_pairs={{0,2},{1,3},{2,0},{3,1},{4,6},{5,7},{6,4},{7,5},{8,10},{9,11},{10,... | collective-permute-start | bytes 1572872 | tf_op jit(solution)/shard_map/ppermute | solution.py:653
  92.8 10.8 %collective-permute-start.22 = (bf16[128,1024]{1,0:T(8,128)(2,1)S(1)}, bf16[128,1024]{1,0:T(8,128)(2,1)S(1)}, u32[]{:S(2)}, u32[]{:S(2)}) collective-permute-start(bf16[128,1024]{1,0:T(8,128)(2,1)S(1)} %get-tuple-element.79), channel_id=1, source_target_pairs={{0,16},{8,24},{16,32},{24,40},{32,48},{40,56},{48,0},{56,8},{1,17}... | collective-permute-start | bytes 786440 | tf_op jit(solution)/shard_map/ppermute | solution.py:616
  100.5 15.0 %collective-permute-start.21 = (bf16[2,256,512]{2,1,0:T(8,128)(2,1)S(1)}, bf16[2,256,512]{2,1,0:T(8,128)(2,1)S(1)}, u32[]{:S(2)}, u32[]{:S(2)}) collective-permute-start(bf16[2,256,512]{2,1,0:T(8,128)(2,1)S(1)} %get-tuple-element.57), channel_id=1, source_target_pairs={{0,64},{64,0},{1,65},{65,1},{2,66},{66,2},{3,67},{67,3},{4,68},{68... | collective-permute-start | bytes 1572872 | tf_op jit(solution)/shard_map/ppermute | solution.py:651
  103.7 26.7 %collective-permute-start.28 = (bf16[2,256,512]{2,1,0:T(8,128)(2,1)S(1)}, bf16[2,256,512]{2,1,0:T(8,128)(2,1)S(1)}, u32[]{:S(2)}, u32[]{:S(2)}) collective-permute-start(bf16[2,256,512]{2,1,0:T(8,128)(2,1)S(1)} %get-tuple-element.55.refs_7_), channel_id=1, source_target_pairs={{0,32},{8,40},{16,48},{24,56},{32,0},{40,8},{48,16},{56,24},{1,33}... | collective-permute-start | bytes 1572872 | tf_op jit(solution)/shard_map/ppermute | solution.py:654
  109.9 22.3 %collective-permute-start.31 = (bf16[2,256,512]{2,1,0:T(8,128)(2,1)S(1)}, bf16[2,256,512]{2,1,0:T(8,128)(2,1)S(1)}, u32[]{:S(2)}, u32[]{:S(2)}) collective-permute-start(bf16[2,256,512]{2,1,0:T(8,128)(2,1)S(1)} %get-tuple-element.55.refs_7_), channel_id=1, source_target_pairs={{0,16},{8,24},{16,32},{24,40},{32,48},{40,56},{48,0},{56,8},{1,17}... | collective-permute-start | bytes 1572872 | tf_op jit(solution)/shard_map/ppermute | solution.py:654
  113.3 33.0 %collective-permute-start.32 = (bf16[2,256,512]{2,1,0:T(8,128)(2,1)S(1)}, bf16[2,256,512]{2,1,0:T(8,128)(2,1)S(1)}, u32[]{:S(2)}, u32[]{:S(2)}) collective-permute-start(bf16[2,256,512]{2,1,0:T(8,128)(2,1)S(1)} %get-tuple-element.55.refs_7_), channel_id=1, source_target_pairs={{0,48},{8,56},{16,0},{24,8},{32,16},{40,24},{48,32},{56,40},{1,49}... | collective-permute-start | bytes 1572872 | tf_op jit(solution)/shard_map/ppermute | solution.py:654
  113.9 16.5 %collective-permute-start.13 = (bf16[32,4096]{1,0:T(8,128)(2,1)S(1)}, bf16[32,4096]{1,0:T(8,128)(2,1)S(1)}, u32[]{:S(2)}, u32[]{:S(2)}) collective-permute-start(bf16[32,4096]{1,0:T(8,128)(2,1)S(1)} %get-tuple-element.51.refs_0_), channel_id=1, source_target_pairs={{0,4},{1,5},{2,6},{3,7},{4,0},{5,1},{6,2},{7,3},{8,12},{9,13},{10,... | collective-permute-start | bytes 786440 | tf_op jit(solution)/shard_map/ppermute | solution.py:664
  127.1 34.1 %copy-start.36 = (bf16[1,4096]{1,0:T(2,128)(2,1)S(1)}, bf16[1,4096]{1,0:T(2,128)(2,1)}, u32[]{:S(2)}) copy-start(bf16[1,4096]{1,0:T(2,128)(2,1)} %gain.5) | copy-start | bytes 24580
  127.1 7.9 %collective-permute-start.25 = (bf16[5,16,2048]{2,1,0:T(8,128)(2,1)S(1)}, bf16[5,16,2048]{2,1,0:T(8,128)(2,1)S(1)}, u32[]{:S(2)}, u32[]{:S(2)}) collective-permute-start(bf16[5,16,2048]{2,1,0:T(8,128)(2,1)S(1)} %get-tuple-element.61), channel_id=1, source_target_pairs={{0,3},{1,0},{2,1},{3,2},{4,7},{5,4},{6,5},{7,6},{8,11},{9,8},{10,9... | collective-permute-start | bytes 983048 | tf_op jit(solution)/shard_map/ppermute | solution.py:663
  130.4 11.8 %collective-permute-start.26 = (bf16[5,16,2048]{2,1,0:T(8,128)(2,1)S(1)}, bf16[5,16,2048]{2,1,0:T(8,128)(2,1)S(1)}, u32[]{:S(2)}, u32[]{:S(2)}) collective-permute-start(bf16[5,16,2048]{2,1,0:T(8,128)(2,1)S(1)} %get-tuple-element.62), channel_id=1, source_target_pairs={{0,1},{1,2},{2,3},{3,0},{4,5},{5,6},{6,7},{7,4},{8,9},{9,10},{10,1... | collective-permute-start | bytes 983048 | tf_op jit(solution)/shard_map/ppermute | solution.py:663
  130.4 28.1 %copy-start.15 = (bf16[2,256,512]{2,1,0:T(8,128)(2,1)}, bf16[2,256,512]{2,1,0:T(8,128)(2,1)S(1)}, u32[]{:S(2)}) copy-start(bf16[2,256,512]{2,1,0:T(8,128)(2,1)S(1)} %collective-permute-done.28.refs_0_.refs_10_) | copy-start | bytes 1572868
  130.4 11.8 %collective-permute-start.27 = (bf16[5,16,2048]{2,1,0:T(8,128)(2,1)S(1)}, bf16[5,16,2048]{2,1,0:T(8,128)(2,1)S(1)}, u32[]{:S(2)}, u32[]{:S(2)}) collective-permute-start(bf16[5,16,2048]{2,1,0:T(8,128)(2,1)S(1)} %get-tuple-element.63), channel_id=1, source_target_pairs={{0,2},{1,3},{2,0},{3,1},{4,6},{5,7},{6,4},{7,5},{8,10},{9,11},{10,... | collective-permute-start | bytes 983048 | tf_op jit(solution)/shard_map/ppermute | solution.py:663
  132.2 36.8 %collective-permute-start.40 = (bf16[3,128,1024]{2,1,0:T(8,128)(2,1)S(1)}, bf16[3,128,1024]{2,1,0:T(8,128)(2,1)}, u32[]{:S(2)}, u32[]{:S(2)}) collective-permute-start(bf16[3,128,1024]{2,1,0:T(8,128)(2,1)S(1)} %pad_maximum_fusion.1.refs_0_.refs_2_), channel_id=1, source_target_pairs={{0,4},{1,5},{2,6},{3,7},{4,0},{5,1},{6,2},{7,3},{8,12},{9,13},{10,... | collective-permute-start | bytes 2359304 | tf_op jit(solution)/shard_map/ppermute | solution.py:617
  135.0 27.2 %collective-permute-start.30 = (bf16[4,32,2048]{2,1,0:T(8,128)(2,1)}, bf16[4,32,2048]{2,1,0:T(8,128)(2,1)}, u32[]{:S(2)}, u32[]{:S(2)}) collective-permute-start(bf16[4,32,2048]{2,1,0:T(8,128)(2,1)} %get-tuple-element.67), channel_id=1, source_target_pairs={{0,4},{1,5},{2,6},{3,7},{4,0},{5,1},{6,2},{7,3},{8,12},{9,13},{10,... | collective-permute-start | bytes 1572872 | tf_op jit(solution)/shard_map/ppermute | solution.py:661
  142.2 28.1 %collective-permute-start.41 = (bf16[2,256,512]{2,1,0:T(8,128)(2,1)S(1)}, bf16[2,256,512]{2,1,0:T(8,128)(2,1)}, u32[]{:S(2)}, u32[]{:S(2)}) collective-permute-start(bf16[2,256,512]{2,1,0:T(8,128)(2,1)S(1)} %sum_keys.1.refs_4_), channel_id=1, source_target_pairs={{0,16},{8,24},{16,32},{24,40},{32,48},{40,56},{48,0},{56,8},{1,17}... | collective-permute-start | bytes 1572872 | tf_op jit(solution)/shard_map/ppermute | solution.py:656
  142.2 30.6 %collective-permute-start.42 = (bf16[2,256,512]{2,1,0:T(8,128)(2,1)S(1)}, bf16[2,256,512]{2,1,0:T(8,128)(2,1)}, u32[]{:S(2)}, u32[]{:S(2)}) collective-permute-start(bf16[2,256,512]{2,1,0:T(8,128)(2,1)S(1)} %sum_keys.1.refs_4_), channel_id=1, source_target_pairs={{0,48},{8,56},{16,0},{24,8},{32,16},{40,24},{48,32},{56,40},{1,49}... | collective-permute-start | bytes 1572872 | tf_op jit(solution)/shard_map/ppermute | solution.py:656
  147.2 11.4 %collective-permute-start.29 = (bf16[3,16,2048]{2,1,0:T(8,128)(2,1)S(1)}, bf16[3,16,2048]{2,1,0:T(8,128)(2,1)S(1)}, u32[]{:S(2)}, u32[]{:S(2)}) collective-permute-start(bf16[3,16,2048]{2,1,0:T(8,128)(2,1)S(1)} %get-tuple-element.65), channel_id=1, source_target_pairs={{0,4},{1,5},{2,6},{3,7},{4,0},{5,1},{6,2},{7,3},{8,12},{9,13},{10,... | collective-permute-start | bytes 589832 | tf_op jit(solution)/shard_map/ppermute | solution.py:670
  159.2 21.8 %collective-permute-start.36 = (bf16[2,256,512]{2,1,0:T(8,128)(2,1)S(1)}, bf16[2,256,512]{2,1,0:T(8,128)(2,1)}, u32[]{:S(2)}, u32[]{:S(2)}) collective-permute-start(bf16[2,256,512]{2,1,0:T(8,128)(2,1)S(1)} %sum_keys.1.refs_4_), channel_id=1, source_target_pairs={{0,32},{8,40},{16,48},{24,56},{32,0},{40,8},{48,16},{56,24},{1,33}... | collective-permute-start | bytes 1572872 | tf_op jit(solution)/shard_map/ppermute | solution.py:656
  162.2 5.9 %collective-permute-start.37 = (f32[1,4096]{1,0:T(1,128)S(1)}, f32[1,4096]{1,0:T(1,128)S(1)}, u32[]{:S(2)}, u32[]{:S(2)}) collective-permute-start(f32[1,4096]{1,0:T(1,128)S(1)} %sum_gain.1), channel_id=1, source_target_pairs={{0,16},{8,24},{16,0},{24,8},{32,48},{40,56},{48,32},{56,40},{1,17}... | collective-permute-start | bytes 49160 | tf_op jit(solution)/shard_map/ppermute | solution.py:683
  168.1 21.5 %collective-permute-start.33 = (bf16[32,2048]{1,0:T(8,128)(2,1)S(1)}, bf16[32,2048]{1,0:T(8,128)(2,1)S(1)}, u32[]{:S(2)}, u32[]{:S(2)}) collective-permute-start(bf16[32,2048]{1,0:T(8,128)(2,1)S(1)} %get-tuple-element.69), channel_id=1, source_target_pairs={{0,3},{1,0},{2,1},{3,2},{4,7},{5,4},{6,5},{7,6},{8,11},{9,8},{10,9... | collective-permute-start | bytes 393224 | tf_op jit(solution)/shard_map/ppermute | solution.py:667
  169.0 20.6 %collective-permute-start.34 = (bf16[32,2048]{1,0:T(8,128)(2,1)S(1)}, bf16[32,2048]{1,0:T(8,128)(2,1)S(1)}, u32[]{:S(2)}, u32[]{:S(2)}) collective-permute-start(bf16[32,2048]{1,0:T(8,128)(2,1)S(1)} %get-tuple-element.70), channel_id=1, source_target_pairs={{0,1},{1,2},{2,3},{3,0},{4,5},{5,6},{6,7},{7,4},{8,9},{9,10},{10,1... | collective-permute-start | bytes 393224 | tf_op jit(solution)/shard_map/ppermute | solution.py:667
  170.3 19.4 %collective-permute-start.35 = (bf16[32,2048]{1,0:T(8,128)(2,1)S(1)}, bf16[32,2048]{1,0:T(8,128)(2,1)S(1)}, u32[]{:S(2)}, u32[]{:S(2)}) collective-permute-start(bf16[32,2048]{1,0:T(8,128)(2,1)S(1)} %get-tuple-element.71), channel_id=1, source_target_pairs={{0,2},{1,3},{2,0},{3,1},{4,6},{5,7},{6,4},{7,5},{8,10},{9,11},{10,... | collective-permute-start | bytes 393224 | tf_op jit(solution)/shard_map/ppermute | solution.py:667
  172.8 8.1 %collective-permute-start.38 = (f32[1,4096]{1,0:T(1,128)S(1)}, f32[1,4096]{1,0:T(1,128)S(1)}, u32[]{:S(2)}, u32[]{:S(2)}) collective-permute-start(f32[1,4096]{1,0:T(1,128)S(1)} %add.82), channel_id=1, source_target_pairs={{0,32},{8,40},{16,48},{24,56},{32,0},{40,8},{48,16},{56,24},{1,33}... | collective-permute-start | bytes 49160 | tf_op jit(solution)/shard_map/ppermute | solution.py:683
  180.8 9.9 %collective-permute-start.43 = (bf16[2,512,512]{2,1,0:T(8,128)(2,1)S(1)}, bf16[2,512,512]{2,1,0:T(8,128)(2,1)S(1)}, u32[]{:S(2)}, u32[]{:S(2)}) collective-permute-start(bf16[2,512,512]{2,1,0:T(8,128)(2,1)S(1)} %get-tuple-element.74), channel_id=1, source_target_pairs={{0,8},{8,0},{16,24},{24,16},{32,40},{40,32},{48,56},{56,48},{1,9},... | collective-permute-start | bytes 3145736 | tf_op jit(solution)/shard_map/ppermute | solution.py:684
  181.0 6.9 %collective-permute-start.39 = (f32[1,4096]{1,0:T(1,128)S(1)}, f32[1,4096]{1,0:T(1,128)S(1)}, u32[]{:S(2)}, u32[]{:S(2)}) collective-permute-start(f32[1,4096]{1,0:T(1,128)S(1)} %add.83), channel_id=1, source_target_pairs={{0,8},{8,0},{16,24},{24,16},{32,40},{40,32},{48,56},{56,48},{1,9},... | collective-permute-start | bytes 49160 | tf_op jit(solution)/shard_map/ppermute | solution.py:683
  187.9 4.3 %collective-permute-start.44 = (bf16[2,512,512]{2,1,0:T(8,128)(2,1)S(1)}, bf16[2,512,512]{2,1,0:T(8,128)(2,1)S(1)}, u32[]{:S(2)}, u32[]{:S(2)}) collective-permute-start(bf16[2,512,512]{2,1,0:T(8,128)(2,1)S(1)} %get-tuple-element.76), channel_id=1, source_target_pairs={{0,8},{8,0},{16,24},{24,16},{32,40},{40,32},{48,56},{56,48},{1,9},... | collective-permute-start | bytes 3145736 | tf_op jit(solution)/shard_map/ppermute | solution.py:685
  (41 other events, 258.5 us)

commit v4 on v3

--- a/solution.py
+++ b/solution.py
@@ -18,7 +18,7 @@
 FAR = 1073741824
 f32 = jnp.float32
 bf16 = jnp.bfloat16
-VMEM_LIMIT = 40 * 1024 * 1024
+MIB = 1024 * 1024
 
 STEPS = (0, 1, 3, 2)
 
@@ -42,11 +42,11 @@
     return jax.ShapeDtypeStruct(shape, dtype)
 
 
-def call(kernel, out_shape, flops=0, nbytes=0, **kwargs):
+def call(kernel, out_shape, vmem, flops=0, nbytes=0, **kwargs):
     return pl.pallas_call(
         kernel,
         out_shape=out_shape,
-        compiler_params=pltpu.CompilerParams(vmem_limit_bytes=VMEM_LIMIT),
+        compiler_params=pltpu.CompilerParams(vmem_limit_bytes=vmem * MIB),
         cost_estimate=pl.CostEstimate(flops=flops, bytes_accessed=nbytes, transcendentals=0),
         **kwargs,
     )
@@ -88,6 +88,7 @@
     return call(
         norm_kernel,
         [part, part, sds((ROWS, WIDTH), bf16), sds((ROWS, 128), f32)],
+        vmem=4,
         nbytes=4 * ROWS * WIDTH * 2,
         in_specs=[SMEM] + [VMEM] * 3,
         name="norm_rows",
@@ -115,27 +116,6 @@
 
 
 PIECE_SHAPES = [(4, ROWS, HALF)] * 2 + [(2, ROWS, HALF)] * 4
-
-
-def sum_z_kernel(own, c1, c2, c3, *refs):
-    kept, sent = refs[-2:]
-    total = own[...].astype(f32)
-    for came in (c1, c2, c3):
-        total = total + came[...].astype(f32)
-    kept[...] = total[0]
-    sent[...] = total[1].astype(bf16)
-
-
-def sum_z(own, came, after=()):
-    shape = own.shape[1:]
-    return call(
-        sum_z_kernel,
-        [sds(shape, f32), sds(shape, bf16)],
-        nbytes=11 * shape[0] * shape[1] * 2,
-        in_specs=[VMEM] * 4 + [ANY] * len(after),
-        out_specs=[VMEM] * 2,
-        name="sum_z",
-    )(own, *came, *after)
 
 
 def sum_left_kernel(own, c1, c2, c3, *refs):
@@ -162,6 +142,7 @@
     return call(
         sum_left_kernel,
         [sds((ROWS, HALF), f32), sds((3, 16, HALF), bf16), sds((2, HALF), f32)],
+        vmem=4,
         nbytes=11 * ROWS * HALF * 2,
         in_specs=[VMEM] * 4 + [ANY] * len(after),
         out_specs=[VMEM] * 3,
@@ -179,6 +160,7 @@
     return call(
         sum_gain_kernel,
         sds((1, WIDTH), f32),
+        vmem=2,
         nbytes=10 * WIDTH * 2,
         in_specs=[VMEM] * 3,
         out_specs=VMEM,
@@ -198,6 +180,7 @@
     return call(
         sum_x_kernel,
         [sds(shape, f32)] + [sds(shape, bf16)] * 3,
+        vmem=4,
         nbytes=13 * shape[0] * shape[1] * 2,
         in_specs=[VMEM] * 2 + [ANY] * len(after),
         out_specs=[VMEM] * 4,
@@ -213,6 +196,7 @@
     return call(
         sum_keys_kernel,
         sds(came.shape, bf16),
+        vmem=6,
         nbytes=8 * came.size,
         in_specs=[VMEM] * 2 + [ANY] * len(after),
         out_specs=VMEM,
@@ -244,6 +228,7 @@
     return call(
         rows_kernel,
         sds((ROWS, WIDTH), bf16),
+        vmem=4,
         nbytes=6 * ROWS * WIDTH * 2,
         in_specs=[VMEM] * 10 + [ANY] * len(after),
         out_specs=VMEM,
@@ -256,68 +241,61 @@
 
 
 def key_value_kernel(*refs):
-    pieces, weight, grad, grad_other = refs[:6], refs[6], refs[7], refs[8]
-    full, out, pair = refs[9:]
+    pieces, weight, full, out = refs[:6], refs[6], refs[7], refs[8]
 
     @pl.when(first_step())
     def _():
         place_pieces(pieces, full)
-        pair[0] = grad[...]
-        pair[1] = grad_other[...]
 
     out[0] = dot(full[...], weight[0]).astype(bf16)
 
 
-def key_value(pieces, weights, grad, grad_other):
+def key_value(pieces, weights):
     block = 256
     return call(
         key_value_kernel,
-        [
-            sds((SLOTS, WIDTH), bf16),
-            sds((2, SLOTS, COLS), bf16),
-            sds((2, ROWS, WIDTH), bf16),
-        ],
+        [sds((SLOTS, WIDTH), bf16), sds((2, SLOTS, COLS), bf16)],
+        vmem=18,
         flops=4 * SLOTS * WIDTH * COLS,
         nbytes=2 * WIDTH * COLS * 2 + 2 * SLOTS * WIDTH * 2,
         grid=(2, COLS // block),
         in_specs=[whole(s) for s in PIECE_SHAPES]
-        + [pl.BlockSpec((1, WIDTH, block), lambda p, j: (p + 1, 0, j))]
-        + [whole((ROWS, WIDTH))] * 2,
+        + [pl.BlockSpec((1, WIDTH, block), lambda p, j: (p + 1, 0, j))],
         out_specs=[
             whole((SLOTS, WIDTH)),
             pl.BlockSpec((1, SLOTS, block), lambda p, j: (p, 0, j)),
-            whole((2, ROWS, WIDTH)),
         ],
         name="key_value",
-    )(*pieces, weights, grad, grad_other)
-
-
-def grad_mixed_kernel(p0, p1, p2, p3, weight, *refs):
-    full, out = refs[-2:]
-
+    )(*pieces, weights)
+
+
+def grad_mixed_kernel(order, came, weight, full, out):
     @pl.when(pl.program_id(0) == 0)
     def _():
-        for slot, pair in enumerate((p0, p1, p2, p3)):
-            full[pl.ds(slot * ROWS, ROWS)] = pair[0]
-            full[pl.ds((4 + slot) * ROWS, ROWS)] = pair[1]
+        for block in range(8):
+            start = pl.multiple_of(order[block] * ROWS, ROWS)
+            full[pl.ds(block * ROWS, ROWS)] = came[pl.ds(start, ROWS)]
 
     out[...] = dot(full[...], weight[0]).astype(bf16)
 
 
-def grad_mixed_of(pairs, weights, after):
+def grad_mixed_of(order, came, weights):
     block = 256
     return call(
         grad_mixed_kernel,
         [sds((SLOTS, WIDTH), bf16), sds((SLOTS, COLS), bf16)],
+        vmem=16,
         flops=2 * SLOTS * WIDTH * COLS,
         nbytes=WIDTH * COLS * 2 + 2 * SLOTS * WIDTH * 2,
         grid=(COLS // block,),
-        in_specs=[whole((2, ROWS, WIDTH))] * 4
-        + [pl.BlockSpec((1, WIDTH, block), lambda j: (0, 0, j))]
-        + [ANY] * len(after),
+        in_specs=[
+            SMEM,
+            whole((SLOTS, WIDTH)),
+            pl.BlockSpec((1, WIDTH, block), lambda j: (0, 0, j)),
+        ],
         out_specs=[whole((SLOTS, WIDTH)), pl.BlockSpec((SLOTS, block), lambda j: (0, j))],
         name="grad_mixed",
-    )(*pairs, weights, *after)
+    )(order, came, weights)
 
 
 def one_dot_kernel(full, weight, out):
@@ -329,6 +307,7 @@
     return call(
         one_dot_kernel,
         sds((SLOTS, COLS), bf16),
+        vmem=12,
         flops=2 * SLOTS * WIDTH * COLS,
         nbytes=WIDTH * COLS * 2 + SLOTS * WIDTH * 2,
         grid=(COLS // block,),
@@ -356,26 +335,26 @@
     return rows[0:1] + rows[1:2], rows[2:3] + rows[3:4]
 
 
-def back_total(lefts, weight, normed):
-    total = dot_rows(lefts[0][...], weight[0])
-    for part in range(1, 3):
-        total = total + dot_rows(lefts[part][...], weight[part])
+def back_total(pair, kv_grad, weight, normed):
+    total = dot_rows(pair[1], weight[0])
+    for part in range(2):
+        total = total + dot_rows(kv_grad[part], weight[1 + part])
     rounded = total.astype(bf16)
     gain = jnp.sum(rounded.astype(f32) * normed[...].astype(f32), axis=0, keepdims=True)
     return rounded, gain
 
 
-def back_right_kernel(l0, l1, l2, weight, normed, *refs):
+def back_right_kernel(pair, kv_grad, weight, normed, *refs):
     own, sent, gain = refs[-3:]
-    rounded, gain[...] = back_total((l0, l1, l2), weight, normed)
+    rounded, gain[...] = back_total(pair, kv_grad, weight, normed)
     for xbit, out in enumerate((own, sent)):
         for slot in range(4):
             start = (xbit * 4 + slot) * ROWS
             out[slot] = rounded[start:start + ROWS]
 
 
-def back_left_kernel(l0, l1, l2, weight, normed, gain_right, *refs):
-    rounded, gain = back_total((l0, l1, l2), weight, normed)
+def back_left_kernel(pair, kv_grad, weight, normed, gain_right, *refs):
+    rounded, gain = back_total(pair, kv_grad, weight, normed)
     gains = gain_rows_of(gain, gain_right[...])
     for slot, out in enumerate(refs[-4:]):
         for xbit in range(2):
@@ -390,10 +369,11 @@
     return call(
         kernel,
         out_shape,
+        vmem=12,
         flops=2 * 3 * SLOTS * HALF * COLS,
         nbytes=3 * HALF * COLS * 2 + 2 * SLOTS * HALF * 2,
         grid=(HALF // block,),
-        in_specs=[whole((SLOTS, COLS))] * 3
+        in_specs=[whole((2, SLOTS, COLS))] * 2
         + [
             pl.BlockSpec((3, block, COLS), lambda j: (0, j + first, 0)),
             pl.BlockSpec((SLOTS, block), lambda j: (0, j + first)),
@@ -422,26 +402,30 @@
     )
 
 
-def proj_kernel(left, weight, *refs):
+def proj_kernel(order, left, weight, out):
     rounded = dot_rows(left[...], weight[0]).astype(bf16)
-    for slot in range(4):
-        for xbit in range(2):
-            start = (xbit * 4 + slot) * ROWS
-            refs[slot][xbit] = rounded[start:start + ROWS]
-
-
-def proj_parts(mixed, weights):
+    for block in range(8):
+        start = pl.multiple_of(order[block] * ROWS, ROWS)
+        out[pl.ds(start, ROWS)] = rounded[block * ROWS:(block + 1) * ROWS]
+
+
+def proj_parts(order, mixed, weights):
     block = 512
     return call(
         proj_kernel,
-        [sds((2, ROWS, WIDTH), bf16)] * 4,
+        sds((SLOTS, WIDTH), bf16),
+        vmem=6,
         flops=2 * SLOTS * WIDTH * COLS,
         nbytes=WIDTH * COLS * 2 + SLOTS * WIDTH * 2,
         grid=(WIDTH // block,),
-        in_specs=[whole((SLOTS, COLS)), pl.BlockSpec((1, block, COLS), lambda j: (0, j, 0))],
-        out_specs=[pl.BlockSpec((2, ROWS, block), lambda j: (0, 0, j))] * 4,
+        in_specs=[
+            SMEM,
+            whole((SLOTS, COLS)),
+            pl.BlockSpec((1, block, COLS), lambda j: (0, j, 0)),
+        ],
+        out_specs=pl.BlockSpec((SLOTS, block), lambda j: (0, j)),
         name="proj_parts",
-    )(mixed, weights)
+    )(order, mixed, weights)
 
 
 def slot_of(row, x_index, z_index):
@@ -536,6 +520,7 @@
     return call(
         forward_kernel,
         sds((SLOTS, COLS), bf16),
+        vmem=10,
         flops=4 * ATTN_FLOPS,
         nbytes=6 * SLOTS * COLS * 2,
         in_specs=[SMEM] + [VMEM] * 3,
@@ -549,6 +534,7 @@
     return call(
         backward_kernel,
         [sds(kv, bf16), sds(kv, f32), sds(kv, bf16)],
+        vmem=14,
         flops=8 * ATTN_FLOPS,
         nbytes=12 * SLOTS * COLS * 2,
         in_specs=[SMEM] + [VMEM] * 5 + [ANY] * len(after),
@@ -557,16 +543,25 @@
     )(meta, query, own_kv, other_kv, mixed, grad, *after)
 
 
-def share_kernel(count, *refs):
-    refs = refs[1:]
-    grads = refs[3 * count:3 * count + 4]
-    sent, mine = refs[-2:]
-
-    def share(part, own, came, other):
-        total = dot_tokens(own[...], grads[0][part])
+def share_kernel(arrays, column, *refs):
+    count = len(arrays)
+    chunks, grads = refs[:3 * count], refs[3 * count:3 * count + 4]
+    sent, mine, lefts, rights = refs[-4:]
+
+    @pl.when(pl.program_id(0) == 0)
+    def _():
+        for k, grad in enumerate(grads):
+            rights[:, pl.ds(k * SLOTS, SLOTS)] = grad[...]
+
+    for i in range(count):
+        own, came, other = chunks[3 * i:3 * i + 3]
+        lefts[i, :SLOTS] = own[...]
         for k in range(3):
-            total = total + dot_tokens(came[k], grads[k + 1][part, :SLOTS // 2])
-            total = total + dot_tokens(other[k], grads[k + 1][part, SLOTS // 2:])
+            start = (k + 1) * SLOTS
+            lefts[i, start:start + SLOTS // 2] = came[k, 0]
+            lefts[i, start + SLOTS // 2:start + SLOTS] = other[k, 0]
+    for part in range(2):
+        total = dot_tokens(lefts[part % count], rights[part])
 
         @pl.when(pl.program_id(0) == 0)
         def _():
@@ -576,47 +571,46 @@
         def _():
             mine[part] = total
 
-    for part in range(2):
-        first = 3 * (part if count == 2 else 0)
-        share(part, *refs[first:first + 3])
-
-
-def weight_shares(core, chunks, grads, after=()):
-    count = len(chunks)
-    flat = [ref for triple in chunks for ref in triple]
-
-    def column(i, core):
-        return jnp.abs(core[0] - 1 + i)
-
-    triple = [
-        pl.BlockSpec((SLOTS, COLS), lambda i, core: (0, column(i, core))),
-        pl.BlockSpec((3, SLOTS // 2, COLS), lambda i, core: (0, 0, column(i, core))),
-        pl.BlockSpec((3, SLOTS // 2, COLS), lambda i, core: (0, 0, column(i, core))),
-    ]
-    return call(
-        functools.partial(share_kernel, count),
+
+def weight_shares(column, fulls, came, other, grads, arrays, after=()):
+    half = SLOTS // 2
+    chunks, specs = [], []
+    for array in arrays:
+        chunks += [fulls[array], came, other]
+        specs += [pl.BlockSpec((SLOTS, COLS), lambda i, column: (0, column[i]))]
+        specs += [
+            pl.BlockSpec(
+                (3, 1, half, COLS), lambda i, column, array=array: (0, array, 0, column[2 + i])
+            )
+        ] * 2
+    return call(
+        functools.partial(share_kernel, arrays),
         [sds((2, COLS, COLS), bf16), sds((2, COLS, COLS), f32)],
+        vmem=24,
         flops=4 * 4 * SLOTS * 2 * COLS * COLS,
-        nbytes=8 * SLOTS * COLS * 2 * (count + 2) + 2 * COLS * COLS * 6,
+        nbytes=8 * SLOTS * COLS * 2 * 4 + 2 * COLS * COLS * 6,
         grid_spec=pltpu.PrefetchScalarGridSpec(
             num_scalar_prefetch=1,
             grid=(2,),
-            in_specs=triple * count + [whole((2, SLOTS, COLS))] * 4 + [ANY] * len(after),
+            in_specs=specs + [whole((2, SLOTS, COLS))] * 4 + [ANY] * len(after),
             out_specs=[whole((2, COLS, COLS))] * 2,
+            scratch_shapes=[
+                pltpu.VMEM((len(arrays), 4 * SLOTS, COLS), bf16),
+                pltpu.VMEM((2, 4 * SLOTS, COLS), bf16),
+            ],
         ),
         name="weight_shares",
-    )(core, *flat, *grads, *after)
-
-
-def chunks_over_y(full, y_index):
-    sent = [
-        lax.dynamic_slice(full, (0, (y_index + k) % 4 * 1024), (SLOTS // 2, 1024))
-        for k in STEPS[1:]
-    ]
-    came = jnp.stack([lax.ppermute(v, "seq", y_shift(k)) for v, k in zip(sent, STEPS[1:])])
-    other = lax.ppermute(came, "tp", X_SWAP)
-    own = lax.dynamic_slice_in_dim(full, y_index * 1024, 1024, 1)
-    return own, came, other
+    )(column, *chunks, *grads, *after)
+
+
+def chunks_over_y(fulls, y_index):
+    came = []
+    for k in STEPS[1:]:
+        start = (y_index + k) % 4 * 1024
+        sent = jnp.stack([lax.dynamic_slice(v, (0, start), (SLOTS // 2, 1024)) for v in fulls])
+        came.append(lax.ppermute(sent, "seq", y_shift(k)))
+    came = jnp.stack(came)
+    return came, lax.ppermute(came, "tp", X_SWAP)
 
 
 def per_device(tokens, text_gaps, image_runs, gains, w_qkv, w_out, cotangent):
@@ -632,52 +626,59 @@
         [text_gaps[0], image_runs[0], jnp.stack([group, x_index, z_index]).astype(jnp.int32)]
     )
 
+    order = jnp.stack(
+        [
+            jnp.where(xbit == 0, x_index, 1 - x_index) * 4 + (z_index + 4 - k) % 4
+            for xbit in range(2)
+            for k in STEPS
+        ]
+    ).astype(jnp.int32)
+
     n_left, n_right, grad_rows, inv = norm_rows(valid.reshape(1), x_rows, gains, cotangent[0, 0])
+    grad_came = lax.all_gather(grad_rows, "tp", axis=0, tiled=True)
     pieces = gather_blocks(n_left, n_right)
-    grad_other = lax.ppermute(grad_rows, "tp", X_SWAP)
-    normed_full, own_kv, grad_pair = key_value(pieces, w_parts, grad_rows, grad_other)
+    normed_full, own_kv = key_value(pieces, w_parts)
     other_kv = lax.ppermute(own_kv, "grp", GRP_SWAP)
-    grad_pairs = [grad_pair] + [lax.ppermute(grad_pair, "tp", z_shift(k)) for k in STEPS[1:]]
     query = one_dot(normed_full, w_parts, 0)
-    normed_chunks = chunks_over_y(normed_full, y_index)
+    grad_full, grad_mixed = grad_mixed_of(order, grad_came, w_out)
+    fulls = (normed_full, grad_full)
+    chunk_came, chunk_other = chunks_over_y(fulls, y_index)
 
     mixed = attend_forward(meta, query, own_kv, other_kv)
-    proj = proj_parts(mixed, w_out)
-    grad_full, grad_mixed = grad_mixed_of(grad_pairs, w_out, [proj[0]])
-    grad_chunks = chunks_over_y(grad_full, y_index)
     pair, own_part, other_part = attend_backward(
-        meta, query, own_kv, other_kv, mixed, grad_mixed, [normed_chunks[2]]
+        meta, query, own_kv, other_kv, mixed, grad_mixed, []
+    )
+    proj_rows = lax.psum_scatter(
+        proj_parts(order, mixed, w_out), "tp", scatter_dimension=0, tiled=True
     )
     back = lax.ppermute(other_part, "grp", GRP_SWAP)
 
-    proj_came = [lax.ppermute(proj[i], "tp", z_shift(-STEPS[i])) for i in range(1, 4)]
     pairs = [pair] + [lax.ppermute(pair, "seq", y_shift(k)) for k in STEPS[1:]]
-    kv_grad = sum_keys(own_part, back, [grad_chunks[1]])
+    kv_grad = sum_keys(own_part, back, [chunk_came])
     kv_grads = [kv_grad] + [lax.ppermute(kv_grad, "seq", y_shift(k)) for k in STEPS[1:]]
 
-    lefts = [pair[1], kv_grad[0], kv_grad[1]]
+    lefts = [pair, kv_grad]
     right = back_right(lefts, w_parts, normed_full)
-    proj_kept, proj_sent = sum_z(proj[0], proj_came)
     right_x = lax.ppermute(right[1], "tp", X_SWAP)
-    left = back_left(lefts, w_parts, normed_full, right[2], [proj_sent])
+    left = back_left(lefts, w_parts, normed_full, right[2])
     left_came = [lax.ppermute(left[i], "tp", z_shift(-STEPS[i])) for i in range(1, 4)]
-    proj_x = lax.ppermute(proj_sent, "tp", X_SWAP)
-    right_kept, *right_sends = sum_x(right[0], right_x, pairs[1:3] + [proj_x])
+    right_kept, *right_sends = sum_x(right[0], right_x, pairs[1:3])
     right_came = [
         lax.ppermute(sent, "tp", z_shift(-k)) for sent, k in zip(right_sends, STEPS[1:])
     ]
     left_kept, left_sent, gain_kept = sum_left(left[0], left_came, pairs[3:])
     left_x = lax.ppermute(left_sent, "tp", X_SWAP)
-    layer_out = ((x_rows.astype(f32) + proj_kept + proj_x.astype(f32)) * valid).astype(bf16)
-
-    core_ref = core.reshape(1).astype(jnp.int32)
-    pair_sent, pair_mine = weight_shares(
-        core_ref, [grad_chunks, normed_chunks], pairs, kv_grads[1:3]
-    )
+    layer_out = ((x_rows.astype(f32) + proj_rows.astype(f32)) * valid).astype(bf16)
+
+    columns = jnp.stack(
+        [y_index * 2 + 1 - core, y_index * 2 + core, 1 - core, core]
+    ).astype(jnp.int32)
+    chunks = (columns, fulls, chunk_came, chunk_other)
+    pair_sent, pair_mine = weight_shares(*chunks, pairs, (1, 0), kv_grads[1:3])
     tokens_grad = token_rows(
         x_rows, grad_rows, gains, inv, (left_kept, left_x), (right_kept, *right_came), kv_grads[3:]
     )
-    kv_sent, kv_mine = weight_shares(core_ref, [normed_chunks], kv_grads)
+    kv_sent, kv_mine = weight_shares(*chunks, kv_grads, (0,))
     gain_grad = sum_gain(gain_kept, left_x, gains)
     for flip in (2, 4, 1):
         gain_grad = gain_grad + lax.ppermute(gain_grad, "seq", [(i, i ^ flip) for i in range(8)])

time: 197 us -> 252 us (1.28)
  waiting for transfers between devices: 49.2 us -> 103 us
  starting transfers between devices: 70.2 us -> 42.2 us
  local copies, waits for them, and re-layouts: 18.9 us -> 37.2 us
  between operations: 1.22 us -> 14.5 us
  Pallas kernels: 49.5 us -> 43.2 us
  other arithmetic: 5.55 us -> 10 us
    ppermute x3, waiting for transfers between devices: 0.01 us -> 22.9 us  [gather_blocks(): lax.ppermute(right_pair, 'tp', z_shift(k))]
    ppermute x16 -> x4, starting transfers between devices: 28.1 us -> 6.29 us  [the longest x3 6.29 us: chunks_over_y(): came.append(lax.ppermute(sent, 'seq', y_shift(k)))]
    unnamed x88 -> x76, local copies, waits for them, and re-layouts: 16.3 us -> 35.1 us
    ppermute x3, waiting for transfers between devices: 1.3 us -> 19.9 us  [per_device(): lax.ppermute(gain_grad, 'seq', [(i, i ^ flip) for i in range(8)])]
    ppermute x1, waiting for transfers between devices: 0.01 us -> 6.8 us  [per_device(): other_kv = lax.ppermute(own_kv, 'grp', GRP_SWAP)]
    ppermute x3, waiting for transfers between devices: 0.01 us -> 6.3 us  [per_device(): lax.ppermute(sent, 'tp', z_shift(-k))]
    ppermute x3, starting transfers between devices: 5.1 us -> 0.01 us  [per_device(): lax.ppermute(kv_grad, 'seq', y_shift(k))]
    pallas_call x13 -> x12, Pallas kernels: 39.7 us -> 35.5 us  [the longest x2 12.9 us: weight_shares(): call(functools.partial(share_kernel, arrays), [sds((2, COLS, COLS), bf16)...]
  transfers between devices with their start and end apart: 45 -> 35, of which waited for: 13 -> 15; matrix products, arithmetic and copies ran while one was open for 3% -> 4% of each run, Pallas kernels for 22% -> 17%
where the time goes in v4:
time: 252 us; the launch traced here: 250 us
  waiting for transfers between devices  103 us (41%)
  Pallas kernels  43.2 us (17%)
  starting transfers between devices  42.2 us (17%)
  local copies, waits for them, and re-layouts  37.2 us (15%)
  between operations  14.5 us (6%)
  other arithmetic  10 us (4%)
    unnamed x76, local copies, waits for them, and re-layouts  35.1 us
    ppermute x3, waiting for transfers between devices, gather_blocks(): lax.ppermute(right_pair, 'tp', z_shift(k))  22.9 us
    ppermute x3, waiting for transfers between devices, chunks_over_y(): came.append(lax.ppermute(sent, 'seq', y_shift(k)))  22.9 us
    ppermute x3, waiting for transfers between devices, per_device(): lax.ppermute(gain_grad, 'seq', [(i, i ^ flip) for i in range(8)])  19.9 us
    pallas_call x2, Pallas kernels, weight_shares(): call(functools.partial(share_kernel, arrays), [sds((2, COLS, COLS), bf16)...  12.9 us
    ppermute x1, waiting for transfers between devices, per_device(): left_x = lax.ppermute(left_sent, 'tp', X_SWAP)  11.6 us
    ppermute x3, waiting for transfers between devices, per_device(): lax.ppermute(left[i], 'tp', z_shift(-STEPS[i]))  8.68 us
    ppermute x3, starting transfers between devices, per_device(): pairs = [pair] + [lax.ppermute(pair, 'seq', y_shift(k)) for k in STEPS[1:]]  7.2 us
  transfers between devices with their start and end apart: 35, of which 15 were waited for; matrix products, arithmetic and copies ran while one was open for 4% of the time, Pallas kernels for 17%

profile of v4, /device:TPU:0, one launch (start us, length us, event | category | flops | bytes accessed | tf_op | source)
XLA Modules:
  0.0 249.7 jit_solution(15757191687218995542)
XLA Ops:
  10.8 4.0 %collective-permute-start.2 = (bf16[32,2048]{1,0:T(8,128)(2,1)S(1)}, bf16[32,2048]{1,0:T(8,128)(2,1)S(1)}, u32[]{:S(2)}, u32[]{:S(2)}) collective-permute-start(bf16[32,2048]{1,0:T(8,128)(2,1)S(1)} %get-tuple-element.34), channel_id=1, source_target_pairs={{0,2},{1,3},{2,0},{3,1},{4,6},{5,7},{6,4},{7,5},{8,10},{9,11},{10,... | collective-permute-start | bytes 393224 | tf_op jit(solution)/shard_map/ppermute | solution.py:100
  16.9 1.5 collective-permute-start.4
  18.8 3.2 %collective-permute-done.1 = bf16[32,2048]{1,0:T(8,128)(2,1)S(1)} collective-permute-done((bf16[32,2048]{1,0:T(8,128)(2,1)S(1)}, bf16[32,2048]{1,0:T(8,128)(2,1)S(1)}, u32[]{:S(2)}, u32[]{:S(2)}) %collective-permute-start.1) | collective-permute-done | bytes 131104 | tf_op jit(solution)/shard_map/ppermute | solution.py:100
  22.0 1.6 collective-permute-start.3
  23.6 2.5 %collective-permute-start.7 = (bf16[2,32,2048]{2,1,0:T(8,128)(2,1)S(1)}, bf16[2,32,2048]{2,1,0:T(8,128)(2,1)S(1)}, u32[]{:S(2)}, u32[]{:S(2)}) collective-permute-start(bf16[2,32,2048]{2,1,0:T(8,128)(2,1)S(1)} %pad_maximum_fusion.5.refs_2_), channel_id=1, source_target_pairs={{0,2},{1,3},{2,0},{3,1},{4,6},{5,7},{6,4},{7,5},{8,10},{9,11},{10,... | collective-permute-start | bytes 786440 | tf_op jit(solution)/shard_map/ppermute | solution.py:101
  28.2 11.5 %collective-permute-done.7.refs_5_ = bf16[2,32,2048]{2,1,0:T(8,128)(2,1)S(1)} collective-permute-done((bf16[2,32,2048]{2,1,0:T(8,128)(2,1)S(1)}, bf16[2,32,2048]{2,1,0:T(8,128)(2,1)S(1)}, u32[]{:S(2)}, u32[]{:S(2)}) %collective-permute-start.7) | collective-permute-done | bytes 262176 | tf_op jit(solution)/shard_map/ppermute | solution.py:101
  39.7 8.5 %collective-permute-done.6.refs_4_ = bf16[2,32,2048]{2,1,0:T(8,128)(2,1)S(1)} collective-permute-done((bf16[2,32,2048]{2,1,0:T(8,128)(2,1)S(1)}, bf16[2,32,2048]{2,1,0:T(8,128)(2,1)S(1)}, u32[]{:S(2)}, u32[]{:S(2)}) %collective-permute-start.6) | collective-permute-done | bytes 262176 | tf_op jit(solution)/shard_map/ppermute | solution.py:101
  48.2 2.9 %collective-permute-done.5.refs_3_ = bf16[2,32,2048]{2,1,0:T(8,128)(2,1)S(1)} collective-permute-done((bf16[2,32,2048]{2,1,0:T(8,128)(2,1)S(1)}, bf16[2,32,2048]{2,1,0:T(8,128)(2,1)S(1)}, u32[]{:S(2)}, u32[]{:S(2)}) %collective-permute-start.5) | collective-permute-done | bytes 262176 | tf_op jit(solution)/shard_map/ppermute | solution.py:101
  51.1 4.7 %copy-done = bf16[1,4096,3,512]{3,1,2,0:T(8,128)(2,1)S(1)} copy-done((bf16[1,4096,3,512]{3,1,2,0:T(8,128)(2,1)S(1)}, bf16[1,4096,3,512]{3,1,2,0:T(8,128)(2,1)}, u32[]{:S(2)}) %copy-start) | copy-done | bytes 12582936
  55.8 4.3 %key_value.1 = (bf16[256,4096]{1,0:T(8,128)(2,1)S(1)}, bf16[2,256,512]{2,1,0:T(8,128)(2,1)}) custom-call(bf16[4,32,2048]{2,1,0:T(8,128)(2,1)S(1)} %pad_maximum_fusion.1.refs_0_, bf16[4,32,2048]{2,1,0:T(8,128)(2,1)S(1)} %collective-permute-done.3.refs_1_, bf16[2,32,2048]{2,1,0:T(8,128)(2,1)S(1)} %pad_maximum_fusion.5.refs_2_, ...), custom_call_target="tpu_custom_call" | custom-call | flops 2147483648 | bytes 12582912 | tf_op jit(solution)/shard_map/key_value/pallas_call | solution.py:255
  60.1 1.5 collective-permute-start.8
  61.8 4.6 %copy-done.1 = bf16[1,4096,3,512]{3,1,2,0:T(8,128)(2,1)S(1)} copy-done((bf16[1,4096,3,512]{3,1,2,0:T(8,128)(2,1)S(1)}, bf16[1,4096,3,512]{3,1,2,0:T(8,128)(2,1)}, u32[]{:S(2)}) %copy-start.1) | copy-done | bytes 12582936
  66.3 1.7 one_dot.1.query
  68.1 6.8 %collective-permute-done.8.other_kv = bf16[2,256,512]{2,1,0:T(8,128)(2,1)} collective-permute-done((bf16[2,256,512]{2,1,0:T(8,128)(2,1)}, bf16[2,256,512]{2,1,0:T(8,128)(2,1)}, u32[]{:S(2)}, u32[]{:S(2)}) %collective-permute-start.8) | collective-permute-done | bytes 524320 | tf_op jit(solution)/shard_map/ppermute | solution.py:641
  74.9 3.1 %attend_forward.1.left.mixed = bf16[256,512]{1,0:T(8,128)(2,1)S(1)} custom-call(s32[12]{0:T(128)S(1)} %concatenate.6.meta, bf16[256,512]{1,0:T(8,128)(2,1)S(1)} %one_dot.1.query, bf16[2,256,512]{2,1,0:T(8,128)(2,1)} %get-tuple-element.37.own_kv, bf16[2,256,512]{2,1,0:T(8,128)(2,1)} %collective-permute-done.8.other_kv), custom_call_target="tpu_custom_call" | custom-call | flops 536870912 | bytes 1572864 | tf_op jit(solution)/shard_map/attend_forward/pallas_call | solution.py:520
  78.0 3.5 %proj_parts.1 = bf16[256,4096]{1,0:T(8,128)(2,1)S(1)} custom-call(s32[8]{0:T(128)S(1)} %stack.122.order, bf16[256,512]{1,0:T(8,128)(2,1)S(1)} %attend_forward.1.left.mixed, bf16[1,4096,512]{2,1,0:T(8,128)(2,1)S(1)} %copy-done.3), custom_call_target="tpu_custom_call" | custom-call | flops 1073741824 | bytes 6291456 | tf_op jit(solution)/shard_map/proj_parts/pallas_call | solution.py:414
  83.7 2.2 copy-done.4
  85.9 1.6 copy-done.10
  87.5 2.3 grad_mixed.1
  89.9 4.3 %collective-permute-start.11 = (bf16[2,128,1024]{2,1,0:T(8,128)(2,1)S(1)}, bf16[2,128,1024]{2,1,0:T(8,128)(2,1)S(1)}, u32[]{:S(2)}, u32[]{:S(2)}) collective-permute-start(bf16[2,128,1024]{2,1,0:T(8,128)(2,1)S(1)} %pad_maximum_fusion.3), channel_id=1, source_target_pairs={{0,48},{8,56},{16,0},{24,8},{32,16},{40,24},{48,32},{56,40},{1,49}... | collective-permute-start | bytes 1572872 | tf_op jit(solution)/shard_map/ppermute | solution.py:611
  94.7 1.7 collective-permute-start.10
  96.4 5.0 %attend_backward.1 = (bf16[2,256,512]{2,1,0:T(8,128)(2,1)S(1)}, f32[2,256,512]{2,1,0:T(8,128)S(1)}, bf16[2,256,512]{2,1,0:T(8,128)(2,1)S(1)}) custom-call(s32[12]{0:T(128)S(1)} %concatenate.6.meta, bf16[256,512]{1,0:T(8,128)(2,1)S(1)} %one_dot.1.query, bf16[2,256,512]{2,1,0:T(8,128)(2,1)} %get-tuple-element.37.own_kv, ...), custom_call_target="tpu_custom_call" | custom-call | flops 1073741824 | bytes 3145728 | tf_op jit(solution)/shard_map/attend_backward/pallas_call | solution.py:534
  102.4 1.9 collective-permute-start.16
  104.3 22.9 %collective-permute-done.11 = bf16[2,128,1024]{2,1,0:T(8,128)(2,1)S(1)} collective-permute-done((bf16[2,128,1024]{2,1,0:T(8,128)(2,1)S(1)}, bf16[2,128,1024]{2,1,0:T(8,128)(2,1)S(1)}, u32[]{:S(2)}, u32[]{:S(2)}) %collective-permute-start.11) | collective-permute-done | bytes 524320 | tf_op jit(solution)/shard_map/ppermute | solution.py:611
  128.7 4.6 %copy-done.2 = bf16[1,4096,3,512]{3,1,2,0:T(8,128)(2,1)S(1)} copy-done((bf16[1,4096,3,512]{3,1,2,0:T(8,128)(2,1)S(1)}, bf16[1,4096,3,512]{3,1,2,0:T(8,128)(2,1)}, u32[]{:S(2)}) %copy-start.2) | copy-done | bytes 12582936
  133.3 3.2 %back_right.1 = (bf16[4,32,2048]{2,1,0:T(8,128)(2,1)S(1)}, bf16[4,32,2048]{2,1,0:T(8,128)(2,1)S(1)}, f32[1,2048]{1,0:T(1,128)S(1)}) custom-call(bf16[2,256,512]{2,1,0:T(8,128)(2,1)S(1)} %get-tuple-element.41.pair.refs_6_, bf16[2,256,512]{2,1,0:T(8,128)(2,1)S(1)} %sum_keys.1.kv_grad.refs_3_, bf16[3,4096,512]{2,1,0:T(8,128)(2,1)S(1)} %bitcast.54, ...), custom_call_target="tpu_custom_call" | custom-call | flops 1610612736 | bytes 8388608 | tf_op jit(solution)/shard_map/back_right/pallas_call | solution.py:369
  136.5 3.2 %back_left.1 = (bf16[5,16,2048]{2,1,0:T(8,128)(2,1)S(1)}, bf16[5,16,2048]{2,1,0:T(8,128)(2,1)S(1)}, bf16[5,16,2048]{2,1,0:T(8,128)(2,1)S(1)}, bf16[5,16,2048]{2,1,0:T(8,128)(2,1)S(1)}) custom-call(bf16[2,256,512]{2,1,0:T(8,128)(2,1)S(1)} %get-tuple-element.41.pair.refs_6_, bf16[2,256,512]{2,1,0:T(8,128)(2,1)S(1)} %sum_keys.1.kv_grad.refs_3_, ...), custom_call_target="tpu_custom_call" | custom-call | flops 1610612736 | bytes 8388608 | tf_op jit(solution)/shard_map/back_left/pallas_call | solution.py:369
  140.1 1.7 collective-permute-start.14
  141.8 3.7 %collective-permute-start.20 = (bf16[2,256,512]{2,1,0:T(8,128)(2,1)S(1)}, bf16[2,256,512]{2,1,0:T(8,128)(2,1)S(1)}, u32[]{:S(2)}, u32[]{:S(2)}) collective-permute-start(bf16[2,256,512]{2,1,0:T(8,128)(2,1)S(1)} %get-tuple-element.41.pair.refs_6_), channel_id=1, source_target_pairs={{0,48},{8,56},{16,0},{24,8},{32,16},{40,24},{48,32},{56,40},{1,49}... | collective-permute-start | bytes 1572872 | tf_op jit(solution)/shard_map/ppermute | solution.py:656
  145.5 4.9 %collective-permute-done.13.c1 = bf16[5,16,2048]{2,1,0:T(8,128)(2,1)S(1)} collective-permute-done((bf16[5,16,2048]{2,1,0:T(8,128)(2,1)S(1)}, bf16[5,16,2048]{2,1,0:T(8,128)(2,1)S(1)}, u32[]{:S(2)}, u32[]{:S(2)}) %collective-permute-start.13) | collective-permute-done | bytes 327712 | tf_op jit(solution)/shard_map/ppermute | solution.py:664
  150.4 1.6 collective-permute-start.19
  152.0 3.8 %collective-permute-done.14.c2 = bf16[5,16,2048]{2,1,0:T(8,128)(2,1)S(1)} collective-permute-done((bf16[5,16,2048]{2,1,0:T(8,128)(2,1)S(1)}, bf16[5,16,2048]{2,1,0:T(8,128)(2,1)S(1)}, u32[]{:S(2)}, u32[]{:S(2)}) %collective-permute-start.14) | collective-permute-done | bytes 327712 | tf_op jit(solution)/shard_map/ppermute | solution.py:664
  156.7 1.7 collective-permute-start.17
  158.7 11.6 %collective-permute-done.17.l_came.came = bf16[3,16,2048]{2,1,0:T(8,128)(2,1)S(1)} collective-permute-done((bf16[3,16,2048]{2,1,0:T(8,128)(2,1)S(1)}, bf16[3,16,2048]{2,1,0:T(8,128)(2,1)S(1)}, u32[]{:S(2)}, u32[]{:S(2)}) %collective-permute-start.17) | collective-permute-done | bytes 196640 | tf_op jit(solution)/shard_map/ppermute | solution.py:670
  170.4 4.6 %collective-permute-start.25 = (f32[1,4096]{1,0:T(1,128)S(1)}, f32[1,4096]{1,0:T(1,128)S(1)}, u32[]{:S(2)}, u32[]{:S(2)}) collective-permute-start(f32[1,4096]{1,0:T(1,128)S(1)} %sum_gain.1), channel_id=1, source_target_pairs={{0,16},{8,24},{16,0},{24,8},{32,48},{40,56},{48,32},{56,40},{1,17}... | collective-permute-start | bytes 49160 | tf_op jit(solution)/shard_map/ppermute | solution.py:684
  175.0 12.7 %collective-permute-done.25 = f32[1,4096]{1,0:T(1,128)S(1)} collective-permute-done((f32[1,4096]{1,0:T(1,128)S(1)}, f32[1,4096]{1,0:T(1,128)S(1)}, u32[]{:S(2)}, u32[]{:S(2)}) %collective-permute-start.25) | collective-permute-done | bytes 16416 | tf_op jit(solution)/shard_map/ppermute | solution.py:684
  190.2 5.8 %collective-permute-done.26 = f32[1,4096]{1,0:T(1,128)S(1)} collective-permute-done((f32[1,4096]{1,0:T(1,128)S(1)}, f32[1,4096]{1,0:T(1,128)S(1)}, u32[]{:S(2)}, u32[]{:S(2)}) %collective-permute-start.26) | collective-permute-done | bytes 16416 | tf_op jit(solution)/shard_map/ppermute | solution.py:684
  197.4 1.4 collective-permute-done.27
  198.8 2.0 collective-permute-start.22
  201.1 1.5 add.150
  202.6 6.2 %collective-permute-done.22.r2 = bf16[32,2048]{1,0:T(8,128)(2,1)} collective-permute-done((bf16[32,2048]{1,0:T(8,128)(2,1)}, bf16[32,2048]{1,0:T(8,128)(2,1)}, u32[]{:S(2)}, u32[]{:S(2)}) %collective-permute-start.22) | collective-permute-done | bytes 131104 | tf_op jit(solution)/shard_map/ppermute | solution.py:667
  213.3 2.1 token_rows.1
  218.6 6.4 %weight_shares.2 = (bf16[2,512,512]{2,1,0:T(8,128)(2,1)}, f32[2,512,512]{2,1,0:T(8,128)S(1)}) custom-call(s32[4]{0:T(128)S(1)} %pad_add_fusion.column, bf16[256,4096]{1,0:T(8,128)(2,1)S(1)} %copy-done.7, bf16[3,2,128,1024]{3,2,1,0:T(8,128)(2,1)} %pad_maximum_fusion.refs_0_.refs_1_.refs_4_, bf16[3,2,128,1024]{3,2,1,0:T(8,128)(2,1)} %collective-permute-done.28.refs_2_.refs_5_, ...), custom_call_target="tpu_custom_call" | custom-call | flops 2147483648 | bytes 11534336 | tf_op jit(solution)/shard_map/weight_shares/pallas_call | solution.py:586
  226.3 6.5 %weight_shares.3 = (bf16[2,512,512]{2,1,0:T(8,128)(2,1)}, f32[2,512,512]{2,1,0:T(8,128)S(1)}) custom-call(s32[4]{0:T(128)S(1)} %pad_add_fusion.column, bf16[256,4096]{1,0:T(8,128)(2,1)S(1)} %get-tuple-element.36.full.normed.refs_3_.refs_0_, bf16[3,2,128,1024]{3,2,1,0:T(8,128)(2,1)} %pad_maximum_fusion.refs_0_.refs_1_.refs_4_, ...), custom_call_target="tpu_custom_call" | custom-call | flops 2147483648 | bytes 11534336 | tf_op jit(solution)/shard_map/weight_shares/pallas_call | solution.py:586
  232.8 1.4 copy-done.12
  234.7 1.7 fusion
  236.4 2.2 convert_add_fusion.1
  240.9 2.0 maximum_bitcast_fusion
  (135 shorter events, 31.2 us)
Async XLA Ops:
  7.2 76.5 %all-gather.2.cloned.1.call-start = ((), (), s32[]{:S(2)}) async-start(), calls=%async_computation.2 | async-start | bytes 2359296 | tf_op jit(solution)/shard_map/all_gather | solution.py:638
  10.8 40.4 %copy-start.32 = (f32[32,128]{1,0:T(8,128)}, f32[32,128]{1,0:T(8,128)S(1)}, u32[]{:S(2)}) copy-start(f32[32,128]{1,0:T(8,128)S(1)} %get-tuple-element.39.inv) | copy-start | bytes 49156
  10.8 223.9 %reduce-scatter.2.cloned.1.call-start = ((), (), s32[]{:S(2)}) async-start(), calls=%async_computation.1 | async-start | bytes 2359296 | tf_op jit(solution)/shard_map/reduce_scatter | solution.py:651
  10.8 7.9 %collective-permute-start.2 = (bf16[32,2048]{1,0:T(8,128)(2,1)S(1)}, bf16[32,2048]{1,0:T(8,128)(2,1)S(1)}, u32[]{:S(2)}, u32[]{:S(2)}) collective-permute-start(bf16[32,2048]{1,0:T(8,128)(2,1)S(1)} %get-tuple-element.34), channel_id=1, source_target_pairs={{0,2},{1,3},{2,0},{3,1},{4,6},{5,7},{6,4},{7,5},{8,10},{9,11},{10,... | collective-permute-start | bytes 393224 | tf_op jit(solution)/shard_map/ppermute | solution.py:100
  14.9 7.1 %collective-permute-start.1 = (bf16[32,2048]{1,0:T(8,128)(2,1)S(1)}, bf16[32,2048]{1,0:T(8,128)(2,1)S(1)}, u32[]{:S(2)}, u32[]{:S(2)}) collective-permute-start(bf16[32,2048]{1,0:T(8,128)(2,1)S(1)} %get-tuple-element.34), channel_id=1, source_target_pairs={{0,3},{1,0},{2,1},{3,2},{4,7},{5,4},{6,5},{7,6},{8,11},{9,8},{10,9... | collective-permute-start | bytes 393224 | tf_op jit(solution)/shard_map/ppermute | solution.py:100
  15.6 6.4 %collective-permute-start = (bf16[32,2048]{1,0:T(8,128)(2,1)S(1)}, bf16[32,2048]{1,0:T(8,128)(2,1)S(1)}, u32[]{:S(2)}, u32[]{:S(2)}) collective-permute-start(bf16[32,2048]{1,0:T(8,128)(2,1)S(1)} %get-tuple-element.34), channel_id=1, source_target_pairs={{0,1},{1,2},{2,3},{3,0},{4,5},{5,6},{6,7},{7,4},{8,9},{9,10},{10,1... | collective-permute-start | bytes 393224 | tf_op jit(solution)/shard_map/ppermute | solution.py:100
  16.9 6.7 %collective-permute-start.4 = (bf16[32,2048]{1,0:T(8,128)(2,1)S(1)}, bf16[32,2048]{1,0:T(8,128)(2,1)S(1)}, u32[]{:S(2)}, u32[]{:S(2)}) collective-permute-start(bf16[32,2048]{1,0:T(8,128)(2,1)S(1)} %get-tuple-element.35), channel_id=1, source_target_pairs={{0,4},{1,5},{2,6},{3,7},{4,0},{5,1},{6,2},{7,3},{8,12},{9,13},{10,... | collective-permute-start | bytes 393224 | tf_op jit(solution)/shard_map/ppermute | solution.py:99
  22.0 29.1 %collective-permute-start.3 = (bf16[4,32,2048]{2,1,0:T(8,128)(2,1)S(1)}, bf16[4,32,2048]{2,1,0:T(8,128)(2,1)S(1)}, u32[]{:S(2)}, u32[]{:S(2)}) collective-permute-start(bf16[4,32,2048]{2,1,0:T(8,128)(2,1)S(1)} %pad_maximum_fusion.1.refs_0_), channel_id=1, source_target_pairs={{0,4},{1,5},{2,6},{3,7},{4,0},{5,1},{6,2},{7,3},{8,12},{9,13},{10,... | collective-permute-start | bytes 1572872 | tf_op jit(solution)/shard_map/ppermute | solution.py:103
  23.6 16.1 %collective-permute-start.7 = (bf16[2,32,2048]{2,1,0:T(8,128)(2,1)S(1)}, bf16[2,32,2048]{2,1,0:T(8,128)(2,1)S(1)}, u32[]{:S(2)}, u32[]{:S(2)}) collective-permute-start(bf16[2,32,2048]{2,1,0:T(8,128)(2,1)S(1)} %pad_maximum_fusion.5.refs_2_), channel_id=1, source_target_pairs={{0,2},{1,3},{2,0},{3,1},{4,6},{5,7},{6,4},{7,5},{8,10},{9,11},{10,... | collective-permute-start | bytes 786440 | tf_op jit(solution)/shard_map/ppermute | solution.py:101
  26.2 22.0 %collective-permute-start.6 = (bf16[2,32,2048]{2,1,0:T(8,128)(2,1)S(1)}, bf16[2,32,2048]{2,1,0:T(8,128)(2,1)S(1)}, u32[]{:S(2)}, u32[]{:S(2)}) collective-permute-start(bf16[2,32,2048]{2,1,0:T(8,128)(2,1)S(1)} %pad_maximum_fusion.5.refs_2_), channel_id=1, source_target_pairs={{0,3},{1,0},{2,1},{3,2},{4,7},{5,4},{6,5},{7,6},{8,11},{9,8},{10,9... | collective-permute-start | bytes 786440 | tf_op jit(solution)/shard_map/ppermute | solution.py:101
  27.4 23.8 %collective-permute-start.5 = (bf16[2,32,2048]{2,1,0:T(8,128)(2,1)S(1)}, bf16[2,32,2048]{2,1,0:T(8,128)(2,1)S(1)}, u32[]{:S(2)}, u32[]{:S(2)}) collective-permute-start(bf16[2,32,2048]{2,1,0:T(8,128)(2,1)S(1)} %pad_maximum_fusion.5.refs_2_), channel_id=1, source_target_pairs={{0,1},{1,2},{2,3},{3,0},{4,5},{5,6},{6,7},{7,4},{8,9},{9,10},{10,1... | collective-permute-start | bytes 786440 | tf_op jit(solution)/shard_map/ppermute | solution.py:101
  55.8 5.8 %copy-start.36 = (s32[1,5]{1,0:T(1,128)S(1)}, s32[1,5]{1,0:T(1,128)}, u32[]{:S(2)}) copy-start(s32[1,5]{1,0:T(1,128)} %param.8) | copy-start | bytes 64
  55.8 5.8 %copy-start.37 = (s32[1,4]{1,0:T(1,128)S(1)}, s32[1,4]{1,0:T(1,128)}, u32[]{:S(2)}) copy-start(s32[1,4]{1,0:T(1,128)} %param.9) | copy-start | bytes 52
  60.1 14.8 %collective-permute-start.8 = (bf16[2,256,512]{2,1,0:T(8,128)(2,1)}, bf16[2,256,512]{2,1,0:T(8,128)(2,1)}, u32[]{:S(2)}, u32[]{:S(2)}) collective-permute-start(bf16[2,256,512]{2,1,0:T(8,128)(2,1)} %get-tuple-element.37.own_kv), channel_id=1, source_target_pairs={{0,64},{64,0},{1,65},{65,1},{2,66},{66,2},{3,67},{67,3},{4,68},{68... | collective-permute-start | bytes 1572872 | tf_op jit(solution)/shard_map/ppermute | solution.py:641
  66.3 11.6 %copy-start.3 = (bf16[1,4096,512]{2,1,0:T(8,128)(2,1)S(1)}, bf16[1,4096,512]{2,1,0:T(8,128)(2,1)}, u32[]{:S(2)}) copy-start(bf16[1,4096,512]{2,1,0:T(8,128)(2,1)} %weight.3) | copy-start | bytes 12582916
  89.8 4.9 %copy-start.6 = (bf16[256,4096]{1,0:T(8,128)(2,1)}, bf16[256,4096]{1,0:T(8,128)(2,1)S(1)}, u32[]{:S(2)}) copy-start(bf16[256,4096]{1,0:T(8,128)(2,1)S(1)} %get-tuple-element.44.refs_0_) | copy-start | bytes 6291460
  89.9 37.3 %collective-permute-start.11 = (bf16[2,128,1024]{2,1,0:T(8,128)(2,1)S(1)}, bf16[2,128,1024]{2,1,0:T(8,128)(2,1)S(1)}, u32[]{:S(2)}, u32[]{:S(2)}) collective-permute-start(bf16[2,128,1024]{2,1,0:T(8,128)(2,1)S(1)} %pad_maximum_fusion.3), channel_id=1, source_target_pairs={{0,48},{8,56},{16,0},{24,8},{32,16},{40,24},{48,32},{56,40},{1,49}... | collective-permute-start | bytes 1572872 | tf_op jit(solution)/shard_map/ppermute | solution.py:611
  94.3 32.9 %collective-permute-start.12 = (bf16[2,128,1024]{2,1,0:T(8,128)(2,1)S(1)}, bf16[2,128,1024]{2,1,0:T(8,128)(2,1)S(1)}, u32[]{:S(2)}, u32[]{:S(2)}) collective-permute-start(bf16[2,128,1024]{2,1,0:T(8,128)(2,1)S(1)} %pad_maximum_fusion.4), channel_id=1, source_target_pairs={{0,32},{8,40},{16,48},{24,56},{32,0},{40,8},{48,16},{56,24},{1,33}... | collective-permute-start | bytes 1572872 | tf_op jit(solution)/shard_map/ppermute | solution.py:611
  94.7 32.5 %collective-permute-start.10 = (bf16[2,128,1024]{2,1,0:T(8,128)(2,1)S(1)}, bf16[2,128,1024]{2,1,0:T(8,128)(2,1)S(1)}, u32[]{:S(2)}, u32[]{:S(2)}) collective-permute-start(bf16[2,128,1024]{2,1,0:T(8,128)(2,1)S(1)} %pad_maximum_fusion.2), channel_id=1, source_target_pairs={{0,16},{8,24},{16,32},{24,40},{32,48},{40,56},{48,0},{56,8},{1,17}... | collective-permute-start | bytes 1572872 | tf_op jit(solution)/shard_map/ppermute | solution.py:611
  101.3 27.2 %collective-permute-start.9 = (bf16[2,256,512]{2,1,0:T(8,128)(2,1)S(1)}, bf16[2,256,512]{2,1,0:T(8,128)(2,1)S(1)}, u32[]{:S(2)}, u32[]{:S(2)}) collective-permute-start(bf16[2,256,512]{2,1,0:T(8,128)(2,1)S(1)} %get-tuple-element.43), channel_id=1, source_target_pairs={{0,64},{64,0},{1,65},{65,1},{2,66},{66,2},{3,67},{67,3},{4,68},{68... | collective-permute-start | bytes 1572872 | tf_op jit(solution)/shard_map/ppermute | solution.py:654
  102.4 39.4 %collective-permute-start.16 = (bf16[2,256,512]{2,1,0:T(8,128)(2,1)S(1)}, bf16[2,256,512]{2,1,0:T(8,128)(2,1)S(1)}, u32[]{:S(2)}, u32[]{:S(2)}) collective-permute-start(bf16[2,256,512]{2,1,0:T(8,128)(2,1)S(1)} %get-tuple-element.41.pair.refs_6_), channel_id=1, source_target_pairs={{0,32},{8,40},{16,48},{24,56},{32,0},{40,8},{48,16},{56,24},{1,33}... | collective-permute-start | bytes 1572872 | tf_op jit(solution)/shard_map/ppermute | solution.py:656
  128.6 86.9 %collective-permute-start.28 = (bf16[3,2,128,1024]{3,2,1,0:T(8,128)(2,1)}, bf16[3,2,128,1024]{3,2,1,0:T(8,128)(2,1)}, u32[]{:S(2)}, u32[]{:S(2)}) collective-permute-start(bf16[3,2,128,1024]{3,2,1,0:T(8,128)(2,1)} %pad_maximum_fusion.refs_0_.refs_1_.refs_4_), channel_id=1, source_target_pairs={{0,4},{1,5},{2,6},{3,7},{4,0},{5,1},{6,2},{7,3},{8,12},{9,13},{10,... | collective-permute-start | bytes 4718600 | tf_op jit(solution)/shard_map/ppermute | solution.py:613
  136.5 33.9 %copy-start.31 = (bf16[1,4096]{1,0:T(2,128)(2,1)S(1)}, bf16[1,4096]{1,0:T(2,128)(2,1)}, u32[]{:S(2)}) copy-start(bf16[1,4096]{1,0:T(2,128)(2,1)} %gain.5) | copy-start | bytes 24580
  139.7 10.7 %collective-permute-start.13 = (bf16[5,16,2048]{2,1,0:T(8,128)(2,1)S(1)}, bf16[5,16,2048]{2,1,0:T(8,128)(2,1)S(1)}, u32[]{:S(2)}, u32[]{:S(2)}) collective-permute-start(bf16[5,16,2048]{2,1,0:T(8,128)(2,1)S(1)} %get-tuple-element.47), channel_id=1, source_target_pairs={{0,3},{1,0},{2,1},{3,2},{4,7},{5,4},{6,5},{7,6},{8,11},{9,8},{10,9... | collective-permute-start | bytes 983048 | tf_op jit(solution)/shard_map/ppermute | solution.py:664
  140.1 15.7 %collective-permute-start.14 = (bf16[5,16,2048]{2,1,0:T(8,128)(2,1)S(1)}, bf16[5,16,2048]{2,1,0:T(8,128)(2,1)S(1)}, u32[]{:S(2)}, u32[]{:S(2)}) collective-permute-start(bf16[5,16,2048]{2,1,0:T(8,128)(2,1)S(1)} %get-tuple-element.48), channel_id=1, source_target_pairs={{0,1},{1,2},{2,3},{3,0},{4,5},{5,6},{6,7},{7,4},{8,9},{9,10},{10,1... | collective-permute-start | bytes 983048 | tf_op jit(solution)/shard_map/ppermute | solution.py:664
  141.8 14.0 %collective-permute-start.15 = (bf16[5,16,2048]{2,1,0:T(8,128)(2,1)S(1)}, bf16[5,16,2048]{2,1,0:T(8,128)(2,1)S(1)}, u32[]{:S(2)}, u32[]{:S(2)}) collective-permute-start(bf16[5,16,2048]{2,1,0:T(8,128)(2,1)S(1)} %get-tuple-element.49), channel_id=1, source_target_pairs={{0,2},{1,3},{2,0},{3,1},{4,6},{5,7},{6,4},{7,5},{8,10},{9,11},{10,... | collective-permute-start | bytes 983048 | tf_op jit(solution)/shard_map/ppermute | solution.py:664
  141.8 47.6 %copy-start.14 = (bf16[2,256,512]{2,1,0:T(8,128)(2,1)}, bf16[2,256,512]{2,1,0:T(8,128)(2,1)S(1)}, u32[]{:S(2)}) copy-start(bf16[2,256,512]{2,1,0:T(8,128)(2,1)S(1)} %collective-permute-done.16.refs_0_.refs_9_) | copy-start | bytes 1572868
  141.8 28.5 %collective-permute-start.20 = (bf16[2,256,512]{2,1,0:T(8,128)(2,1)S(1)}, bf16[2,256,512]{2,1,0:T(8,128)(2,1)S(1)}, u32[]{:S(2)}, u32[]{:S(2)}) collective-permute-start(bf16[2,256,512]{2,1,0:T(8,128)(2,1)S(1)} %get-tuple-element.41.pair.refs_6_), channel_id=1, source_target_pairs={{0,48},{8,56},{16,0},{24,8},{32,16},{40,24},{48,32},{56,40},{1,49}... | collective-permute-start | bytes 1572872 | tf_op jit(solution)/shard_map/ppermute | solution.py:656
  150.4 24.6 %collective-permute-start.19 = (bf16[2,256,512]{2,1,0:T(8,128)(2,1)S(1)}, bf16[2,256,512]{2,1,0:T(8,128)(2,1)S(1)}, u32[]{:S(2)}, u32[]{:S(2)}) collective-permute-start(bf16[2,256,512]{2,1,0:T(8,128)(2,1)S(1)} %get-tuple-element.41.pair.refs_6_), channel_id=1, source_target_pairs={{0,16},{8,24},{16,32},{24,40},{32,48},{40,56},{48,0},{56,8},{1,17}... | collective-permute-start | bytes 1572872 | tf_op jit(solution)/shard_map/ppermute | solution.py:656
  155.8 53.0 %copy-start.9 = (bf16[1,1,32,4096]{3,2,1,0:T(8,128)(2,1)S(1)}, bf16[1,1,32,4096]{3,2,1,0:T(8,128)(2,1)}, u32[]{:S(2)}) copy-start(bf16[1,1,32,4096]{3,2,1,0:T(8,128)(2,1)} %param.7) | copy-start | bytes 786436
  156.7 13.6 %collective-permute-start.17 = (bf16[3,16,2048]{2,1,0:T(8,128)(2,1)S(1)}, bf16[3,16,2048]{2,1,0:T(8,128)(2,1)S(1)}, u32[]{:S(2)}, u32[]{:S(2)}) collective-permute-start(bf16[3,16,2048]{2,1,0:T(8,128)(2,1)S(1)} %get-tuple-element.51), channel_id=1, source_target_pairs={{0,4},{1,5},{2,6},{3,7},{4,0},{5,1},{6,2},{7,3},{8,12},{9,13},{10,... | collective-permute-start | bytes 589832 | tf_op jit(solution)/shard_map/ppermute | solution.py:670
  158.4 29.3 %collective-permute-start.18 = (bf16[4,32,2048]{2,1,0:T(8,128)(2,1)S(1)}, bf16[4,32,2048]{2,1,0:T(8,128)(2,1)S(1)}, u32[]{:S(2)}, u32[]{:S(2)}) collective-permute-start(bf16[4,32,2048]{2,1,0:T(8,128)(2,1)S(1)} %get-tuple-element.53), channel_id=1, source_target_pairs={{0,4},{1,5},{2,6},{3,7},{4,0},{5,1},{6,2},{7,3},{8,12},{9,13},{10,... | collective-permute-start | bytes 1572872 | tf_op jit(solution)/shard_map/ppermute | solution.py:662
  170.3 4.7 %copy-start.20 = (bf16[3,16,2048]{2,1,0:T(8,128)(2,1)}, bf16[3,16,2048]{2,1,0:T(8,128)(2,1)S(1)}, u32[]{:S(2)}) copy-start(bf16[3,16,2048]{2,1,0:T(8,128)(2,1)S(1)} %collective-permute-done.17.l_came.came) | copy-start | bytes 589828
  170.3 26.3 %collective-permute-start.24 = (bf16[2,256,512]{2,1,0:T(8,128)(2,1)S(1)}, bf16[2,256,512]{2,1,0:T(8,128)(2,1)S(1)}, u32[]{:S(2)}, u32[]{:S(2)}) collective-permute-start(bf16[2,256,512]{2,1,0:T(8,128)(2,1)S(1)} %sum_keys.1.kv_grad.refs_3_), channel_id=1, source_target_pairs={{0,32},{8,40},{16,48},{24,56},{32,0},{40,8},{48,16},{56,24},{1,33}... | collective-permute-start | bytes 1572872 | tf_op jit(solution)/shard_map/ppermute | solution.py:658
  170.4 26.3 %copy-start.16 = (bf16[2,256,512]{2,1,0:T(8,128)(2,1)}, bf16[2,256,512]{2,1,0:T(8,128)(2,1)S(1)}, u32[]{:S(2)}) copy-start(bf16[2,256,512]{2,1,0:T(8,128)(2,1)S(1)} %collective-permute-done.20.refs_1_.refs_8_) | copy-start | bytes 1572868
  170.4 17.3 %collective-permute-start.25 = (f32[1,4096]{1,0:T(1,128)S(1)}, f32[1,4096]{1,0:T(1,128)S(1)}, u32[]{:S(2)}, u32[]{:S(2)}) collective-permute-start(f32[1,4096]{1,0:T(1,128)S(1)} %sum_gain.1), channel_id=1, source_target_pairs={{0,16},{8,24},{16,0},{24,8},{32,48},{40,56},{48,32},{56,40},{1,17}... | collective-permute-start | bytes 49160 | tf_op jit(solution)/shard_map/ppermute | solution.py:684
  175.0 22.5 %copy-start.18 = (bf16[2,256,512]{2,1,0:T(8,128)(2,1)}, bf16[2,256,512]{2,1,0:T(8,128)(2,1)S(1)}, u32[]{:S(2)}) copy-start(bf16[2,256,512]{2,1,0:T(8,128)(2,1)S(1)} %collective-permute-done.19.refs_0_.refs_7_) | copy-start | bytes 1572868
  175.0 40.5 %collective-permute-start.30 = (bf16[2,256,512]{2,1,0:T(8,128)(2,1)S(1)}, bf16[2,256,512]{2,1,0:T(8,128)(2,1)}, u32[]{:S(2)}, u32[]{:S(2)}) collective-permute-start(bf16[2,256,512]{2,1,0:T(8,128)(2,1)S(1)} %sum_keys.1.kv_grad.refs_3_), channel_id=1, source_target_pairs={{0,48},{8,56},{16,0},{24,8},{32,16},{40,24},{48,32},{56,40},{1,49}... | collective-permute-start | bytes 1572872 | tf_op jit(solution)/shard_map/ppermute | solution.py:658
  187.7 27.8 %collective-permute-start.29 = (bf16[2,256,512]{2,1,0:T(8,128)(2,1)S(1)}, bf16[2,256,512]{2,1,0:T(8,128)(2,1)}, u32[]{:S(2)}, u32[]{:S(2)}) collective-permute-start(bf16[2,256,512]{2,1,0:T(8,128)(2,1)S(1)} %sum_keys.1.kv_grad.refs_3_), channel_id=1, source_target_pairs={{0,16},{8,24},{16,32},{24,40},{32,48},{40,56},{48,0},{56,8},{1,17}... | collective-permute-start | bytes 1572872 | tf_op jit(solution)/shard_map/ppermute | solution.py:658
  187.7 8.3 %collective-permute-start.26 = (f32[1,4096]{1,0:T(1,128)S(1)}, f32[1,4096]{1,0:T(1,128)S(1)}, u32[]{:S(2)}, u32[]{:S(2)}) collective-permute-start(f32[1,4096]{1,0:T(1,128)S(1)} %add.148), channel_id=1, source_target_pairs={{0,32},{8,40},{16,48},{24,56},{32,0},{40,8},{48,16},{56,24},{1,33}... | collective-permute-start | bytes 49160 | tf_op jit(solution)/shard_map/ppermute | solution.py:684
  196.0 5.0 %collective-permute-start.21 = (bf16[32,2048]{1,0:T(8,128)(2,1)S(1)}, bf16[32,2048]{1,0:T(8,128)(2,1)S(1)}, u32[]{:S(2)}, u32[]{:S(2)}) collective-permute-start(bf16[32,2048]{1,0:T(8,128)(2,1)S(1)} %get-tuple-element.55), channel_id=1, source_target_pairs={{0,3},{1,0},{2,1},{3,2},{4,7},{5,4},{6,5},{7,6},{8,11},{9,8},{10,9... | collective-permute-start | bytes 393224 | tf_op jit(solution)/shard_map/ppermute | solution.py:667
  197.4 1.4 collective-permute-start.27
  198.8 9.9 %collective-permute-start.22 = (bf16[32,2048]{1,0:T(8,128)(2,1)}, bf16[32,2048]{1,0:T(8,128)(2,1)}, u32[]{:S(2)}, u32[]{:S(2)}) collective-permute-start(bf16[32,2048]{1,0:T(8,128)(2,1)} %get-tuple-element.56), channel_id=1, source_target_pairs={{0,1},{1,2},{2,3},{3,0},{4,5},{5,6},{6,7},{7,4},{8,9},{9,10},{10,1... | collective-permute-start | bytes 393224 | tf_op jit(solution)/shard_map/ppermute | solution.py:667
  201.0 7.8 %collective-permute-start.23 = (bf16[32,2048]{1,0:T(8,128)(2,1)}, bf16[32,2048]{1,0:T(8,128)(2,1)}, u32[]{:S(2)}, u32[]{:S(2)}) collective-permute-start(bf16[32,2048]{1,0:T(8,128)(2,1)} %get-tuple-element.57), channel_id=1, source_target_pairs={{0,2},{1,3},{2,0},{3,1},{4,6},{5,7},{6,4},{7,5},{8,10},{9,11},{10,... | collective-permute-start | bytes 393224 | tf_op jit(solution)/shard_map/ppermute | solution.py:667
  201.0 14.5 %copy-start.7 = (bf16[256,4096]{1,0:T(8,128)(2,1)S(1)}, bf16[256,4096]{1,0:T(8,128)(2,1)}, u32[]{:S(2)}) copy-start(bf16[256,4096]{1,0:T(8,128)(2,1)} %copy-done.6) | copy-start | bytes 6291460
  218.6 7.7 %copy-start.24 = (bf16[2,256,512]{2,1,0:T(8,128)(2,1)S(1)}, bf16[2,256,512]{2,1,0:T(8,128)(2,1)}, u32[]{:S(2)}) copy-start(bf16[2,256,512]{2,1,0:T(8,128)(2,1)} %copy-done.22) | copy-start | bytes 1572868
  226.3 10.1 %collective-permute-start.31 = (bf16[2,512,512]{2,1,0:T(8,128)(2,1)}, bf16[2,512,512]{2,1,0:T(8,128)(2,1)}, u32[]{:S(2)}, u32[]{:S(2)}) collective-permute-start(bf16[2,512,512]{2,1,0:T(8,128)(2,1)} %get-tuple-element.60), channel_id=1, source_target_pairs={{0,8},{8,0},{16,24},{24,16},{32,40},{40,32},{48,56},{56,48},{1,9},... | collective-permute-start | bytes 3145736 | tf_op jit(solution)/shard_map/ppermute | solution.py:685
  234.2 5.6 %collective-permute-start.32 = (bf16[2,512,512]{2,1,0:T(8,128)(2,1)}, bf16[2,512,512]{2,1,0:T(8,128)(2,1)S(1)}, u32[]{:S(2)}, u32[]{:S(2)}) collective-permute-start(bf16[2,512,512]{2,1,0:T(8,128)(2,1)} %get-tuple-element.62), channel_id=1, source_target_pairs={{0,8},{8,0},{16,24},{24,16},{32,40},{40,32},{48,56},{56,48},{1,9},... | collective-permute-start | bytes 3145736 | tf_op jit(solution)/shard_map/ppermute | solution.py:686
  (25 other events, 40.7 us)
Sparse Core Ops, SparseCore 0:
  10.9 50.3 all-gather.1
  83.0 47.6 reduce-scatter.1

commit v5 on v4

--- a/solution.py
+++ b/solution.py
@@ -71,6 +71,32 @@
 
 def dot_tokens(left, right):
     return lax.dot_general(left, right, (((0,), (0,)), ((), ())), preferred_element_type=f32)
+
+
+def hold_kernel(*refs):
+    count = (len(refs) - 1) // 2
+    sems = refs[-1]
+    copies = [
+        pltpu.make_async_copy(refs[i], refs[count + i], sems.at[i]) for i in range(count)
+    ]
+    for copy in copies:
+        copy.start()
+    for copy in copies:
+        copy.wait()
+
+
+def hold(*arrays):
+    count = len(arrays)
+    return call(
+        hold_kernel,
+        [sds(v.shape, v.dtype) for v in arrays],
+        vmem=1,
+        nbytes=2 * sum(v.size * 2 for v in arrays),
+        in_specs=[ANY] * count,
+        out_specs=[ANY] * count,
+        scratch_shapes=[pltpu.SemaphoreType.DMA((count,))],
+        name="hold",
+    )(*arrays)
 
 
 def norm_kernel(valid, x, gain, cot, n_left, n_right, grad, inv):
@@ -180,7 +206,7 @@
     return call(
         sum_x_kernel,
         [sds(shape, f32)] + [sds(shape, bf16)] * 3,
-        vmem=4,
+        vmem=12,
         nbytes=13 * shape[0] * shape[1] * 2,
         in_specs=[VMEM] * 2 + [ANY] * len(after),
         out_specs=[VMEM] * 4,
@@ -269,33 +295,30 @@
     )(*pieces, weights)
 
 
-def grad_mixed_kernel(order, came, weight, full, out):
+def grad_mixed_kernel(p0, p1, p2, p3, weight, full, out):
     @pl.when(pl.program_id(0) == 0)
     def _():
-        for block in range(8):
-            start = pl.multiple_of(order[block] * ROWS, ROWS)
-            full[pl.ds(block * ROWS, ROWS)] = came[pl.ds(start, ROWS)]
+        for slot, pair in enumerate((p0, p1, p2, p3)):
+            full[pl.ds(slot * ROWS, ROWS)] = pair[0]
+            full[pl.ds((4 + slot) * ROWS, ROWS)] = pair[1]
 
     out[...] = dot(full[...], weight[0]).astype(bf16)
 
 
-def grad_mixed_of(order, came, weights):
-    block = 256
+def grad_mixed_of(pairs, weights):
+    block = 512
     return call(
         grad_mixed_kernel,
         [sds((SLOTS, WIDTH), bf16), sds((SLOTS, COLS), bf16)],
-        vmem=16,
+        vmem=18,
         flops=2 * SLOTS * WIDTH * COLS,
         nbytes=WIDTH * COLS * 2 + 2 * SLOTS * WIDTH * 2,
         grid=(COLS // block,),
-        in_specs=[
-            SMEM,
-            whole((SLOTS, WIDTH)),
-            pl.BlockSpec((1, WIDTH, block), lambda j: (0, 0, j)),
-        ],
+        in_specs=[whole((2, ROWS, WIDTH))] * 4
+        + [pl.BlockSpec((1, WIDTH, block), lambda j: (0, 0, j))],
         out_specs=[whole((SLOTS, WIDTH)), pl.BlockSpec((SLOTS, block), lambda j: (0, j))],
         name="grad_mixed",
-    )(order, came, weights)
+    )(*pairs, weights)
 
 
 def one_dot_kernel(full, weight, out):
@@ -303,11 +326,11 @@
 
 
 def one_dot(full, weights, part):
-    block = 256
+    block = 512
     return call(
         one_dot_kernel,
         sds((SLOTS, COLS), bf16),
-        vmem=12,
+        vmem=18,
         flops=2 * SLOTS * WIDTH * COLS,
         nbytes=WIDTH * COLS * 2 + SLOTS * WIDTH * 2,
         grid=(COLS // block,),
@@ -336,25 +359,25 @@
 
 
 def back_total(pair, kv_grad, weight, normed):
-    total = dot_rows(pair[1], weight[0])
+    total = dot_rows(pair[...], weight[0][0])
     for part in range(2):
-        total = total + dot_rows(kv_grad[part], weight[1 + part])
+        total = total + dot_rows(kv_grad[part], weight[1 + part][0])
     rounded = total.astype(bf16)
     gain = jnp.sum(rounded.astype(f32) * normed[...].astype(f32), axis=0, keepdims=True)
     return rounded, gain
 
 
-def back_right_kernel(pair, kv_grad, weight, normed, *refs):
+def back_right_kernel(pair, kv_grad, w0, w1, w2, normed, *refs):
     own, sent, gain = refs[-3:]
-    rounded, gain[...] = back_total(pair, kv_grad, weight, normed)
+    rounded, gain[...] = back_total(pair, kv_grad, (w0, w1, w2), normed)
     for xbit, out in enumerate((own, sent)):
         for slot in range(4):
             start = (xbit * 4 + slot) * ROWS
             out[slot] = rounded[start:start + ROWS]
 
 
-def back_left_kernel(pair, kv_grad, weight, normed, gain_right, *refs):
-    rounded, gain = back_total(pair, kv_grad, weight, normed)
+def back_left_kernel(pair, kv_grad, w0, w1, w2, normed, gain_right, *refs):
+    rounded, gain = back_total(pair, kv_grad, (w0, w1, w2), normed)
     gains = gain_rows_of(gain, gain_right[...])
     for slot, out in enumerate(refs[-4:]):
         for xbit in range(2):
@@ -373,11 +396,12 @@
         flops=2 * 3 * SLOTS * HALF * COLS,
         nbytes=3 * HALF * COLS * 2 + 2 * SLOTS * HALF * 2,
         grid=(HALF // block,),
-        in_specs=[whole((2, SLOTS, COLS))] * 2
+        in_specs=[whole((SLOTS, COLS)), whole((2, SLOTS, COLS))]
         + [
-            pl.BlockSpec((3, block, COLS), lambda j: (0, j + first, 0)),
-            pl.BlockSpec((SLOTS, block), lambda j: (0, j + first)),
+            pl.BlockSpec((1, block, COLS), lambda j, part=part: (part, j + first, 0))
+            for part in range(3)
         ]
+        + [pl.BlockSpec((SLOTS, block), lambda j: (0, j + first))]
         + [pl.BlockSpec((1, block), lambda j: (0, j))] * len(extra)
         + [ANY] * len(after),
         out_specs=[
@@ -385,7 +409,7 @@
             for v in out_shape
         ],
         name=name,
-    )(*lefts, weights, normed, *extra, *after)
+    )(*lefts, weights, weights, weights, normed, *extra, *after)
 
 
 def back_right(lefts, weights, normed, after=()):
@@ -402,30 +426,27 @@
     )
 
 
-def proj_kernel(order, left, weight, out):
+def proj_kernel(left, weight, own, sent):
     rounded = dot_rows(left[...], weight[0]).astype(bf16)
-    for block in range(8):
-        start = pl.multiple_of(order[block] * ROWS, ROWS)
-        out[pl.ds(start, ROWS)] = rounded[block * ROWS:(block + 1) * ROWS]
-
-
-def proj_parts(order, mixed, weights):
+    for xbit, out in enumerate((own, sent)):
+        for slot in range(4):
+            start = (xbit * 4 + slot) * ROWS
+            out[slot] = rounded[start:start + ROWS]
+
+
+def proj_parts(mixed, weights):
     block = 512
     return call(
         proj_kernel,
-        sds((SLOTS, WIDTH), bf16),
+        [sds((4, ROWS, WIDTH), bf16)] * 2,
         vmem=6,
         flops=2 * SLOTS * WIDTH * COLS,
         nbytes=WIDTH * COLS * 2 + SLOTS * WIDTH * 2,
         grid=(WIDTH // block,),
-        in_specs=[
-            SMEM,
-            whole((SLOTS, COLS)),
-            pl.BlockSpec((1, block, COLS), lambda j: (0, j, 0)),
-        ],
-        out_specs=pl.BlockSpec((SLOTS, block), lambda j: (0, j)),
+        in_specs=[whole((SLOTS, COLS)), pl.BlockSpec((1, block, COLS), lambda j: (0, j, 0))],
+        out_specs=[pl.BlockSpec((4, ROWS, block), lambda j: (0, 0, j))] * 2,
         name="proj_parts",
-    )(order, mixed, weights)
+    )(mixed, weights)
 
 
 def slot_of(row, x_index, z_index):
@@ -478,7 +499,8 @@
     return own * share, other * share
 
 
-def forward_kernel(meta, query, own_kv, other_kv, mixed):
+def forward_kernel(meta, query, own_kv, other_kv, *refs):
+    mixed = refs[-1]
     own_ok, other_ok = admitted(meta)
     for head in range(HEADS):
         cols = slice(head * HS, (head + 1) * HS)
@@ -491,8 +513,7 @@
 
 
 def backward_kernel(meta, query, own_kv, other_kv, mixed, grad, *refs):
-    pair, own_grad, other_grad = refs[-3:]
-    pair[0] = mixed[...]
+    q_grad, own_grad, other_grad = refs[-3:]
     scale = HS ** (-0.5)
     own_ok, other_ok = admitted(meta)
     for head in range(HEADS):
@@ -510,30 +531,30 @@
             key_grad = dot_tokens(score_grad, q) * scale
             kv_grad[0, :, cols] = key_grad.astype(kv_grad.dtype)
             kv_grad[1, :, cols] = value_grad.astype(kv_grad.dtype)
-        pair[1, :, cols] = (dq * scale).astype(bf16)
+        q_grad[:, cols] = (dq * scale).astype(bf16)
 
 
 ATTN_FLOPS = 2 * HEADS * SLOTS * 2 * SLOTS * HS
 
 
-def attend_forward(meta, query, own_kv, other_kv):
+def attend_forward(meta, query, own_kv, other_kv, after):
     return call(
         forward_kernel,
         sds((SLOTS, COLS), bf16),
         vmem=10,
         flops=4 * ATTN_FLOPS,
         nbytes=6 * SLOTS * COLS * 2,
-        in_specs=[SMEM] + [VMEM] * 3,
+        in_specs=[SMEM] + [VMEM] * 3 + [ANY] * len(after),
         out_specs=VMEM,
         name="attend_forward",
-    )(meta, query, own_kv, other_kv)
+    )(meta, query, own_kv, other_kv, *after)
 
 
 def attend_backward(meta, query, own_kv, other_kv, mixed, grad, after):
     kv = (2, SLOTS, COLS)
     return call(
         backward_kernel,
-        [sds(kv, bf16), sds(kv, f32), sds(kv, bf16)],
+        [sds((SLOTS, COLS), bf16), sds(kv, f32), sds(kv, bf16)],
         vmem=14,
         flops=8 * ATTN_FLOPS,
         nbytes=12 * SLOTS * COLS * 2,
@@ -543,71 +564,105 @@
     )(meta, query, own_kv, other_kv, mixed, grad, *after)
 
 
-def share_kernel(arrays, column, *refs):
-    count = len(arrays)
-    chunks, grads = refs[:3 * count], refs[3 * count:3 * count + 4]
-    sent, mine, lefts, rights = refs[-4:]
-
-    @pl.when(pl.program_id(0) == 0)
+def out_kernel(order, grad, mixed, own, sent):
+    share = dot_tokens(grad[...], mixed[...]).astype(bf16)
+
+    @pl.when(pl.program_id(0) < 4)
     def _():
-        for k, grad in enumerate(grads):
-            rights[:, pl.ds(k * SLOTS, SLOTS)] = grad[...]
-
-    for i in range(count):
-        own, came, other = chunks[3 * i:3 * i + 3]
-        lefts[i, :SLOTS] = own[...]
-        for k in range(3):
-            start = (k + 1) * SLOTS
-            lefts[i, start:start + SLOTS // 2] = came[k, 0]
-            lefts[i, start + SLOTS // 2:start + SLOTS] = other[k, 0]
-    for part in range(2):
-        total = dot_tokens(lefts[part % count], rights[part])
-
-        @pl.when(pl.program_id(0) == 0)
-        def _():
-            sent[part] = total.astype(bf16)
-
-        @pl.when(pl.program_id(0) == 1)
-        def _():
-            mine[part] = total
-
-
-def weight_shares(column, fulls, came, other, grads, arrays, after=()):
-    half = SLOTS // 2
-    chunks, specs = [], []
-    for array in arrays:
-        chunks += [fulls[array], came, other]
-        specs += [pl.BlockSpec((SLOTS, COLS), lambda i, column: (0, column[i]))]
-        specs += [
-            pl.BlockSpec(
-                (3, 1, half, COLS), lambda i, column, array=array: (0, array, 0, column[2 + i])
-            )
-        ] * 2
-    return call(
-        functools.partial(share_kernel, arrays),
-        [sds((2, COLS, COLS), bf16), sds((2, COLS, COLS), f32)],
-        vmem=24,
-        flops=4 * 4 * SLOTS * 2 * COLS * COLS,
-        nbytes=8 * SLOTS * COLS * 2 * 4 + 2 * COLS * COLS * 6,
+        sent[0] = share
+
+    @pl.when(pl.program_id(0) >= 4)
+    def _():
+        own[0] = share
+
+
+def out_weight_parts(order, grad_full, mixed):
+    return call(
+        out_kernel,
+        [sds((4, COLS, COLS), bf16)] * 2,
+        vmem=6,
+        flops=2 * SLOTS * WIDTH * COLS,
+        nbytes=SLOTS * WIDTH * 2 + WIDTH * COLS * 2,
         grid_spec=pltpu.PrefetchScalarGridSpec(
             num_scalar_prefetch=1,
-            grid=(2,),
-            in_specs=specs + [whole((2, SLOTS, COLS))] * 4 + [ANY] * len(after),
-            out_specs=[whole((2, COLS, COLS))] * 2,
-            scratch_shapes=[
-                pltpu.VMEM((len(arrays), 4 * SLOTS, COLS), bf16),
-                pltpu.VMEM((2, 4 * SLOTS, COLS), bf16),
+            grid=(8,),
+            in_specs=[
+                pl.BlockSpec((SLOTS, COLS), lambda i, order: (0, order[i])),
+                pl.BlockSpec((SLOTS, COLS), lambda i, order: (0, 0)),
+            ],
+            out_specs=[
+                pl.BlockSpec((1, COLS, COLS), lambda i, order: (jnp.maximum(i - 4, 0), 0, 0)),
+                pl.BlockSpec((1, COLS, COLS), lambda i, order: (jnp.minimum(i, 3), 0, 0)),
             ],
         ),
+        name="out_weight_parts",
+    )(order, grad_full, mixed)
+
+
+def share_kernel(columns, own, came, other, *refs):
+    q_grads, kv_grads = refs[:4], refs[4:8]
+    out, lefts = refs[-2:]
+    half = SLOTS // 2
+    part = pl.program_id(0)
+
+    @pl.when(part == 0)
+    def _():
+        lefts[0] = own[...]
+        for k in range(3):
+            lefts[k + 1, :half] = came[k]
+            lefts[k + 1, half:] = other[k]
+
+    def share(grads):
+        total = dot_tokens(lefts[0], grads[0])
+        for k in range(1, 4):
+            total = total + dot_tokens(lefts[k], grads[k])
+        out[0] = total.astype(out.dtype)
+
+    @pl.when(part == 0)
+    def _():
+        share([grad[...] for grad in q_grads])
+
+    @pl.when(part > 0)
+    def _():
+        share([grad[0] for grad in kv_grads])
+
+
+def weight_shares(columns, which, full, came, other, q_grads, kv_grads, dtype, after=()):
+    half = SLOTS // 2
+    return call(
+        share_kernel,
+        sds((3, COLS, COLS), dtype),
+        vmem=16,
+        flops=3 * 4 * 2 * SLOTS * COLS * COLS,
+        nbytes=16 * SLOTS * COLS * 2 + 3 * COLS * COLS * 4,
+        grid_spec=pltpu.PrefetchScalarGridSpec(
+            num_scalar_prefetch=1,
+            grid=(3,),
+            in_specs=[
+                pl.BlockSpec((SLOTS, COLS), lambda p, columns: (0, columns[which])),
+                pl.BlockSpec((3, half, COLS), lambda p, columns: (0, 0, columns[2 + which])),
+                pl.BlockSpec((3, half, COLS), lambda p, columns: (0, 0, columns[2 + which])),
+            ]
+            + [whole((SLOTS, COLS))] * 4
+            + [
+                pl.BlockSpec(
+                    (1, SLOTS, COLS), lambda p, columns: (jnp.maximum(p - 1, 0), 0, 0)
+                )
+            ]
+            * 4
+            + [ANY] * len(after),
+            out_specs=pl.BlockSpec((1, COLS, COLS), lambda p, columns: (p, 0, 0)),
+            scratch_shapes=[pltpu.VMEM((4, SLOTS, COLS), bf16)],
+        ),
         name="weight_shares",
-    )(column, *chunks, *grads, *after)
-
-
-def chunks_over_y(fulls, y_index):
+    )(columns, full, came, other, *q_grads, *kv_grads, *after)
+
+
+def chunks_over_y(full, y_index):
     came = []
     for k in STEPS[1:]:
         start = (y_index + k) % 4 * 1024
-        sent = jnp.stack([lax.dynamic_slice(v, (0, start), (SLOTS // 2, 1024)) for v in fulls])
+        sent = lax.dynamic_slice(full, (0, start), (SLOTS // 2, 1024))
         came.append(lax.ppermute(sent, "seq", y_shift(k)))
     came = jnp.stack(came)
     return came, lax.ppermute(came, "tp", X_SWAP)
@@ -626,66 +681,74 @@
         [text_gaps[0], image_runs[0], jnp.stack([group, x_index, z_index]).astype(jnp.int32)]
     )
 
-    order = jnp.stack(
-        [
-            jnp.where(xbit == 0, x_index, 1 - x_index) * 4 + (z_index + 4 - k) % 4
-            for xbit in range(2)
-            for k in STEPS
-        ]
+    back_y = jnp.stack([(y_index - k) % 4 for k in STEPS]) * 2
+    out_order = jnp.concatenate([back_y + 1 - core, back_y + core]).astype(jnp.int32)
+    columns = jnp.stack(
+        [y_index * 2 + 1 - core, y_index * 2 + core, 1 - core, core]
     ).astype(jnp.int32)
 
     n_left, n_right, grad_rows, inv = norm_rows(valid.reshape(1), x_rows, gains, cotangent[0, 0])
-    grad_came = lax.all_gather(grad_rows, "tp", axis=0, tiled=True)
+    w_parts, w_out = hold(w_parts, w_out)
     pieces = gather_blocks(n_left, n_right)
+    grad_other = lax.ppermute(grad_rows, "tp", X_SWAP)
+    grad_pair = jnp.stack([grad_rows, grad_other])
+    grad_pairs = [grad_pair] + [lax.ppermute(grad_pair, "tp", z_shift(k)) for k in STEPS[1:]]
     normed_full, own_kv = key_value(pieces, w_parts)
     other_kv = lax.ppermute(own_kv, "grp", GRP_SWAP)
     query = one_dot(normed_full, w_parts, 0)
-    grad_full, grad_mixed = grad_mixed_of(order, grad_came, w_out)
-    fulls = (normed_full, grad_full)
-    chunk_came, chunk_other = chunks_over_y(fulls, y_index)
-
-    mixed = attend_forward(meta, query, own_kv, other_kv)
-    pair, own_part, other_part = attend_backward(
-        meta, query, own_kv, other_kv, mixed, grad_mixed, []
-    )
-    proj_rows = lax.psum_scatter(
-        proj_parts(order, mixed, w_out), "tp", scatter_dimension=0, tiled=True
+    grad_full, grad_mixed = grad_mixed_of(grad_pairs, w_out)
+    chunk_came, chunk_other = chunks_over_y(normed_full, y_index)
+
+    mixed = attend_forward(meta, query, own_kv, other_kv, [grad_mixed])
+    proj = proj_parts(mixed, w_out)
+    proj_x = lax.ppermute(proj[1], "tp", X_SWAP)
+    q_grad, own_part, other_part = attend_backward(
+        meta, query, own_kv, other_kv, mixed, grad_mixed, [proj[0]]
     )
     back = lax.ppermute(other_part, "grp", GRP_SWAP)
-
-    pairs = [pair] + [lax.ppermute(pair, "seq", y_shift(k)) for k in STEPS[1:]]
-    kv_grad = sum_keys(own_part, back, [chunk_came])
+    q_grads = [q_grad] + [lax.ppermute(q_grad, "seq", y_shift(k)) for k in STEPS[1:]]
+    out_own, out_sent = out_weight_parts(out_order, grad_full, mixed)
+    out_came = lax.ppermute(out_sent, "seq", CORE_SWAP)
+    kv_grad = sum_keys(own_part, back, [chunk_came, out_own] + q_grads[1:3])
     kv_grads = [kv_grad] + [lax.ppermute(kv_grad, "seq", y_shift(k)) for k in STEPS[1:]]
 
-    lefts = [pair, kv_grad]
-    right = back_right(lefts, w_parts, normed_full)
+    lefts = [q_grad, kv_grad]
+    right = back_right(lefts, w_parts, normed_full, [chunk_other])
     right_x = lax.ppermute(right[1], "tp", X_SWAP)
-    left = back_left(lefts, w_parts, normed_full, right[2])
+    left = back_left(lefts, w_parts, normed_full, right[2], q_grads[3:] + kv_grads[1:3] + [proj_x, out_came])
     left_came = [lax.ppermute(left[i], "tp", z_shift(-STEPS[i])) for i in range(1, 4)]
-    right_kept, *right_sends = sum_x(right[0], right_x, pairs[1:3])
-    right_came = [
-        lax.ppermute(sent, "tp", z_shift(-k)) for sent, k in zip(right_sends, STEPS[1:])
-    ]
-    left_kept, left_sent, gain_kept = sum_left(left[0], left_came, pairs[3:])
+    out_kept, *out_sends = sum_x(out_own, out_came, left_came[:1])
+    out_terms = [lax.ppermute(v, "seq", y_shift(-k)) for v, k in zip(out_sends, STEPS[1:])]
+    left_kept, left_sent, gain_kept = sum_left(
+        left[0], left_came, [kv_grads[3], right_x, out_sends[0]]
+    )
     left_x = lax.ppermute(left_sent, "tp", X_SWAP)
-    layer_out = ((x_rows.astype(f32) + proj_rows.astype(f32)) * valid).astype(bf16)
-
-    columns = jnp.stack(
-        [y_index * 2 + 1 - core, y_index * 2 + core, 1 - core, core]
-    ).astype(jnp.int32)
-    chunks = (columns, fulls, chunk_came, chunk_other)
-    pair_sent, pair_mine = weight_shares(*chunks, pairs, (1, 0), kv_grads[1:3])
+    shares = (normed_full, chunk_came, chunk_other, q_grads, kv_grads)
+    qkv_sent = weight_shares(columns, 0, *shares, bf16)
+    right_kept, *right_sends = sum_x(
+        right[0], right_x, [left_x, qkv_sent] + out_terms[:2]
+    )
+    right_came = [lax.ppermute(v, "tp", z_shift(-k)) for v, k in zip(right_sends, STEPS[1:])]
+    proj_kept, *proj_sends = sum_x(proj[0], proj_x, [right_sends[0]])
+    proj_came = [lax.ppermute(v, "tp", z_shift(-k)) for v, k in zip(proj_sends, STEPS[1:])]
+    gain_sum = sum_gain(gain_kept, left_x, gains)
+    gain_sum = gain_sum + lax.ppermute(gain_sum, "seq", CORE_SWAP)
+    gain_grad = gain_sum
+    for k in STEPS[1:]:
+        gain_grad = gain_grad + lax.ppermute(gain_sum, "seq", y_shift(k))
     tokens_grad = token_rows(
-        x_rows, grad_rows, gains, inv, (left_kept, left_x), (right_kept, *right_came), kv_grads[3:]
-    )
-    kv_sent, kv_mine = weight_shares(*chunks, kv_grads, (0,))
-    gain_grad = sum_gain(gain_kept, left_x, gains)
-    for flip in (2, 4, 1):
-        gain_grad = gain_grad + lax.ppermute(gain_grad, "seq", [(i, i ^ flip) for i in range(8)])
-    pair_share = pair_mine + lax.ppermute(pair_sent, "seq", CORE_SWAP).astype(f32)
-    kv_share = kv_mine + lax.ppermute(kv_sent, "seq", CORE_SWAP).astype(f32)
-    out_share = pair_share[0]
-    qkv_share = jnp.concatenate([pair_share[1:], kv_share], axis=0)
+        x_rows, grad_rows, gains, inv, (left_kept, left_x), (right_kept, *right_came)
+    )
+
+    qkv_mine = weight_shares(columns, 1, *shares, f32, [qkv_sent] + out_terms[2:])
+    qkv_share = qkv_mine + lax.ppermute(qkv_sent, "seq", CORE_SWAP).astype(f32)
+    proj_rows = proj_kept
+    for came in proj_came:
+        proj_rows = proj_rows + came.astype(f32)
+    layer_out = ((x_rows.astype(f32) + proj_rows) * valid).astype(bf16)
+    out_share = out_kept
+    for came in out_terms:
+        out_share = out_share + came.astype(f32)
     return (
         layer_out[None, None],
         tokens_grad[None, None],

time: 252 us -> 226 us (0.90)
  waiting for transfers between devices: 103 us -> 87.5 us
  starting transfers between devices: 42.2 us -> 56.3 us
  between operations: 14.5 us -> 1.06 us
  local copies, waits for them, and re-layouts: 37.2 us -> 32.5 us
  other arithmetic: 10 us -> 5.43 us
    ppermute x3, waiting for transfers between devices: 22.9 us -> 0.01 us  [chunks_over_y(): came.append(lax.ppermute(sent, 'seq', y_shift(k)))]
    ppermute x11 -> x23, waiting for transfers between devices: 26.2 us -> 47.3 us  [the longest x3 16.3 us: per_device(): lax.ppermute(v, 'seq', y_shift(-k))]
    ppermute x1, waiting for transfers between devices: 0.01 us -> 17.4 us  [per_device(): back = lax.ppermute(other_part, 'grp', GRP_SWAP)]
    ppermute x3, waiting for transfers between devices: 22.9 us -> 10.5 us  [gather_blocks(): lax.ppermute(right_pair, 'tp', z_shift(k))]
    ppermute x1, waiting for transfers between devices: 11.6 us -> 4.18 us  [per_device(): left_x = lax.ppermute(left_sent, 'tp', X_SWAP)]
    ppermute x1, waiting for transfers between devices: 6.8 us -> 0.01 us  [per_device(): other_kv = lax.ppermute(own_kv, 'grp', GRP_SWAP)]
    ppermute x11 -> x23, starting transfers between devices: 15.4 us -> 20.8 us  [the longest x6 7.72 us: per_device(): lax.ppermute(v, 'tp', z_shift(-k))]
    pallas_call x6 -> x10, Pallas kernels: 23.8 us -> 28.6 us  [the longest x2 8.62 us: weight_shares(): call(share_kernel, sds((3, COLS, COLS), dtype), vmem=16, flops=3 * 4 * 2...]
  transfers between devices with their start and end apart: 35 -> 45, of which waited for: 15 -> 17; matrix products, arithmetic and copies ran while one was open for 4% -> 2% of each run, Pallas kernels for 17% -> 16%
where the time goes in v5:
time: 226 us
  waiting for transfers between devices  87.5 us (39%)
  starting transfers between devices  56.3 us (25%)
  Pallas kernels  43 us (19%)
  local copies, waits for them, and re-layouts  32.5 us (14%)
  other arithmetic  5.43 us (2%)
    unnamed x76, local copies, waits for them, and re-layouts  32.3 us
    ppermute x1, waiting for transfers between devices, per_device(): back = lax.ppermute(other_part, 'grp', GRP_SWAP)  17.4 us
    ppermute x3, waiting for transfers between devices, per_device(): lax.ppermute(v, 'seq', y_shift(-k))  16.3 us
    ppermute x3, waiting for transfers between devices, per_device(): lax.ppermute(q_grad, 'seq', y_shift(k))  11 us
    ppermute x3, waiting for transfers between devices, gather_blocks(): lax.ppermute(right_pair, 'tp', z_shift(k))  10.5 us
    pallas_call x2, Pallas kernels, weight_shares(): call(share_kernel, sds((3, COLS, COLS), dtype), vmem=16, flops=3 * 4 * 2...  8.62 us
    ppermute x6, starting transfers between devices, per_device(): lax.ppermute(v, 'tp', z_shift(-k))  7.72 us
    ppermute x3, waiting for transfers between devices, per_device(): lax.ppermute(grad_pair, 'tp', z_shift(k))  7.47 us
  transfers between devices with their start and end apart: 45, of which 17 were waited for; matrix products, arithmetic and copies ran while one was open for 2% of the time, Pallas kernels for 16%

profile of v5, /device:TPU:0, one launch (start us, length us, event | category | flops | bytes accessed | tf_op | source)
XLA Modules:
  0.0 225.8 jit_solution(12160883404858150834)
XLA Ops:
  3.5 4.2 %collective-permute-start.1 = (bf16[32,2048]{1,0:T(8,128)(2,1)S(1)}, bf16[32,2048]{1,0:T(8,128)(2,1)S(1)}, u32[]{:S(2)}, u32[]{:S(2)}) collective-permute-start(bf16[32,2048]{1,0:T(8,128)(2,1)S(1)} %get-tuple-element.44), channel_id=1, source_target_pairs={{0,3},{1,0},{2,1},{3,2},{4,7},{5,4},{6,5},{7,6},{8,11},{9,8},{10,9... | collective-permute-start | bytes 393224 | tf_op jit(solution)/shard_map/ppermute | solution.py:126
  11.0 4.6 %copy-done.6 = bf16[1,4096,3,512]{3,1,2,0:T(8,128)(2,1)S(1)} copy-done((bf16[1,4096,3,512]{3,1,2,0:T(8,128)(2,1)S(1)}, bf16[1,4096,3,512]{3,1,2,0:T(8,128)(2,1)}, u32[]{:S(2)}) %copy-start.6) | copy-done | bytes 12582936
  15.6 2.2 copy-done.16
  18.9 4.6 %copy-done = bf16[3,4096,512]{2,1,0:T(8,128)(2,1)} copy-done((bf16[3,4096,512]{2,1,0:T(8,128)(2,1)}, bf16[3,4096,512]{2,1,0:T(8,128)(2,1)S(1)}, u32[]{:S(2)}) %copy-start) | copy-done | bytes 12582936
  23.5 1.9 copy-done.3
  25.7 1.6 collective-permute-start.3
  27.3 2.3 %collective-permute-start.5 = (bf16[2,32,2048]{2,1,0:T(8,128)(2,1)S(1)}, bf16[2,32,2048]{2,1,0:T(8,128)(2,1)S(1)}, u32[]{:S(2)}, u32[]{:S(2)}) collective-permute-start(bf16[2,32,2048]{2,1,0:T(8,128)(2,1)S(1)} %pad_maximum_fusion.3.refs_2_), channel_id=1, source_target_pairs={{0,1},{1,2},{2,3},{3,0},{4,5},{5,6},{6,7},{7,4},{8,9},{9,10},{10,1... | collective-permute-start | bytes 786440 | tf_op jit(solution)/shard_map/ppermute | solution.py:127
  32.4 8.9 %collective-permute-done.5.refs_3_ = bf16[2,32,2048]{2,1,0:T(8,128)(2,1)S(1)} collective-permute-done((bf16[2,32,2048]{2,1,0:T(8,128)(2,1)S(1)}, bf16[2,32,2048]{2,1,0:T(8,128)(2,1)S(1)}, u32[]{:S(2)}, u32[]{:S(2)}) %collective-permute-start.5) | collective-permute-done | bytes 262176 | tf_op jit(solution)/shard_map/ppermute | solution.py:127
  42.1 1.6 collective-permute-done.7.refs_5_
  43.7 4.6 %copy-done.1 = bf16[3,4096,512]{2,1,0:T(8,128)(2,1)S(1)} copy-done((bf16[3,4096,512]{2,1,0:T(8,128)(2,1)S(1)}, bf16[3,4096,512]{2,1,0:T(8,128)(2,1)}, u32[]{:S(2)}) %copy-start.1) | copy-done | bytes 12582936
  48.2 3.7 %key_value.1 = (bf16[256,4096]{1,0:T(8,128)(2,1)S(1)}, bf16[2,256,512]{2,1,0:T(8,128)(2,1)S(1)}) custom-call(bf16[4,32,2048]{2,1,0:T(8,128)(2,1)S(1)} %pad_maximum_fusion.1.refs_0_, bf16[4,32,2048]{2,1,0:T(8,128)(2,1)S(1)} %collective-permute-done.3.refs_1_, bf16[2,32,2048]{2,1,0:T(8,128)(2,1)S(1)} %pad_maximum_fusion.3.refs_2_, ...), custom_call_target="tpu_custom_call" | custom-call | flops 2147483648 | bytes 12582912 | tf_op jit(solution)/shard_map/key_value/pallas_call | solution.py:281
  51.9 2.8 %collective-permute-start.8 = (bf16[2,256,512]{2,1,0:T(8,128)(2,1)S(1)}, bf16[2,256,512]{2,1,0:T(8,128)(2,1)S(1)}, u32[]{:S(2)}, u32[]{:S(2)}) collective-permute-start(bf16[2,256,512]{2,1,0:T(8,128)(2,1)S(1)} %get-tuple-element.48.own_kv), channel_id=1, source_target_pairs={{0,64},{64,0},{1,65},{65,1},{2,66},{66,2},{3,67},{67,3},{4,68},{68... | collective-permute-start | bytes 1572872 | tf_op jit(solution)/shard_map/ppermute | solution.py:697
  56.1 7.4 %collective-permute-done.12.p3 = bf16[2,32,4096]{2,1,0:T(8,128)(2,1)S(1)} collective-permute-done((bf16[2,32,4096]{2,1,0:T(8,128)(2,1)S(1)}, bf16[2,32,4096]{2,1,0:T(8,128)(2,1)S(1)}, u32[]{:S(2)}, u32[]{:S(2)}) %collective-permute-start.12) | collective-permute-done | bytes 524320 | tf_op jit(solution)/shard_map/ppermute | solution.py:695
  64.8 2.4 %attend_forward.1.left.mixed = bf16[256,512]{1,0:T(8,128)(2,1)S(1)} custom-call(s32[12]{0:T(128)S(1)} %concatenate.6.meta, bf16[256,512]{1,0:T(8,128)(2,1)S(1)} %one_dot.1.query, bf16[2,256,512]{2,1,0:T(8,128)(2,1)S(1)} %get-tuple-element.48.own_kv, bf16[2,256,512]{2,1,0:T(8,128)(2,1)S(1)} %collective-permute-done.8.other_kv, ...), custom_call_target="tpu_custom_call" | custom-call | flops 536870912 | bytes 1572864 | tf_op jit(solution)/shard_map/attend_forward/pallas_call | solution.py:541
  67.2 5.4 %out_weight_parts.1 = (bf16[4,512,512]{2,1,0:T(8,128)(2,1)S(1)}, bf16[4,512,512]{2,1,0:T(8,128)(2,1)}) custom-call(s32[8]{0:T(128)S(1)} %pad_add_fusion.order, bf16[256,4096]{1,0:T(8,128)(2,1)S(1)} %get-tuple-element.57.grad, bf16[256,512]{1,0:T(8,128)(2,1)S(1)} %attend_forward.1.left.mixed), custom_call_target="tpu_custom_call" | custom-call | flops 1073741824 | bytes 6291456 | tf_op jit(solution)/shard_map/out_weight_parts/pallas_call | solution.py:580
  74.0 1.6 collective-permute-start.15
  75.6 1.7 collective-permute-start.16
  77.3 2.0 collective-permute-start.17
  79.3 2.2 copy-done.5
  81.5 4.3 %proj_parts.1 = (bf16[4,32,4096]{2,1,0:T(8,128)(2,1)S(1)}, bf16[4,32,4096]{2,1,0:T(8,128)(2,1)}) custom-call(bf16[256,512]{1,0:T(8,128)(2,1)S(1)} %attend_forward.1.left.mixed, bf16[1,4096,512]{2,1,0:T(8,128)(2,1)S(1)} %copy-done.5), custom_call_target="tpu_custom_call" | custom-call | flops 1073741824 | bytes 6291456 | tf_op jit(solution)/shard_map/proj_parts/pallas_call | solution.py:439
  85.8 4.3 %attend_backward.1 = (bf16[256,512]{1,0:T(8,128)(2,1)S(1)}, f32[2,256,512]{2,1,0:T(8,128)S(1)}, bf16[2,256,512]{2,1,0:T(8,128)(2,1)S(1)}) custom-call(s32[12]{0:T(128)S(1)} %concatenate.6.meta, bf16[256,512]{1,0:T(8,128)(2,1)S(1)} %one_dot.1.query, bf16[2,256,512]{2,1,0:T(8,128)(2,1)S(1)} %get-tuple-element.48.own_kv, bf16[2,256,512]{2,1,0:T(8,128)(2,1)S(1)} %copy-done.33, ...), custom_call_target="tpu_custom_call" | custom-call | flops 1073741824 | bytes 3145728 | tf_op jit(solution)/shard_map/attend_backward/pallas_call | solution.py:555
  91.5 3.0 %collective-permute-start.14 = (bf16[2,256,512]{2,1,0:T(8,128)(2,1)S(1)}, bf16[2,256,512]{2,1,0:T(8,128)(2,1)S(1)}, u32[]{:S(2)}, u32[]{:S(2)}) collective-permute-start(bf16[2,256,512]{2,1,0:T(8,128)(2,1)S(1)} %get-tuple-element.56), channel_id=1, source_target_pairs={{0,64},{64,0},{1,65},{65,1},{2,66},{66,2},{3,67},{67,3},{4,68},{68... | collective-permute-start | bytes 1572872 | tf_op jit(solution)/shard_map/ppermute | solution.py:708
  95.2 4.1 %collective-permute-done.18.refs_2_.refs_1_ = bf16[256,512]{1,0:T(8,128)(2,1)S(1)} collective-permute-done((bf16[256,512]{1,0:T(8,128)(2,1)S(1)}, bf16[256,512]{1,0:T(8,128)(2,1)S(1)}, u32[]{:S(2)}, u32[]{:S(2)}) %collective-permute-start.18) | collective-permute-done | bytes 262176 | tf_op jit(solution)/shard_map/ppermute | solution.py:709
  99.2 7.0 %collective-permute-done.19.refs_3_.refs_2_ = bf16[256,512]{1,0:T(8,128)(2,1)S(1)} collective-permute-done((bf16[256,512]{1,0:T(8,128)(2,1)S(1)}, bf16[256,512]{1,0:T(8,128)(2,1)S(1)}, u32[]{:S(2)}, u32[]{:S(2)}) %collective-permute-start.19) | collective-permute-done | bytes 262176 | tf_op jit(solution)/shard_map/ppermute | solution.py:709
  106.8 17.4 %collective-permute-done.14.came = bf16[2,256,512]{2,1,0:T(8,128)(2,1)S(1)} collective-permute-done((bf16[2,256,512]{2,1,0:T(8,128)(2,1)S(1)}, bf16[2,256,512]{2,1,0:T(8,128)(2,1)S(1)}, u32[]{:S(2)}, u32[]{:S(2)}) %collective-permute-start.14) | collective-permute-done | bytes 524320 | tf_op jit(solution)/shard_map/ppermute | solution.py:708
  126.3 2.1 collective-permute-start.24
  130.2 4.6 %copy-done.2 = bf16[3,4096,512]{2,1,0:T(8,128)(2,1)S(1)} copy-done((bf16[3,4096,512]{2,1,0:T(8,128)(2,1)S(1)}, bf16[3,4096,512]{2,1,0:T(8,128)(2,1)}, u32[]{:S(2)}) %copy-start.2) | copy-done | bytes 12582936
  136.8 2.7 %back_right.1 = (bf16[4,32,2048]{2,1,0:T(8,128)(2,1)S(1)}, bf16[4,32,2048]{2,1,0:T(8,128)(2,1)S(1)}, f32[1,2048]{1,0:T(1,128)S(1)}) custom-call(bf16[256,512]{1,0:T(8,128)(2,1)S(1)} %copy-done.14, bf16[2,256,512]{2,1,0:T(8,128)(2,1)S(1)} %sum_keys.1.kv_grad.refs_4_, bf16[3,4096,512]{2,1,0:T(8,128)(2,1)S(1)} %copy-done.2, ...), custom_call_target="tpu_custom_call" | custom-call | flops 1610612736 | bytes 8388608 | tf_op jit(solution)/shard_map/back_right/pallas_call | solution.py:392
  139.6 4.4 %collective-permute-done.13.refs_3_.came = bf16[4,32,4096]{2,1,0:T(8,128)(2,1)} collective-permute-done((bf16[4,32,4096]{2,1,0:T(8,128)(2,1)}, bf16[4,32,4096]{2,1,0:T(8,128)(2,1)}, u32[]{:S(2)}, u32[]{:S(2)}) %collective-permute-start.13) | collective-permute-done | bytes 1048608 | tf_op jit(solution)/shard_map/ppermute | solution.py:704
  144.5 3.7 %collective-permute-done.24.refs_2_.refs_6_ = bf16[2,256,512]{2,1,0:T(8,128)(2,1)} collective-permute-done((bf16[2,256,512]{2,1,0:T(8,128)(2,1)S(1)}, bf16[2,256,512]{2,1,0:T(8,128)(2,1)}, u32[]{:S(2)}, u32[]{:S(2)}) %collective-permute-start.24) | collective-permute-done | bytes 524320 | tf_op jit(solution)/shard_map/ppermute | solution.py:713
  148.3 2.8 %back_left.1 = (bf16[5,16,2048]{2,1,0:T(8,128)(2,1)S(1)}, bf16[5,16,2048]{2,1,0:T(8,128)(2,1)S(1)}, bf16[5,16,2048]{2,1,0:T(8,128)(2,1)S(1)}, bf16[5,16,2048]{2,1,0:T(8,128)(2,1)S(1)}) custom-call(bf16[256,512]{1,0:T(8,128)(2,1)S(1)} %copy-done.15, bf16[2,256,512]{2,1,0:T(8,128)(2,1)S(1)} %sum_keys.1.kv_grad.refs_4_, bf16[3,4096,512]{2,1,0:T(8,128)(2,1)S(1)} %copy-done.2, ...), custom_call_target="tpu_custom_call" | custom-call | flops 1610612736 | bytes 8388608 | tf_op jit(solution)/shard_map/back_left/pallas_call | solution.py:392
  151.1 3.0 %collective-permute-start.26 = (bf16[5,16,2048]{2,1,0:T(8,128)(2,1)S(1)}, bf16[5,16,2048]{2,1,0:T(8,128)(2,1)S(1)}, u32[]{:S(2)}, u32[]{:S(2)}) collective-permute-start(bf16[5,16,2048]{2,1,0:T(8,128)(2,1)S(1)} %get-tuple-element.64), channel_id=1, source_target_pairs={{0,3},{1,0},{2,1},{3,2},{4,7},{5,4},{6,5},{7,6},{8,11},{9,8},{10,9... | collective-permute-start | bytes 983048 | tf_op jit(solution)/shard_map/ppermute | solution.py:719
  154.1 1.5 collective-permute-start.28
  155.6 4.3 %weight_shares.2.refs_1_.refs_8_ = bf16[3,512,512]{2,1,0:T(8,128)(2,1)S(1)} custom-call(s32[4]{0:T(128)S(1)} %pad_add_fusion.1.columns, bf16[256,4096]{1,0:T(8,128)(2,1)S(1)} %get-tuple-element.47.full.normed.own, bf16[3,128,1024]{2,1,0:T(8,128)(2,1)S(1)} %pad_maximum_fusion.refs_0_.came, bf16[3,128,1024]{2,1,0:T(8,128)(2,1)S(1)} %copy-done.12, ...), custom_call_target="tpu_custom_call" | custom-call | flops 1610612736 | bytes 7340032 | tf_op jit(solution)/shard_map/weight_shares/pallas_call | solution.py:632
  160.1 3.3 %collective-permute-done.26.refs_0_.c1 = bf16[5,16,2048]{2,1,0:T(8,128)(2,1)S(1)} collective-permute-done((bf16[5,16,2048]{2,1,0:T(8,128)(2,1)S(1)}, bf16[5,16,2048]{2,1,0:T(8,128)(2,1)S(1)}, u32[]{:S(2)}, u32[]{:S(2)}) %collective-permute-start.26) | collective-permute-done | bytes 327712 | tf_op jit(solution)/shard_map/ppermute | solution.py:719
  163.3 2.0 sum_x.3
  166.7 1.6 collective-permute-start.30
  168.3 4.2 %collective-permute-done.30.refs_0_.l_came.came = bf16[3,16,2048]{2,1,0:T(8,128)(2,1)S(1)} collective-permute-done((bf16[3,16,2048]{2,1,0:T(8,128)(2,1)S(1)}, bf16[3,16,2048]{2,1,0:T(8,128)(2,1)S(1)}, u32[]{:S(2)}, u32[]{:S(2)}) %collective-permute-start.30) | collective-permute-done | bytes 196640 | tf_op jit(solution)/shard_map/ppermute | solution.py:725
  174.5 2.8 %collective-permute-start.41 = (f32[1,4096]{1,0:T(1,128)S(1)}, f32[1,4096]{1,0:T(1,128)S(1)}, u32[]{:S(2)}, u32[]{:S(2)}) collective-permute-start(f32[1,4096]{1,0:T(1,128)S(1)} %add.123), channel_id=1, source_target_pairs={{0,48},{8,56},{16,0},{24,8},{32,16},{40,24},{48,32},{56,40},{1,49}... | collective-permute-start | bytes 49160 | tf_op jit(solution)/shard_map/ppermute | solution.py:738
  180.7 2.2 collective-permute-start.43
  183.5 10.0 %collective-permute-done.31.refs_2_ = bf16[512,512]{1,0:T(8,128)(2,1)S(1)} collective-permute-done((bf16[512,512]{1,0:T(8,128)(2,1)S(1)}, bf16[512,512]{1,0:T(8,128)(2,1)S(1)}, u32[]{:S(2)}, u32[]{:S(2)}) %collective-permute-start.31) | collective-permute-done | bytes 524320 | tf_op jit(solution)/shard_map/ppermute | solution.py:721
  193.5 1.8 collective-permute-done.32.refs_3_
  195.4 2.3 %collective-permute-start.36 = (bf16[32,2048]{1,0:T(8,128)(2,1)S(1)}, bf16[32,2048]{1,0:T(8,128)(2,1)S(1)}, u32[]{:S(2)}, u32[]{:S(2)}) collective-permute-start(bf16[32,2048]{1,0:T(8,128)(2,1)S(1)} %get-tuple-element.70.refs_0_), channel_id=1, source_target_pairs={{0,3},{1,0},{2,1},{3,2},{4,7},{5,4},{6,5},{7,6},{8,11},{9,8},{10,9... | collective-permute-start | bytes 393224 | tf_op jit(solution)/shard_map/ppermute | solution.py:731
  200.7 4.5 %collective-permute-done.43.refs_9_ = bf16[512,512]{1,0:T(8,128)(2,1)S(1)} collective-permute-done((bf16[512,512]{1,0:T(8,128)(2,1)S(1)}, bf16[512,512]{1,0:T(8,128)(2,1)S(1)}, u32[]{:S(2)}, u32[]{:S(2)}) %collective-permute-start.43) | collective-permute-done | bytes 524320 | tf_op jit(solution)/shard_map/ppermute | solution.py:721
  205.2 2.4 %collective-permute-start.33 = (bf16[32,4096]{1,0:T(8,128)(2,1)S(1)}, bf16[32,4096]{1,0:T(8,128)(2,1)S(1)}, u32[]{:S(2)}, u32[]{:S(2)}) collective-permute-start(bf16[32,4096]{1,0:T(8,128)(2,1)S(1)} %get-tuple-element.72), channel_id=1, source_target_pairs={{0,3},{1,0},{2,1},{3,2},{4,7},{5,4},{6,5},{7,6},{8,11},{9,8},{10,9... | collective-permute-start | bytes 786440 | tf_op jit(solution)/shard_map/ppermute | solution.py:733
  207.6 4.3 %weight_shares.3 = f32[3,512,512]{2,1,0:T(8,128)S(1)} custom-call(s32[4]{0:T(128)S(1)} %pad_add_fusion.1.columns, bf16[256,4096]{1,0:T(8,128)(2,1)S(1)} %get-tuple-element.47.full.normed.own, bf16[3,128,1024]{2,1,0:T(8,128)(2,1)S(1)} %pad_maximum_fusion.refs_0_.came, bf16[3,128,1024]{2,1,0:T(8,128)(2,1)S(1)} %copy-done.12, bf16[256,512]{1,0:T(8,128)(2,1)S(1)} %copy-done.15, ...), custom_call_target="tpu_custom_call" | custom-call | flops 1610612736 | bytes 7340032 | tf_op jit(solution)/shard_map/weight_shares/pallas_call | solution.py:632
  212.0 2.2 add_bitcast_fusion
  218.0 6.9 %collective-permute-done.34 = bf16[32,4096]{1,0:T(8,128)(2,1)S(1)} collective-permute-done((bf16[32,4096]{1,0:T(8,128)(2,1)S(1)}, bf16[32,4096]{1,0:T(8,128)(2,1)S(1)}, u32[]{:S(2)}, u32[]{:S(2)}) %collective-permute-start.34) | collective-permute-done | bytes 262176 | tf_op jit(solution)/shard_map/ppermute | solution.py:733
  (153 shorter events, 39.7 us)
Async XLA Ops:
  3.5 22.1 %collective-permute-start.1 = (bf16[32,2048]{1,0:T(8,128)(2,1)S(1)}, bf16[32,2048]{1,0:T(8,128)(2,1)S(1)}, u32[]{:S(2)}, u32[]{:S(2)}) collective-permute-start(bf16[32,2048]{1,0:T(8,128)(2,1)S(1)} %get-tuple-element.44), channel_id=1, source_target_pairs={{0,3},{1,0},{2,1},{3,2},{4,7},{5,4},{6,5},{7,6},{8,11},{9,8},{10,9... | collective-permute-start | bytes 393224 | tf_op jit(solution)/shard_map/ppermute | solution.py:126
  7.7 17.9 %collective-permute-start.2 = (bf16[32,2048]{1,0:T(8,128)(2,1)S(1)}, bf16[32,2048]{1,0:T(8,128)(2,1)S(1)}, u32[]{:S(2)}, u32[]{:S(2)}) collective-permute-start(bf16[32,2048]{1,0:T(8,128)(2,1)S(1)} %get-tuple-element.44), channel_id=1, source_target_pairs={{0,2},{1,3},{2,0},{3,1},{4,6},{5,7},{6,4},{7,5},{8,10},{9,11},{10,... | collective-permute-start | bytes 393224 | tf_op jit(solution)/shard_map/ppermute | solution.py:126
  7.7 17.9 %collective-permute-start = (bf16[32,2048]{1,0:T(8,128)(2,1)S(1)}, bf16[32,2048]{1,0:T(8,128)(2,1)S(1)}, u32[]{:S(2)}, u32[]{:S(2)}) collective-permute-start(bf16[32,2048]{1,0:T(8,128)(2,1)S(1)} %get-tuple-element.44), channel_id=1, source_target_pairs={{0,1},{1,2},{2,3},{3,0},{4,5},{5,6},{6,7},{7,4},{8,9},{9,10},{10,1... | collective-permute-start | bytes 393224 | tf_op jit(solution)/shard_map/ppermute | solution.py:126
  9.0 18.3 %collective-permute-start.4 = (bf16[32,2048]{1,0:T(8,128)(2,1)S(1)}, bf16[32,2048]{1,0:T(8,128)(2,1)S(1)}, u32[]{:S(2)}, u32[]{:S(2)}) collective-permute-start(bf16[32,2048]{1,0:T(8,128)(2,1)S(1)} %get-tuple-element.45), channel_id=1, source_target_pairs={{0,4},{1,5},{2,6},{3,7},{4,0},{5,1},{6,2},{7,3},{8,12},{9,13},{10,... | collective-permute-start | bytes 393224 | tf_op jit(solution)/shard_map/ppermute | solution.py:125
  10.4 21.3 %collective-permute-start.9 = (bf16[32,4096]{1,0:T(8,128)(2,1)S(1)}, bf16[32,4096]{1,0:T(8,128)(2,1)S(1)}, u32[]{:S(2)}, u32[]{:S(2)}) collective-permute-start(bf16[32,4096]{1,0:T(8,128)(2,1)S(1)} %get-tuple-element.49.grad), channel_id=1, source_target_pairs={{0,4},{1,5},{2,6},{3,7},{4,0},{5,1},{6,2},{7,3},{8,12},{9,13},{10,... | collective-permute-start | bytes 786440 | tf_op jit(solution)/shard_map/ppermute | solution.py:693
  25.7 18.0 %collective-permute-start.3 = (bf16[4,32,2048]{2,1,0:T(8,128)(2,1)S(1)}, bf16[4,32,2048]{2,1,0:T(8,128)(2,1)S(1)}, u32[]{:S(2)}, u32[]{:S(2)}) collective-permute-start(bf16[4,32,2048]{2,1,0:T(8,128)(2,1)S(1)} %pad_maximum_fusion.1.refs_0_), channel_id=1, source_target_pairs={{0,4},{1,5},{2,6},{3,7},{4,0},{5,1},{6,2},{7,3},{8,12},{9,13},{10,... | collective-permute-start | bytes 1572872 | tf_op jit(solution)/shard_map/ppermute | solution.py:129
  27.3 13.9 %collective-permute-start.5 = (bf16[2,32,2048]{2,1,0:T(8,128)(2,1)S(1)}, bf16[2,32,2048]{2,1,0:T(8,128)(2,1)S(1)}, u32[]{:S(2)}, u32[]{:S(2)}) collective-permute-start(bf16[2,32,2048]{2,1,0:T(8,128)(2,1)S(1)} %pad_maximum_fusion.3.refs_2_), channel_id=1, source_target_pairs={{0,1},{1,2},{2,3},{3,0},{4,5},{5,6},{6,7},{7,4},{8,9},{9,10},{10,1... | collective-permute-start | bytes 786440 | tf_op jit(solution)/shard_map/ppermute | solution.py:127
  29.6 11.6 %collective-permute-start.6 = (bf16[2,32,2048]{2,1,0:T(8,128)(2,1)S(1)}, bf16[2,32,2048]{2,1,0:T(8,128)(2,1)S(1)}, u32[]{:S(2)}, u32[]{:S(2)}) collective-permute-start(bf16[2,32,2048]{2,1,0:T(8,128)(2,1)S(1)} %pad_maximum_fusion.3.refs_2_), channel_id=1, source_target_pairs={{0,3},{1,0},{2,1},{3,2},{4,7},{5,4},{6,5},{7,6},{8,11},{9,8},{10,9... | collective-permute-start | bytes 786440 | tf_op jit(solution)/shard_map/ppermute | solution.py:127
  30.6 13.0 %collective-permute-start.7 = (bf16[2,32,2048]{2,1,0:T(8,128)(2,1)S(1)}, bf16[2,32,2048]{2,1,0:T(8,128)(2,1)S(1)}, u32[]{:S(2)}, u32[]{:S(2)}) collective-permute-start(bf16[2,32,2048]{2,1,0:T(8,128)(2,1)S(1)} %pad_maximum_fusion.3.refs_2_), channel_id=1, source_target_pairs={{0,2},{1,3},{2,0},{3,1},{4,6},{5,7},{6,4},{7,5},{8,10},{9,11},{10,... | collective-permute-start | bytes 786440 | tf_op jit(solution)/shard_map/ppermute | solution.py:127
  31.8 24.2 %collective-permute-start.10 = (bf16[2,32,4096]{2,1,0:T(8,128)(2,1)S(1)}, bf16[2,32,4096]{2,1,0:T(8,128)(2,1)S(1)}, u32[]{:S(2)}, u32[]{:S(2)}) collective-permute-start(bf16[2,32,4096]{2,1,0:T(8,128)(2,1)S(1)} %pad_maximum_fusion.2.p0), channel_id=1, source_target_pairs={{0,1},{1,2},{2,3},{3,0},{4,5},{5,6},{6,7},{7,4},{8,9},{9,10},{10,1... | collective-permute-start | bytes 1572872 | tf_op jit(solution)/shard_map/ppermute | solution.py:695
  41.3 14.9 %collective-permute-start.11 = (bf16[2,32,4096]{2,1,0:T(8,128)(2,1)S(1)}, bf16[2,32,4096]{2,1,0:T(8,128)(2,1)S(1)}, u32[]{:S(2)}, u32[]{:S(2)}) collective-permute-start(bf16[2,32,4096]{2,1,0:T(8,128)(2,1)S(1)} %pad_maximum_fusion.2.p0), channel_id=1, source_target_pairs={{0,3},{1,0},{2,1},{3,2},{4,7},{5,4},{6,5},{7,6},{8,11},{9,8},{10,9... | collective-permute-start | bytes 1572872 | tf_op jit(solution)/shard_map/ppermute | solution.py:695
  41.3 22.3 %collective-permute-start.12 = (bf16[2,32,4096]{2,1,0:T(8,128)(2,1)S(1)}, bf16[2,32,4096]{2,1,0:T(8,128)(2,1)S(1)}, u32[]{:S(2)}, u32[]{:S(2)}) collective-permute-start(bf16[2,32,4096]{2,1,0:T(8,128)(2,1)S(1)} %pad_maximum_fusion.2.p0), channel_id=1, source_target_pairs={{0,2},{1,3},{2,0},{3,1},{4,6},{5,7},{6,4},{7,5},{8,10},{9,11},{10,... | collective-permute-start | bytes 1572872 | tf_op jit(solution)/shard_map/ppermute | solution.py:695
  51.9 12.9 %collective-permute-start.8 = (bf16[2,256,512]{2,1,0:T(8,128)(2,1)S(1)}, bf16[2,256,512]{2,1,0:T(8,128)(2,1)S(1)}, u32[]{:S(2)}, u32[]{:S(2)}) collective-permute-start(bf16[2,256,512]{2,1,0:T(8,128)(2,1)S(1)} %get-tuple-element.48.own_kv), channel_id=1, source_target_pairs={{0,64},{64,0},{1,65},{65,1},{2,66},{66,2},{3,67},{67,3},{4,68},{68... | collective-permute-start | bytes 1572872 | tf_op jit(solution)/shard_map/ppermute | solution.py:697
  73.9 74.3 %collective-permute-start.25 = (bf16[4,512,512]{2,1,0:T(8,128)(2,1)}, bf16[4,512,512]{2,1,0:T(8,128)(2,1)}, u32[]{:S(2)}, u32[]{:S(2)}) collective-permute-start(bf16[4,512,512]{2,1,0:T(8,128)(2,1)} %get-tuple-element.62), channel_id=1, source_target_pairs={{0,8},{8,0},{16,24},{24,16},{32,40},{40,32},{48,56},{56,48},{1,9},... | collective-permute-start | bytes 6291464 | tf_op jit(solution)/shard_map/ppermute | solution.py:711
  74.0 16.8 %collective-permute-start.15 = (bf16[128,1024]{1,0:T(8,128)(2,1)S(1)}, bf16[128,1024]{1,0:T(8,128)(2,1)S(1)}, u32[]{:S(2)}, u32[]{:S(2)}) collective-permute-start(bf16[128,1024]{1,0:T(8,128)(2,1)S(1)} %get-tuple-element.85), channel_id=1, source_target_pairs={{0,16},{8,24},{16,32},{24,40},{32,48},{40,56},{48,0},{56,8},{1,17}... | collective-permute-start | bytes 786440 | tf_op jit(solution)/shard_map/ppermute | solution.py:666
  75.6 15.2 %collective-permute-start.16 = (bf16[128,1024]{1,0:T(8,128)(2,1)S(1)}, bf16[128,1024]{1,0:T(8,128)(2,1)S(1)}, u32[]{:S(2)}, u32[]{:S(2)}) collective-permute-start(bf16[128,1024]{1,0:T(8,128)(2,1)S(1)} %get-tuple-element.87), channel_id=1, source_target_pairs={{0,48},{8,56},{16,0},{24,8},{32,16},{40,24},{48,32},{56,40},{1,49}... | collective-permute-start | bytes 786440 | tf_op jit(solution)/shard_map/ppermute | solution.py:666
  77.3 13.5 %collective-permute-start.17 = (bf16[128,1024]{1,0:T(8,128)(2,1)S(1)}, bf16[128,1024]{1,0:T(8,128)(2,1)S(1)}, u32[]{:S(2)}, u32[]{:S(2)}) collective-permute-start(bf16[128,1024]{1,0:T(8,128)(2,1)S(1)} %get-tuple-element.86), channel_id=1, source_target_pairs={{0,32},{8,40},{16,48},{24,56},{32,0},{40,8},{48,16},{56,24},{1,33}... | collective-permute-start | bytes 786440 | tf_op jit(solution)/shard_map/ppermute | solution.py:666
  85.8 38.5 %copy-start.25 = (bf16[4,32,4096]{2,1,0:T(8,128)(2,1)}, bf16[4,32,4096]{2,1,0:T(8,128)(2,1)S(1)}, u32[]{:S(2)}) copy-start(bf16[4,32,4096]{2,1,0:T(8,128)(2,1)S(1)} %get-tuple-element.52.refs_0_.own) | copy-start | bytes 3145732
  85.8 38.4 %copy-start.8 = (bf16[4,512,512]{2,1,0:T(8,128)(2,1)S(1)}, bf16[4,512,512]{2,1,0:T(8,128)(2,1)}, u32[]{:S(2)}) copy-start(bf16[4,512,512]{2,1,0:T(8,128)(2,1)} %copy-done.7) | copy-start | bytes 6291460
  90.1 34.3 %copy-start.13 = (bf16[256,512]{1,0:T(8,128)(2,1)}, bf16[256,512]{1,0:T(8,128)(2,1)S(1)}, u32[]{:S(2)}) copy-start(bf16[256,512]{1,0:T(8,128)(2,1)S(1)} %get-tuple-element.54.pair.refs_0_) | copy-start | bytes 786436
  90.1 9.1 %collective-permute-start.18 = (bf16[256,512]{1,0:T(8,128)(2,1)S(1)}, bf16[256,512]{1,0:T(8,128)(2,1)S(1)}, u32[]{:S(2)}, u32[]{:S(2)}) collective-permute-start(bf16[256,512]{1,0:T(8,128)(2,1)S(1)} %get-tuple-element.54.pair.refs_0_), channel_id=1, source_target_pairs={{0,16},{8,24},{16,32},{24,40},{32,48},{40,56},{48,0},{56,8},{1,17}... | collective-permute-start | bytes 786440 | tf_op jit(solution)/shard_map/ppermute | solution.py:709
  90.9 37.4 %collective-permute-start.20 = (bf16[3,128,1024]{2,1,0:T(8,128)(2,1)S(1)}, bf16[3,128,1024]{2,1,0:T(8,128)(2,1)S(1)}, u32[]{:S(2)}, u32[]{:S(2)}) collective-permute-start(bf16[3,128,1024]{2,1,0:T(8,128)(2,1)S(1)} %pad_maximum_fusion.refs_0_.came), channel_id=1, source_target_pairs={{0,4},{1,5},{2,6},{3,7},{4,0},{5,1},{6,2},{7,3},{8,12},{9,13},{10,... | collective-permute-start | bytes 2359304 | tf_op jit(solution)/shard_map/ppermute | solution.py:668
  91.5 32.7 %collective-permute-start.14 = (bf16[2,256,512]{2,1,0:T(8,128)(2,1)S(1)}, bf16[2,256,512]{2,1,0:T(8,128)(2,1)S(1)}, u32[]{:S(2)}, u32[]{:S(2)}) collective-permute-start(bf16[2,256,512]{2,1,0:T(8,128)(2,1)S(1)} %get-tuple-element.56), channel_id=1, source_target_pairs={{0,64},{64,0},{1,65},{65,1},{2,66},{66,2},{3,67},{67,3},{4,68},{68... | collective-permute-start | bytes 1572872 | tf_op jit(solution)/shard_map/ppermute | solution.py:708
  94.6 49.4 %collective-permute-start.13 = (bf16[4,32,4096]{2,1,0:T(8,128)(2,1)}, bf16[4,32,4096]{2,1,0:T(8,128)(2,1)}, u32[]{:S(2)}, u32[]{:S(2)}) collective-permute-start(bf16[4,32,4096]{2,1,0:T(8,128)(2,1)} %get-tuple-element.53), channel_id=1, source_target_pairs={{0,4},{1,5},{2,6},{3,7},{4,0},{5,1},{6,2},{7,3},{8,12},{9,13},{10,... | collective-permute-start | bytes 3145736 | tf_op jit(solution)/shard_map/ppermute | solution.py:704
  99.2 7.0 %collective-permute-start.19 = (bf16[256,512]{1,0:T(8,128)(2,1)S(1)}, bf16[256,512]{1,0:T(8,128)(2,1)S(1)}, u32[]{:S(2)}, u32[]{:S(2)}) collective-permute-start(bf16[256,512]{1,0:T(8,128)(2,1)S(1)} %get-tuple-element.54.pair.refs_0_), channel_id=1, source_target_pairs={{0,48},{8,56},{16,0},{24,8},{32,16},{40,24},{48,32},{56,40},{1,49}... | collective-permute-start | bytes 786440 | tf_op jit(solution)/shard_map/ppermute | solution.py:709
  106.2 19.4 %collective-permute-start.22 = (bf16[256,512]{1,0:T(8,128)(2,1)S(1)}, bf16[256,512]{1,0:T(8,128)(2,1)S(1)}, u32[]{:S(2)}, u32[]{:S(2)}) collective-permute-start(bf16[256,512]{1,0:T(8,128)(2,1)S(1)} %get-tuple-element.54.pair.refs_0_), channel_id=1, source_target_pairs={{0,32},{8,40},{16,48},{24,56},{32,0},{40,8},{48,16},{56,24},{1,33}... | collective-permute-start | bytes 786440 | tf_op jit(solution)/shard_map/ppermute | solution.py:709
  124.3 20.2 %collective-permute-start.23 = (bf16[2,256,512]{2,1,0:T(8,128)(2,1)S(1)}, bf16[2,256,512]{2,1,0:T(8,128)(2,1)}, u32[]{:S(2)}, u32[]{:S(2)}) collective-permute-start(bf16[2,256,512]{2,1,0:T(8,128)(2,1)S(1)} %sum_keys.1.kv_grad.refs_4_), channel_id=1, source_target_pairs={{0,16},{8,24},{16,32},{24,40},{32,48},{40,56},{48,0},{56,8},{1,17}... | collective-permute-start | bytes 1572872 | tf_op jit(solution)/shard_map/ppermute | solution.py:713
  126.3 21.9 %collective-permute-start.24 = (bf16[2,256,512]{2,1,0:T(8,128)(2,1)S(1)}, bf16[2,256,512]{2,1,0:T(8,128)(2,1)}, u32[]{:S(2)}, u32[]{:S(2)}) collective-permute-start(bf16[2,256,512]{2,1,0:T(8,128)(2,1)S(1)} %sum_keys.1.kv_grad.refs_4_), channel_id=1, source_target_pairs={{0,48},{8,56},{16,0},{24,8},{32,16},{40,24},{48,32},{56,40},{1,49}... | collective-permute-start | bytes 1572872 | tf_op jit(solution)/shard_map/ppermute | solution.py:713
  129.3 26.4 %collective-permute-start.29 = (bf16[2,256,512]{2,1,0:T(8,128)(2,1)S(1)}, bf16[2,256,512]{2,1,0:T(8,128)(2,1)}, u32[]{:S(2)}, u32[]{:S(2)}) collective-permute-start(bf16[2,256,512]{2,1,0:T(8,128)(2,1)S(1)} %sum_keys.1.kv_grad.refs_4_), channel_id=1, source_target_pairs={{0,32},{8,40},{16,48},{24,56},{32,0},{40,8},{48,16},{56,24},{1,33}... | collective-permute-start | bytes 1572872 | tf_op jit(solution)/shard_map/ppermute | solution.py:713
  144.0 21.4 %collective-permute-start.21 = (bf16[4,32,2048]{2,1,0:T(8,128)(2,1)S(1)}, bf16[4,32,2048]{2,1,0:T(8,128)(2,1)S(1)}, u32[]{:S(2)}, u32[]{:S(2)}) collective-permute-start(bf16[4,32,2048]{2,1,0:T(8,128)(2,1)S(1)} %get-tuple-element.60), channel_id=1, source_target_pairs={{0,4},{1,5},{2,6},{3,7},{4,0},{5,1},{6,2},{7,3},{8,12},{9,13},{10,... | collective-permute-start | bytes 1572872 | tf_op jit(solution)/shard_map/ppermute | solution.py:717
  151.1 12.2 %collective-permute-start.26 = (bf16[5,16,2048]{2,1,0:T(8,128)(2,1)S(1)}, bf16[5,16,2048]{2,1,0:T(8,128)(2,1)S(1)}, u32[]{:S(2)}, u32[]{:S(2)}) collective-permute-start(bf16[5,16,2048]{2,1,0:T(8,128)(2,1)S(1)} %get-tuple-element.64), channel_id=1, source_target_pairs={{0,3},{1,0},{2,1},{3,2},{4,7},{5,4},{6,5},{7,6},{8,11},{9,8},{10,9... | collective-permute-start | bytes 983048 | tf_op jit(solution)/shard_map/ppermute | solution.py:719
  154.1 12.4 %collective-permute-start.27 = (bf16[5,16,2048]{2,1,0:T(8,128)(2,1)S(1)}, bf16[5,16,2048]{2,1,0:T(8,128)(2,1)S(1)}, u32[]{:S(2)}, u32[]{:S(2)}) collective-permute-start(bf16[5,16,2048]{2,1,0:T(8,128)(2,1)S(1)} %get-tuple-element.65), channel_id=1, source_target_pairs={{0,1},{1,2},{2,3},{3,0},{4,5},{5,6},{6,7},{7,4},{8,9},{9,10},{10,1... | collective-permute-start | bytes 983048 | tf_op jit(solution)/shard_map/ppermute | solution.py:719
  154.1 12.4 %collective-permute-start.28 = (bf16[5,16,2048]{2,1,0:T(8,128)(2,1)S(1)}, bf16[5,16,2048]{2,1,0:T(8,128)(2,1)S(1)}, u32[]{:S(2)}, u32[]{:S(2)}) collective-permute-start(bf16[5,16,2048]{2,1,0:T(8,128)(2,1)S(1)} %get-tuple-element.66), channel_id=1, source_target_pairs={{0,2},{1,3},{2,0},{3,1},{4,6},{5,7},{6,4},{7,5},{8,10},{9,11},{10,... | collective-permute-start | bytes 983048 | tf_op jit(solution)/shard_map/ppermute | solution.py:719
  160.0 51.9 %collective-permute-start.44 = (bf16[3,512,512]{2,1,0:T(8,128)(2,1)S(1)}, bf16[3,512,512]{2,1,0:T(8,128)(2,1)S(1)}, u32[]{:S(2)}, u32[]{:S(2)}) collective-permute-start(bf16[3,512,512]{2,1,0:T(8,128)(2,1)S(1)} %weight_shares.2.refs_1_.refs_8_), channel_id=1, source_target_pairs={{0,8},{8,0},{16,24},{24,16},{32,40},{40,32},{48,56},{56,48},{1,9},... | collective-permute-start | bytes 4718600 | tf_op jit(solution)/shard_map/ppermute | solution.py:744
  166.7 5.7 %collective-permute-start.30 = (bf16[3,16,2048]{2,1,0:T(8,128)(2,1)S(1)}, bf16[3,16,2048]{2,1,0:T(8,128)(2,1)S(1)}, u32[]{:S(2)}, u32[]{:S(2)}) collective-permute-start(bf16[3,16,2048]{2,1,0:T(8,128)(2,1)S(1)} %get-tuple-element.68), channel_id=1, source_target_pairs={{0,4},{1,5},{2,6},{3,7},{4,0},{5,1},{6,2},{7,3},{8,12},{9,13},{10,... | collective-permute-start | bytes 589832 | tf_op jit(solution)/shard_map/ppermute | solution.py:725
  172.5 1.3 collective-permute-start.39
  173.8 5.5 %collective-permute-start.40 = (f32[1,4096]{1,0:T(1,128)S(1)}, f32[1,4096]{1,0:T(1,128)S(1)}, u32[]{:S(2)}, u32[]{:S(2)}) collective-permute-start(f32[1,4096]{1,0:T(1,128)S(1)} %add.123), channel_id=1, source_target_pairs={{0,16},{8,24},{16,32},{24,40},{32,48},{40,56},{48,0},{56,8},{1,17}... | collective-permute-start | bytes 49160 | tf_op jit(solution)/shard_map/ppermute | solution.py:738
  174.5 6.2 %collective-permute-start.41 = (f32[1,4096]{1,0:T(1,128)S(1)}, f32[1,4096]{1,0:T(1,128)S(1)}, u32[]{:S(2)}, u32[]{:S(2)}) collective-permute-start(f32[1,4096]{1,0:T(1,128)S(1)} %add.123), channel_id=1, source_target_pairs={{0,48},{8,56},{16,0},{24,8},{32,16},{40,24},{48,32},{56,40},{1,49}... | collective-permute-start | bytes 49160 | tf_op jit(solution)/shard_map/ppermute | solution.py:738
  177.3 5.6 %collective-permute-start.42 = (f32[1,4096]{1,0:T(1,128)S(1)}, f32[1,4096]{1,0:T(1,128)S(1)}, u32[]{:S(2)}, u32[]{:S(2)}) collective-permute-start(f32[1,4096]{1,0:T(1,128)S(1)} %add.123), channel_id=1, source_target_pairs={{0,32},{8,40},{16,48},{24,56},{32,0},{40,8},{48,16},{56,24},{1,33}... | collective-permute-start | bytes 49160 | tf_op jit(solution)/shard_map/ppermute | solution.py:738
  178.7 14.8 %collective-permute-start.31 = (bf16[512,512]{1,0:T(8,128)(2,1)S(1)}, bf16[512,512]{1,0:T(8,128)(2,1)S(1)}, u32[]{:S(2)}, u32[]{:S(2)}) collective-permute-start(bf16[512,512]{1,0:T(8,128)(2,1)S(1)} %get-tuple-element.67.refs_2_), channel_id=1, source_target_pairs={{0,48},{8,56},{16,0},{24,8},{32,16},{40,24},{48,32},{56,40},{1,49}... | collective-permute-start | bytes 1572872 | tf_op jit(solution)/shard_map/ppermute | solution.py:721
  179.2 16.1 %collective-permute-start.32 = (bf16[512,512]{1,0:T(8,128)(2,1)S(1)}, bf16[512,512]{1,0:T(8,128)(2,1)S(1)}, u32[]{:S(2)}, u32[]{:S(2)}) collective-permute-start(bf16[512,512]{1,0:T(8,128)(2,1)S(1)} %get-tuple-element.69), channel_id=1, source_target_pairs={{0,16},{8,24},{16,32},{24,40},{32,48},{40,56},{48,0},{56,8},{1,17}... | collective-permute-start | bytes 1572872 | tf_op jit(solution)/shard_map/ppermute | solution.py:721
  180.7 24.5 %collective-permute-start.43 = (bf16[512,512]{1,0:T(8,128)(2,1)S(1)}, bf16[512,512]{1,0:T(8,128)(2,1)S(1)}, u32[]{:S(2)}, u32[]{:S(2)}) collective-permute-start(bf16[512,512]{1,0:T(8,128)(2,1)S(1)} %get-tuple-element.81), channel_id=1, source_target_pairs={{0,32},{8,40},{16,48},{24,56},{32,0},{40,8},{48,16},{56,24},{1,33}... | collective-permute-start | bytes 1572872 | tf_op jit(solution)/shard_map/ppermute | solution.py:721
  195.4 18.8 %collective-permute-start.36 = (bf16[32,2048]{1,0:T(8,128)(2,1)S(1)}, bf16[32,2048]{1,0:T(8,128)(2,1)S(1)}, u32[]{:S(2)}, u32[]{:S(2)}) collective-permute-start(bf16[32,2048]{1,0:T(8,128)(2,1)S(1)} %get-tuple-element.70.refs_0_), channel_id=1, source_target_pairs={{0,3},{1,0},{2,1},{3,2},{4,7},{5,4},{6,5},{7,6},{8,11},{9,8},{10,9... | collective-permute-start | bytes 393224 | tf_op jit(solution)/shard_map/ppermute | solution.py:731
  197.7 19.2 %collective-permute-start.37 = (bf16[32,2048]{1,0:T(8,128)(2,1)S(1)}, bf16[32,2048]{1,0:T(8,128)(2,1)S(1)}, u32[]{:S(2)}, u32[]{:S(2)}) collective-permute-start(bf16[32,2048]{1,0:T(8,128)(2,1)S(1)} %get-tuple-element.78), channel_id=1, source_target_pairs={{0,1},{1,2},{2,3},{3,0},{4,5},{5,6},{6,7},{7,4},{8,9},{9,10},{10,1... | collective-permute-start | bytes 393224 | tf_op jit(solution)/shard_map/ppermute | solution.py:731
  197.7 19.2 %collective-permute-start.38 = (bf16[32,2048]{1,0:T(8,128)(2,1)S(1)}, bf16[32,2048]{1,0:T(8,128)(2,1)S(1)}, u32[]{:S(2)}, u32[]{:S(2)}) collective-permute-start(bf16[32,2048]{1,0:T(8,128)(2,1)S(1)} %get-tuple-element.79), channel_id=1, source_target_pairs={{0,2},{1,3},{2,0},{3,1},{4,6},{5,7},{6,4},{7,5},{8,10},{9,11},{10,... | collective-permute-start | bytes 393224 | tf_op jit(solution)/shard_map/ppermute | solution.py:731
  205.2 12.8 %collective-permute-start.33 = (bf16[32,4096]{1,0:T(8,128)(2,1)S(1)}, bf16[32,4096]{1,0:T(8,128)(2,1)S(1)}, u32[]{:S(2)}, u32[]{:S(2)}) collective-permute-start(bf16[32,4096]{1,0:T(8,128)(2,1)S(1)} %get-tuple-element.72), channel_id=1, source_target_pairs={{0,3},{1,0},{2,1},{3,2},{4,7},{5,4},{6,5},{7,6},{8,11},{9,8},{10,9... | collective-permute-start | bytes 786440 | tf_op jit(solution)/shard_map/ppermute | solution.py:733
  211.9 13.0 %collective-permute-start.34 = (bf16[32,4096]{1,0:T(8,128)(2,1)S(1)}, bf16[32,4096]{1,0:T(8,128)(2,1)S(1)}, u32[]{:S(2)}, u32[]{:S(2)}) collective-permute-start(bf16[32,4096]{1,0:T(8,128)(2,1)S(1)} %get-tuple-element.73), channel_id=1, source_target_pairs={{0,1},{1,2},{2,3},{3,0},{4,5},{5,6},{6,7},{7,4},{8,9},{9,10},{10,1... | collective-permute-start | bytes 786440 | tf_op jit(solution)/shard_map/ppermute | solution.py:733
  214.2 10.7 %collective-permute-start.35 = (bf16[32,4096]{1,0:T(8,128)(2,1)S(1)}, bf16[32,4096]{1,0:T(8,128)(2,1)S(1)}, u32[]{:S(2)}, u32[]{:S(2)}) collective-permute-start(bf16[32,4096]{1,0:T(8,128)(2,1)S(1)} %get-tuple-element.74), channel_id=1, source_target_pairs={{0,2},{1,3},{2,0},{3,1},{4,6},{5,7},{6,4},{7,5},{8,10},{9,11},{10,... | collective-permute-start | bytes 786440 | tf_op jit(solution)/shard_map/ppermute | solution.py:733
  (35 other events, 281.5 us)

commit v6 on v5

--- a/solution.py
+++ b/solution.py
@@ -59,6 +59,7 @@
 SMEM = pl.BlockSpec(memory_space=pltpu.SMEM)
 VMEM = pl.BlockSpec(memory_space=pltpu.VMEM)
 ANY = pl.BlockSpec(memory_space=pl.ANY)
+HBM = pl.BlockSpec(memory_space=pltpu.HBM)
 
 
 def dot(left, right):
@@ -73,30 +74,32 @@
     return lax.dot_general(left, right, (((0,), (0,)), ((), ())), preferred_element_type=f32)
 
 
-def hold_kernel(*refs):
-    count = (len(refs) - 1) // 2
-    sems = refs[-1]
+def load(sources, targets, sems):
     copies = [
-        pltpu.make_async_copy(refs[i], refs[count + i], sems.at[i]) for i in range(count)
+        pltpu.make_async_copy(source, target, sems.at[i])
+        for i, (source, target) in enumerate(zip(sources, targets))
     ]
     for copy in copies:
         copy.start()
-    for copy in copies:
+    return copies
+
+
+KCUT = 1024
+KCUTS = WIDTH // KCUT
+
+
+def dot_loaded(full, buffer, copies):
+    total = None
+    for i, copy in enumerate(copies):
         copy.wait()
-
-
-def hold(*arrays):
-    count = len(arrays)
-    return call(
-        hold_kernel,
-        [sds(v.shape, v.dtype) for v in arrays],
-        vmem=1,
-        nbytes=2 * sum(v.size * 2 for v in arrays),
-        in_specs=[ANY] * count,
-        out_specs=[ANY] * count,
-        scratch_shapes=[pltpu.SemaphoreType.DMA((count,))],
-        name="hold",
-    )(*arrays)
+        cut = slice(i * KCUT, (i + 1) * KCUT)
+        part = dot(full[:, cut], buffer[cut])
+        total = part if total is None else total + part
+    return total
+
+
+def k_cuts(ref):
+    return [ref.at[pl.ds(i * KCUT, KCUT)] for i in range(KCUTS)]
 
 
 def norm_kernel(valid, x, gain, cot, n_left, n_right, grad, inv):
@@ -142,6 +145,28 @@
 
 
 PIECE_SHAPES = [(4, ROWS, HALF)] * 2 + [(2, ROWS, HALF)] * 4
+
+
+def sum_z_kernel(own, c1, c2, c3, *refs):
+    kept, sent = refs[-2:]
+    total = own[...].astype(f32)
+    for came in (c1, c2, c3):
+        total = total + came[...].astype(f32)
+    kept[...] = total[0]
+    sent[...] = total[1].astype(bf16)
+
+
+def sum_z(own, came, after=()):
+    shape = own.shape[1:]
+    return call(
+        sum_z_kernel,
+        [sds(shape, f32), sds(shape, bf16)],
+        vmem=6,
+        nbytes=11 * shape[0] * shape[1] * 2,
+        in_specs=[VMEM] * 4 + [ANY] * len(after),
+        out_specs=[VMEM] * 2,
+        name="sum_z",
+    )(own, *came, *after)
 
 
 def sum_left_kernel(own, c1, c2, c3, *refs):
@@ -214,20 +239,41 @@
     )(own, came, *after)
 
 
-def sum_keys_kernel(own, came, *refs):
-    refs[-1][...] = (own[...] + came[...].astype(f32)).astype(bf16)
-
-
-def sum_keys(own, came, after=()):
+def sum_rest_kernel(kept, c1, c2, c3, *refs):
+    total = kept[...]
+    for came in (c1, c2, c3):
+        total = total + came[...].astype(f32)
+    refs[-1][...] = total
+
+
+def sum_rest(kept, came, after=()):
+    return call(
+        sum_rest_kernel,
+        sds(kept.shape, f32),
+        vmem=6,
+        nbytes=14 * kept.size,
+        in_specs=[VMEM] * 4 + [ANY] * len(after),
+        out_specs=VMEM,
+        name="sum_rest",
+    )(kept, *came, *after)
+
+
+def sum_keys_kernel(q_grad, own, came, *refs):
+    out = refs[-1]
+    out[0] = q_grad[...]
+    out[1:] = (own[...] + came[...].astype(f32)).astype(bf16)
+
+
+def sum_keys(q_grad, own, came, after=()):
     return call(
         sum_keys_kernel,
-        sds(came.shape, bf16),
-        vmem=6,
-        nbytes=8 * came.size,
-        in_specs=[VMEM] * 2 + [ANY] * len(after),
+        sds((3, SLOTS, COLS), bf16),
+        vmem=8,
+        nbytes=10 * came.size,
+        in_specs=[VMEM] * 3 + [ANY] * len(after),
         out_specs=VMEM,
         name="sum_keys",
-    )(own, came, *after)
+    )(q_grad, own, came, *after)
 
 
 def rows_kernel(x, grad, gain, inv, l_kept, l_came, r_kept, r1, r2, r3, *refs):
@@ -262,85 +308,79 @@
     )(x, grad, gain, inv, *left, *right, *after)
 
 
-def first_step():
-    return jnp.logical_and(pl.program_id(0) == 0, pl.program_id(1) == 0)
-
-
 def key_value_kernel(*refs):
-    pieces, weight, full, out = refs[:6], refs[6], refs[7], refs[8]
-
-    @pl.when(first_step())
-    def _():
-        place_pieces(pieces, full)
-
-    out[0] = dot(full[...], weight[0]).astype(bf16)
-
-
-def key_value(pieces, weights):
-    block = 256
+    pieces, weight = refs[:6], refs[6]
+    full, out, buffer, sems = refs[-4:]
+    copies = [
+        load(k_cuts(weight.at[part + 1]), k_cuts(buffer.at[part]), sems.at[part])
+        for part in range(2)
+    ]
+    place_pieces(pieces, full)
+    for part in range(2):
+        out[part] = dot_loaded(full, buffer.at[part], copies[part]).astype(bf16)
+
+
+def key_value(pieces, weights, after):
     return call(
         key_value_kernel,
         [sds((SLOTS, WIDTH), bf16), sds((2, SLOTS, COLS), bf16)],
-        vmem=18,
+        vmem=20,
         flops=4 * SLOTS * WIDTH * COLS,
         nbytes=2 * WIDTH * COLS * 2 + 2 * SLOTS * WIDTH * 2,
-        grid=(2, COLS // block),
-        in_specs=[whole(s) for s in PIECE_SHAPES]
-        + [pl.BlockSpec((1, WIDTH, block), lambda p, j: (p + 1, 0, j))],
-        out_specs=[
-            whole((SLOTS, WIDTH)),
-            pl.BlockSpec((1, SLOTS, block), lambda p, j: (p, 0, j)),
+        in_specs=[VMEM] * 6 + [HBM] + [ANY] * len(after),
+        out_specs=[VMEM] * 2,
+        scratch_shapes=[
+            pltpu.VMEM((2, WIDTH, COLS), bf16),
+            pltpu.SemaphoreType.DMA((2, KCUTS)),
         ],
         name="key_value",
-    )(*pieces, weights)
-
-
-def grad_mixed_kernel(p0, p1, p2, p3, weight, full, out):
-    @pl.when(pl.program_id(0) == 0)
-    def _():
-        for slot, pair in enumerate((p0, p1, p2, p3)):
-            full[pl.ds(slot * ROWS, ROWS)] = pair[0]
-            full[pl.ds((4 + slot) * ROWS, ROWS)] = pair[1]
-
-    out[...] = dot(full[...], weight[0]).astype(bf16)
-
-
-def grad_mixed_of(pairs, weights):
-    block = 512
+    )(*pieces, weights, *after)
+
+
+def query_kernel(full, weight, *refs):
+    out, buffer, sems = refs[-3:]
+    copies = load(k_cuts(weight.at[0]), k_cuts(buffer), sems)
+    out[...] = dot_loaded(full, buffer, copies).astype(bf16)
+
+
+DOT_SCRATCH = [pltpu.VMEM((WIDTH, COLS), bf16), pltpu.SemaphoreType.DMA((KCUTS,))]
+
+
+def query_of(full, weights, after):
+    return call(
+        query_kernel,
+        sds((SLOTS, COLS), bf16),
+        vmem=12,
+        flops=2 * SLOTS * WIDTH * COLS,
+        nbytes=WIDTH * COLS * 2 + SLOTS * WIDTH * 2,
+        in_specs=[VMEM, HBM] + [ANY] * len(after),
+        out_specs=VMEM,
+        scratch_shapes=DOT_SCRATCH,
+        name="query",
+    )(full, weights, *after)
+
+
+def grad_mixed_kernel(p0, p1, p2, p3, weight, *refs):
+    full, out, buffer, sems = refs[-4:]
+    copies = load(k_cuts(weight.at[0]), k_cuts(buffer), sems)
+    for slot, pair in enumerate((p0, p1, p2, p3)):
+        full[pl.ds(slot * ROWS, ROWS)] = pair[0]
+        full[pl.ds((4 + slot) * ROWS, ROWS)] = pair[1]
+    out[...] = dot_loaded(full, buffer, copies).astype(bf16)
+
+
+def grad_mixed_of(pairs, weights, after):
     return call(
         grad_mixed_kernel,
         [sds((SLOTS, WIDTH), bf16), sds((SLOTS, COLS), bf16)],
-        vmem=18,
+        vmem=16,
         flops=2 * SLOTS * WIDTH * COLS,
         nbytes=WIDTH * COLS * 2 + 2 * SLOTS * WIDTH * 2,
-        grid=(COLS // block,),
-        in_specs=[whole((2, ROWS, WIDTH))] * 4
-        + [pl.BlockSpec((1, WIDTH, block), lambda j: (0, 0, j))],
-        out_specs=[whole((SLOTS, WIDTH)), pl.BlockSpec((SLOTS, block), lambda j: (0, j))],
+        in_specs=[VMEM] * 4 + [HBM] + [ANY] * len(after),
+        out_specs=[VMEM] * 2,
+        scratch_shapes=DOT_SCRATCH,
         name="grad_mixed",
-    )(*pairs, weights)
-
-
-def one_dot_kernel(full, weight, out):
-    out[...] = dot(full[...], weight[0]).astype(bf16)
-
-
-def one_dot(full, weights, part):
-    block = 512
-    return call(
-        one_dot_kernel,
-        sds((SLOTS, COLS), bf16),
-        vmem=18,
-        flops=2 * SLOTS * WIDTH * COLS,
-        nbytes=WIDTH * COLS * 2 + SLOTS * WIDTH * 2,
-        grid=(COLS // block,),
-        in_specs=[
-            whole((SLOTS, WIDTH)),
-            pl.BlockSpec((1, WIDTH, block), lambda j: (part, 0, j)),
-        ],
-        out_specs=pl.BlockSpec((SLOTS, block), lambda j: (0, j)),
-        name="one_dot",
-    )(full, weights)
+    )(*pairs, weights, *after)
 
 
 def gain_rows_of(left, right):
@@ -358,93 +398,108 @@
     return rows[0:1] + rows[1:2], rows[2:3] + rows[3:4]
 
 
-def back_total(pair, kv_grad, weight, normed):
-    total = dot_rows(pair[...], weight[0][0])
-    for part in range(2):
-        total = total + dot_rows(kv_grad[part], weight[1 + part][0])
-    rounded = total.astype(bf16)
-    gain = jnp.sum(rounded.astype(f32) * normed[...].astype(f32), axis=0, keepdims=True)
-    return rounded, gain
-
-
-def back_right_kernel(pair, kv_grad, w0, w1, w2, normed, *refs):
-    own, sent, gain = refs[-3:]
-    rounded, gain[...] = back_total(pair, kv_grad, (w0, w1, w2), normed)
-    for xbit, out in enumerate((own, sent)):
-        for slot in range(4):
-            start = (xbit * 4 + slot) * ROWS
-            out[slot] = rounded[start:start + ROWS]
-
-
-def back_left_kernel(pair, kv_grad, w0, w1, w2, normed, gain_right, *refs):
-    rounded, gain = back_total(pair, kv_grad, (w0, w1, w2), normed)
-    gains = gain_rows_of(gain, gain_right[...])
-    for slot, out in enumerate(refs[-4:]):
-        for xbit in range(2):
-            start = (xbit * 4 + slot) * ROWS
-            out[2 * xbit] = rounded[start:start + 16]
-            out[2 * xbit + 1] = rounded[start + 16:start + ROWS]
-        out[4] = gains
-
-
-def back_dot(kernel, first, lefts, weights, normed, extra, out_shape, after, name):
-    block = 512
-    return call(
-        kernel,
+FCUT = 512
+FCUTS = HALF // FCUT
+
+
+def back_products(grads, weight, first, normed, buffer, sems):
+    copies = [
+        load(
+            [weight.at[part, pl.ds(first + cut * FCUT, FCUT)] for part in range(3)],
+            [buffer.at[part, pl.ds(cut * FCUT, FCUT)] for part in range(3)],
+            sems.at[cut],
+        )
+        for cut in range(FCUTS)
+    ]
+    for cut in range(FCUTS):
+        for copy in copies[cut]:
+            copy.wait()
+        rows = slice(cut * FCUT, (cut + 1) * FCUT)
+        total = dot_rows(grads[0], buffer[0, rows])
+        for part in range(1, 3):
+            total = total + dot_rows(grads[part], buffer[part, rows])
+        rounded = total.astype(bf16)
+        terms = normed[:, first + cut * FCUT:first + (cut + 1) * FCUT].astype(f32)
+        gain = jnp.sum(rounded.astype(f32) * terms, axis=0, keepdims=True)
+        yield rows, rounded, gain
+
+
+def back_right_kernel(waits, grads, weight, normed, *refs):
+    own, sent, gain, buffer, sems = refs[waits:]
+    for cols, rounded, terms in back_products(
+        grads, weight, HALF, normed, buffer, sems
+    ):
+        gain[:, cols] = terms
+        for xbit, out in enumerate((own, sent)):
+            for slot in range(4):
+                start = (xbit * 4 + slot) * ROWS
+                out[slot, :, cols] = rounded[start:start + ROWS]
+
+
+def back_left_kernel(waits, grads, weight, normed, gain_right, *refs):
+    outs, buffer, sems = refs[waits:waits + 4], refs[-2], refs[-1]
+    for cols, rounded, terms in back_products(
+        grads, weight, 0, normed, buffer, sems
+    ):
+        gains = gain_rows_of(terms, gain_right[:, cols])
+        for slot, out in enumerate(outs):
+            for xbit in range(2):
+                start = (xbit * 4 + slot) * ROWS
+                out[2 * xbit, :, cols] = rounded[start:start + 16]
+                out[2 * xbit + 1, :, cols] = rounded[start + 16:start + ROWS]
+            out[4, :, cols] = gains
+
+
+def back_dot(kernel, grads, weights, normed, extra, out_shape, after, name):
+    return call(
+        functools.partial(kernel, len(after)),
         out_shape,
-        vmem=12,
+        vmem=20,
         flops=2 * 3 * SLOTS * HALF * COLS,
         nbytes=3 * HALF * COLS * 2 + 2 * SLOTS * HALF * 2,
-        grid=(HALF // block,),
-        in_specs=[whole((SLOTS, COLS)), whole((2, SLOTS, COLS))]
-        + [
-            pl.BlockSpec((1, block, COLS), lambda j, part=part: (part, j + first, 0))
-            for part in range(3)
-        ]
-        + [pl.BlockSpec((SLOTS, block), lambda j: (0, j + first))]
-        + [pl.BlockSpec((1, block), lambda j: (0, j))] * len(extra)
-        + [ANY] * len(after),
-        out_specs=[
-            pl.BlockSpec(v.shape[:-1] + (block,), lambda j, n=len(v.shape): (0,) * (n - 1) + (j,))
-            for v in out_shape
+        in_specs=[VMEM, HBM, VMEM] + [VMEM] * len(extra) + [ANY] * len(after),
+        out_specs=[VMEM] * len(out_shape),
+        scratch_shapes=[
+            pltpu.VMEM((3, HALF, COLS), bf16),
+            pltpu.SemaphoreType.DMA((FCUTS, 3)),
         ],
         name=name,
-    )(*lefts, weights, weights, weights, normed, *extra, *after)
-
-
-def back_right(lefts, weights, normed, after=()):
+    )(grads, weights, normed, *extra, *after)
+
+
+def back_right(grads, weights, normed, after=()):
     out = [sds((4, ROWS, HALF), bf16)] * 2 + [sds((1, HALF), f32)]
-    return back_dot(
-        back_right_kernel, HALF // 512, lefts, weights, normed, [], out, after, "back_right"
-    )
-
-
-def back_left(lefts, weights, normed, gain_right, after=()):
+    return back_dot(back_right_kernel, grads, weights, normed, [], out, after, "back_right")
+
+
+def back_left(grads, weights, normed, gain_right, after=()):
     out = [sds((5, 16, HALF), bf16)] * 4
-    return back_dot(
-        back_left_kernel, 0, lefts, weights, normed, [gain_right], out, after, "back_left"
-    )
-
-
-def proj_kernel(left, weight, own, sent):
-    rounded = dot_rows(left[...], weight[0]).astype(bf16)
-    for xbit, out in enumerate((own, sent)):
+    return back_dot(back_left_kernel, grads, weights, normed, [gain_right], out, after, "back_left")
+
+
+def proj_kernel(left, weight, *refs):
+    outs, buffer, sems = refs[:4], refs[4], refs[5]
+    copies = load(k_cuts(weight.at[0]), k_cuts(buffer), sems)
+    for cut, copy in enumerate(copies):
+        copy.wait()
+        cols = slice(cut * KCUT, (cut + 1) * KCUT)
+        rounded = dot_rows(left[...], buffer[cols]).astype(bf16)
         for slot in range(4):
-            start = (xbit * 4 + slot) * ROWS
-            out[slot] = rounded[start:start + ROWS]
+            for xbit in range(2):
+                start = (xbit * 4 + slot) * ROWS
+                outs[slot][xbit, :, cols] = rounded[start:start + ROWS]
 
 
 def proj_parts(mixed, weights):
-    block = 512
     return call(
         proj_kernel,
-        [sds((4, ROWS, WIDTH), bf16)] * 2,
-        vmem=6,
+        [sds((2, ROWS, WIDTH), bf16)] * 4,
+        vmem=14,
         flops=2 * SLOTS * WIDTH * COLS,
         nbytes=WIDTH * COLS * 2 + SLOTS * WIDTH * 2,
-        grid=(WIDTH // block,),
-        in_specs=[whole((SLOTS, COLS)), pl.BlockSpec((1, block, COLS), lambda j: (0, j, 0))],
-        out_specs=[pl.BlockSpec((4, ROWS, block), lambda j: (0, 0, j))] * 2,
+        in_specs=[VMEM, HBM],
+        out_specs=[VMEM] * 4,
+        scratch_shapes=DOT_SCRATCH,
         name="proj_parts",
     )(mixed, weights)
 
@@ -564,108 +619,66 @@
     )(meta, query, own_kv, other_kv, mixed, grad, *after)
 
 
-def out_kernel(order, grad, mixed, own, sent):
-    share = dot_tokens(grad[...], mixed[...]).astype(bf16)
-
-    @pl.when(pl.program_id(0) < 4)
-    def _():
-        sent[0] = share
-
-    @pl.when(pl.program_id(0) >= 4)
-    def _():
-        own[0] = share
+def out_kernel(order, grad, mixed, *refs):
+    own, sent = refs[-2:]
+    for i in range(8):
+        start = pl.multiple_of(order[i] * COLS, COLS)
+        share = dot_tokens(grad[:, pl.ds(start, COLS)], mixed[...]).astype(bf16)
+        if i < 4:
+            sent[i] = share
+        else:
+            own[i - 4] = share
 
 
 def out_weight_parts(order, grad_full, mixed):
     return call(
         out_kernel,
         [sds((4, COLS, COLS), bf16)] * 2,
-        vmem=6,
+        vmem=12,
         flops=2 * SLOTS * WIDTH * COLS,
         nbytes=SLOTS * WIDTH * 2 + WIDTH * COLS * 2,
-        grid_spec=pltpu.PrefetchScalarGridSpec(
-            num_scalar_prefetch=1,
-            grid=(8,),
-            in_specs=[
-                pl.BlockSpec((SLOTS, COLS), lambda i, order: (0, order[i])),
-                pl.BlockSpec((SLOTS, COLS), lambda i, order: (0, 0)),
-            ],
-            out_specs=[
-                pl.BlockSpec((1, COLS, COLS), lambda i, order: (jnp.maximum(i - 4, 0), 0, 0)),
-                pl.BlockSpec((1, COLS, COLS), lambda i, order: (jnp.minimum(i, 3), 0, 0)),
-            ],
-        ),
+        in_specs=[SMEM, VMEM, VMEM],
+        out_specs=[VMEM] * 2,
         name="out_weight_parts",
     )(order, grad_full, mixed)
 
 
-def share_kernel(columns, own, came, other, *refs):
-    q_grads, kv_grads = refs[:4], refs[4:8]
+def share_kernel(which, columns, full, c1, c2, c3, g0, g1, g2, g3, g4, *refs):
     out, lefts = refs[-2:]
-    half = SLOTS // 2
-    part = pl.program_id(0)
-
-    @pl.when(part == 0)
-    def _():
-        lefts[0] = own[...]
-        for k in range(3):
-            lefts[k + 1, :half] = came[k]
-            lefts[k + 1, half:] = other[k]
-
-    def share(grads):
-        total = dot_tokens(lefts[0], grads[0])
-        for k in range(1, 4):
-            total = total + dot_tokens(lefts[k], grads[k])
-        out[0] = total.astype(out.dtype)
-
-    @pl.when(part == 0)
-    def _():
-        share([grad[...] for grad in q_grads])
-
-    @pl.when(part > 0)
-    def _():
-        share([grad[0] for grad in kv_grads])
-
-
-def weight_shares(columns, which, full, came, other, q_grads, kv_grads, dtype, after=()):
-    half = SLOTS // 2
-    return call(
-        share_kernel,
+    start = pl.multiple_of(columns[which] * COLS, COLS)
+    lefts[0] = full[:, pl.ds(start, COLS)].T
+    start = pl.multiple_of(columns[2 + which] * COLS, COLS)
+    for k, came in enumerate((c1, c2, c3), 1):
+        lefts[k] = came[:, pl.ds(start, COLS)].T
+    for part in range(3):
+        total = dot(lefts[0], g0[part])
+        for k, grad in enumerate((g1, g2), 1):
+            total = total + dot(lefts[k], grad[part])
+        total = total + dot(lefts[3, :, :SLOTS // 2], g3[part])
+        total = total + dot(lefts[3, :, SLOTS // 2:], g4[part])
+        out[part] = total.astype(out.dtype)
+
+
+def weight_shares(columns, which, full, came, grads, dtype, after=()):
+    return call(
+        functools.partial(share_kernel, which),
         sds((3, COLS, COLS), dtype),
-        vmem=16,
+        vmem=20,
         flops=3 * 4 * 2 * SLOTS * COLS * COLS,
         nbytes=16 * SLOTS * COLS * 2 + 3 * COLS * COLS * 4,
-        grid_spec=pltpu.PrefetchScalarGridSpec(
-            num_scalar_prefetch=1,
-            grid=(3,),
-            in_specs=[
-                pl.BlockSpec((SLOTS, COLS), lambda p, columns: (0, columns[which])),
-                pl.BlockSpec((3, half, COLS), lambda p, columns: (0, 0, columns[2 + which])),
-                pl.BlockSpec((3, half, COLS), lambda p, columns: (0, 0, columns[2 + which])),
-            ]
-            + [whole((SLOTS, COLS))] * 4
-            + [
-                pl.BlockSpec(
-                    (1, SLOTS, COLS), lambda p, columns: (jnp.maximum(p - 1, 0), 0, 0)
-                )
-            ]
-            * 4
-            + [ANY] * len(after),
-            out_specs=pl.BlockSpec((1, COLS, COLS), lambda p, columns: (p, 0, 0)),
-            scratch_shapes=[pltpu.VMEM((4, SLOTS, COLS), bf16)],
-        ),
+        in_specs=[SMEM] + [VMEM] * 9 + [ANY] * len(after),
+        out_specs=VMEM,
+        scratch_shapes=[pltpu.VMEM((4, COLS, SLOTS), bf16)],
         name="weight_shares",
-    )(columns, full, came, other, *q_grads, *kv_grads, *after)
+    )(columns, full, *came, *grads, *after)
 
 
 def chunks_over_y(full, y_index):
     came = []
     for k in STEPS[1:]:
-        start = (y_index + k) % 4 * 1024
-        sent = lax.dynamic_slice(full, (0, start), (SLOTS // 2, 1024))
+        sent = lax.dynamic_slice_in_dim(full, (y_index + k) % 4 * 1024, 1024, 1)
         came.append(lax.ppermute(sent, "seq", y_shift(k)))
-    came = jnp.stack(came)
-    return came, lax.ppermute(came, "tp", X_SWAP)
+    return came
 
 
 def per_device(tokens, text_gaps, image_runs, gains, w_qkv, w_out, cotangent):
@@ -688,67 +701,62 @@
     ).astype(jnp.int32)
 
     n_left, n_right, grad_rows, inv = norm_rows(valid.reshape(1), x_rows, gains, cotangent[0, 0])
-    w_parts, w_out = hold(w_parts, w_out)
     pieces = gather_blocks(n_left, n_right)
     grad_other = lax.ppermute(grad_rows, "tp", X_SWAP)
     grad_pair = jnp.stack([grad_rows, grad_other])
     grad_pairs = [grad_pair] + [lax.ppermute(grad_pair, "tp", z_shift(k)) for k in STEPS[1:]]
-    normed_full, own_kv = key_value(pieces, w_parts)
+    normed_full, own_kv = key_value(pieces, w_parts, [grad_pair])
     other_kv = lax.ppermute(own_kv, "grp", GRP_SWAP)
-    query = one_dot(normed_full, w_parts, 0)
-    grad_full, grad_mixed = grad_mixed_of(grad_pairs, w_out)
-    chunk_came, chunk_other = chunks_over_y(normed_full, y_index)
-
-    mixed = attend_forward(meta, query, own_kv, other_kv, [grad_mixed])
+    query = query_of(normed_full, w_parts, grad_pairs[1:3])
+    chunks = chunks_over_y(normed_full, y_index)
+
+    mixed = attend_forward(meta, query, own_kv, other_kv, [])
     proj = proj_parts(mixed, w_out)
-    proj_x = lax.ppermute(proj[1], "tp", X_SWAP)
+    proj_came = [lax.ppermute(proj[i], "tp", z_shift(-STEPS[i])) for i in range(1, 4)]
+    grad_full, grad_mixed = grad_mixed_of(grad_pairs, w_out, [proj[0]] + chunks[:2])
     q_grad, own_part, other_part = attend_backward(
-        meta, query, own_kv, other_kv, mixed, grad_mixed, [proj[0]]
+        meta, query, own_kv, other_kv, mixed, grad_mixed, []
     )
     back = lax.ppermute(other_part, "grp", GRP_SWAP)
-    q_grads = [q_grad] + [lax.ppermute(q_grad, "seq", y_shift(k)) for k in STEPS[1:]]
     out_own, out_sent = out_weight_parts(out_order, grad_full, mixed)
     out_came = lax.ppermute(out_sent, "seq", CORE_SWAP)
-    kv_grad = sum_keys(own_part, back, [chunk_came, out_own] + q_grads[1:3])
-    kv_grads = [kv_grad] + [lax.ppermute(kv_grad, "seq", y_shift(k)) for k in STEPS[1:]]
-
-    lefts = [q_grad, kv_grad]
-    right = back_right(lefts, w_parts, normed_full, [chunk_other])
+    out_kept, *out_sends = sum_x(out_own, out_came)
+    out_terms = [lax.ppermute(v, "seq", y_shift(-k)) for v, k in zip(out_sends, STEPS[1:])]
+    own_grads = sum_keys(q_grad, own_part, back, [out_own] + proj_came[:2])
+    half = SLOTS // 2
+    back_grads = lax.ppermute(own_grads, "seq", y_shift(1))
+    next_grads = lax.ppermute(own_grads, "seq", y_shift(3))
+    far_grads = [
+        lax.ppermute(back_grads[:, :half], "seq", y_shift(1)),
+        lax.ppermute(next_grads[:, half:], "seq", y_shift(3)),
+    ]
+    grads = [own_grads, back_grads, next_grads] + far_grads
+
+    right = back_right(own_grads, w_parts, normed_full, chunks[2:])
     right_x = lax.ppermute(right[1], "tp", X_SWAP)
-    left = back_left(lefts, w_parts, normed_full, right[2], q_grads[3:] + kv_grads[1:3] + [proj_x, out_came])
+    left = back_left(own_grads, w_parts, normed_full, right[2], [out_sends[0]])
     left_came = [lax.ppermute(left[i], "tp", z_shift(-STEPS[i])) for i in range(1, 4)]
-    out_kept, *out_sends = sum_x(out_own, out_came, left_came[:1])
-    out_terms = [lax.ppermute(v, "seq", y_shift(-k)) for v, k in zip(out_sends, STEPS[1:])]
-    left_kept, left_sent, gain_kept = sum_left(
-        left[0], left_came, [kv_grads[3], right_x, out_sends[0]]
-    )
+    left_kept, left_sent, gain_kept = sum_left(left[0], left_came, [right_x])
     left_x = lax.ppermute(left_sent, "tp", X_SWAP)
-    shares = (normed_full, chunk_came, chunk_other, q_grads, kv_grads)
-    qkv_sent = weight_shares(columns, 0, *shares, bf16)
-    right_kept, *right_sends = sum_x(
-        right[0], right_x, [left_x, qkv_sent] + out_terms[:2]
-    )
-    right_came = [lax.ppermute(v, "tp", z_shift(-k)) for v, k in zip(right_sends, STEPS[1:])]
-    proj_kept, *proj_sends = sum_x(proj[0], proj_x, [right_sends[0]])
-    proj_came = [lax.ppermute(v, "tp", z_shift(-k)) for v, k in zip(proj_sends, STEPS[1:])]
     gain_sum = sum_gain(gain_kept, left_x, gains)
     gain_sum = gain_sum + lax.ppermute(gain_sum, "seq", CORE_SWAP)
     gain_grad = gain_sum
     for k in STEPS[1:]:
         gain_grad = gain_grad + lax.ppermute(gain_sum, "seq", y_shift(k))
+    shares = (normed_full, chunks, grads)
+    qkv_sent = weight_shares(columns, 0, *shares, bf16)
+    right_kept, *right_sends = sum_x(right[0], right_x, [left_x, qkv_sent])
+    proj_kept, proj_sent = sum_z(proj[0], proj_came, [left_sent])
+    right_came = [lax.ppermute(v, "tp", z_shift(-k)) for v, k in zip(right_sends, STEPS[1:])]
     tokens_grad = token_rows(
         x_rows, grad_rows, gains, inv, (left_kept, left_x), (right_kept, *right_came)
     )
 
-    qkv_mine = weight_shares(columns, 1, *shares, f32, [qkv_sent] + out_terms[2:])
+    qkv_mine = weight_shares(columns, 1, *shares, f32, [qkv_sent, right_came[0]] + out_terms[:2])
     qkv_share = qkv_mine + lax.ppermute(qkv_sent, "seq", CORE_SWAP).astype(f32)
-    proj_rows = proj_kept
-    for came in proj_came:
-        proj_rows = proj_rows + came.astype(f32)
+    proj_rows = proj_kept + lax.ppermute(proj_sent, "tp", X_SWAP).astype(f32)
     layer_out = ((x_rows.astype(f32) + proj_rows) * valid).astype(bf16)
-    out_share = out_kept
-    for came in out_terms:
-        out_share = out_share + came.astype(f32)
+    out_share = sum_rest(out_kept, out_terms, right_came[:2])
     return (
         layer_out[None, None],
         tokens_grad[None, None],

time: 226 us -> 202 us (0.89)
  waiting for transfers between devices: 87.5 us -> 69.3 us
  local copies, waits for them, and re-layouts: 32.5 us -> 27.8 us
  Pallas kernels: 43 us -> 39.1 us
  starting transfers between devices: 56.3 us -> 59.8 us
    ppermute x1, waiting for transfers between devices: 17.4 us -> 5.86 us  [per_device(): back = lax.ppermute(other_part, 'grp', GRP_SWAP)]
    ppermute x3, waiting for transfers between devices: 4.37 us -> 13.8 us  [per_device(): lax.ppermute(left[i], 'tp', z_shift(-STEPS[i]))]
    ppermute x3, waiting for transfers between devices: 7.47 us -> 0.01 us  [per_device(): lax.ppermute(grad_pair, 'tp', z_shift(k))]
    ppermute x8, starting transfers between devices: 6.71 us -> 14 us  [the longest x3 5.4 us: per_device(): lax.ppermute(proj[i], 'tp', z_shift(-STEPS[i]))]
    ppermute x8, waiting for transfers between devices: 19.1 us -> 11.9 us  [the longest x1 4.36 us: per_device(): back_grads = lax.ppermute(own_grads, 'seq', y_shift(1))]
    unnamed x76 -> x100, local copies, waits for them, and re-layouts: 32.3 us -> 26 us
    ppermute x6 -> x3, starting transfers between devices: 7.72 us -> 2.03 us  [per_device(): lax.ppermute(v, 'tp', z_shift(-k))]
    pallas_call x9 -> x10, Pallas kernels: 26.3 us -> 22.3 us  [the longest x2 6.89 us: weight_shares(): call(functools.partial(share_kernel, which), sds((3, COLS, COLS), dtype),...]
  transfers between devices with their start and end apart: 45 -> 42, of which waited for: 17 -> 17; matrix products, arithmetic and copies ran while one was open for 2% -> 2% of each run, Pallas kernels for 16% -> 17%
where the time goes in v6:
time: 202 us; the launch traced here: 201 us
  waiting for transfers between devices  69.3 us (34%)
  starting transfers between devices  59.8 us (30%)
  Pallas kernels  39.1 us (19%)
  local copies, waits for them, and re-layouts  27.8 us (14%)
  other arithmetic  4.04 us (2%)
    unnamed x100, local copies, waits for them, and re-layouts  26 us
    ppermute x3, waiting for transfers between devices, per_device(): lax.ppermute(v, 'seq', y_shift(-k))  15.2 us
    ppermute x3, waiting for transfers between devices, per_device(): lax.ppermute(left[i], 'tp', z_shift(-STEPS[i]))  13.8 us
    ppermute x3, waiting for transfers between devices, gather_blocks(): lax.ppermute(right_pair, 'tp', z_shift(k))  7.6 us
    pallas_call x2, Pallas kernels, weight_shares(): call(functools.partial(share_kernel, which), sds((3, COLS, COLS), dtype),...  6.89 us
    ppermute x3, starting transfers between devices, chunks_over_y(): came.append(lax.ppermute(sent, 'seq', y_shift(k)))  6.55 us
    pallas_call x2, Pallas kernels, back_dot(): call(functools.partial(kernel, len(after)), out_shape, vmem=20, flops=2 *...  6.2 us
    ppermute x3, starting transfers between devices, gather_blocks(): lax.ppermute(left, 'tp', z_shift(k))  5.9 us
  transfers between devices with their start and end apart: 42, of which 17 were waited for; matrix products, arithmetic and copies ran while one was open for 2% of the time, Pallas kernels for 17%

profile of v6, /device:TPU:0, one launch (start us, length us, event | category | flops | bytes accessed | tf_op | source)
XLA Modules:
  0.0 201.3 jit_solution(7663018602626192564)
XLA Ops:
  3.5 1.7 collective-permute-start.4
  5.2 3.9 %collective-permute-start.2 = (bf16[32,2048]{1,0:T(8,128)(2,1)S(1)}, bf16[32,2048]{1,0:T(8,128)(2,1)S(1)}, u32[]{:S(2)}, u32[]{:S(2)}) collective-permute-start(bf16[32,2048]{1,0:T(8,128)(2,1)S(1)} %get-tuple-element.42), channel_id=1, source_target_pairs={{0,2},{1,3},{2,0},{3,1},{4,6},{5,7},{6,4},{7,5},{8,10},{9,11},{10,... | collective-permute-start | bytes 393224 | tf_op jit(solution)/shard_map/ppermute | solution.py:129
  9.8 1.3 collective-permute-start
  12.9 4.3 %collective-permute-start.6 = (bf16[2,32,2048]{2,1,0:T(8,128)(2,1)S(1)}, bf16[2,32,2048]{2,1,0:T(8,128)(2,1)S(1)}, u32[]{:S(2)}, u32[]{:S(2)}) collective-permute-start(bf16[2,32,2048]{2,1,0:T(8,128)(2,1)S(1)} %pad_maximum_fusion.2.refs_2_), channel_id=1, source_target_pairs={{0,3},{1,0},{2,1},{3,2},{4,7},{5,4},{6,5},{7,6},{8,11},{9,8},{10,9... | collective-permute-start | bytes 786440 | tf_op jit(solution)/shard_map/ppermute | solution.py:130
  18.1 2.3 %collective-permute-start.9 = (bf16[2,32,4096]{2,1,0:T(8,128)(2,1)S(1)}, bf16[2,32,4096]{2,1,0:T(8,128)(2,1)S(1)}, u32[]{:S(2)}, u32[]{:S(2)}) collective-permute-start(bf16[2,32,4096]{2,1,0:T(8,128)(2,1)S(1)} %pad_maximum_fusion.1.refs_7_.p0), channel_id=1, source_target_pairs={{0,1},{1,2},{2,3},{3,0},{4,5},{5,6},{6,7},{7,4},{8,9},{9,10},{10,1... | collective-permute-start | bytes 1572872 | tf_op jit(solution)/shard_map/ppermute | solution.py:707
  20.5 7.6 %collective-permute-done.5.refs_3_ = bf16[2,32,2048]{2,1,0:T(8,128)(2,1)S(1)} collective-permute-done((bf16[2,32,2048]{2,1,0:T(8,128)(2,1)S(1)}, bf16[2,32,2048]{2,1,0:T(8,128)(2,1)S(1)}, u32[]{:S(2)}, u32[]{:S(2)}) %collective-permute-start.5) | collective-permute-done | bytes 262176 | tf_op jit(solution)/shard_map/ppermute | solution.py:130
  29.5 1.7 collective-permute-start.15
  32.7 4.6 %copy-done = bf16[1,4096,3,512]{3,1,2,0:T(8,128)(2,1)S(1)} copy-done((bf16[1,4096,3,512]{3,1,2,0:T(8,128)(2,1)S(1)}, bf16[1,4096,3,512]{3,1,2,0:T(8,128)(2,1)}, u32[]{:S(2)}) %copy-start) | copy-done | bytes 12582936
  42.3 3.7 %key_value.1 = (bf16[256,4096]{1,0:T(8,128)(2,1)S(1)}, bf16[2,256,512]{2,1,0:T(8,128)(2,1)S(1)}) custom-call(bf16[4,32,2048]{2,1,0:T(8,128)(2,1)S(1)} %copy-done.22, bf16[4,32,2048]{2,1,0:T(8,128)(2,1)S(1)} %copy-done.32, bf16[2,32,2048]{2,1,0:T(8,128)(2,1)S(1)} %pad_maximum_fusion.2.refs_2_, bf16[2,32,2048]{2,1,0:T(8,128)(2,1)S(1)} %copy-done.37, ...), custom_call_target="tpu_custom_call" | custom-call | flops 2147483648 | bytes 12582912 | tf_op jit(solution)/shard_map/key_value/pallas_call | solution.py:324
  46.0 2.8 %collective-permute-start.11 = (bf16[2,256,512]{2,1,0:T(8,128)(2,1)S(1)}, bf16[2,256,512]{2,1,0:T(8,128)(2,1)S(1)}, u32[]{:S(2)}, u32[]{:S(2)}) collective-permute-start(bf16[2,256,512]{2,1,0:T(8,128)(2,1)S(1)} %get-tuple-element.46.own_kv), channel_id=1, source_target_pairs={{0,64},{64,0},{1,65},{65,1},{2,66},{66,2},{3,67},{67,3},{4,68},{68... | collective-permute-start | bytes 1572872 | tf_op jit(solution)/shard_map/ppermute | solution.py:709
  48.9 1.6 collective-permute-start.16
  50.6 1.7 collective-permute-start.17
  52.4 1.8 query.1
  54.1 2.6 %collective-permute-done.11.other_kv = bf16[2,256,512]{2,1,0:T(8,128)(2,1)S(1)} collective-permute-done((bf16[2,256,512]{2,1,0:T(8,128)(2,1)S(1)}, bf16[2,256,512]{2,1,0:T(8,128)(2,1)S(1)}, u32[]{:S(2)}, u32[]{:S(2)}) %collective-permute-start.11) | collective-permute-done | bytes 524320 | tf_op jit(solution)/shard_map/ppermute | solution.py:709
  56.7 2.4 %attend_forward.1.left.mixed = bf16[256,512]{1,0:T(8,128)(2,1)S(1)} custom-call(s32[12]{0:T(128)S(1)} %concatenate.6.meta, bf16[256,512]{1,0:T(8,128)(2,1)S(1)} %query.1, bf16[2,256,512]{2,1,0:T(8,128)(2,1)S(1)} %get-tuple-element.46.own_kv, bf16[2,256,512]{2,1,0:T(8,128)(2,1)S(1)} %collective-permute-done.11.other_kv), custom_call_target="tpu_custom_call" | custom-call | flops 536870912 | bytes 1572864 | tf_op jit(solution)/shard_map/attend_forward/pallas_call | solution.py:596
  59.1 3.0 %proj_parts.1 = (bf16[2,32,4096]{2,1,0:T(8,128)(2,1)S(1)}, bf16[2,32,4096]{2,1,0:T(8,128)(2,1)S(1)}, bf16[2,32,4096]{2,1,0:T(8,128)(2,1)S(1)}, bf16[2,32,4096]{2,1,0:T(8,128)(2,1)}) custom-call(bf16[256,512]{1,0:T(8,128)(2,1)S(1)} %attend_forward.1.left.mixed, bf16[1,4096,512]{2,1,0:T(8,128)(2,1)S(1)} %copy-done.2), custom_call_target="tpu_custom_call" | custom-call | flops 1073741824 | bytes 6291456 | tf_op jit(solution)/shard_map/proj_parts/pallas_call | solution.py:494
  62.2 1.9 grad_mixed.1
  64.1 1.8 out_weight_parts.1
  66.1 3.0 %collective-permute-start.12 = (bf16[2,32,4096]{2,1,0:T(8,128)(2,1)S(1)}, bf16[2,32,4096]{2,1,0:T(8,128)(2,1)S(1)}, u32[]{:S(2)}, u32[]{:S(2)}) collective-permute-start(bf16[2,32,4096]{2,1,0:T(8,128)(2,1)S(1)} %get-tuple-element.48), channel_id=1, source_target_pairs={{0,3},{1,0},{2,1},{3,2},{4,7},{5,4},{6,5},{7,6},{8,11},{9,8},{10,9... | collective-permute-start | bytes 1572872 | tf_op jit(solution)/shard_map/ppermute | solution.py:715
  69.1 1.3 collective-permute-start.13
  70.4 4.3 %attend_backward.1 = (bf16[256,512]{1,0:T(8,128)(2,1)S(1)}, f32[2,256,512]{2,1,0:T(8,128)S(1)}, bf16[2,256,512]{2,1,0:T(8,128)(2,1)S(1)}) custom-call(s32[12]{0:T(128)S(1)} %concatenate.6.meta, bf16[256,512]{1,0:T(8,128)(2,1)S(1)} %query.1, bf16[2,256,512]{2,1,0:T(8,128)(2,1)S(1)} %get-tuple-element.46.own_kv, ...), custom_call_target="tpu_custom_call" | custom-call | flops 1073741824 | bytes 3145728 | tf_op jit(solution)/shard_map/attend_backward/pallas_call | solution.py:610
  74.7 2.8 %collective-permute-start.18 = (bf16[2,256,512]{2,1,0:T(8,128)(2,1)S(1)}, bf16[2,256,512]{2,1,0:T(8,128)(2,1)S(1)}, u32[]{:S(2)}, u32[]{:S(2)}) collective-permute-start(bf16[2,256,512]{2,1,0:T(8,128)(2,1)S(1)} %get-tuple-element.54), channel_id=1, source_target_pairs={{0,64},{64,0},{1,65},{65,1},{2,66},{66,2},{3,67},{67,3},{4,68},{68... | collective-permute-start | bytes 1572872 | tf_op jit(solution)/shard_map/ppermute | solution.py:720
  77.5 3.2 %collective-permute-start.19 = (bf16[256,1024]{1,0:T(8,128)(2,1)S(1)}, bf16[256,1024]{1,0:T(8,128)(2,1)S(1)}, u32[]{:S(2)}, u32[]{:S(2)}) collective-permute-start(bf16[256,1024]{1,0:T(8,128)(2,1)S(1)} %get-tuple-element.81), channel_id=1, source_target_pairs={{0,32},{8,40},{16,48},{24,56},{32,0},{40,8},{48,16},{56,24},{1,33}... | collective-permute-start | bytes 1572872 | tf_op jit(solution)/shard_map/ppermute | solution.py:680
  80.7 2.2 %collective-permute-done.12.refs_1_.c1 = bf16[2,32,4096]{2,1,0:T(8,128)(2,1)S(1)} collective-permute-done((bf16[2,32,4096]{2,1,0:T(8,128)(2,1)S(1)}, bf16[2,32,4096]{2,1,0:T(8,128)(2,1)S(1)}, u32[]{:S(2)}, u32[]{:S(2)}) %collective-permute-start.12) | collective-permute-done | bytes 524320 | tf_op jit(solution)/shard_map/ppermute | solution.py:715
  82.8 1.5 collective-permute-done.13.refs_2_.c2
  84.3 5.9 %collective-permute-done.18.came = bf16[2,256,512]{2,1,0:T(8,128)(2,1)S(1)} collective-permute-done((bf16[2,256,512]{2,1,0:T(8,128)(2,1)S(1)}, bf16[2,256,512]{2,1,0:T(8,128)(2,1)S(1)}, u32[]{:S(2)}, u32[]{:S(2)}) %collective-permute-start.18) | collective-permute-done | bytes 524320 | tf_op jit(solution)/shard_map/ppermute | solution.py:720
  91.9 1.6 collective-permute-start.27
  93.5 1.7 collective-permute-start.28
  95.1 3.1 %back_right.1 = (bf16[4,32,2048]{2,1,0:T(8,128)(2,1)S(1)}, bf16[4,32,2048]{2,1,0:T(8,128)(2,1)S(1)}, f32[1,2048]{1,0:T(1,128)S(1)}) custom-call(bf16[3,256,512]{2,1,0:T(8,128)(2,1)S(1)} %sum_keys.1.grads.g0, bf16[3,4096,512]{2,1,0:T(8,128)(2,1)S(1)} %bitcast.38, bf16[256,4096]{1,0:T(8,128)(2,1)S(1)} %get-tuple-element.45.full.normed, ...), custom_call_target="tpu_custom_call" | custom-call | flops 1610612736 | bytes 8388608 | tf_op jit(solution)/shard_map/back_right/pallas_call | solution.py:454
  101.9 3.1 %back_left.1 = (bf16[5,16,2048]{2,1,0:T(8,128)(2,1)S(1)}, bf16[5,16,2048]{2,1,0:T(8,128)(2,1)S(1)}, bf16[5,16,2048]{2,1,0:T(8,128)(2,1)S(1)}, bf16[5,16,2048]{2,1,0:T(8,128)(2,1)S(1)}) custom-call(bf16[3,256,512]{2,1,0:T(8,128)(2,1)S(1)} %sum_keys.1.grads.g0, bf16[3,4096,512]{2,1,0:T(8,128)(2,1)S(1)} %bitcast.39, ...), custom_call_target="tpu_custom_call" | custom-call | flops 1610612736 | bytes 8388608 | tf_op jit(solution)/shard_map/back_left/pallas_call | solution.py:454
  105.0 2.4 %collective-permute-start.21 = (bf16[5,16,2048]{2,1,0:T(8,128)(2,1)S(1)}, bf16[5,16,2048]{2,1,0:T(8,128)(2,1)S(1)}, u32[]{:S(2)}, u32[]{:S(2)}) collective-permute-start(bf16[5,16,2048]{2,1,0:T(8,128)(2,1)S(1)} %get-tuple-element.61), channel_id=1, source_target_pairs={{0,3},{1,0},{2,1},{3,2},{4,7},{5,4},{6,5},{7,6},{8,11},{9,8},{10,9... | collective-permute-start | bytes 983048 | tf_op jit(solution)/shard_map/ppermute | solution.py:738
  107.5 4.4 %collective-permute-done.27.g1 = bf16[3,256,512]{2,1,0:T(8,128)(2,1)S(1)} collective-permute-done((bf16[3,256,512]{2,1,0:T(8,128)(2,1)S(1)}, bf16[3,256,512]{2,1,0:T(8,128)(2,1)S(1)}, u32[]{:S(2)}, u32[]{:S(2)}) %collective-permute-start.27) | collective-permute-done | bytes 786464 | tf_op jit(solution)/shard_map/ppermute | solution.py:727
  111.8 2.2 %collective-permute-start.23 = (bf16[5,16,2048]{2,1,0:T(8,128)(2,1)S(1)}, bf16[5,16,2048]{2,1,0:T(8,128)(2,1)S(1)}, u32[]{:S(2)}, u32[]{:S(2)}) collective-permute-start(bf16[5,16,2048]{2,1,0:T(8,128)(2,1)S(1)} %get-tuple-element.63), channel_id=1, source_target_pairs={{0,2},{1,3},{2,0},{3,1},{4,6},{5,7},{6,4},{7,5},{8,10},{9,11},{10,... | collective-permute-start | bytes 983048 | tf_op jit(solution)/shard_map/ppermute | solution.py:738
  116.8 2.9 %collective-permute-start.30 = (bf16[3,128,512]{2,1,0:T(8,128)(2,1)}, bf16[3,128,512]{2,1,0:T(8,128)(2,1)}, u32[]{:S(2)}, u32[]{:S(2)}) collective-permute-start(bf16[3,128,512]{2,1,0:T(8,128)(2,1)} %slice.9), channel_id=1, source_target_pairs={{0,48},{8,56},{16,0},{24,8},{32,16},{40,24},{48,32},{56,40},{1,49}... | collective-permute-start | bytes 1179656 | tf_op jit(solution)/shard_map/ppermute | solution.py:731
  121.0 13.5 %collective-permute-done.22.c2 = bf16[5,16,2048]{2,1,0:T(8,128)(2,1)S(1)} collective-permute-done((bf16[5,16,2048]{2,1,0:T(8,128)(2,1)S(1)}, bf16[5,16,2048]{2,1,0:T(8,128)(2,1)S(1)}, u32[]{:S(2)}, u32[]{:S(2)}) %collective-permute-start.22) | collective-permute-done | bytes 327712 | tf_op jit(solution)/shard_map/ppermute | solution.py:738
  137.7 5.1 %collective-permute-done.26.refs_0_.l_came.came = bf16[3,16,2048]{2,1,0:T(8,128)(2,1)} collective-permute-done((bf16[3,16,2048]{2,1,0:T(8,128)(2,1)}, bf16[3,16,2048]{2,1,0:T(8,128)(2,1)}, u32[]{:S(2)}, u32[]{:S(2)}) %collective-permute-start.26) | collective-permute-done | bytes 196640 | tf_op jit(solution)/shard_map/ppermute | solution.py:740
  152.3 3.5 %weight_shares.2.refs_1_.refs_0_ = bf16[3,512,512]{2,1,0:T(8,128)(2,1)S(1)} custom-call(s32[4]{0:T(128)S(1)} %pad_add_fusion.1.columns, bf16[256,4096]{1,0:T(8,128)(2,1)S(1)} %get-tuple-element.45.full.normed, bf16[256,1024]{1,0:T(8,128)(2,1)S(1)} %copy-done.8, bf16[256,1024]{1,0:T(8,128)(2,1)S(1)} %copy-done.10, ...), custom_call_target="tpu_custom_call" | custom-call | flops 1610612736 | bytes 7340032 | tf_op jit(solution)/shard_map/weight_shares/pallas_call | solution.py:663
  156.0 2.4 %collective-permute-start.38 = (bf16[512,512]{1,0:T(8,128)(2,1)S(1)}, bf16[512,512]{1,0:T(8,128)(2,1)S(1)}, u32[]{:S(2)}, u32[]{:S(2)}) collective-permute-start(bf16[512,512]{1,0:T(8,128)(2,1)S(1)} %copy-done.28), channel_id=1, source_target_pairs={{0,48},{8,56},{16,0},{24,8},{32,16},{40,24},{48,32},{56,40},{1,49}... | collective-permute-start | bytes 1572872 | tf_op jit(solution)/shard_map/ppermute | solution.py:724
  158.4 1.3 sum_z.1
  159.8 2.1 %collective-permute-start.25 = (bf16[32,4096]{1,0:T(8,128)(2,1)S(1)}, bf16[32,4096]{1,0:T(8,128)(2,1)S(1)}, u32[]{:S(2)}, u32[]{:S(2)}) collective-permute-start(bf16[32,4096]{1,0:T(8,128)(2,1)S(1)} %get-tuple-element.67), channel_id=1, source_target_pairs={{0,4},{1,5},{2,6},{3,7},{4,0},{5,1},{6,2},{7,3},{8,12},{9,13},{10,... | collective-permute-start | bytes 786440 | tf_op jit(solution)/shard_map/ppermute | solution.py:757
  162.0 2.0 %collective-permute-start.32 = (bf16[32,2048]{1,0:T(8,128)(2,1)S(1)}, bf16[32,2048]{1,0:T(8,128)(2,1)S(1)}, u32[]{:S(2)}, u32[]{:S(2)}) collective-permute-start(bf16[32,2048]{1,0:T(8,128)(2,1)S(1)} %get-tuple-element.73), channel_id=1, source_target_pairs={{0,1},{1,2},{2,3},{3,0},{4,5},{5,6},{6,7},{7,4},{8,9},{9,10},{10,1... | collective-permute-start | bytes 393224 | tf_op jit(solution)/shard_map/ppermute | solution.py:750
  164.6 3.9 %collective-permute-done.25 = bf16[32,4096]{1,0:T(8,128)(2,1)S(1)} collective-permute-done((bf16[32,4096]{1,0:T(8,128)(2,1)S(1)}, bf16[32,4096]{1,0:T(8,128)(2,1)S(1)}, u32[]{:S(2)}, u32[]{:S(2)}) %collective-permute-start.25) | collective-permute-done | bytes 262176 | tf_op jit(solution)/shard_map/ppermute | solution.py:757
  168.6 2.3 %collective-permute-start.41 = (bf16[512,512]{1,0:T(8,128)(2,1)S(1)}, bf16[512,512]{1,0:T(8,128)(2,1)S(1)}, u32[]{:S(2)}, u32[]{:S(2)}) collective-permute-start(bf16[512,512]{1,0:T(8,128)(2,1)S(1)} %copy-done.45), channel_id=1, source_target_pairs={{0,32},{8,40},{16,48},{24,56},{32,0},{40,8},{48,16},{56,24},{1,33}... | collective-permute-start | bytes 1572872 | tf_op jit(solution)/shard_map/ppermute | solution.py:724
  171.7 5.7 %collective-permute-done.33.r3 = bf16[32,2048]{1,0:T(8,128)(2,1)S(1)} collective-permute-done((bf16[32,2048]{1,0:T(8,128)(2,1)S(1)}, bf16[32,2048]{1,0:T(8,128)(2,1)S(1)}, u32[]{:S(2)}, u32[]{:S(2)}) %collective-permute-start.33) | collective-permute-done | bytes 131104 | tf_op jit(solution)/shard_map/ppermute | solution.py:750
  177.3 2.0 token_rows.1
  179.3 15.2 %collective-permute-done.39.refs_3_.c2 = bf16[512,512]{1,0:T(8,128)(2,1)S(1)} collective-permute-done((bf16[512,512]{1,0:T(8,128)(2,1)S(1)}, bf16[512,512]{1,0:T(8,128)(2,1)S(1)}, u32[]{:S(2)}, u32[]{:S(2)}) %collective-permute-start.39) | collective-permute-done | bytes 524320 | tf_op jit(solution)/shard_map/ppermute | solution.py:724
  195.7 3.4 %weight_shares.3 = f32[3,512,512]{2,1,0:T(8,128)S(1)} custom-call(s32[4]{0:T(128)S(1)} %pad_add_fusion.1.columns, bf16[256,4096]{1,0:T(8,128)(2,1)S(1)} %get-tuple-element.45.full.normed, bf16[256,1024]{1,0:T(8,128)(2,1)S(1)} %copy-done.8, bf16[256,1024]{1,0:T(8,128)(2,1)S(1)} %copy-done.10, bf16[256,1024]{1,0:T(8,128)(2,1)S(1)} %collective-permute-done.19.refs_0_.c3, ...), custom_call_target="tpu_custom_call" | custom-call | flops 1610612736 | bytes 7340032 | tf_op jit(solution)/shard_map/weight_shares/pallas_call | solution.py:663
  199.1 2.2 %add_bitcast_fusion = f32[1,512,3,512]{3,1,2,0:T(8,128)} fusion(f32[3,512,512]{2,1,0:T(8,128)S(1)} %weight_shares.3, bf16[3,512,512]{2,1,0:T(8,128)(2,1)S(1)} %collective-permute-done.40), kind=kLoop, calls=%fused_computation | loop fusion | flops 1572864 | bytes 7864320 | tf_op jit(solution)/shard_map/broadcast_in_dim | solution.py:764
  (171 shorter events, 39.6 us)
Async XLA Ops:
  0.6 19.7 %copy-start.48 = (s32[1,5]{1,0:T(1,128)S(1)}, s32[1,5]{1,0:T(1,128)}, u32[]{:S(2)}) copy-start(s32[1,5]{1,0:T(1,128)} %param.8) | copy-start | bytes 64
  0.6 19.7 %copy-start.49 = (s32[1,4]{1,0:T(1,128)S(1)}, s32[1,4]{1,0:T(1,128)}, u32[]{:S(2)}) copy-start(s32[1,4]{1,0:T(1,128)} %param.9) | copy-start | bytes 52
  3.5 28.4 %copy-start.25 = (bf16[32,4096]{1,0:T(8,128)(2,1)}, bf16[32,4096]{1,0:T(8,128)(2,1)S(1)}, u32[]{:S(2)}) copy-start(bf16[32,4096]{1,0:T(8,128)(2,1)S(1)} %get-tuple-element.44.grad) | copy-start | bytes 786436
  3.5 8.1 %collective-permute-start.4 = (bf16[32,2048]{1,0:T(8,128)(2,1)S(1)}, bf16[32,2048]{1,0:T(8,128)(2,1)S(1)}, u32[]{:S(2)}, u32[]{:S(2)}) collective-permute-start(bf16[32,2048]{1,0:T(8,128)(2,1)S(1)} %get-tuple-element.43), channel_id=1, source_target_pairs={{0,4},{1,5},{2,6},{3,7},{4,0},{5,1},{6,2},{7,3},{8,12},{9,13},{10,... | collective-permute-start | bytes 393224 | tf_op jit(solution)/shard_map/ppermute | solution.py:128
  5.2 7.7 %collective-permute-start.2 = (bf16[32,2048]{1,0:T(8,128)(2,1)S(1)}, bf16[32,2048]{1,0:T(8,128)(2,1)S(1)}, u32[]{:S(2)}, u32[]{:S(2)}) collective-permute-start(bf16[32,2048]{1,0:T(8,128)(2,1)S(1)} %get-tuple-element.42), channel_id=1, source_target_pairs={{0,2},{1,3},{2,0},{3,1},{4,6},{5,7},{6,4},{7,5},{8,10},{9,11},{10,... | collective-permute-start | bytes 393224 | tf_op jit(solution)/shard_map/ppermute | solution.py:129
  9.1 8.2 %collective-permute-start.1 = (bf16[32,2048]{1,0:T(8,128)(2,1)S(1)}, bf16[32,2048]{1,0:T(8,128)(2,1)S(1)}, u32[]{:S(2)}, u32[]{:S(2)}) collective-permute-start(bf16[32,2048]{1,0:T(8,128)(2,1)S(1)} %get-tuple-element.42), channel_id=1, source_target_pairs={{0,3},{1,0},{2,1},{3,2},{4,7},{5,4},{6,5},{7,6},{8,11},{9,8},{10,9... | collective-permute-start | bytes 393224 | tf_op jit(solution)/shard_map/ppermute | solution.py:129
  9.8 7.7 %collective-permute-start = (bf16[32,2048]{1,0:T(8,128)(2,1)S(1)}, bf16[32,2048]{1,0:T(8,128)(2,1)S(1)}, u32[]{:S(2)}, u32[]{:S(2)}) collective-permute-start(bf16[32,2048]{1,0:T(8,128)(2,1)S(1)} %get-tuple-element.42), channel_id=1, source_target_pairs={{0,1},{1,2},{2,3},{3,0},{4,5},{5,6},{6,7},{7,4},{8,9},{9,10},{10,1... | collective-permute-start | bytes 393224 | tf_op jit(solution)/shard_map/ppermute | solution.py:129
  11.1 6.9 %collective-permute-start.8 = (bf16[32,4096]{1,0:T(8,128)(2,1)S(1)}, bf16[32,4096]{1,0:T(8,128)(2,1)S(1)}, u32[]{:S(2)}, u32[]{:S(2)}) collective-permute-start(bf16[32,4096]{1,0:T(8,128)(2,1)S(1)} %get-tuple-element.44.grad), channel_id=1, source_target_pairs={{0,4},{1,5},{2,6},{3,7},{4,0},{5,1},{6,2},{7,3},{8,12},{9,13},{10,... | collective-permute-start | bytes 786440 | tf_op jit(solution)/shard_map/ppermute | solution.py:705
  11.7 16.4 %collective-permute-start.5 = (bf16[2,32,2048]{2,1,0:T(8,128)(2,1)S(1)}, bf16[2,32,2048]{2,1,0:T(8,128)(2,1)S(1)}, u32[]{:S(2)}, u32[]{:S(2)}) collective-permute-start(bf16[2,32,2048]{2,1,0:T(8,128)(2,1)S(1)} %pad_maximum_fusion.2.refs_2_), channel_id=1, source_target_pairs={{0,1},{1,2},{2,3},{3,0},{4,5},{5,6},{6,7},{7,4},{8,9},{9,10},{10,1... | collective-permute-start | bytes 786440 | tf_op jit(solution)/shard_map/ppermute | solution.py:130
  12.9 15.9 %collective-permute-start.6 = (bf16[2,32,2048]{2,1,0:T(8,128)(2,1)S(1)}, bf16[2,32,2048]{2,1,0:T(8,128)(2,1)S(1)}, u32[]{:S(2)}, u32[]{:S(2)}) collective-permute-start(bf16[2,32,2048]{2,1,0:T(8,128)(2,1)S(1)} %pad_maximum_fusion.2.refs_2_), channel_id=1, source_target_pairs={{0,3},{1,0},{2,1},{3,2},{4,7},{5,4},{6,5},{7,6},{8,11},{9,8},{10,9... | collective-permute-start | bytes 786440 | tf_op jit(solution)/shard_map/ppermute | solution.py:130
  17.3 14.0 %collective-permute-start.7 = (bf16[2,32,2048]{2,1,0:T(8,128)(2,1)S(1)}, bf16[2,32,2048]{2,1,0:T(8,128)(2,1)S(1)}, u32[]{:S(2)}, u32[]{:S(2)}) collective-permute-start(bf16[2,32,2048]{2,1,0:T(8,128)(2,1)S(1)} %pad_maximum_fusion.2.refs_2_), channel_id=1, source_target_pairs={{0,2},{1,3},{2,0},{3,1},{4,6},{5,7},{6,4},{7,5},{8,10},{9,11},{10,... | collective-permute-start | bytes 786440 | tf_op jit(solution)/shard_map/ppermute | solution.py:130
  17.5 14.4 %collective-permute-start.3 = (bf16[4,32,2048]{2,1,0:T(8,128)(2,1)S(1)}, bf16[4,32,2048]{2,1,0:T(8,128)(2,1)S(1)}, u32[]{:S(2)}, u32[]{:S(2)}) collective-permute-start(bf16[4,32,2048]{2,1,0:T(8,128)(2,1)S(1)} %pad_maximum_fusion.refs_0_), channel_id=1, source_target_pairs={{0,4},{1,5},{2,6},{3,7},{4,0},{5,1},{6,2},{7,3},{8,12},{9,13},{10,... | collective-permute-start | bytes 1572872 | tf_op jit(solution)/shard_map/ppermute | solution.py:132
  18.1 32.5 %collective-permute-start.9 = (bf16[2,32,4096]{2,1,0:T(8,128)(2,1)S(1)}, bf16[2,32,4096]{2,1,0:T(8,128)(2,1)S(1)}, u32[]{:S(2)}, u32[]{:S(2)}) collective-permute-start(bf16[2,32,4096]{2,1,0:T(8,128)(2,1)S(1)} %pad_maximum_fusion.1.refs_7_.p0), channel_id=1, source_target_pairs={{0,1},{1,2},{2,3},{3,0},{4,5},{5,6},{6,7},{7,4},{8,9},{9,10},{10,1... | collective-permute-start | bytes 1572872 | tf_op jit(solution)/shard_map/ppermute | solution.py:707
  28.8 23.6 %collective-permute-start.10 = (bf16[2,32,4096]{2,1,0:T(8,128)(2,1)S(1)}, bf16[2,32,4096]{2,1,0:T(8,128)(2,1)S(1)}, u32[]{:S(2)}, u32[]{:S(2)}) collective-permute-start(bf16[2,32,4096]{2,1,0:T(8,128)(2,1)S(1)} %pad_maximum_fusion.1.refs_7_.p0), channel_id=1, source_target_pairs={{0,3},{1,0},{2,1},{3,2},{4,7},{5,4},{6,5},{7,6},{8,11},{9,8},{10,9... | collective-permute-start | bytes 1572872 | tf_op jit(solution)/shard_map/ppermute | solution.py:707
  29.5 32.6 %collective-permute-start.15 = (bf16[2,32,4096]{2,1,0:T(8,128)(2,1)S(1)}, bf16[2,32,4096]{2,1,0:T(8,128)(2,1)S(1)}, u32[]{:S(2)}, u32[]{:S(2)}) collective-permute-start(bf16[2,32,4096]{2,1,0:T(8,128)(2,1)S(1)} %pad_maximum_fusion.1.refs_7_.p0), channel_id=1, source_target_pairs={{0,2},{1,3},{2,0},{3,1},{4,6},{5,7},{6,4},{7,5},{8,10},{9,11},{10,... | collective-permute-start | bytes 1572872 | tf_op jit(solution)/shard_map/ppermute | solution.py:707
  46.0 10.8 %collective-permute-start.11 = (bf16[2,256,512]{2,1,0:T(8,128)(2,1)S(1)}, bf16[2,256,512]{2,1,0:T(8,128)(2,1)S(1)}, u32[]{:S(2)}, u32[]{:S(2)}) collective-permute-start(bf16[2,256,512]{2,1,0:T(8,128)(2,1)S(1)} %get-tuple-element.46.own_kv), channel_id=1, source_target_pairs={{0,64},{64,0},{1,65},{65,1},{2,66},{66,2},{3,67},{67,3},{4,68},{68... | collective-permute-start | bytes 1572872 | tf_op jit(solution)/shard_map/ppermute | solution.py:709
  48.9 13.2 %collective-permute-start.16 = (bf16[256,1024]{1,0:T(8,128)(2,1)S(1)}, bf16[256,1024]{1,0:T(8,128)(2,1)S(1)}, u32[]{:S(2)}, u32[]{:S(2)}) collective-permute-start(bf16[256,1024]{1,0:T(8,128)(2,1)S(1)} %get-tuple-element.83), channel_id=1, source_target_pairs={{0,16},{8,24},{16,32},{24,40},{32,48},{40,56},{48,0},{56,8},{1,17}... | collective-permute-start | bytes 1572872 | tf_op jit(solution)/shard_map/ppermute | solution.py:680
  50.6 11.6 %collective-permute-start.17 = (bf16[256,1024]{1,0:T(8,128)(2,1)S(1)}, bf16[256,1024]{1,0:T(8,128)(2,1)S(1)}, u32[]{:S(2)}, u32[]{:S(2)}) collective-permute-start(bf16[256,1024]{1,0:T(8,128)(2,1)S(1)} %get-tuple-element.82), channel_id=1, source_target_pairs={{0,48},{8,56},{16,0},{24,8},{32,16},{40,24},{48,32},{56,40},{1,49}... | collective-permute-start | bytes 1572872 | tf_op jit(solution)/shard_map/ppermute | solution.py:680
  66.0 32.9 %collective-permute-start.20 = (bf16[4,512,512]{2,1,0:T(8,128)(2,1)S(1)}, bf16[4,512,512]{2,1,0:T(8,128)(2,1)S(1)}, u32[]{:S(2)}, u32[]{:S(2)}) collective-permute-start(bf16[4,512,512]{2,1,0:T(8,128)(2,1)S(1)} %get-tuple-element.58), channel_id=1, source_target_pairs={{0,8},{8,0},{16,24},{24,16},{32,40},{40,32},{48,56},{56,48},{1,9},... | collective-permute-start | bytes 6291464 | tf_op jit(solution)/shard_map/ppermute | solution.py:722
  66.1 16.8 %collective-permute-start.12 = (bf16[2,32,4096]{2,1,0:T(8,128)(2,1)S(1)}, bf16[2,32,4096]{2,1,0:T(8,128)(2,1)S(1)}, u32[]{:S(2)}, u32[]{:S(2)}) collective-permute-start(bf16[2,32,4096]{2,1,0:T(8,128)(2,1)S(1)} %get-tuple-element.48), channel_id=1, source_target_pairs={{0,3},{1,0},{2,1},{3,2},{4,7},{5,4},{6,5},{7,6},{8,11},{9,8},{10,9... | collective-permute-start | bytes 1572872 | tf_op jit(solution)/shard_map/ppermute | solution.py:715
  69.1 15.2 %collective-permute-start.13 = (bf16[2,32,4096]{2,1,0:T(8,128)(2,1)S(1)}, bf16[2,32,4096]{2,1,0:T(8,128)(2,1)S(1)}, u32[]{:S(2)}, u32[]{:S(2)}) collective-permute-start(bf16[2,32,4096]{2,1,0:T(8,128)(2,1)S(1)} %get-tuple-element.49), channel_id=1, source_target_pairs={{0,1},{1,2},{2,3},{3,0},{4,5},{5,6},{6,7},{7,4},{8,9},{9,10},{10,1... | collective-permute-start | bytes 1572872 | tf_op jit(solution)/shard_map/ppermute | solution.py:715
  74.7 15.5 %collective-permute-start.18 = (bf16[2,256,512]{2,1,0:T(8,128)(2,1)S(1)}, bf16[2,256,512]{2,1,0:T(8,128)(2,1)S(1)}, u32[]{:S(2)}, u32[]{:S(2)}) collective-permute-start(bf16[2,256,512]{2,1,0:T(8,128)(2,1)S(1)} %get-tuple-element.54), channel_id=1, source_target_pairs={{0,64},{64,0},{1,65},{65,1},{2,66},{66,2},{3,67},{67,3},{4,68},{68... | collective-permute-start | bytes 1572872 | tf_op jit(solution)/shard_map/ppermute | solution.py:720
  77.5 17.6 %collective-permute-start.19 = (bf16[256,1024]{1,0:T(8,128)(2,1)S(1)}, bf16[256,1024]{1,0:T(8,128)(2,1)S(1)}, u32[]{:S(2)}, u32[]{:S(2)}) collective-permute-start(bf16[256,1024]{1,0:T(8,128)(2,1)S(1)} %get-tuple-element.81), channel_id=1, source_target_pairs={{0,32},{8,40},{16,48},{24,56},{32,0},{40,8},{48,16},{56,24},{1,33}... | collective-permute-start | bytes 1572872 | tf_op jit(solution)/shard_map/ppermute | solution.py:680
  91.9 19.9 %collective-permute-start.27 = (bf16[3,256,512]{2,1,0:T(8,128)(2,1)S(1)}, bf16[3,256,512]{2,1,0:T(8,128)(2,1)S(1)}, u32[]{:S(2)}, u32[]{:S(2)}) collective-permute-start(bf16[3,256,512]{2,1,0:T(8,128)(2,1)S(1)} %sum_keys.1.grads.g0), channel_id=1, source_target_pairs={{0,16},{8,24},{16,32},{24,40},{32,48},{40,56},{48,0},{56,8},{1,17}... | collective-permute-start | bytes 2359304 | tf_op jit(solution)/shard_map/ppermute | solution.py:727
  93.5 21.3 %collective-permute-start.28 = (bf16[3,256,512]{2,1,0:T(8,128)(2,1)S(1)}, bf16[3,256,512]{2,1,0:T(8,128)(2,1)S(1)}, u32[]{:S(2)}, u32[]{:S(2)}) collective-permute-start(bf16[3,256,512]{2,1,0:T(8,128)(2,1)S(1)} %sum_keys.1.grads.g0), channel_id=1, source_target_pairs={{0,48},{8,56},{16,0},{24,8},{32,16},{40,24},{48,32},{56,40},{1,49}... | collective-permute-start | bytes 2359304 | tf_op jit(solution)/shard_map/ppermute | solution.py:728
  98.2 18.5 %collective-permute-start.24 = (bf16[4,32,2048]{2,1,0:T(8,128)(2,1)S(1)}, bf16[4,32,2048]{2,1,0:T(8,128)(2,1)S(1)}, u32[]{:S(2)}, u32[]{:S(2)}) collective-permute-start(bf16[4,32,2048]{2,1,0:T(8,128)(2,1)S(1)} %get-tuple-element.64), channel_id=1, source_target_pairs={{0,4},{1,5},{2,6},{3,7},{4,0},{5,1},{6,2},{7,3},{8,12},{9,13},{10,... | collective-permute-start | bytes 1572872 | tf_op jit(solution)/shard_map/ppermute | solution.py:736
  105.0 37.8 %copy-start.43 = (bf16[1,4096]{1,0:T(2,128)(2,1)S(1)}, bf16[1,4096]{1,0:T(2,128)(2,1)}, u32[]{:S(2)}) copy-start(bf16[1,4096]{1,0:T(2,128)(2,1)} %gain.5) | copy-start | bytes 24580
  105.0 15.0 %collective-permute-start.21 = (bf16[5,16,2048]{2,1,0:T(8,128)(2,1)S(1)}, bf16[5,16,2048]{2,1,0:T(8,128)(2,1)S(1)}, u32[]{:S(2)}, u32[]{:S(2)}) collective-permute-start(bf16[5,16,2048]{2,1,0:T(8,128)(2,1)S(1)} %get-tuple-element.61), channel_id=1, source_target_pairs={{0,3},{1,0},{2,1},{3,2},{4,7},{5,4},{6,5},{7,6},{8,11},{9,8},{10,9... | collective-permute-start | bytes 983048 | tf_op jit(solution)/shard_map/ppermute | solution.py:738
  107.5 27.0 %collective-permute-start.22 = (bf16[5,16,2048]{2,1,0:T(8,128)(2,1)S(1)}, bf16[5,16,2048]{2,1,0:T(8,128)(2,1)S(1)}, u32[]{:S(2)}, u32[]{:S(2)}) collective-permute-start(bf16[5,16,2048]{2,1,0:T(8,128)(2,1)S(1)} %get-tuple-element.62), channel_id=1, source_target_pairs={{0,1},{1,2},{2,3},{3,0},{4,5},{5,6},{6,7},{7,4},{8,9},{9,10},{10,1... | collective-permute-start | bytes 983048 | tf_op jit(solution)/shard_map/ppermute | solution.py:738
  111.8 22.7 %collective-permute-start.23 = (bf16[5,16,2048]{2,1,0:T(8,128)(2,1)S(1)}, bf16[5,16,2048]{2,1,0:T(8,128)(2,1)S(1)}, u32[]{:S(2)}, u32[]{:S(2)}) collective-permute-start(bf16[5,16,2048]{2,1,0:T(8,128)(2,1)S(1)} %get-tuple-element.63), channel_id=1, source_target_pairs={{0,2},{1,3},{2,0},{3,1},{4,6},{5,7},{6,4},{7,5},{8,10},{9,11},{10,... | collective-permute-start | bytes 983048 | tf_op jit(solution)/shard_map/ppermute | solution.py:738
  114.8 32.2 %collective-permute-start.29 = (bf16[3,128,512]{2,1,0:T(8,128)(2,1)}, bf16[3,128,512]{2,1,0:T(8,128)(2,1)}, u32[]{:S(2)}, u32[]{:S(2)}) collective-permute-start(bf16[3,128,512]{2,1,0:T(8,128)(2,1)} %slice.8), channel_id=1, source_target_pairs={{0,16},{8,24},{16,32},{24,40},{32,48},{40,56},{48,0},{56,8},{1,17}... | collective-permute-start | bytes 1179656 | tf_op jit(solution)/shard_map/ppermute | solution.py:730
  116.8 31.2 %collective-permute-start.30 = (bf16[3,128,512]{2,1,0:T(8,128)(2,1)}, bf16[3,128,512]{2,1,0:T(8,128)(2,1)}, u32[]{:S(2)}, u32[]{:S(2)}) collective-permute-start(bf16[3,128,512]{2,1,0:T(8,128)(2,1)} %slice.9), channel_id=1, source_target_pairs={{0,48},{8,56},{16,0},{24,8},{32,16},{40,24},{48,32},{56,40},{1,49}... | collective-permute-start | bytes 1179656 | tf_op jit(solution)/shard_map/ppermute | solution.py:731
  120.0 36.0 %collective-permute-start.14 = (bf16[2,32,4096]{2,1,0:T(8,128)(2,1)}, bf16[2,32,4096]{2,1,0:T(8,128)(2,1)}, u32[]{:S(2)}, u32[]{:S(2)}) collective-permute-start(bf16[2,32,4096]{2,1,0:T(8,128)(2,1)} %get-tuple-element.50), channel_id=1, source_target_pairs={{0,2},{1,3},{2,0},{3,1},{4,6},{5,7},{6,4},{7,5},{8,10},{9,11},{10,... | collective-permute-start | bytes 1572872 | tf_op jit(solution)/shard_map/ppermute | solution.py:715
  136.9 6.0 %collective-permute-start.26 = (bf16[3,16,2048]{2,1,0:T(8,128)(2,1)}, bf16[3,16,2048]{2,1,0:T(8,128)(2,1)}, u32[]{:S(2)}, u32[]{:S(2)}) collective-permute-start(bf16[3,16,2048]{2,1,0:T(8,128)(2,1)} %get-tuple-element.65.refs_0_), channel_id=1, source_target_pairs={{0,4},{1,5},{2,6},{3,7},{4,0},{5,1},{6,2},{7,3},{8,12},{9,13},{10,... | collective-permute-start | bytes 589832 | tf_op jit(solution)/shard_map/ppermute | solution.py:740
  143.8 1.3 collective-permute-start.34
  145.1 14.7 %collective-permute-start.37 = (f32[1,4096]{1,0:T(1,128)S(1)}, f32[1,4096]{1,0:T(1,128)S(1)}, u32[]{:S(2)}, u32[]{:S(2)}) collective-permute-start(f32[1,4096]{1,0:T(1,128)S(1)} %add.106), channel_id=1, source_target_pairs={{0,32},{8,40},{16,48},{24,56},{32,0},{40,8},{48,16},{56,24},{1,33}... | collective-permute-start | bytes 49160 | tf_op jit(solution)/shard_map/ppermute | solution.py:745
  145.9 16.0 %collective-permute-start.36 = (f32[1,4096]{1,0:T(1,128)S(1)}, f32[1,4096]{1,0:T(1,128)S(1)}, u32[]{:S(2)}, u32[]{:S(2)}) collective-permute-start(f32[1,4096]{1,0:T(1,128)S(1)} %add.106), channel_id=1, source_target_pairs={{0,48},{8,56},{16,0},{24,8},{32,16},{40,24},{48,32},{56,40},{1,49}... | collective-permute-start | bytes 49160 | tf_op jit(solution)/shard_map/ppermute | solution.py:745
  147.0 15.0 %collective-permute-start.35 = (f32[1,4096]{1,0:T(1,128)S(1)}, f32[1,4096]{1,0:T(1,128)S(1)}, u32[]{:S(2)}, u32[]{:S(2)}) collective-permute-start(f32[1,4096]{1,0:T(1,128)S(1)} %add.106), channel_id=1, source_target_pairs={{0,16},{8,24},{16,32},{24,40},{32,48},{40,56},{48,0},{56,8},{1,17}... | collective-permute-start | bytes 49160 | tf_op jit(solution)/shard_map/ppermute | solution.py:745
  155.9 43.2 %collective-permute-start.40 = (bf16[3,512,512]{2,1,0:T(8,128)(2,1)S(1)}, bf16[3,512,512]{2,1,0:T(8,128)(2,1)S(1)}, u32[]{:S(2)}, u32[]{:S(2)}) collective-permute-start(bf16[3,512,512]{2,1,0:T(8,128)(2,1)S(1)} %weight_shares.2.refs_1_.refs_0_), channel_id=1, source_target_pairs={{0,8},{8,0},{16,24},{24,16},{32,40},{40,32},{48,56},{56,48},{1,9},... | collective-permute-start | bytes 4718600 | tf_op jit(solution)/shard_map/ppermute | solution.py:756
  156.0 23.3 %collective-permute-start.38 = (bf16[512,512]{1,0:T(8,128)(2,1)S(1)}, bf16[512,512]{1,0:T(8,128)(2,1)S(1)}, u32[]{:S(2)}, u32[]{:S(2)}) collective-permute-start(bf16[512,512]{1,0:T(8,128)(2,1)S(1)} %copy-done.28), channel_id=1, source_target_pairs={{0,48},{8,56},{16,0},{24,8},{32,16},{40,24},{48,32},{56,40},{1,49}... | collective-permute-start | bytes 1572872 | tf_op jit(solution)/shard_map/ppermute | solution.py:724
  159.7 17.6 %copy-start.26 = (bf16[32,4096]{1,0:T(8,128)(2,1)S(1)}, bf16[32,4096]{1,0:T(8,128)(2,1)}, u32[]{:S(2)}) copy-start(bf16[32,4096]{1,0:T(8,128)(2,1)} %copy-done.25) | copy-start | bytes 786436
  159.8 34.7 %copy-start.24 = (f32[512,512]{1,0:T(8,128)S(1)}, f32[512,512]{1,0:T(8,128)}, u32[]{:S(2)}) copy-start(f32[512,512]{1,0:T(8,128)} %copy-done.23) | copy-start | bytes 3145732
  159.8 8.7 %collective-permute-start.25 = (bf16[32,4096]{1,0:T(8,128)(2,1)S(1)}, bf16[32,4096]{1,0:T(8,128)(2,1)S(1)}, u32[]{:S(2)}, u32[]{:S(2)}) collective-permute-start(bf16[32,4096]{1,0:T(8,128)(2,1)S(1)} %get-tuple-element.67), channel_id=1, source_target_pairs={{0,4},{1,5},{2,6},{3,7},{4,0},{5,1},{6,2},{7,3},{8,12},{9,13},{10,... | collective-permute-start | bytes 786440 | tf_op jit(solution)/shard_map/ppermute | solution.py:757
  161.9 6.6 %collective-permute-start.31 = (bf16[32,2048]{1,0:T(8,128)(2,1)S(1)}, bf16[32,2048]{1,0:T(8,128)(2,1)S(1)}, u32[]{:S(2)}, u32[]{:S(2)}) collective-permute-start(bf16[32,2048]{1,0:T(8,128)(2,1)S(1)} %get-tuple-element.72), channel_id=1, source_target_pairs={{0,3},{1,0},{2,1},{3,2},{4,7},{5,4},{6,5},{7,6},{8,11},{9,8},{10,9... | collective-permute-start | bytes 393224 | tf_op jit(solution)/shard_map/ppermute | solution.py:750
  162.0 8.9 %collective-permute-start.32 = (bf16[32,2048]{1,0:T(8,128)(2,1)S(1)}, bf16[32,2048]{1,0:T(8,128)(2,1)S(1)}, u32[]{:S(2)}, u32[]{:S(2)}) collective-permute-start(bf16[32,2048]{1,0:T(8,128)(2,1)S(1)} %get-tuple-element.73), channel_id=1, source_target_pairs={{0,1},{1,2},{2,3},{3,0},{4,5},{5,6},{6,7},{7,4},{8,9},{9,10},{10,1... | collective-permute-start | bytes 393224 | tf_op jit(solution)/shard_map/ppermute | solution.py:750
  168.6 25.9 %collective-permute-start.39 = (bf16[512,512]{1,0:T(8,128)(2,1)S(1)}, bf16[512,512]{1,0:T(8,128)(2,1)S(1)}, u32[]{:S(2)}, u32[]{:S(2)}) collective-permute-start(bf16[512,512]{1,0:T(8,128)(2,1)S(1)} %copy-done.47), channel_id=1, source_target_pairs={{0,16},{8,24},{16,32},{24,40},{32,48},{40,56},{48,0},{56,8},{1,17}... | collective-permute-start | bytes 1572872 | tf_op jit(solution)/shard_map/ppermute | solution.py:724
  168.6 25.9 %collective-permute-start.41 = (bf16[512,512]{1,0:T(8,128)(2,1)S(1)}, bf16[512,512]{1,0:T(8,128)(2,1)S(1)}, u32[]{:S(2)}, u32[]{:S(2)}) collective-permute-start(bf16[512,512]{1,0:T(8,128)(2,1)S(1)} %copy-done.45), channel_id=1, source_target_pairs={{0,32},{8,40},{16,48},{24,56},{32,0},{40,8},{48,16},{56,24},{1,33}... | collective-permute-start | bytes 1572872 | tf_op jit(solution)/shard_map/ppermute | solution.py:724
  170.8 6.5 %collective-permute-start.33 = (bf16[32,2048]{1,0:T(8,128)(2,1)S(1)}, bf16[32,2048]{1,0:T(8,128)(2,1)S(1)}, u32[]{:S(2)}, u32[]{:S(2)}) collective-permute-start(bf16[32,2048]{1,0:T(8,128)(2,1)S(1)} %get-tuple-element.74), channel_id=1, source_target_pairs={{0,2},{1,3},{2,0},{3,1},{4,6},{5,7},{6,4},{7,5},{8,10},{9,11},{10,... | collective-permute-start | bytes 393224 | tf_op jit(solution)/shard_map/ppermute | solution.py:750
  (44 other events, 157.8 us)

commit v7 on v6

--- a/solution.py
+++ b/solution.py
@@ -74,6 +74,16 @@
     return lax.dot_general(left, right, (((0,), (0,)), ((), ())), preferred_element_type=f32)
 
 
+def where_am_i():
+    tp, seq = lax.axis_index("tp"), lax.axis_index("seq")
+    return tp >> 2, tp & 3, seq >> 1, seq & 1, lax.axis_index("grp")
+
+
+def valid_rows():
+    used = jnp.logical_or(lax.axis_index("grp") == 0, lax.axis_index("tp") * ROWS < LI)
+    return jnp.where(used, 1.0, 0.0).astype(f32)
+
+
 def load(sources, targets, sems):
     copies = [
         pltpu.make_async_copy(source, target, sems.at[i])
@@ -102,26 +112,26 @@
     return [ref.at[pl.ds(i * KCUT, KCUT)] for i in range(KCUTS)]
 
 
-def norm_kernel(valid, x, gain, cot, n_left, n_right, grad, inv):
+def norm_kernel(x, gain, cot, n_left, n_right, grad, inv):
     x_float = x[...].astype(f32)
     scale = lax.rsqrt(jnp.mean(x_float * x_float, axis=1, keepdims=True) + 1e-05)
     normed = (x_float * scale * gain[...].astype(f32)).astype(bf16)
     n_left[...] = normed[:, :HALF]
     n_right[...] = normed[:, HALF:]
-    grad[...] = (cot[...].astype(f32) * valid[0]).astype(bf16)
+    grad[...] = (cot[...].astype(f32) * valid_rows()).astype(bf16)
     inv[...] = jnp.broadcast_to(scale, (ROWS, 128))
 
 
-def norm_rows(valid, x, gain, cot):
+def norm_rows(x, gain, cot):
     part = sds((ROWS, HALF), bf16)
     return call(
         norm_kernel,
         [part, part, sds((ROWS, WIDTH), bf16), sds((ROWS, 128), f32)],
         vmem=4,
         nbytes=4 * ROWS * WIDTH * 2,
-        in_specs=[SMEM] + [VMEM] * 3,
+        in_specs=[VMEM] * 3,
         name="norm_rows",
-    )(valid, x, gain, cot)
+    )(x, gain, cot)
 
 
 def gather_blocks(left, right):
@@ -515,28 +525,30 @@
     return (x_from * 4 + z_from) * ROWS + (row - block * ROWS)
 
 
-def places(meta, rows, is_text):
-    slot = slot_of(rows, meta[10], meta[11])
+def places(gaps, runs, rows, is_text):
+    x_index, z_index = where_am_i()[:2]
+    slot = slot_of(rows, x_index, z_index)
     text = slot
     end = jnp.int32(0)
     for run in range(4):
-        end = end + meta[run]
-        text = text + jnp.where(slot >= end, meta[5 + run], 0)
-    image = slot + meta[0]
+        end = end + gaps[0, run]
+        text = text + jnp.where(slot >= end, runs[0, run], 0)
+    image = slot + gaps[0, 0]
     end = jnp.int32(0)
     for run in range(3):
-        end = end + meta[5 + run]
-        image = image + jnp.where(slot >= end, meta[run + 1], 0)
+        end = end + runs[0, run]
+        image = image + jnp.where(slot >= end, gaps[0, run + 1], 0)
     image = jnp.where(slot < LI, image, FAR)
     return jnp.where(is_text, text, image)
 
 
-def admitted(meta):
-    group = meta[9]
-    query = places(meta, lax.broadcasted_iota(jnp.int32, (SLOTS, 1), 0), group == 0)
+def admitted(gaps, runs):
+    group = lax.axis_index("grp")
+    rows = lax.broadcasted_iota(jnp.int32, (SLOTS, 1), 0)
+    query = places(gaps, runs, rows, group == 0)
     key_row = lax.broadcasted_iota(jnp.int32, (1, SLOTS), 1)
-    own = places(meta, key_row, group == 0)
-    other = places(meta, key_row, group != 0)
+    own = places(gaps, runs, key_row, group == 0)
+    other = places(gaps, runs, key_row, group != 0)
     return own <= query, other <= query
 
 
@@ -554,9 +566,9 @@
     return own * share, other * share
 
 
-def forward_kernel(meta, query, own_kv, other_kv, *refs):
+def forward_kernel(gaps, runs, query, own_kv, other_kv, *refs):
     mixed = refs[-1]
-    own_ok, other_ok = admitted(meta)
+    own_ok, other_ok = admitted(gaps, runs)
     for head in range(HEADS):
         cols = slice(head * HS, (head + 1) * HS)
         own, other = head_attn(
@@ -567,10 +579,10 @@
         mixed[:, cols] = total.astype(bf16)
 
 
-def backward_kernel(meta, query, own_kv, other_kv, mixed, grad, *refs):
+def backward_kernel(gaps, runs, query, own_kv, other_kv, mixed, grad, *refs):
     q_grad, own_grad, other_grad = refs[-3:]
     scale = HS ** (-0.5)
-    own_ok, other_ok = admitted(meta)
+    own_ok, other_ok = admitted(gaps, runs)
     for head in range(HEADS):
         cols = slice(head * HS, (head + 1) * HS)
         q, g = query[:, cols], grad[:, cols]
@@ -592,20 +604,20 @@
 ATTN_FLOPS = 2 * HEADS * SLOTS * 2 * SLOTS * HS
 
 
-def attend_forward(meta, query, own_kv, other_kv, after):
+def attend_forward(spans, query, own_kv, other_kv, after):
     return call(
         forward_kernel,
         sds((SLOTS, COLS), bf16),
         vmem=10,
         flops=4 * ATTN_FLOPS,
         nbytes=6 * SLOTS * COLS * 2,
-        in_specs=[SMEM] + [VMEM] * 3 + [ANY] * len(after),
+        in_specs=[SMEM] * 2 + [VMEM] * 3 + [ANY] * len(after),
         out_specs=VMEM,
         name="attend_forward",
-    )(meta, query, own_kv, other_kv, *after)
-
-
-def attend_backward(meta, query, own_kv, other_kv, mixed, grad, after):
+    )(*spans, query, own_kv, other_kv, *after)
+
+
+def attend_backward(spans, query, own_kv, other_kv, mixed, grad, after):
     kv = (2, SLOTS, COLS)
     return call(
         backward_kernel,
@@ -613,16 +625,18 @@
         vmem=14,
         flops=8 * ATTN_FLOPS,
         nbytes=12 * SLOTS * COLS * 2,
-        in_specs=[SMEM] + [VMEM] * 5 + [ANY] * len(after),
+        in_specs=[SMEM] * 2 + [VMEM] * 5 + [ANY] * len(after),
         out_specs=[VMEM] * 3,
         name="attend_backward",
-    )(meta, query, own_kv, other_kv, mixed, grad, *after)
-
-
-def out_kernel(order, grad, mixed, *refs):
+    )(*spans, query, own_kv, other_kv, mixed, grad, *after)
+
+
+def out_kernel(grad, mixed, *refs):
     own, sent = refs[-2:]
+    y_index, core = where_am_i()[2:4]
     for i in range(8):
-        start = pl.multiple_of(order[i] * COLS, COLS)
+        column = ((y_index - STEPS[i % 4]) & 3) * 2 + (1 - core if i < 4 else core)
+        start = pl.multiple_of(column * COLS, COLS)
         share = dot_tokens(grad[:, pl.ds(start, COLS)], mixed[...]).astype(bf16)
         if i < 4:
             sent[i] = share
@@ -630,24 +644,26 @@
             own[i - 4] = share
 
 
-def out_weight_parts(order, grad_full, mixed):
+def out_weight_parts(grad_full, mixed):
     return call(
         out_kernel,
         [sds((4, COLS, COLS), bf16)] * 2,
         vmem=12,
         flops=2 * SLOTS * WIDTH * COLS,
         nbytes=SLOTS * WIDTH * 2 + WIDTH * COLS * 2,
-        in_specs=[SMEM, VMEM, VMEM],
+        in_specs=[VMEM] * 2,
         out_specs=[VMEM] * 2,
         name="out_weight_parts",
-    )(order, grad_full, mixed)
-
-
-def share_kernel(which, columns, full, c1, c2, c3, g0, g1, g2, g3, g4, *refs):
+    )(grad_full, mixed)
+
+
+def share_kernel(which, full, c1, c2, c3, g0, g1, g2, g3, g4, *refs):
     out, lefts = refs[-2:]
-    start = pl.multiple_of(columns[which] * COLS, COLS)
+    y_index, core = where_am_i()[2:4]
+    column = core if which else 1 - core
+    start = pl.multiple_of((y_index * 2 + column) * COLS, COLS)
     lefts[0] = full[:, pl.ds(start, COLS)].T
-    start = pl.multiple_of(columns[2 + which] * COLS, COLS)
+    start = pl.multiple_of(column * COLS, COLS)
     for k, came in enumerate((c1, c2, c3), 1):
         lefts[k] = came[:, pl.ds(start, COLS)].T
     for part in range(3):
@@ -659,48 +675,63 @@
         out[part] = total.astype(out.dtype)
 
 
-def weight_shares(columns, which, full, came, grads, dtype, after=()):
+def weight_shares(which, full, came, grads, dtype, after=()):
     return call(
         functools.partial(share_kernel, which),
         sds((3, COLS, COLS), dtype),
         vmem=20,
         flops=3 * 4 * 2 * SLOTS * COLS * COLS,
         nbytes=16 * SLOTS * COLS * 2 + 3 * COLS * COLS * 4,
-        in_specs=[SMEM] + [VMEM] * 9 + [ANY] * len(after),
+        in_specs=[VMEM] * 9 + [ANY] * len(after),
         out_specs=VMEM,
         scratch_shapes=[pltpu.VMEM((4, COLS, SLOTS), bf16)],
         name="weight_shares",
-    )(columns, full, *came, *grads, *after)
-
-
-def chunks_over_y(full, y_index):
-    came = []
-    for k in STEPS[1:]:
-        sent = lax.dynamic_slice_in_dim(full, (y_index + k) % 4 * 1024, 1024, 1)
-        came.append(lax.ppermute(sent, "seq", y_shift(k)))
-    return came
+    )(full, *came, *grads, *after)
+
+
+def chunk_kernel(full, *outs):
+    y_index = where_am_i()[2]
+    for k, out in zip(STEPS[1:], outs):
+        start = pl.multiple_of(((y_index + k) & 3) * 1024, 1024)
+        out[...] = full[:, pl.ds(start, 1024)]
+
+
+def chunks_over_y(full):
+    sends = call(
+        chunk_kernel,
+        [sds((SLOTS, 1024), bf16)] * 3,
+        vmem=6,
+        nbytes=6 * SLOTS * 1024 * 2,
+        in_specs=[VMEM],
+        out_specs=[VMEM] * 3,
+        name="chunks",
+    )(full)
+    return [lax.ppermute(sent, "seq", y_shift(k)) for sent, k in zip(sends, STEPS[1:])]
+
+
+def layer_kernel(x, kept, came, *refs):
+    total = x[...].astype(f32) + (kept[...] + came[...].astype(f32))
+    refs[-1][...] = (total * valid_rows()).astype(bf16)
+
+
+def layer_rows(x, kept, came, after=()):
+    return call(
+        layer_kernel,
+        sds((ROWS, WIDTH), bf16),
+        vmem=4,
+        nbytes=5 * ROWS * WIDTH * 2,
+        in_specs=[VMEM] * 3 + [ANY] * len(after),
+        out_specs=VMEM,
+        name="layer_rows",
+    )(x, kept, came, *after)
 
 
 def per_device(tokens, text_gaps, image_runs, gains, w_qkv, w_out, cotangent):
-    group = lax.axis_index("grp")
-    tp_index = lax.axis_index("tp")
-    seq_index = lax.axis_index("seq")
-    x_index, z_index = tp_index // 4, tp_index % 4
-    y_index, core = seq_index // 2, seq_index % 2
     x_rows = tokens[0, 0]
     w_parts = jnp.transpose(w_qkv[0], (1, 0, 2))
-    valid = jnp.where((group == 0) | (tp_index * ROWS < LI), 1.0, 0.0).astype(f32)
-    meta = jnp.concatenate(
-        [text_gaps[0], image_runs[0], jnp.stack([group, x_index, z_index]).astype(jnp.int32)]
-    )
-
-    back_y = jnp.stack([(y_index - k) % 4 for k in STEPS]) * 2
-    out_order = jnp.concatenate([back_y + 1 - core, back_y + core]).astype(jnp.int32)
-    columns = jnp.stack(
-        [y_index * 2 + 1 - core, y_index * 2 + core, 1 - core, core]
-    ).astype(jnp.int32)
-
-    n_left, n_right, grad_rows, inv = norm_rows(valid.reshape(1), x_rows, gains, cotangent[0, 0])
+    spans = (text_gaps, image_runs)
+
+    n_left, n_right, grad_rows, inv = norm_rows(x_rows, gains, cotangent[0, 0])
     pieces = gather_blocks(n_left, n_right)
     grad_other = lax.ppermute(grad_rows, "tp", X_SWAP)
     grad_pair = jnp.stack([grad_rows, grad_other])
@@ -708,17 +739,17 @@
     normed_full, own_kv = key_value(pieces, w_parts, [grad_pair])
     other_kv = lax.ppermute(own_kv, "grp", GRP_SWAP)
     query = query_of(normed_full, w_parts, grad_pairs[1:3])
-    chunks = chunks_over_y(normed_full, y_index)
-
-    mixed = attend_forward(meta, query, own_kv, other_kv, [])
+    chunks = chunks_over_y(normed_full)
+
+    mixed = attend_forward(spans, query, own_kv, other_kv, [])
     proj = proj_parts(mixed, w_out)
     proj_came = [lax.ppermute(proj[i], "tp", z_shift(-STEPS[i])) for i in range(1, 4)]
     grad_full, grad_mixed = grad_mixed_of(grad_pairs, w_out, [proj[0]] + chunks[:2])
     q_grad, own_part, other_part = attend_backward(
-        meta, query, own_kv, other_kv, mixed, grad_mixed, []
+        spans, query, own_kv, other_kv, mixed, grad_mixed, []
     )
     back = lax.ppermute(other_part, "grp", GRP_SWAP)
-    out_own, out_sent = out_weight_parts(out_order, grad_full, mixed)
+    out_own, out_sent = out_weight_parts(grad_full, mixed)
     out_came = lax.ppermute(out_sent, "seq", CORE_SWAP)
     out_kept, *out_sends = sum_x(out_own, out_came)
     out_terms = [lax.ppermute(v, "seq", y_shift(-k)) for v, k in zip(out_sends, STEPS[1:])]
@@ -732,7 +763,9 @@
     ]
     grads = [own_grads, back_grads, next_grads] + far_grads
 
-    right = back_right(own_grads, w_parts, normed_full, chunks[2:])
+    right = back_right(
+        own_grads, w_parts, normed_full, chunks[2:] + proj_came[2:]
+    )
     right_x = lax.ppermute(right[1], "tp", X_SWAP)
     left = back_left(own_grads, w_parts, normed_full, right[2], [out_sends[0]])
     left_came = [lax.ppermute(left[i], "tp", z_shift(-STEPS[i])) for i in range(1, 4)]
@@ -744,19 +777,21 @@
     for k in STEPS[1:]:
         gain_grad = gain_grad + lax.ppermute(gain_sum, "seq", y_shift(k))
     shares = (normed_full, chunks, grads)
-    qkv_sent = weight_shares(columns, 0, *shares, bf16)
-    right_kept, *right_sends = sum_x(right[0], right_x, [left_x, qkv_sent])
-    proj_kept, proj_sent = sum_z(proj[0], proj_came, [left_sent])
+    qkv_sent = weight_shares(0, *shares, bf16)
+    right_kept, *right_sends = sum_x(
+        right[0], right_x, [left_x, qkv_sent] + out_terms[:2]
+    )
+    proj_kept, proj_sent = sum_z(proj[0], proj_came)
     right_came = [lax.ppermute(v, "tp", z_shift(-k)) for v, k in zip(right_sends, STEPS[1:])]
     tokens_grad = token_rows(
         x_rows, grad_rows, gains, inv, (left_kept, left_x), (right_kept, *right_came)
     )
 
-    qkv_mine = weight_shares(columns, 1, *shares, f32, [qkv_sent, right_came[0]] + out_terms[:2])
+    qkv_mine = weight_shares(1, *shares, f32, [qkv_sent, right_sends[0]])
     qkv_share = qkv_mine + lax.ppermute(qkv_sent, "seq", CORE_SWAP).astype(f32)
-    proj_rows = proj_kept + lax.ppermute(proj_sent, "tp", X_SWAP).astype(f32)
-    layer_out = ((x_rows.astype(f32) + proj_rows) * valid).astype(bf16)
-    out_share = sum_rest(out_kept, out_terms, right_came[:2])
+    proj_x = lax.ppermute(proj_sent, "tp", X_SWAP)
+    layer_out = layer_rows(x_rows, proj_kept, proj_x)
+    out_share = sum_rest(out_kept, out_terms, right_came[:1])
     return (
         layer_out[None, None],
         tokens_grad[None, None],

time: 202 us -> 172 us (0.85)
  local copies, waits for them, and re-layouts: 27.8 us -> 7.27 us
  Pallas kernels: 39.1 us -> 32.7 us
  waiting for transfers between devices: 69.3 us -> 63.6 us
  starting transfers between devices: 59.8 us -> 64.1 us
    unnamed x100 -> x20, local copies, waits for them, and re-layouts: 26 us -> 7.21 us
    ppermute x3, waiting for transfers between devices: 15.2 us -> 0.01 us  [per_device(): lax.ppermute(v, 'seq', y_shift(-k))]
    ppermute x3, waiting for transfers between devices: 0.01 us -> 8.36 us  [per_device(): gain_grad = gain_grad + lax.ppermute(gain_sum, 'seq', y_shift(k))]
    ppermute x3, waiting for transfers between devices: 13.8 us -> 8.49 us  [per_device(): lax.ppermute(left[i], 'tp', z_shift(-STEPS[i]))]
    ppermute x1, waiting for transfers between devices: 4.36 us -> 9.05 us  [per_device(): back_grads = lax.ppermute(own_grads, 'seq', y_shift(1))]
    ppermute x4, waiting for transfers between devices: 3.96 us -> 0.01 us  [the longest x3 0.01 us: chunks_over_y(): lax.ppermute(sent, 'seq', y_shift(k))]
    ppermute x3, waiting for transfers between devices: 3.62 us -> 7.35 us  [per_device(): lax.ppermute(proj[i], 'tp', z_shift(-STEPS[i]))]
    ppermute x3, starting transfers between devices: 2.03 us -> 5.12 us  [per_device(): lax.ppermute(v, 'tp', z_shift(-k))]
  transfers between devices with their start and end apart: 42 -> 42, of which waited for: 17 -> 21; matrix products, arithmetic and copies ran while one was open for 2% -> 0% of each run, Pallas kernels for 17% -> 17%
where the time goes in v7:
time: 172 us
  starting transfers between devices  64.1 us (37%)
  waiting for transfers between devices  63.6 us (37%)
  Pallas kernels  32.7 us (19%)
  local copies, waits for them, and re-layouts  7.27 us (4%)
  other arithmetic  3.03 us (2%)
    ppermute x1, waiting for transfers between devices, per_device(): back_grads = lax.ppermute(own_grads, 'seq', y_shift(1))  9.05 us
    ppermute x3, waiting for transfers between devices, per_device(): lax.ppermute(left[i], 'tp', z_shift(-STEPS[i]))  8.49 us
    ppermute x3, waiting for transfers between devices, per_device(): gain_grad = gain_grad + lax.ppermute(gain_sum, 'seq', y_shift(k))  8.36 us
    ppermute x3, waiting for transfers between devices, gather_blocks(): lax.ppermute(right_pair, 'tp', z_shift(k))  7.78 us
    ppermute x1, waiting for transfers between devices, per_device(): left_x = lax.ppermute(left_sent, 'tp', X_SWAP)  7.57 us
    ppermute x3, waiting for transfers between devices, per_device(): lax.ppermute(proj[i], 'tp', z_shift(-STEPS[i]))  7.35 us
    unnamed x20, local copies, waits for them, and re-layouts  7.21 us
    ppermute x3, starting transfers between devices, per_device(): lax.ppermute(proj[i], 'tp', z_shift(-STEPS[i]))  7.03 us
  transfers between devices with their start and end apart: 42, of which 21 were waited for; matrix products, arithmetic and copies ran while one was open for 0% of the time, Pallas kernels for 17%

profile of v7, /device:TPU:0, one launch (start us, length us, event | category | flops | bytes accessed | tf_op | source)
XLA Modules:
  0.0 171.6 jit_solution(6396091325881716049)
XLA Ops:
  3.5 1.7 collective-permute-start.4
  5.1 3.9 %collective-permute-start.2 = (bf16[32,2048]{1,0:T(8,128)(2,1)S(1)}, bf16[32,2048]{1,0:T(8,128)(2,1)S(1)}, u32[]{:S(2)}, u32[]{:S(2)}) collective-permute-start(bf16[32,2048]{1,0:T(8,128)(2,1)S(1)} %get-tuple-element.45), channel_id=1, source_target_pairs={{0,2},{1,3},{2,0},{3,1},{4,6},{5,7},{6,4},{7,5},{8,10},{9,11},{10,... | collective-permute-start | bytes 393224 | tf_op jit(solution)/shard_map/ppermute | solution.py:139
  9.7 1.3 collective-permute-start
  12.8 4.3 %collective-permute-start.6 = (bf16[2,32,2048]{2,1,0:T(8,128)(2,1)S(1)}, bf16[2,32,2048]{2,1,0:T(8,128)(2,1)S(1)}, u32[]{:S(2)}, u32[]{:S(2)}) collective-permute-start(bf16[2,32,2048]{2,1,0:T(8,128)(2,1)S(1)} %pad_maximum_fusion.2.refs_2_), channel_id=1, source_target_pairs={{0,3},{1,0},{2,1},{3,2},{4,7},{5,4},{6,5},{7,6},{8,11},{9,8},{10,9... | collective-permute-start | bytes 786440 | tf_op jit(solution)/shard_map/ppermute | solution.py:140
  18.0 2.3 %collective-permute-start.9 = (bf16[2,32,4096]{2,1,0:T(8,128)(2,1)S(1)}, bf16[2,32,4096]{2,1,0:T(8,128)(2,1)S(1)}, u32[]{:S(2)}, u32[]{:S(2)}) collective-permute-start(bf16[2,32,4096]{2,1,0:T(8,128)(2,1)S(1)} %pad_maximum_fusion.1.refs_7_.p0), channel_id=1, source_target_pairs={{0,1},{1,2},{2,3},{3,0},{4,5},{5,6},{6,7},{7,4},{8,9},{9,10},{10,1... | collective-permute-start | bytes 1572872 | tf_op jit(solution)/shard_map/ppermute | solution.py:738
  20.3 7.8 %collective-permute-done.5.refs_3_ = bf16[2,32,2048]{2,1,0:T(8,128)(2,1)S(1)} collective-permute-done((bf16[2,32,2048]{2,1,0:T(8,128)(2,1)S(1)}, bf16[2,32,2048]{2,1,0:T(8,128)(2,1)S(1)}, u32[]{:S(2)}, u32[]{:S(2)}) %collective-permute-start.5) | collective-permute-done | bytes 262176 | tf_op jit(solution)/shard_map/ppermute | solution.py:140
  29.3 4.6 %copy-done = bf16[1,4096,3,512]{3,1,2,0:T(8,128)(2,1)S(1)} copy-done((bf16[1,4096,3,512]{3,1,2,0:T(8,128)(2,1)S(1)}, bf16[1,4096,3,512]{3,1,2,0:T(8,128)(2,1)}, u32[]{:S(2)}) %copy-start) | copy-done | bytes 12582936
  33.9 3.7 %key_value.1 = (bf16[256,4096]{1,0:T(8,128)(2,1)S(1)}, bf16[2,256,512]{2,1,0:T(8,128)(2,1)S(1)}) custom-call(bf16[4,32,2048]{2,1,0:T(8,128)(2,1)S(1)} %pad_maximum_fusion.refs_0_, bf16[4,32,2048]{2,1,0:T(8,128)(2,1)S(1)} %collective-permute-done.3.refs_1_, bf16[2,32,2048]{2,1,0:T(8,128)(2,1)S(1)} %pad_maximum_fusion.2.refs_2_, ...), custom_call_target="tpu_custom_call" | custom-call | flops 2147483648 | bytes 12582912 | tf_op jit(solution)/shard_map/key_value/pallas_call | solution.py:334
  37.5 2.8 %collective-permute-start.11 = (bf16[2,256,512]{2,1,0:T(8,128)(2,1)S(1)}, bf16[2,256,512]{2,1,0:T(8,128)(2,1)S(1)}, u32[]{:S(2)}, u32[]{:S(2)}) collective-permute-start(bf16[2,256,512]{2,1,0:T(8,128)(2,1)S(1)} %get-tuple-element.49.own_kv), channel_id=1, source_target_pairs={{0,64},{64,0},{1,65},{65,1},{2,66},{66,2},{3,67},{67,3},{4,68},{68... | collective-permute-start | bytes 1572872 | tf_op jit(solution)/shard_map/ppermute | solution.py:740
  40.4 2.5 %collective-permute-start.16 = (bf16[2,32,4096]{2,1,0:T(8,128)(2,1)S(1)}, bf16[2,32,4096]{2,1,0:T(8,128)(2,1)S(1)}, u32[]{:S(2)}, u32[]{:S(2)}) collective-permute-start(bf16[2,32,4096]{2,1,0:T(8,128)(2,1)S(1)} %pad_maximum_fusion.1.refs_7_.p0), channel_id=1, source_target_pairs={{0,2},{1,3},{2,0},{3,1},{4,6},{5,7},{6,4},{7,5},{8,10},{9,11},{10,... | collective-permute-start | bytes 1572872 | tf_op jit(solution)/shard_map/ppermute | solution.py:738
  42.9 1.6 collective-permute-start.17
  44.6 1.9 %collective-permute-start.18 = (bf16[256,1024]{1,0:T(8,128)(2,1)S(1)}, bf16[256,1024]{1,0:T(8,128)(2,1)S(1)}, u32[]{:S(2)}, u32[]{:S(2)}) collective-permute-start(bf16[256,1024]{1,0:T(8,128)(2,1)S(1)} %get-tuple-element.58), channel_id=1, source_target_pairs={{0,48},{8,56},{16,0},{24,8},{32,16},{40,24},{48,32},{56,40},{1,49}... | collective-permute-start | bytes 1572872 | tf_op jit(solution)/shard_map/ppermute | solution.py:709
  46.5 1.8 %query.1 = bf16[256,512]{1,0:T(8,128)(2,1)S(1)} custom-call(bf16[256,4096]{1,0:T(8,128)(2,1)S(1)} %get-tuple-element.48.full.normed, bf16[3,4096,512]{2,1,0:T(8,128)(2,1)S(1)} %bitcast.21, bf16[2,32,4096]{2,1,0:T(8,128)(2,1)S(1)} %collective-permute-done.9.refs_0_.p1, bf16[2,32,4096]{2,1,0:T(8,128)(2,1)S(1)} %collective-permute-done.10.refs_1_.p2), custom_call_target="tpu_custom_call" | custom-call | flops 1073741824 | bytes 6291456 | tf_op jit(solution)/shard_map/query/pallas_call | solution.py:360
  48.2 1.7 collective-permute-done.11.other_kv
  49.9 2.4 %attend_forward.1.left.mixed = bf16[256,512]{1,0:T(8,128)(2,1)S(1)} custom-call(s32[1,5]{1,0:T(1,128)S(1)} %copy-done.8, s32[1,4]{1,0:T(1,128)S(1)} %copy-done.9, bf16[256,512]{1,0:T(8,128)(2,1)S(1)} %query.1, bf16[2,256,512]{2,1,0:T(8,128)(2,1)S(1)} %get-tuple-element.49.own_kv, bf16[2,256,512]{2,1,0:T(8,128)(2,1)S(1)} %collective-permute-done.11.other_kv), custom_call_target="tpu_custom_call" | custom-call | flops 536870912 | bytes 1572864 | tf_op jit(solution)/shard_map/attend_forward/pallas_call | solution.py:608
  52.4 2.2 %proj_parts.1 = (bf16[2,32,4096]{2,1,0:T(8,128)(2,1)S(1)}, bf16[2,32,4096]{2,1,0:T(8,128)(2,1)S(1)}, bf16[2,32,4096]{2,1,0:T(8,128)(2,1)S(1)}, bf16[2,32,4096]{2,1,0:T(8,128)(2,1)S(1)}) custom-call(bf16[256,512]{1,0:T(8,128)(2,1)S(1)} %attend_forward.1.left.mixed, bf16[1,4096,512]{2,1,0:T(8,128)(2,1)S(1)} %copy-done.2), custom_call_target="tpu_custom_call" | custom-call | flops 1073741824 | bytes 6291456 | tf_op jit(solution)/shard_map/proj_parts/pallas_call | solution.py:504
  54.6 1.9 %grad_mixed.1 = (bf16[256,4096]{1,0:T(8,128)(2,1)S(1)}, bf16[256,512]{1,0:T(8,128)(2,1)S(1)}) custom-call(bf16[2,32,4096]{2,1,0:T(8,128)(2,1)S(1)} %pad_maximum_fusion.1.refs_7_.p0, bf16[2,32,4096]{2,1,0:T(8,128)(2,1)S(1)} %collective-permute-done.9.refs_0_.p1, bf16[2,32,4096]{2,1,0:T(8,128)(2,1)S(1)} %collective-permute-done.10.refs_1_.p2, ...), custom_call_target="tpu_custom_call" | custom-call | flops 1073741824 | bytes 8388608 | tf_op jit(solution)/shard_map/grad_mixed/pallas_call | solution.py:383
  56.5 1.3 out_weight_parts.1
  57.9 5.4 %collective-permute-start.12 = (bf16[2,32,4096]{2,1,0:T(8,128)(2,1)S(1)}, bf16[2,32,4096]{2,1,0:T(8,128)(2,1)S(1)}, u32[]{:S(2)}, u32[]{:S(2)}) collective-permute-start(bf16[2,32,4096]{2,1,0:T(8,128)(2,1)S(1)} %get-tuple-element.51), channel_id=1, source_target_pairs={{0,3},{1,0},{2,1},{3,2},{4,7},{5,4},{6,5},{7,6},{8,11},{9,8},{10,9... | collective-permute-start | bytes 1572872 | tf_op jit(solution)/shard_map/ppermute | solution.py:746
  63.3 4.3 %attend_backward.1 = (bf16[256,512]{1,0:T(8,128)(2,1)S(1)}, f32[2,256,512]{2,1,0:T(8,128)S(1)}, bf16[2,256,512]{2,1,0:T(8,128)(2,1)S(1)}) custom-call(s32[1,5]{1,0:T(1,128)S(1)} %copy-done.8, s32[1,4]{1,0:T(1,128)S(1)} %copy-done.9, bf16[256,512]{1,0:T(8,128)(2,1)S(1)} %query.1, bf16[2,256,512]{2,1,0:T(8,128)(2,1)S(1)} %get-tuple-element.49.own_kv, ...), custom_call_target="tpu_custom_call" | custom-call | flops 1073741824 | bytes 3145728 | tf_op jit(solution)/shard_map/attend_backward/pallas_call | solution.py:622
  67.6 2.7 %collective-permute-start.19 = (bf16[2,256,512]{2,1,0:T(8,128)(2,1)S(1)}, bf16[2,256,512]{2,1,0:T(8,128)(2,1)S(1)}, u32[]{:S(2)}, u32[]{:S(2)}) collective-permute-start(bf16[2,256,512]{2,1,0:T(8,128)(2,1)S(1)} %get-tuple-element.62), channel_id=1, source_target_pairs={{0,64},{64,0},{1,65},{65,1},{2,66},{66,2},{3,67},{67,3},{4,68},{68... | collective-permute-start | bytes 1572872 | tf_op jit(solution)/shard_map/ppermute | solution.py:751
  70.3 3.2 %collective-permute-start.20 = (bf16[256,1024]{1,0:T(8,128)(2,1)S(1)}, bf16[256,1024]{1,0:T(8,128)(2,1)S(1)}, u32[]{:S(2)}, u32[]{:S(2)}) collective-permute-start(bf16[256,1024]{1,0:T(8,128)(2,1)S(1)} %get-tuple-element.65), channel_id=1, source_target_pairs={{0,32},{8,40},{16,48},{24,56},{32,0},{40,8},{48,16},{56,24},{1,33}... | collective-permute-start | bytes 1572872 | tf_op jit(solution)/shard_map/ppermute | solution.py:709
  73.5 2.2 %collective-permute-done.12.c1.refs_1_ = bf16[2,32,4096]{2,1,0:T(8,128)(2,1)S(1)} collective-permute-done((bf16[2,32,4096]{2,1,0:T(8,128)(2,1)S(1)}, bf16[2,32,4096]{2,1,0:T(8,128)(2,1)S(1)}, u32[]{:S(2)}, u32[]{:S(2)}) %collective-permute-start.12) | collective-permute-done | bytes 524320 | tf_op jit(solution)/shard_map/ppermute | solution.py:746
  75.7 1.6 collective-permute-start.14
  77.3 1.2 collective-permute-done.13.c2.refs_2_
  78.5 4.6 %collective-permute-done.19.came = bf16[2,256,512]{2,1,0:T(8,128)(2,1)S(1)} collective-permute-done((bf16[2,256,512]{2,1,0:T(8,128)(2,1)S(1)}, bf16[2,256,512]{2,1,0:T(8,128)(2,1)S(1)}, u32[]{:S(2)}, u32[]{:S(2)}) %collective-permute-start.19) | collective-permute-done | bytes 524320 | tf_op jit(solution)/shard_map/ppermute | solution.py:751
  83.3 1.6 collective-permute-start.27
  84.9 1.9 %collective-permute-start.28 = (bf16[3,256,512]{2,1,0:T(8,128)(2,1)S(1)}, bf16[3,256,512]{2,1,0:T(8,128)(2,1)S(1)}, u32[]{:S(2)}, u32[]{:S(2)}) collective-permute-start(bf16[3,256,512]{2,1,0:T(8,128)(2,1)S(1)} %sum_keys.1.grads.g0), channel_id=1, source_target_pairs={{0,48},{8,56},{16,0},{24,8},{32,16},{40,24},{48,32},{56,40},{1,49}... | collective-permute-start | bytes 2359304 | tf_op jit(solution)/shard_map/ppermute | solution.py:759
  86.9 4.0 %collective-permute-done.14.c3.refs_1_ = bf16[2,32,4096]{2,1,0:T(8,128)(2,1)S(1)} collective-permute-done((bf16[2,32,4096]{2,1,0:T(8,128)(2,1)S(1)}, bf16[2,32,4096]{2,1,0:T(8,128)(2,1)S(1)}, u32[]{:S(2)}, u32[]{:S(2)}) %collective-permute-start.14) | collective-permute-done | bytes 524320 | tf_op jit(solution)/shard_map/ppermute | solution.py:746
  90.9 3.1 %back_right.1 = (bf16[4,32,2048]{2,1,0:T(8,128)(2,1)S(1)}, bf16[4,32,2048]{2,1,0:T(8,128)(2,1)S(1)}, f32[1,2048]{1,0:T(1,128)S(1)}) custom-call(bf16[3,256,512]{2,1,0:T(8,128)(2,1)S(1)} %sum_keys.1.grads.g0, bf16[3,4096,512]{2,1,0:T(8,128)(2,1)S(1)} %bitcast.22, bf16[256,4096]{1,0:T(8,128)(2,1)S(1)} %get-tuple-element.48.full.normed, ...), custom_call_target="tpu_custom_call" | custom-call | flops 1610612736 | bytes 8388608 | tf_op jit(solution)/shard_map/back_right/pallas_call | solution.py:464
  94.6 9.0 %collective-permute-done.27.g1 = bf16[3,256,512]{2,1,0:T(8,128)(2,1)S(1)} collective-permute-done((bf16[3,256,512]{2,1,0:T(8,128)(2,1)S(1)}, bf16[3,256,512]{2,1,0:T(8,128)(2,1)S(1)}, u32[]{:S(2)}, u32[]{:S(2)}) %collective-permute-start.27) | collective-permute-done | bytes 786464 | tf_op jit(solution)/shard_map/ppermute | solution.py:758
  104.1 2.9 %collective-permute-start.30 = (bf16[3,128,512]{2,1,0:T(8,128)(2,1)S(1)}, bf16[3,128,512]{2,1,0:T(8,128)(2,1)S(1)}, u32[]{:S(2)}, u32[]{:S(2)}) collective-permute-start(bf16[3,128,512]{2,1,0:T(8,128)(2,1)S(1)} %slice.9), channel_id=1, source_target_pairs={{0,48},{8,56},{16,0},{24,8},{32,16},{40,24},{48,32},{56,40},{1,49}... | collective-permute-start | bytes 1179656 | tf_op jit(solution)/shard_map/ppermute | solution.py:762
  107.5 3.1 %back_left.1 = (bf16[5,16,2048]{2,1,0:T(8,128)(2,1)S(1)}, bf16[5,16,2048]{2,1,0:T(8,128)(2,1)S(1)}, bf16[5,16,2048]{2,1,0:T(8,128)(2,1)S(1)}, bf16[5,16,2048]{2,1,0:T(8,128)(2,1)S(1)}) custom-call(bf16[3,256,512]{2,1,0:T(8,128)(2,1)S(1)} %sum_keys.1.grads.g0, bf16[3,4096,512]{2,1,0:T(8,128)(2,1)S(1)} %bitcast.23, ...), custom_call_target="tpu_custom_call" | custom-call | flops 1610612736 | bytes 8388608 | tf_op jit(solution)/shard_map/back_left/pallas_call | solution.py:464
  110.6 2.7 %collective-permute-start.22 = (bf16[5,16,2048]{2,1,0:T(8,128)(2,1)S(1)}, bf16[5,16,2048]{2,1,0:T(8,128)(2,1)S(1)}, u32[]{:S(2)}, u32[]{:S(2)}) collective-permute-start(bf16[5,16,2048]{2,1,0:T(8,128)(2,1)S(1)} %get-tuple-element.70), channel_id=1, source_target_pairs={{0,3},{1,0},{2,1},{3,2},{4,7},{5,4},{6,5},{7,6},{8,11},{9,8},{10,9... | collective-permute-start | bytes 983048 | tf_op jit(solution)/shard_map/ppermute | solution.py:771
  114.6 1.5 collective-permute-start.24
  117.7 2.3 %weight_shares.2.refs_1_.refs_0_ = bf16[3,512,512]{2,1,0:T(8,128)(2,1)S(1)} custom-call(bf16[256,4096]{1,0:T(8,128)(2,1)S(1)} %get-tuple-element.48.full.normed, bf16[256,1024]{1,0:T(8,128)(2,1)S(1)} %collective-permute-done.17.refs_1_.c1, bf16[256,1024]{1,0:T(8,128)(2,1)S(1)} %collective-permute-done.18.refs_2_.c2, ...), custom_call_target="tpu_custom_call" | custom-call | flops 1610612736 | bytes 7340032 | tf_op jit(solution)/shard_map/weight_shares/pallas_call | solution.py:679
  120.0 5.3 %collective-permute-done.22.c1 = bf16[5,16,2048]{2,1,0:T(8,128)(2,1)S(1)} collective-permute-done((bf16[5,16,2048]{2,1,0:T(8,128)(2,1)S(1)}, bf16[5,16,2048]{2,1,0:T(8,128)(2,1)S(1)}, u32[]{:S(2)}, u32[]{:S(2)}) %collective-permute-start.22) | collective-permute-done | bytes 327712 | tf_op jit(solution)/shard_map/ppermute | solution.py:771
  125.6 3.2 %collective-permute-done.23.c2 = bf16[5,16,2048]{2,1,0:T(8,128)(2,1)S(1)} collective-permute-done((bf16[5,16,2048]{2,1,0:T(8,128)(2,1)S(1)}, bf16[5,16,2048]{2,1,0:T(8,128)(2,1)S(1)}, u32[]{:S(2)}, u32[]{:S(2)}) %collective-permute-start.23) | collective-permute-done | bytes 327712 | tf_op jit(solution)/shard_map/ppermute | solution.py:771
  129.2 1.9 %collective-permute-start.26 = (bf16[3,16,2048]{2,1,0:T(8,128)(2,1)S(1)}, bf16[3,16,2048]{2,1,0:T(8,128)(2,1)S(1)}, u32[]{:S(2)}, u32[]{:S(2)}) collective-permute-start(bf16[3,16,2048]{2,1,0:T(8,128)(2,1)S(1)} %get-tuple-element.75), channel_id=1, source_target_pairs={{0,4},{1,5},{2,6},{3,7},{4,0},{5,1},{6,2},{7,3},{8,12},{9,13},{10,... | collective-permute-start | bytes 589832 | tf_op jit(solution)/shard_map/ppermute | solution.py:773
  131.0 7.6 %collective-permute-done.26.refs_0_.l_came.came = bf16[3,16,2048]{2,1,0:T(8,128)(2,1)S(1)} collective-permute-done((bf16[3,16,2048]{2,1,0:T(8,128)(2,1)S(1)}, bf16[3,16,2048]{2,1,0:T(8,128)(2,1)S(1)}, u32[]{:S(2)}, u32[]{:S(2)}) %collective-permute-start.26) | collective-permute-done | bytes 196640 | tf_op jit(solution)/shard_map/ppermute | solution.py:773
  139.9 3.4 %collective-permute-start.39 = (f32[1,4096]{1,0:T(1,128)S(1)}, f32[1,4096]{1,0:T(1,128)S(1)}, u32[]{:S(2)}, u32[]{:S(2)}) collective-permute-start(f32[1,4096]{1,0:T(1,128)S(1)} %add.15), channel_id=1, source_target_pairs={{0,32},{8,40},{16,48},{24,56},{32,0},{40,8},{48,16},{56,24},{1,33}... | collective-permute-start | bytes 49160 | tf_op jit(solution)/shard_map/ppermute | solution.py:778
  143.6 1.7 %collective-permute-start.37 = (f32[1,4096]{1,0:T(1,128)S(1)}, f32[1,4096]{1,0:T(1,128)S(1)}, u32[]{:S(2)}, u32[]{:S(2)}) collective-permute-start(f32[1,4096]{1,0:T(1,128)S(1)} %add.15), channel_id=1, source_target_pairs={{0,16},{8,24},{16,32},{24,40},{32,48},{40,56},{48,0},{56,8},{1,17}... | collective-permute-start | bytes 49160 | tf_op jit(solution)/shard_map/ppermute | solution.py:778
  145.4 2.2 %weight_shares.3 = f32[3,512,512]{2,1,0:T(8,128)S(1)} custom-call(bf16[256,4096]{1,0:T(8,128)(2,1)S(1)} %get-tuple-element.48.full.normed, bf16[256,1024]{1,0:T(8,128)(2,1)S(1)} %collective-permute-done.17.refs_1_.c1, bf16[256,1024]{1,0:T(8,128)(2,1)S(1)} %collective-permute-done.18.refs_2_.c2, bf16[256,1024]{1,0:T(8,128)(2,1)S(1)} %collective-permute-done.20.refs_0_.c3, ...), custom_call_target="tpu_custom_call" | custom-call | flops 1610612736 | bytes 7340032 | tf_op jit(solution)/shard_map/weight_shares/pallas_call | solution.py:679
  147.6 8.4 %collective-permute-done.39 = f32[1,4096]{1,0:T(1,128)S(1)} collective-permute-done((f32[1,4096]{1,0:T(1,128)S(1)}, f32[1,4096]{1,0:T(1,128)S(1)}, u32[]{:S(2)}, u32[]{:S(2)}) %collective-permute-start.39) | collective-permute-done | bytes 16416 | tf_op jit(solution)/shard_map/ppermute | solution.py:778
  156.0 3.7 %collective-permute-start.33 = (bf16[32,2048]{1,0:T(8,128)(2,1)S(1)}, bf16[32,2048]{1,0:T(8,128)(2,1)S(1)}, u32[]{:S(2)}, u32[]{:S(2)}) collective-permute-start(bf16[32,2048]{1,0:T(8,128)(2,1)S(1)} %get-tuple-element.79.refs_1_), channel_id=1, source_target_pairs={{0,3},{1,0},{2,1},{3,2},{4,7},{5,4},{6,5},{7,6},{8,11},{9,8},{10,9... | collective-permute-start | bytes 393224 | tf_op jit(solution)/shard_map/ppermute | solution.py:785
  159.6 1.5 collective-permute-start.35
  163.3 4.9 %collective-permute-done.34.r2 = bf16[32,2048]{1,0:T(8,128)(2,1)S(1)} collective-permute-done((bf16[32,2048]{1,0:T(8,128)(2,1)S(1)}, bf16[32,2048]{1,0:T(8,128)(2,1)S(1)}, u32[]{:S(2)}, u32[]{:S(2)}) %collective-permute-start.34) | collective-permute-done | bytes 131104 | tf_op jit(solution)/shard_map/ppermute | solution.py:785
  169.3 2.2 %add_bitcast_fusion = f32[1,512,3,512]{3,1,2,0:T(8,128)} fusion(f32[3,512,512]{2,1,0:T(8,128)S(1)} %weight_shares.3, bf16[3,512,512]{2,1,0:T(8,128)(2,1)S(1)} %collective-permute-done.40), kind=kLoop, calls=%fused_computation | loop fusion | flops 1572864 | bytes 7864320 | tf_op jit(solution)/shard_map/broadcast_in_dim | solution.py:799
  (86 shorter events, 17.8 us)
Async XLA Ops:
  3.5 8.1 %collective-permute-start.4 = (bf16[32,2048]{1,0:T(8,128)(2,1)S(1)}, bf16[32,2048]{1,0:T(8,128)(2,1)S(1)}, u32[]{:S(2)}, u32[]{:S(2)}) collective-permute-start(bf16[32,2048]{1,0:T(8,128)(2,1)S(1)} %get-tuple-element.46), channel_id=1, source_target_pairs={{0,4},{1,5},{2,6},{3,7},{4,0},{5,1},{6,2},{7,3},{8,12},{9,13},{10,... | collective-permute-start | bytes 393224 | tf_op jit(solution)/shard_map/ppermute | solution.py:138
  5.1 7.7 %collective-permute-start.2 = (bf16[32,2048]{1,0:T(8,128)(2,1)S(1)}, bf16[32,2048]{1,0:T(8,128)(2,1)S(1)}, u32[]{:S(2)}, u32[]{:S(2)}) collective-permute-start(bf16[32,2048]{1,0:T(8,128)(2,1)S(1)} %get-tuple-element.45), channel_id=1, source_target_pairs={{0,2},{1,3},{2,0},{3,1},{4,6},{5,7},{6,4},{7,5},{8,10},{9,11},{10,... | collective-permute-start | bytes 393224 | tf_op jit(solution)/shard_map/ppermute | solution.py:139
  9.0 8.2 %collective-permute-start.1 = (bf16[32,2048]{1,0:T(8,128)(2,1)S(1)}, bf16[32,2048]{1,0:T(8,128)(2,1)S(1)}, u32[]{:S(2)}, u32[]{:S(2)}) collective-permute-start(bf16[32,2048]{1,0:T(8,128)(2,1)S(1)} %get-tuple-element.45), channel_id=1, source_target_pairs={{0,3},{1,0},{2,1},{3,2},{4,7},{5,4},{6,5},{7,6},{8,11},{9,8},{10,9... | collective-permute-start | bytes 393224 | tf_op jit(solution)/shard_map/ppermute | solution.py:139
  9.7 7.7 %collective-permute-start = (bf16[32,2048]{1,0:T(8,128)(2,1)S(1)}, bf16[32,2048]{1,0:T(8,128)(2,1)S(1)}, u32[]{:S(2)}, u32[]{:S(2)}) collective-permute-start(bf16[32,2048]{1,0:T(8,128)(2,1)S(1)} %get-tuple-element.45), channel_id=1, source_target_pairs={{0,1},{1,2},{2,3},{3,0},{4,5},{5,6},{6,7},{7,4},{8,9},{9,10},{10,1... | collective-permute-start | bytes 393224 | tf_op jit(solution)/shard_map/ppermute | solution.py:139
  11.0 6.9 %collective-permute-start.8 = (bf16[32,4096]{1,0:T(8,128)(2,1)S(1)}, bf16[32,4096]{1,0:T(8,128)(2,1)S(1)}, u32[]{:S(2)}, u32[]{:S(2)}) collective-permute-start(bf16[32,4096]{1,0:T(8,128)(2,1)S(1)} %get-tuple-element.47.grad), channel_id=1, source_target_pairs={{0,4},{1,5},{2,6},{3,7},{4,0},{5,1},{6,2},{7,3},{8,12},{9,13},{10,... | collective-permute-start | bytes 786440 | tf_op jit(solution)/shard_map/ppermute | solution.py:736
  11.6 16.5 %collective-permute-start.5 = (bf16[2,32,2048]{2,1,0:T(8,128)(2,1)S(1)}, bf16[2,32,2048]{2,1,0:T(8,128)(2,1)S(1)}, u32[]{:S(2)}, u32[]{:S(2)}) collective-permute-start(bf16[2,32,2048]{2,1,0:T(8,128)(2,1)S(1)} %pad_maximum_fusion.2.refs_2_), channel_id=1, source_target_pairs={{0,1},{1,2},{2,3},{3,0},{4,5},{5,6},{6,7},{7,4},{8,9},{9,10},{10,1... | collective-permute-start | bytes 786440 | tf_op jit(solution)/shard_map/ppermute | solution.py:140
  12.8 15.2 %collective-permute-start.6 = (bf16[2,32,2048]{2,1,0:T(8,128)(2,1)S(1)}, bf16[2,32,2048]{2,1,0:T(8,128)(2,1)S(1)}, u32[]{:S(2)}, u32[]{:S(2)}) collective-permute-start(bf16[2,32,2048]{2,1,0:T(8,128)(2,1)S(1)} %pad_maximum_fusion.2.refs_2_), channel_id=1, source_target_pairs={{0,3},{1,0},{2,1},{3,2},{4,7},{5,4},{6,5},{7,6},{8,11},{9,8},{10,9... | collective-permute-start | bytes 786440 | tf_op jit(solution)/shard_map/ppermute | solution.py:140
  17.2 10.8 %collective-permute-start.7 = (bf16[2,32,2048]{2,1,0:T(8,128)(2,1)S(1)}, bf16[2,32,2048]{2,1,0:T(8,128)(2,1)S(1)}, u32[]{:S(2)}, u32[]{:S(2)}) collective-permute-start(bf16[2,32,2048]{2,1,0:T(8,128)(2,1)S(1)} %pad_maximum_fusion.2.refs_2_), channel_id=1, source_target_pairs={{0,2},{1,3},{2,0},{3,1},{4,6},{5,7},{6,4},{7,5},{8,10},{9,11},{10,... | collective-permute-start | bytes 786440 | tf_op jit(solution)/shard_map/ppermute | solution.py:140
  17.5 11.8 %collective-permute-start.3 = (bf16[4,32,2048]{2,1,0:T(8,128)(2,1)S(1)}, bf16[4,32,2048]{2,1,0:T(8,128)(2,1)S(1)}, u32[]{:S(2)}, u32[]{:S(2)}) collective-permute-start(bf16[4,32,2048]{2,1,0:T(8,128)(2,1)S(1)} %pad_maximum_fusion.refs_0_), channel_id=1, source_target_pairs={{0,4},{1,5},{2,6},{3,7},{4,0},{5,1},{6,2},{7,3},{8,12},{9,13},{10,... | collective-permute-start | bytes 1572872 | tf_op jit(solution)/shard_map/ppermute | solution.py:142
  18.0 26.6 %collective-permute-start.9 = (bf16[2,32,4096]{2,1,0:T(8,128)(2,1)S(1)}, bf16[2,32,4096]{2,1,0:T(8,128)(2,1)S(1)}, u32[]{:S(2)}, u32[]{:S(2)}) collective-permute-start(bf16[2,32,4096]{2,1,0:T(8,128)(2,1)S(1)} %pad_maximum_fusion.1.refs_7_.p0), channel_id=1, source_target_pairs={{0,1},{1,2},{2,3},{3,0},{4,5},{5,6},{6,7},{7,4},{8,9},{9,10},{10,1... | collective-permute-start | bytes 1572872 | tf_op jit(solution)/shard_map/ppermute | solution.py:738
  28.1 18.4 %collective-permute-start.10 = (bf16[2,32,4096]{2,1,0:T(8,128)(2,1)S(1)}, bf16[2,32,4096]{2,1,0:T(8,128)(2,1)S(1)}, u32[]{:S(2)}, u32[]{:S(2)}) collective-permute-start(bf16[2,32,4096]{2,1,0:T(8,128)(2,1)S(1)} %pad_maximum_fusion.1.refs_7_.p0), channel_id=1, source_target_pairs={{0,3},{1,0},{2,1},{3,2},{4,7},{5,4},{6,5},{7,6},{8,11},{9,8},{10,9... | collective-permute-start | bytes 1572872 | tf_op jit(solution)/shard_map/ppermute | solution.py:738
  33.9 12.6 %copy-start.1 = (bf16[1,4096,3,512]{3,1,2,0:T(8,128)(2,1)S(1)}, bf16[1,4096,3,512]{3,1,2,0:T(8,128)(2,1)}, u32[]{:S(2)}) copy-start(bf16[1,4096,3,512]{3,1,2,0:T(8,128)(2,1)} %param.11) | copy-start | bytes 37748740
  37.5 12.4 %collective-permute-start.11 = (bf16[2,256,512]{2,1,0:T(8,128)(2,1)S(1)}, bf16[2,256,512]{2,1,0:T(8,128)(2,1)S(1)}, u32[]{:S(2)}, u32[]{:S(2)}) collective-permute-start(bf16[2,256,512]{2,1,0:T(8,128)(2,1)S(1)} %get-tuple-element.49.own_kv), channel_id=1, source_target_pairs={{0,64},{64,0},{1,65},{65,1},{2,66},{66,2},{3,67},{67,3},{4,68},{68... | collective-permute-start | bytes 1572872 | tf_op jit(solution)/shard_map/ppermute | solution.py:740
  40.4 14.2 %collective-permute-start.16 = (bf16[2,32,4096]{2,1,0:T(8,128)(2,1)S(1)}, bf16[2,32,4096]{2,1,0:T(8,128)(2,1)S(1)}, u32[]{:S(2)}, u32[]{:S(2)}) collective-permute-start(bf16[2,32,4096]{2,1,0:T(8,128)(2,1)S(1)} %pad_maximum_fusion.1.refs_7_.p0), channel_id=1, source_target_pairs={{0,2},{1,3},{2,0},{3,1},{4,6},{5,7},{6,4},{7,5},{8,10},{9,11},{10,... | collective-permute-start | bytes 1572872 | tf_op jit(solution)/shard_map/ppermute | solution.py:738
  42.9 11.7 %collective-permute-start.17 = (bf16[256,1024]{1,0:T(8,128)(2,1)S(1)}, bf16[256,1024]{1,0:T(8,128)(2,1)S(1)}, u32[]{:S(2)}, u32[]{:S(2)}) collective-permute-start(bf16[256,1024]{1,0:T(8,128)(2,1)S(1)} %get-tuple-element.57), channel_id=1, source_target_pairs={{0,16},{8,24},{16,32},{24,40},{32,48},{40,56},{48,0},{56,8},{1,17}... | collective-permute-start | bytes 1572872 | tf_op jit(solution)/shard_map/ppermute | solution.py:709
  44.6 5.4 %copy-start.8 = (s32[1,5]{1,0:T(1,128)S(1)}, s32[1,5]{1,0:T(1,128)}, u32[]{:S(2)}) copy-start(s32[1,5]{1,0:T(1,128)} %gaps.3) | copy-start | bytes 64
  44.6 5.4 %copy-start.9 = (s32[1,4]{1,0:T(1,128)S(1)}, s32[1,4]{1,0:T(1,128)}, u32[]{:S(2)}) copy-start(s32[1,4]{1,0:T(1,128)} %runs.3) | copy-start | bytes 52
  44.6 10.0 %collective-permute-start.18 = (bf16[256,1024]{1,0:T(8,128)(2,1)S(1)}, bf16[256,1024]{1,0:T(8,128)(2,1)S(1)}, u32[]{:S(2)}, u32[]{:S(2)}) collective-permute-start(bf16[256,1024]{1,0:T(8,128)(2,1)S(1)} %get-tuple-element.58), channel_id=1, source_target_pairs={{0,48},{8,56},{16,0},{24,8},{32,16},{40,24},{48,32},{56,40},{1,49}... | collective-permute-start | bytes 1572872 | tf_op jit(solution)/shard_map/ppermute | solution.py:709
  46.5 5.9 %copy-start.2 = (bf16[1,4096,512]{2,1,0:T(8,128)(2,1)S(1)}, bf16[1,4096,512]{2,1,0:T(8,128)(2,1)}, u32[]{:S(2)}) copy-start(bf16[1,4096,512]{2,1,0:T(8,128)(2,1)} %weight.3) | copy-start | bytes 12582916
  57.8 49.2 %collective-permute-start.21 = (bf16[4,512,512]{2,1,0:T(8,128)(2,1)S(1)}, bf16[4,512,512]{2,1,0:T(8,128)(2,1)S(1)}, u32[]{:S(2)}, u32[]{:S(2)}) collective-permute-start(bf16[4,512,512]{2,1,0:T(8,128)(2,1)S(1)} %get-tuple-element.67), channel_id=1, source_target_pairs={{0,8},{8,0},{16,24},{24,16},{32,40},{40,32},{48,56},{56,48},{1,9},... | collective-permute-start | bytes 6291464 | tf_op jit(solution)/shard_map/ppermute | solution.py:753
  57.9 17.8 %collective-permute-start.12 = (bf16[2,32,4096]{2,1,0:T(8,128)(2,1)S(1)}, bf16[2,32,4096]{2,1,0:T(8,128)(2,1)S(1)}, u32[]{:S(2)}, u32[]{:S(2)}) collective-permute-start(bf16[2,32,4096]{2,1,0:T(8,128)(2,1)S(1)} %get-tuple-element.51), channel_id=1, source_target_pairs={{0,3},{1,0},{2,1},{3,2},{4,7},{5,4},{6,5},{7,6},{8,11},{9,8},{10,9... | collective-permute-start | bytes 1572872 | tf_op jit(solution)/shard_map/ppermute | solution.py:746
  63.3 15.2 %collective-permute-start.13 = (bf16[2,32,4096]{2,1,0:T(8,128)(2,1)S(1)}, bf16[2,32,4096]{2,1,0:T(8,128)(2,1)S(1)}, u32[]{:S(2)}, u32[]{:S(2)}) collective-permute-start(bf16[2,32,4096]{2,1,0:T(8,128)(2,1)S(1)} %get-tuple-element.52), channel_id=1, source_target_pairs={{0,1},{1,2},{2,3},{3,0},{4,5},{5,6},{6,7},{7,4},{8,9},{9,10},{10,1... | collective-permute-start | bytes 1572872 | tf_op jit(solution)/shard_map/ppermute | solution.py:746
  67.6 15.6 %collective-permute-start.19 = (bf16[2,256,512]{2,1,0:T(8,128)(2,1)S(1)}, bf16[2,256,512]{2,1,0:T(8,128)(2,1)S(1)}, u32[]{:S(2)}, u32[]{:S(2)}) collective-permute-start(bf16[2,256,512]{2,1,0:T(8,128)(2,1)S(1)} %get-tuple-element.62), channel_id=1, source_target_pairs={{0,64},{64,0},{1,65},{65,1},{2,66},{66,2},{3,67},{67,3},{4,68},{68... | collective-permute-start | bytes 1572872 | tf_op jit(solution)/shard_map/ppermute | solution.py:751
  70.3 16.6 %collective-permute-start.20 = (bf16[256,1024]{1,0:T(8,128)(2,1)S(1)}, bf16[256,1024]{1,0:T(8,128)(2,1)S(1)}, u32[]{:S(2)}, u32[]{:S(2)}) collective-permute-start(bf16[256,1024]{1,0:T(8,128)(2,1)S(1)} %get-tuple-element.65), channel_id=1, source_target_pairs={{0,32},{8,40},{16,48},{24,56},{32,0},{40,8},{48,16},{56,24},{1,33}... | collective-permute-start | bytes 1572872 | tf_op jit(solution)/shard_map/ppermute | solution.py:709
  75.7 15.2 %collective-permute-start.14 = (bf16[2,32,4096]{2,1,0:T(8,128)(2,1)S(1)}, bf16[2,32,4096]{2,1,0:T(8,128)(2,1)S(1)}, u32[]{:S(2)}, u32[]{:S(2)}) collective-permute-start(bf16[2,32,4096]{2,1,0:T(8,128)(2,1)S(1)} %get-tuple-element.53), channel_id=1, source_target_pairs={{0,2},{1,3},{2,0},{3,1},{4,6},{5,7},{6,4},{7,5},{8,10},{9,11},{10,... | collective-permute-start | bytes 1572872 | tf_op jit(solution)/shard_map/ppermute | solution.py:746
  83.3 20.3 %collective-permute-start.27 = (bf16[3,256,512]{2,1,0:T(8,128)(2,1)S(1)}, bf16[3,256,512]{2,1,0:T(8,128)(2,1)S(1)}, u32[]{:S(2)}, u32[]{:S(2)}) collective-permute-start(bf16[3,256,512]{2,1,0:T(8,128)(2,1)S(1)} %sum_keys.1.grads.g0), channel_id=1, source_target_pairs={{0,16},{8,24},{16,32},{24,40},{32,48},{40,56},{48,0},{56,8},{1,17}... | collective-permute-start | bytes 2359304 | tf_op jit(solution)/shard_map/ppermute | solution.py:758
  84.9 19.2 %collective-permute-start.28 = (bf16[3,256,512]{2,1,0:T(8,128)(2,1)S(1)}, bf16[3,256,512]{2,1,0:T(8,128)(2,1)S(1)}, u32[]{:S(2)}, u32[]{:S(2)}) collective-permute-start(bf16[3,256,512]{2,1,0:T(8,128)(2,1)S(1)} %sum_keys.1.grads.g0), channel_id=1, source_target_pairs={{0,48},{8,56},{16,0},{24,8},{32,16},{40,24},{48,32},{56,40},{1,49}... | collective-permute-start | bytes 2359304 | tf_op jit(solution)/shard_map/ppermute | solution.py:759
  94.0 19.9 %collective-permute-start.25 = (bf16[4,32,2048]{2,1,0:T(8,128)(2,1)S(1)}, bf16[4,32,2048]{2,1,0:T(8,128)(2,1)S(1)}, u32[]{:S(2)}, u32[]{:S(2)}) collective-permute-start(bf16[4,32,2048]{2,1,0:T(8,128)(2,1)S(1)} %get-tuple-element.73), channel_id=1, source_target_pairs={{0,4},{1,5},{2,6},{3,7},{4,0},{5,1},{6,2},{7,3},{8,12},{9,13},{10,... | collective-permute-start | bytes 1572872 | tf_op jit(solution)/shard_map/ppermute | solution.py:769
  103.7 11.0 %collective-permute-start.29 = (bf16[3,128,512]{2,1,0:T(8,128)(2,1)S(1)}, bf16[3,128,512]{2,1,0:T(8,128)(2,1)S(1)}, u32[]{:S(2)}, u32[]{:S(2)}) collective-permute-start(bf16[3,128,512]{2,1,0:T(8,128)(2,1)S(1)} %slice.8), channel_id=1, source_target_pairs={{0,16},{8,24},{16,32},{24,40},{32,48},{40,56},{48,0},{56,8},{1,17}... | collective-permute-start | bytes 1179656 | tf_op jit(solution)/shard_map/ppermute | solution.py:761
  104.1 12.5 %collective-permute-start.30 = (bf16[3,128,512]{2,1,0:T(8,128)(2,1)S(1)}, bf16[3,128,512]{2,1,0:T(8,128)(2,1)S(1)}, u32[]{:S(2)}, u32[]{:S(2)}) collective-permute-start(bf16[3,128,512]{2,1,0:T(8,128)(2,1)S(1)} %slice.9), channel_id=1, source_target_pairs={{0,48},{8,56},{16,0},{24,8},{32,16},{40,24},{48,32},{56,40},{1,49}... | collective-permute-start | bytes 1179656 | tf_op jit(solution)/shard_map/ppermute | solution.py:762
  110.6 14.7 %collective-permute-start.22 = (bf16[5,16,2048]{2,1,0:T(8,128)(2,1)S(1)}, bf16[5,16,2048]{2,1,0:T(8,128)(2,1)S(1)}, u32[]{:S(2)}, u32[]{:S(2)}) collective-permute-start(bf16[5,16,2048]{2,1,0:T(8,128)(2,1)S(1)} %get-tuple-element.70), channel_id=1, source_target_pairs={{0,3},{1,0},{2,1},{3,2},{4,7},{5,4},{6,5},{7,6},{8,11},{9,8},{10,9... | collective-permute-start | bytes 983048 | tf_op jit(solution)/shard_map/ppermute | solution.py:771
  113.3 26.2 %collective-permute-start.31 = (bf16[512,512]{1,0:T(8,128)(2,1)S(1)}, bf16[512,512]{1,0:T(8,128)(2,1)S(1)}, u32[]{:S(2)}, u32[]{:S(2)}) collective-permute-start(bf16[512,512]{1,0:T(8,128)(2,1)S(1)} %get-tuple-element.68.refs_0_), channel_id=1, source_target_pairs={{0,48},{8,56},{16,0},{24,8},{32,16},{40,24},{48,32},{56,40},{1,49}... | collective-permute-start | bytes 1572872 | tf_op jit(solution)/shard_map/ppermute | solution.py:755
  113.9 14.9 %collective-permute-start.23 = (bf16[5,16,2048]{2,1,0:T(8,128)(2,1)S(1)}, bf16[5,16,2048]{2,1,0:T(8,128)(2,1)S(1)}, u32[]{:S(2)}, u32[]{:S(2)}) collective-permute-start(bf16[5,16,2048]{2,1,0:T(8,128)(2,1)S(1)} %get-tuple-element.71), channel_id=1, source_target_pairs={{0,1},{1,2},{2,3},{3,0},{4,5},{5,6},{6,7},{7,4},{8,9},{9,10},{10,1... | collective-permute-start | bytes 983048 | tf_op jit(solution)/shard_map/ppermute | solution.py:771
  114.6 14.3 %collective-permute-start.24 = (bf16[5,16,2048]{2,1,0:T(8,128)(2,1)S(1)}, bf16[5,16,2048]{2,1,0:T(8,128)(2,1)S(1)}, u32[]{:S(2)}, u32[]{:S(2)}) collective-permute-start(bf16[5,16,2048]{2,1,0:T(8,128)(2,1)S(1)} %get-tuple-element.72), channel_id=1, source_target_pairs={{0,2},{1,3},{2,0},{3,1},{4,6},{5,7},{6,4},{7,5},{8,10},{9,11},{10,... | collective-permute-start | bytes 983048 | tf_op jit(solution)/shard_map/ppermute | solution.py:771
  116.6 22.9 %collective-permute-start.32 = (bf16[512,512]{1,0:T(8,128)(2,1)S(1)}, bf16[512,512]{1,0:T(8,128)(2,1)S(1)}, u32[]{:S(2)}, u32[]{:S(2)}) collective-permute-start(bf16[512,512]{1,0:T(8,128)(2,1)S(1)} %get-tuple-element.77), channel_id=1, source_target_pairs={{0,16},{8,24},{16,32},{24,40},{32,48},{40,56},{48,0},{56,8},{1,17}... | collective-permute-start | bytes 1572872 | tf_op jit(solution)/shard_map/ppermute | solution.py:755
  120.0 18.6 %copy-start.7 = (bf16[1,4096]{1,0:T(2,128)(2,1)S(1)}, bf16[1,4096]{1,0:T(2,128)(2,1)}, u32[]{:S(2)}) copy-start(bf16[1,4096]{1,0:T(2,128)(2,1)} %gain.5) | copy-start | bytes 24580
  120.0 18.8 %copy-start.4 = (bf16[1,1,32,4096]{3,2,1,0:T(8,128)(2,1)S(1)}, bf16[1,1,32,4096]{3,2,1,0:T(8,128)(2,1)}, u32[]{:S(2)}) copy-start(bf16[1,1,32,4096]{3,2,1,0:T(8,128)(2,1)} %param.7) | copy-start | bytes 786436
  125.3 44.0 %collective-permute-start.40 = (bf16[3,512,512]{2,1,0:T(8,128)(2,1)S(1)}, bf16[3,512,512]{2,1,0:T(8,128)(2,1)S(1)}, u32[]{:S(2)}, u32[]{:S(2)}) collective-permute-start(bf16[3,512,512]{2,1,0:T(8,128)(2,1)S(1)} %weight_shares.2.refs_1_.refs_0_), channel_id=1, source_target_pairs={{0,8},{8,0},{16,24},{24,16},{32,40},{40,32},{48,56},{56,48},{1,9},... | collective-permute-start | bytes 4718600 | tf_op jit(solution)/shard_map/ppermute | solution.py:791
  128.7 10.0 %collective-permute-start.15 = (bf16[32,4096]{1,0:T(8,128)(2,1)S(1)}, bf16[32,4096]{1,0:T(8,128)(2,1)S(1)}, u32[]{:S(2)}, u32[]{:S(2)}) collective-permute-start(bf16[32,4096]{1,0:T(8,128)(2,1)S(1)} %get-tuple-element.55), channel_id=1, source_target_pairs={{0,4},{1,5},{2,6},{3,7},{4,0},{5,1},{6,2},{7,3},{8,12},{9,13},{10,... | collective-permute-start | bytes 786440 | tf_op jit(solution)/shard_map/ppermute | solution.py:792
  129.2 9.4 %collective-permute-start.26 = (bf16[3,16,2048]{2,1,0:T(8,128)(2,1)S(1)}, bf16[3,16,2048]{2,1,0:T(8,128)(2,1)S(1)}, u32[]{:S(2)}, u32[]{:S(2)}) collective-permute-start(bf16[3,16,2048]{2,1,0:T(8,128)(2,1)S(1)} %get-tuple-element.75), channel_id=1, source_target_pairs={{0,4},{1,5},{2,6},{3,7},{4,0},{5,1},{6,2},{7,3},{8,12},{9,13},{10,... | collective-permute-start | bytes 589832 | tf_op jit(solution)/shard_map/ppermute | solution.py:773
  138.6 1.3 collective-permute-start.36
  139.6 22.2 %collective-permute-start.41 = (bf16[512,512]{1,0:T(8,128)(2,1)S(1)}, bf16[512,512]{1,0:T(8,128)(2,1)S(1)}, u32[]{:S(2)}, u32[]{:S(2)}) collective-permute-start(bf16[512,512]{1,0:T(8,128)(2,1)S(1)} %get-tuple-element.84), channel_id=1, source_target_pairs={{0,32},{8,40},{16,48},{24,56},{32,0},{40,8},{48,16},{56,24},{1,33}... | collective-permute-start | bytes 1572872 | tf_op jit(solution)/shard_map/ppermute | solution.py:755
  139.9 16.0 %collective-permute-start.39 = (f32[1,4096]{1,0:T(1,128)S(1)}, f32[1,4096]{1,0:T(1,128)S(1)}, u32[]{:S(2)}, u32[]{:S(2)}) collective-permute-start(f32[1,4096]{1,0:T(1,128)S(1)} %add.15), channel_id=1, source_target_pairs={{0,32},{8,40},{16,48},{24,56},{32,0},{40,8},{48,16},{56,24},{1,33}... | collective-permute-start | bytes 49160 | tf_op jit(solution)/shard_map/ppermute | solution.py:778
  143.3 16.3 %collective-permute-start.38 = (f32[1,4096]{1,0:T(1,128)S(1)}, f32[1,4096]{1,0:T(1,128)S(1)}, u32[]{:S(2)}, u32[]{:S(2)}) collective-permute-start(f32[1,4096]{1,0:T(1,128)S(1)} %add.15), channel_id=1, source_target_pairs={{0,48},{8,56},{16,0},{24,8},{32,16},{40,24},{48,32},{56,40},{1,49}... | collective-permute-start | bytes 49160 | tf_op jit(solution)/shard_map/ppermute | solution.py:778
  143.6 16.0 %collective-permute-start.37 = (f32[1,4096]{1,0:T(1,128)S(1)}, f32[1,4096]{1,0:T(1,128)S(1)}, u32[]{:S(2)}, u32[]{:S(2)}) collective-permute-start(f32[1,4096]{1,0:T(1,128)S(1)} %add.15), channel_id=1, source_target_pairs={{0,16},{8,24},{16,32},{24,40},{32,48},{40,56},{48,0},{56,8},{1,17}... | collective-permute-start | bytes 49160 | tf_op jit(solution)/shard_map/ppermute | solution.py:778
  156.0 6.2 %collective-permute-start.33 = (bf16[32,2048]{1,0:T(8,128)(2,1)S(1)}, bf16[32,2048]{1,0:T(8,128)(2,1)S(1)}, u32[]{:S(2)}, u32[]{:S(2)}) collective-permute-start(bf16[32,2048]{1,0:T(8,128)(2,1)S(1)} %get-tuple-element.79.refs_1_), channel_id=1, source_target_pairs={{0,3},{1,0},{2,1},{3,2},{4,7},{5,4},{6,5},{7,6},{8,11},{9,8},{10,9... | collective-permute-start | bytes 393224 | tf_op jit(solution)/shard_map/ppermute | solution.py:785
  159.6 8.6 %collective-permute-start.34 = (bf16[32,2048]{1,0:T(8,128)(2,1)S(1)}, bf16[32,2048]{1,0:T(8,128)(2,1)S(1)}, u32[]{:S(2)}, u32[]{:S(2)}) collective-permute-start(bf16[32,2048]{1,0:T(8,128)(2,1)S(1)} %get-tuple-element.80), channel_id=1, source_target_pairs={{0,1},{1,2},{2,3},{3,0},{4,5},{5,6},{6,7},{7,4},{8,9},{9,10},{10,1... | collective-permute-start | bytes 393224 | tf_op jit(solution)/shard_map/ppermute | solution.py:785
  159.6 8.6 %collective-permute-start.35 = (bf16[32,2048]{1,0:T(8,128)(2,1)S(1)}, bf16[32,2048]{1,0:T(8,128)(2,1)S(1)}, u32[]{:S(2)}, u32[]{:S(2)}) collective-permute-start(bf16[32,2048]{1,0:T(8,128)(2,1)S(1)} %get-tuple-element.81), channel_id=1, source_target_pairs={{0,2},{1,3},{2,0},{3,1},{4,6},{5,7},{6,4},{7,5},{8,10},{9,11},{10,... | collective-permute-start | bytes 393224 | tf_op jit(solution)/shard_map/ppermute | solution.py:785
  (4 other events, 7.2 us)

commit v8 on v7

--- a/solution.py
+++ b/solution.py
@@ -229,24 +229,43 @@
     )(own, came, gain)
 
 
-def sum_x_kernel(own, came, *refs):
-    kept, sends = refs[-4], refs[-3:]
+def sum_x_kernel(waits, own, came, *refs):
+    kept, sends = refs[waits], refs[waits + 1:]
     kept[...] = own[0].astype(f32) + came[0].astype(f32)
     for slot, sent in enumerate(sends, 1):
         sent[...] = (own[slot].astype(f32) + came[slot].astype(f32)).astype(bf16)
 
 
-def sum_x(own, came, after=()):
+def sum_x(own, came, after=(), sends=3):
     shape = own.shape[1:]
     return call(
-        sum_x_kernel,
-        [sds(shape, f32)] + [sds(shape, bf16)] * 3,
+        functools.partial(sum_x_kernel, len(after)),
+        [sds(shape, f32)] + [sds(shape, bf16)] * sends,
         vmem=12,
         nbytes=13 * shape[0] * shape[1] * 2,
         in_specs=[VMEM] * 2 + [ANY] * len(after),
-        out_specs=[VMEM] * 4,
+        out_specs=[VMEM] * (1 + sends),
         name="sum_x",
     )(own, came, *after)
+
+
+def halves_kernel(back, forth, *refs):
+    half = SLOTS // 2
+    refs[-2][...] = back[:, :half]
+    refs[-1][...] = forth[:, half:]
+
+
+def halves(back, forth, after):
+    shape = (3, SLOTS // 2, COLS)
+    return call(
+        halves_kernel,
+        [sds(shape, bf16)] * 2,
+        vmem=6,
+        nbytes=8 * back.size,
+        in_specs=[VMEM] * 2 + [ANY] * len(after),
+        out_specs=[VMEM] * 2,
+        name="halves",
+    )(back, forth, *after)
 
 
 def sum_rest_kernel(kept, c1, c2, c3, *refs):
@@ -266,6 +285,22 @@
         out_specs=VMEM,
         name="sum_rest",
     )(kept, *came, *after)
+
+
+def sum_slot_kernel(slot, own, came, *refs):
+    refs[-1][...] = (own[slot].astype(f32) + came[slot].astype(f32)).astype(bf16)
+
+
+def sum_slot(slot, own, came, after):
+    return call(
+        functools.partial(sum_slot_kernel, slot),
+        sds(own.shape[1:], bf16),
+        vmem=8,
+        nbytes=own.size * 2,
+        in_specs=[VMEM] * 2 + [ANY] * len(after),
+        out_specs=VMEM,
+        name="sum_slot",
+    )(own, came, *after)
 
 
 def sum_keys_kernel(q_grad, own, came, *refs):
@@ -488,7 +523,7 @@
 
 
 def proj_kernel(left, weight, *refs):
-    outs, buffer, sems = refs[:4], refs[4], refs[5]
+    outs, buffer, sems = refs[-6:-2], refs[-2], refs[-1]
     copies = load(k_cuts(weight.at[0]), k_cuts(buffer), sems)
     for cut, copy in enumerate(copies):
         copy.wait()
@@ -500,18 +535,18 @@
                 outs[slot][xbit, :, cols] = rounded[start:start + ROWS]
 
 
-def proj_parts(mixed, weights):
+def proj_parts(mixed, weights, after):
     return call(
         proj_kernel,
         [sds((2, ROWS, WIDTH), bf16)] * 4,
         vmem=14,
         flops=2 * SLOTS * WIDTH * COLS,
         nbytes=WIDTH * COLS * 2 + SLOTS * WIDTH * 2,
-        in_specs=[VMEM, HBM],
+        in_specs=[VMEM, HBM] + [ANY] * len(after),
         out_specs=[VMEM] * 4,
         scratch_shapes=DOT_SCRATCH,
         name="proj_parts",
-    )(mixed, weights)
+    )(mixed, weights, *after)
 
 
 def slot_of(row, x_index, z_index):
@@ -644,17 +679,17 @@
             own[i - 4] = share
 
 
-def out_weight_parts(grad_full, mixed):
+def out_weight_parts(grad_full, mixed, after):
     return call(
         out_kernel,
         [sds((4, COLS, COLS), bf16)] * 2,
         vmem=12,
         flops=2 * SLOTS * WIDTH * COLS,
         nbytes=SLOTS * WIDTH * 2 + WIDTH * COLS * 2,
-        in_specs=[VMEM] * 2,
+        in_specs=[VMEM] * 2 + [ANY] * len(after),
         out_specs=[VMEM] * 2,
         name="out_weight_parts",
-    )(grad_full, mixed)
+    )(grad_full, mixed, *after)
 
 
 def share_kernel(which, full, c1, c2, c3, g0, g1, g2, g3, g4, *refs):
@@ -742,53 +777,50 @@
     chunks = chunks_over_y(normed_full)
 
     mixed = attend_forward(spans, query, own_kv, other_kv, [])
-    proj = proj_parts(mixed, w_out)
-    proj_came = [lax.ppermute(proj[i], "tp", z_shift(-STEPS[i])) for i in range(1, 4)]
-    grad_full, grad_mixed = grad_mixed_of(grad_pairs, w_out, [proj[0]] + chunks[:2])
+    grad_full, grad_mixed = grad_mixed_of(grad_pairs, w_out, [mixed] + chunks[:2])
     q_grad, own_part, other_part = attend_backward(
         spans, query, own_kv, other_kv, mixed, grad_mixed, []
     )
     back = lax.ppermute(other_part, "grp", GRP_SWAP)
-    out_own, out_sent = out_weight_parts(grad_full, mixed)
+    proj = proj_parts(mixed, w_out, [q_grad])
+    proj_came = [lax.ppermute(proj[i], "tp", z_shift(-STEPS[i])) for i in range(1, 4)]
+    out_own, out_sent = out_weight_parts(grad_full, mixed, [q_grad])
     out_came = lax.ppermute(out_sent, "seq", CORE_SWAP)
-    out_kept, *out_sends = sum_x(out_own, out_came)
-    out_terms = [lax.ppermute(v, "seq", y_shift(-k)) for v, k in zip(out_sends, STEPS[1:])]
-    own_grads = sum_keys(q_grad, own_part, back, [out_own] + proj_came[:2])
-    half = SLOTS // 2
+    out_kept, *out_sends = sum_x(out_own, out_came, sends=2)
+    out_terms = [lax.ppermute(v, "seq", y_shift(-k)) for v, k in zip(out_sends, STEPS[1:3])]
+    own_grads = sum_keys(q_grad, own_part, back, [proj[0]])
     back_grads = lax.ppermute(own_grads, "seq", y_shift(1))
     next_grads = lax.ppermute(own_grads, "seq", y_shift(3))
-    far_grads = [
-        lax.ppermute(back_grads[:, :half], "seq", y_shift(1)),
-        lax.ppermute(next_grads[:, half:], "seq", y_shift(3)),
-    ]
-    grads = [own_grads, back_grads, next_grads] + far_grads
-
-    right = back_right(
-        own_grads, w_parts, normed_full, chunks[2:] + proj_came[2:]
-    )
+
+    right = back_right(own_grads, w_parts, normed_full, [out_came] + chunks[2:])
     right_x = lax.ppermute(right[1], "tp", X_SWAP)
-    left = back_left(own_grads, w_parts, normed_full, right[2], [out_sends[0]])
+    left = back_left(own_grads, w_parts, normed_full, right[2], [out_sends[0]] + proj_came[:2])
     left_came = [lax.ppermute(left[i], "tp", z_shift(-STEPS[i])) for i in range(1, 4)]
-    left_kept, left_sent, gain_kept = sum_left(left[0], left_came, [right_x])
+    relayed = halves(back_grads, next_grads, left_came[:1] + [right_x])
+    grads = [own_grads, back_grads, next_grads]
+    grads += [lax.ppermute(v, "seq", y_shift(k)) for v, k in zip(relayed, (1, 3))]
+    left_kept, left_sent, gain_kept = sum_left(left[0], left_came)
     left_x = lax.ppermute(left_sent, "tp", X_SWAP)
     gain_sum = sum_gain(gain_kept, left_x, gains)
     gain_sum = gain_sum + lax.ppermute(gain_sum, "seq", CORE_SWAP)
+    out_far = sum_slot(3, out_own, out_came, [gain_sum])
+    out_terms.append(lax.ppermute(out_far, "seq", y_shift(2)))
     gain_grad = gain_sum
     for k in STEPS[1:]:
         gain_grad = gain_grad + lax.ppermute(gain_sum, "seq", y_shift(k))
     shares = (normed_full, chunks, grads)
     qkv_sent = weight_shares(0, *shares, bf16)
     right_kept, *right_sends = sum_x(
-        right[0], right_x, [left_x, qkv_sent] + out_terms[:2]
+        right[0], right_x, [left_sent]
     )
-    proj_kept, proj_sent = sum_z(proj[0], proj_came)
     right_came = [lax.ppermute(v, "tp", z_shift(-k)) for v, k in zip(right_sends, STEPS[1:])]
     tokens_grad = token_rows(
         x_rows, grad_rows, gains, inv, (left_kept, left_x), (right_kept, *right_came)
     )
 
-    qkv_mine = weight_shares(1, *shares, f32, [qkv_sent, right_sends[0]])
+    qkv_mine = weight_shares(1, *shares, f32, [qkv_sent] + out_terms[:2])
     qkv_share = qkv_mine + lax.ppermute(qkv_sent, "seq", CORE_SWAP).astype(f32)
+    proj_kept, proj_sent = sum_z(proj[0], proj_came, right_came[:1])
     proj_x = lax.ppermute(proj_sent, "tp", X_SWAP)
     layer_out = layer_rows(x_rows, proj_kept, proj_x)
     out_share = sum_rest(out_kept, out_terms, right_came[:1])

time: 172 us -> 188 us (1.093)
  waiting for transfers between devices: 63.6 us -> 82.8 us
  starting transfers between devices: 64.1 us -> 60.9 us
    ppermute x3 -> x2, waiting for transfers between devices: 0.01 us -> 14.4 us  [per_device(): lax.ppermute(v, 'seq', y_shift(-k))]
    ppermute x3, waiting for transfers between devices: 8.49 us -> 19.1 us  [per_device(): lax.ppermute(left[i], 'tp', z_shift(-STEPS[i]))]
    ppermute x3, waiting for transfers between devices: 7.35 us -> 1.94 us  [per_device(): lax.ppermute(proj[i], 'tp', z_shift(-STEPS[i]))]
    ppermute x3, waiting for transfers between devices: 5.35 us -> 0.01 us  [per_device(): lax.ppermute(v, 'tp', z_shift(-k))]
    ppermute x1, waiting for transfers between devices: 9.05 us -> 4.2 us  [per_device(): back_grads = lax.ppermute(own_grads, 'seq', y_shift(1))]
    ppermute x3, waiting for transfers between devices: 7.78 us -> 12.6 us  [gather_blocks(): lax.ppermute(right_pair, 'tp', z_shift(k))]
    ppermute x3, starting transfers between devices: 5.43 us -> 0.94 us  [per_device(): gain_grad = gain_grad + lax.ppermute(gain_sum, 'seq', y_shift(k))]
    ppermute x1, waiting for transfers between devices: 7.57 us -> 3.53 us  [per_device(): left_x = lax.ppermute(left_sent, 'tp', X_SWAP)]
  transfers between devices with their start and end apart: 42 -> 42, of which waited for: 21 -> 24; matrix products, arithmetic and copies ran while one was open for 0% -> 0% of each run, Pallas kernels for 17% -> 13%
where the time goes in v8:
time: 188 us
  waiting for transfers between devices  82.8 us (44%)
  starting transfers between devices  60.9 us (32%)
  Pallas kernels  32.8 us (17%)
  local copies, waits for them, and re-layouts  7.21 us (4%)
  other arithmetic  3.03 us (2%)
    ppermute x3, waiting for transfers between devices, per_device(): lax.ppermute(left[i], 'tp', z_shift(-STEPS[i]))  19.1 us
    ppermute x2, waiting for transfers between devices, per_device(): lax.ppermute(v, 'seq', y_shift(-k))  14.4 us
    ppermute x3, waiting for transfers between devices, gather_blocks(): lax.ppermute(right_pair, 'tp', z_shift(k))  12.6 us
    ppermute x3, starting transfers between devices, per_device(): lax.ppermute(left[i], 'tp', z_shift(-STEPS[i]))  7.95 us
    ppermute x3, starting transfers between devices, per_device(): lax.ppermute(proj[i], 'tp', z_shift(-STEPS[i]))  7.75 us
    ppermute x3, waiting for transfers between devices, per_device(): gain_grad = gain_grad + lax.ppermute(gain_sum, 'seq', y_shift(k))  7.49 us
    unnamed x20, local copies, waits for them, and re-layouts  7.21 us
    ppermute x3, starting transfers between devices, chunks_over_y(): lax.ppermute(sent, 'seq', y_shift(k))  6.63 us
  transfers between devices with their start and end apart: 42, of which 24 were waited for; matrix products, arithmetic and copies ran while one was open for 0% of the time, Pallas kernels for 13%

profile of v8, /device:TPU:0, one launch (start us, length us, event | category | flops | bytes accessed | tf_op | source)
XLA Modules:
  0.0 187.7 jit_solution(16648253267794694473)
XLA Ops:
  3.5 2.1 %collective-permute-start = (bf16[32,2048]{1,0:T(8,128)(2,1)S(1)}, bf16[32,2048]{1,0:T(8,128)(2,1)S(1)}, u32[]{:S(2)}, u32[]{:S(2)}) collective-permute-start(bf16[32,2048]{1,0:T(8,128)(2,1)S(1)} %get-tuple-element.46), channel_id=1, source_target_pairs={{0,1},{1,2},{2,3},{3,0},{4,5},{5,6},{6,7},{7,4},{8,9},{9,10},{10,1... | collective-permute-start | bytes 393224 | tf_op jit(solution)/shard_map/ppermute | solution.py:139
  5.5 2.2 %collective-permute-start.1 = (bf16[32,2048]{1,0:T(8,128)(2,1)S(1)}, bf16[32,2048]{1,0:T(8,128)(2,1)S(1)}, u32[]{:S(2)}, u32[]{:S(2)}) collective-permute-start(bf16[32,2048]{1,0:T(8,128)(2,1)S(1)} %get-tuple-element.46), channel_id=1, source_target_pairs={{0,3},{1,0},{2,1},{3,2},{4,7},{5,4},{6,5},{7,6},{8,11},{9,8},{10,9... | collective-permute-start | bytes 393224 | tf_op jit(solution)/shard_map/ppermute | solution.py:139
  7.7 1.8 collective-permute-start.2
  11.6 1.8 collective-permute-done.1
  13.3 1.8 collective-permute-done.2
  16.8 2.0 %collective-permute-done.8 = bf16[32,4096]{1,0:T(8,128)(2,1)S(1)} collective-permute-done((bf16[32,4096]{1,0:T(8,128)(2,1)S(1)}, bf16[32,4096]{1,0:T(8,128)(2,1)S(1)}, u32[]{:S(2)}, u32[]{:S(2)}) %collective-permute-start.8) | collective-permute-done | bytes 262176 | tf_op jit(solution)/shard_map/ppermute | solution.py:771
  19.6 2.0 %collective-permute-done.4 = bf16[32,2048]{1,0:T(8,128)(2,1)S(1)} collective-permute-done((bf16[32,2048]{1,0:T(8,128)(2,1)S(1)}, bf16[32,2048]{1,0:T(8,128)(2,1)S(1)}, u32[]{:S(2)}, u32[]{:S(2)}) %collective-permute-start.4) | collective-permute-done | bytes 131104 | tf_op jit(solution)/shard_map/ppermute | solution.py:138
  22.7 2.2 %collective-permute-start.6 = (bf16[2,32,2048]{2,1,0:T(8,128)(2,1)S(1)}, bf16[2,32,2048]{2,1,0:T(8,128)(2,1)S(1)}, u32[]{:S(2)}, u32[]{:S(2)}) collective-permute-start(bf16[2,32,2048]{2,1,0:T(8,128)(2,1)S(1)} %pad_maximum_fusion.2.refs_2_), channel_id=1, source_target_pairs={{0,3},{1,0},{2,1},{3,2},{4,7},{5,4},{6,5},{7,6},{8,11},{9,8},{10,9... | collective-permute-start | bytes 786440 | tf_op jit(solution)/shard_map/ppermute | solution.py:140
  25.5 8.8 %collective-permute-done.5.refs_3_ = bf16[2,32,2048]{2,1,0:T(8,128)(2,1)S(1)} collective-permute-done((bf16[2,32,2048]{2,1,0:T(8,128)(2,1)S(1)}, bf16[2,32,2048]{2,1,0:T(8,128)(2,1)S(1)}, u32[]{:S(2)}, u32[]{:S(2)}) %collective-permute-start.5) | collective-permute-done | bytes 262176 | tf_op jit(solution)/shard_map/ppermute | solution.py:140
  34.2 3.8 %collective-permute-done.6.refs_4_ = bf16[2,32,2048]{2,1,0:T(8,128)(2,1)S(1)} collective-permute-done((bf16[2,32,2048]{2,1,0:T(8,128)(2,1)S(1)}, bf16[2,32,2048]{2,1,0:T(8,128)(2,1)S(1)}, u32[]{:S(2)}, u32[]{:S(2)}) %collective-permute-start.6) | collective-permute-done | bytes 262176 | tf_op jit(solution)/shard_map/ppermute | solution.py:140
  38.0 4.6 %copy-done = bf16[1,4096,3,512]{3,1,2,0:T(8,128)(2,1)S(1)} copy-done((bf16[1,4096,3,512]{3,1,2,0:T(8,128)(2,1)S(1)}, bf16[1,4096,3,512]{3,1,2,0:T(8,128)(2,1)}, u32[]{:S(2)}) %copy-start) | copy-done | bytes 12582936
  42.6 3.7 %key_value.1 = (bf16[256,4096]{1,0:T(8,128)(2,1)S(1)}, bf16[2,256,512]{2,1,0:T(8,128)(2,1)S(1)}) custom-call(bf16[4,32,2048]{2,1,0:T(8,128)(2,1)S(1)} %pad_maximum_fusion.refs_0_, bf16[4,32,2048]{2,1,0:T(8,128)(2,1)S(1)} %collective-permute-done.3.refs_1_, bf16[2,32,2048]{2,1,0:T(8,128)(2,1)S(1)} %pad_maximum_fusion.2.refs_2_, ...), custom_call_target="tpu_custom_call" | custom-call | flops 2147483648 | bytes 12582912 | tf_op jit(solution)/shard_map/key_value/pallas_call | solution.py:369
  46.3 2.8 %collective-permute-start.11 = (bf16[2,256,512]{2,1,0:T(8,128)(2,1)S(1)}, bf16[2,256,512]{2,1,0:T(8,128)(2,1)S(1)}, u32[]{:S(2)}, u32[]{:S(2)}) collective-permute-start(bf16[2,256,512]{2,1,0:T(8,128)(2,1)S(1)} %get-tuple-element.50.own_kv), channel_id=1, source_target_pairs={{0,64},{64,0},{1,65},{65,1},{2,66},{66,2},{3,67},{67,3},{4,68},{68... | collective-permute-start | bytes 1572872 | tf_op jit(solution)/shard_map/ppermute | solution.py:775
  49.1 1.8 collective-permute-start.12
  52.6 1.9 collective-permute-start.14
  54.5 1.8 query.1
  57.1 2.4 %attend_forward.1.refs_0_.mixed.left = bf16[256,512]{1,0:T(8,128)(2,1)S(1)} custom-call(s32[1,5]{1,0:T(1,128)S(1)} %copy-done.8, s32[1,4]{1,0:T(1,128)S(1)} %copy-done.9, bf16[256,512]{1,0:T(8,128)(2,1)S(1)} %query.1, bf16[2,256,512]{2,1,0:T(8,128)(2,1)S(1)} %get-tuple-element.50.own_kv, bf16[2,256,512]{2,1,0:T(8,128)(2,1)S(1)} %collective-permute-done.11.other_kv), custom_call_target="tpu_custom_call" | custom-call | flops 536870912 | bytes 1572864 | tf_op jit(solution)/shard_map/attend_forward/pallas_call | solution.py:643
  61.8 1.9 %grad_mixed.1 = (bf16[256,4096]{1,0:T(8,128)(2,1)S(1)}, bf16[256,512]{1,0:T(8,128)(2,1)S(1)}) custom-call(bf16[2,32,4096]{2,1,0:T(8,128)(2,1)S(1)} %pad_maximum_fusion.1.refs_7_.p0, bf16[2,32,4096]{2,1,0:T(8,128)(2,1)S(1)} %collective-permute-done.9.refs_0_.p1, bf16[2,32,4096]{2,1,0:T(8,128)(2,1)S(1)} %collective-permute-done.10.refs_1_.p2, ...), custom_call_target="tpu_custom_call" | custom-call | flops 1073741824 | bytes 8388608 | tf_op jit(solution)/shard_map/grad_mixed/pallas_call | solution.py:418
  63.7 4.3 %attend_backward.1 = (bf16[256,512]{1,0:T(8,128)(2,1)S(1)}, f32[2,256,512]{2,1,0:T(8,128)S(1)}, bf16[2,256,512]{2,1,0:T(8,128)(2,1)S(1)}) custom-call(s32[1,5]{1,0:T(1,128)S(1)} %copy-done.8, s32[1,4]{1,0:T(1,128)S(1)} %copy-done.9, bf16[256,512]{1,0:T(8,128)(2,1)S(1)} %query.1, bf16[2,256,512]{2,1,0:T(8,128)(2,1)S(1)} %get-tuple-element.50.own_kv, ...), custom_call_target="tpu_custom_call" | custom-call | flops 1073741824 | bytes 3145728 | tf_op jit(solution)/shard_map/attend_backward/pallas_call | solution.py:657
  70.0 3.1 %collective-permute-start.20 = (bf16[256,1024]{1,0:T(8,128)(2,1)S(1)}, bf16[256,1024]{1,0:T(8,128)(2,1)S(1)}, u32[]{:S(2)}, u32[]{:S(2)}) collective-permute-start(bf16[256,1024]{1,0:T(8,128)(2,1)S(1)} %get-tuple-element.63), channel_id=1, source_target_pairs={{0,32},{8,40},{16,48},{24,56},{32,0},{40,8},{48,16},{56,24},{1,33}... | collective-permute-start | bytes 1572872 | tf_op jit(solution)/shard_map/ppermute | solution.py:744
  73.1 2.2 %proj_parts.1 = (bf16[2,32,4096]{2,1,0:T(8,128)(2,1)S(1)}, bf16[2,32,4096]{2,1,0:T(8,128)(2,1)S(1)}, bf16[2,32,4096]{2,1,0:T(8,128)(2,1)S(1)}, bf16[2,32,4096]{2,1,0:T(8,128)(2,1)S(1)}) custom-call(bf16[256,512]{1,0:T(8,128)(2,1)S(1)} %attend_forward.1.refs_0_.mixed.left, bf16[1,4096,512]{2,1,0:T(8,128)(2,1)S(1)} %copy-done.2, ...), custom_call_target="tpu_custom_call" | custom-call | flops 1073741824 | bytes 6291456 | tf_op jit(solution)/shard_map/proj_parts/pallas_call | solution.py:539
  75.3 5.5 %collective-permute-start.15 = (bf16[2,32,4096]{2,1,0:T(8,128)(2,1)S(1)}, bf16[2,32,4096]{2,1,0:T(8,128)(2,1)S(1)}, u32[]{:S(2)}, u32[]{:S(2)}) collective-permute-start(bf16[2,32,4096]{2,1,0:T(8,128)(2,1)S(1)} %get-tuple-element.56), channel_id=1, source_target_pairs={{0,3},{1,0},{2,1},{3,2},{4,7},{5,4},{6,5},{7,6},{8,11},{9,8},{10,9... | collective-permute-start | bytes 1572872 | tf_op jit(solution)/shard_map/ppermute | solution.py:786
  80.9 4.4 %collective-permute-done.18.came = bf16[2,256,512]{2,1,0:T(8,128)(2,1)S(1)} collective-permute-done((bf16[2,256,512]{2,1,0:T(8,128)(2,1)S(1)}, bf16[2,256,512]{2,1,0:T(8,128)(2,1)S(1)}, u32[]{:S(2)}, u32[]{:S(2)}) %collective-permute-start.18) | collective-permute-done | bytes 524320 | tf_op jit(solution)/shard_map/ppermute | solution.py:784
  87.0 1.8 collective-permute-start.35
  88.8 3.1 %back_right.1 = (bf16[4,32,2048]{2,1,0:T(8,128)(2,1)S(1)}, bf16[4,32,2048]{2,1,0:T(8,128)(2,1)S(1)}, f32[1,2048]{1,0:T(1,128)S(1)}) custom-call(bf16[3,256,512]{2,1,0:T(8,128)(2,1)S(1)} %sum_keys.1.grads.g0, bf16[3,4096,512]{2,1,0:T(8,128)(2,1)S(1)} %bitcast.22, bf16[256,4096]{1,0:T(8,128)(2,1)S(1)} %get-tuple-element.49.full.normed, ...), custom_call_target="tpu_custom_call" | custom-call | flops 1610612736 | bytes 8388608 | tf_op jit(solution)/shard_map/back_right/pallas_call | solution.py:499
  93.6 1.9 %collective-permute-done.16.refs_2_.c2 = bf16[2,32,4096]{2,1,0:T(8,128)(2,1)S(1)} collective-permute-done((bf16[2,32,4096]{2,1,0:T(8,128)(2,1)S(1)}, bf16[2,32,4096]{2,1,0:T(8,128)(2,1)S(1)}, u32[]{:S(2)}, u32[]{:S(2)}) %collective-permute-start.16) | collective-permute-done | bytes 524320 | tf_op jit(solution)/shard_map/ppermute | solution.py:786
  95.5 3.1 %back_left.1 = (bf16[5,16,2048]{2,1,0:T(8,128)(2,1)S(1)}, bf16[5,16,2048]{2,1,0:T(8,128)(2,1)S(1)}, bf16[5,16,2048]{2,1,0:T(8,128)(2,1)S(1)}, bf16[5,16,2048]{2,1,0:T(8,128)(2,1)S(1)}) custom-call(bf16[3,256,512]{2,1,0:T(8,128)(2,1)S(1)} %sum_keys.1.grads.g0, bf16[3,4096,512]{2,1,0:T(8,128)(2,1)S(1)} %bitcast.23, ...), custom_call_target="tpu_custom_call" | custom-call | flops 1610612736 | bytes 8388608 | tf_op jit(solution)/shard_map/back_left/pallas_call | solution.py:499
  98.6 3.0 %collective-permute-start.22 = (bf16[5,16,2048]{2,1,0:T(8,128)(2,1)S(1)}, bf16[5,16,2048]{2,1,0:T(8,128)(2,1)S(1)}, u32[]{:S(2)}, u32[]{:S(2)}) collective-permute-start(bf16[5,16,2048]{2,1,0:T(8,128)(2,1)S(1)} %get-tuple-element.70), channel_id=1, source_target_pairs={{0,3},{1,0},{2,1},{3,2},{4,7},{5,4},{6,5},{7,6},{8,11},{9,8},{10,9... | collective-permute-start | bytes 983048 | tf_op jit(solution)/shard_map/ppermute | solution.py:798
  101.6 4.2 %collective-permute-done.34.back.g1 = bf16[3,256,512]{2,1,0:T(8,128)(2,1)S(1)} collective-permute-done((bf16[3,256,512]{2,1,0:T(8,128)(2,1)S(1)}, bf16[3,256,512]{2,1,0:T(8,128)(2,1)S(1)}, u32[]{:S(2)}, u32[]{:S(2)}) %collective-permute-start.34) | collective-permute-done | bytes 786464 | tf_op jit(solution)/shard_map/ppermute | solution.py:792
  105.9 1.7 collective-permute-done.22.c1.refs_0_
  107.8 3.1 %collective-permute-start.37 = (bf16[3,128,512]{2,1,0:T(8,128)(2,1)S(1)}, bf16[3,128,512]{2,1,0:T(8,128)(2,1)S(1)}, u32[]{:S(2)}, u32[]{:S(2)}) collective-permute-start(bf16[3,128,512]{2,1,0:T(8,128)(2,1)S(1)} %get-tuple-element.84), channel_id=1, source_target_pairs={{0,48},{8,56},{16,0},{24,8},{32,16},{40,24},{48,32},{56,40},{1,49}... | collective-permute-start | bytes 1179656 | tf_op jit(solution)/shard_map/ppermute | solution.py:801
  110.9 2.2 %collective-permute-start.17 = (bf16[2,32,4096]{2,1,0:T(8,128)(2,1)S(1)}, bf16[2,32,4096]{2,1,0:T(8,128)(2,1)S(1)}, u32[]{:S(2)}, u32[]{:S(2)}) collective-permute-start(bf16[2,32,4096]{2,1,0:T(8,128)(2,1)S(1)} %get-tuple-element.58), channel_id=1, source_target_pairs={{0,2},{1,3},{2,0},{3,1},{4,6},{5,7},{6,4},{7,5},{8,10},{9,11},{10,... | collective-permute-start | bytes 1572872 | tf_op jit(solution)/shard_map/ppermute | solution.py:786
  113.1 2.3 %collective-permute-start.23 = (bf16[5,16,2048]{2,1,0:T(8,128)(2,1)S(1)}, bf16[5,16,2048]{2,1,0:T(8,128)(2,1)S(1)}, u32[]{:S(2)}, u32[]{:S(2)}) collective-permute-start(bf16[5,16,2048]{2,1,0:T(8,128)(2,1)S(1)} %get-tuple-element.71), channel_id=1, source_target_pairs={{0,1},{1,2},{2,3},{3,0},{4,5},{5,6},{6,7},{7,4},{8,9},{9,10},{10,1... | collective-permute-start | bytes 983048 | tf_op jit(solution)/shard_map/ppermute | solution.py:798
  115.5 2.6 %collective-permute-start.24 = (bf16[5,16,2048]{2,1,0:T(8,128)(2,1)S(1)}, bf16[5,16,2048]{2,1,0:T(8,128)(2,1)S(1)}, u32[]{:S(2)}, u32[]{:S(2)}) collective-permute-start(bf16[5,16,2048]{2,1,0:T(8,128)(2,1)S(1)} %get-tuple-element.72), channel_id=1, source_target_pairs={{0,2},{1,3},{2,0},{3,1},{4,6},{5,7},{6,4},{7,5},{8,10},{9,11},{10,... | collective-permute-start | bytes 983048 | tf_op jit(solution)/shard_map/ppermute | solution.py:798
  118.0 2.3 %weight_shares.2.refs_0_ = bf16[3,512,512]{2,1,0:T(8,128)(2,1)S(1)} custom-call(bf16[256,4096]{1,0:T(8,128)(2,1)S(1)} %get-tuple-element.49.full.normed, bf16[256,1024]{1,0:T(8,128)(2,1)S(1)} %collective-permute-done.13.refs_1_.c1, bf16[256,1024]{1,0:T(8,128)(2,1)S(1)} %collective-permute-done.14.refs_2_.c2, ...), custom_call_target="tpu_custom_call" | custom-call | flops 1610612736 | bytes 7340032 | tf_op jit(solution)/shard_map/weight_shares/pallas_call | solution.py:714
  120.4 13.8 %collective-permute-done.23.c2 = bf16[5,16,2048]{2,1,0:T(8,128)(2,1)S(1)} collective-permute-done((bf16[5,16,2048]{2,1,0:T(8,128)(2,1)S(1)}, bf16[5,16,2048]{2,1,0:T(8,128)(2,1)S(1)}, u32[]{:S(2)}, u32[]{:S(2)}) %collective-permute-start.23) | collective-permute-done | bytes 327712 | tf_op jit(solution)/shard_map/ppermute | solution.py:798
  134.2 3.6 %collective-permute-done.24.c3 = bf16[5,16,2048]{2,1,0:T(8,128)(2,1)S(1)} collective-permute-done((bf16[5,16,2048]{2,1,0:T(8,128)(2,1)S(1)}, bf16[5,16,2048]{2,1,0:T(8,128)(2,1)S(1)}, u32[]{:S(2)}, u32[]{:S(2)}) %collective-permute-start.24) | collective-permute-done | bytes 327712 | tf_op jit(solution)/shard_map/ppermute | solution.py:798
  138.0 2.0 %collective-permute-start.27 = (bf16[3,16,2048]{2,1,0:T(8,128)(2,1)S(1)}, bf16[3,16,2048]{2,1,0:T(8,128)(2,1)S(1)}, u32[]{:S(2)}, u32[]{:S(2)}) collective-permute-start(bf16[3,16,2048]{2,1,0:T(8,128)(2,1)S(1)} %get-tuple-element.73.refs_0_), channel_id=1, source_target_pairs={{0,4},{1,5},{2,6},{3,7},{4,0},{5,1},{6,2},{7,3},{8,12},{9,13},{10,... | collective-permute-start | bytes 589832 | tf_op jit(solution)/shard_map/ppermute | solution.py:803
  140.2 3.5 %collective-permute-done.27.l_came.came = bf16[3,16,2048]{2,1,0:T(8,128)(2,1)S(1)} collective-permute-done((bf16[3,16,2048]{2,1,0:T(8,128)(2,1)S(1)}, bf16[3,16,2048]{2,1,0:T(8,128)(2,1)S(1)}, u32[]{:S(2)}, u32[]{:S(2)}) %collective-permute-start.27) | collective-permute-done | bytes 196640 | tf_op jit(solution)/shard_map/ppermute | solution.py:803
  145.0 2.3 %collective-permute-start.29 = (bf16[32,2048]{1,0:T(8,128)(2,1)S(1)}, bf16[32,2048]{1,0:T(8,128)(2,1)S(1)}, u32[]{:S(2)}, u32[]{:S(2)}) collective-permute-start(bf16[32,2048]{1,0:T(8,128)(2,1)S(1)} %get-tuple-element.81), channel_id=1, source_target_pairs={{0,2},{1,3},{2,0},{3,1},{4,6},{5,7},{6,4},{7,5},{8,10},{9,11},{10,... | collective-permute-start | bytes 393224 | tf_op jit(solution)/shard_map/ppermute | solution.py:816
  147.4 4.9 %collective-permute-done.31 = f32[1,4096]{1,0:T(1,128)S(1)} collective-permute-done((f32[1,4096]{1,0:T(1,128)S(1)}, f32[1,4096]{1,0:T(1,128)S(1)}, u32[]{:S(2)}, u32[]{:S(2)}) %collective-permute-start.31) | collective-permute-done | bytes 16416 | tf_op jit(solution)/shard_map/ppermute | solution.py:810
  153.6 2.5 %collective-permute-done.32 = f32[1,4096]{1,0:T(1,128)S(1)} collective-permute-done((f32[1,4096]{1,0:T(1,128)S(1)}, f32[1,4096]{1,0:T(1,128)S(1)}, u32[]{:S(2)}, u32[]{:S(2)}) %collective-permute-start.32) | collective-permute-done | bytes 16416 | tf_op jit(solution)/shard_map/ppermute | solution.py:810
  157.6 2.3 %collective-permute-start.39 = (bf16[512,512]{1,0:T(8,128)(2,1)S(1)}, bf16[512,512]{1,0:T(8,128)(2,1)S(1)}, u32[]{:S(2)}, u32[]{:S(2)}) collective-permute-start(bf16[512,512]{1,0:T(8,128)(2,1)S(1)} %get-tuple-element.85), channel_id=1, source_target_pairs={{0,16},{8,24},{16,32},{24,40},{32,48},{40,56},{48,0},{56,8},{1,17}... | collective-permute-start | bytes 1572872 | tf_op jit(solution)/shard_map/ppermute | solution.py:790
  163.3 3.5 %collective-permute-done.26.came = bf16[32,4096]{1,0:T(8,128)(2,1)S(1)} collective-permute-done((bf16[32,4096]{1,0:T(8,128)(2,1)S(1)}, bf16[32,4096]{1,0:T(8,128)(2,1)S(1)}, u32[]{:S(2)}, u32[]{:S(2)}) %collective-permute-start.26) | collective-permute-done | bytes 262176 | tf_op jit(solution)/shard_map/ppermute | solution.py:824
  167.6 11.0 %collective-permute-done.38.refs_1_.c1 = bf16[512,512]{1,0:T(8,128)(2,1)S(1)} collective-permute-done((bf16[512,512]{1,0:T(8,128)(2,1)S(1)}, bf16[512,512]{1,0:T(8,128)(2,1)S(1)}, u32[]{:S(2)}, u32[]{:S(2)}) %collective-permute-start.38) | collective-permute-done | bytes 524320 | tf_op jit(solution)/shard_map/ppermute | solution.py:790
  178.6 3.4 %collective-permute-done.39.refs_2_.c2 = bf16[512,512]{1,0:T(8,128)(2,1)S(1)} collective-permute-done((bf16[512,512]{1,0:T(8,128)(2,1)S(1)}, bf16[512,512]{1,0:T(8,128)(2,1)S(1)}, u32[]{:S(2)}, u32[]{:S(2)}) %collective-permute-start.39) | collective-permute-done | bytes 524320 | tf_op jit(solution)/shard_map/ppermute | solution.py:790
  182.0 2.3 %weight_shares.3 = f32[3,512,512]{2,1,0:T(8,128)S(1)} custom-call(bf16[256,4096]{1,0:T(8,128)(2,1)S(1)} %get-tuple-element.49.full.normed, bf16[256,1024]{1,0:T(8,128)(2,1)S(1)} %collective-permute-done.13.refs_1_.c1, bf16[256,1024]{1,0:T(8,128)(2,1)S(1)} %collective-permute-done.14.refs_2_.c2, bf16[256,1024]{1,0:T(8,128)(2,1)S(1)} %collective-permute-done.20.refs_1_.c3, ...), custom_call_target="tpu_custom_call" | custom-call | flops 1610612736 | bytes 7340032 | tf_op jit(solution)/shard_map/weight_shares/pallas_call | solution.py:714
  185.5 2.2 %add_bitcast_fusion = f32[1,512,3,512]{3,1,2,0:T(8,128)} fusion(f32[3,512,512]{2,1,0:T(8,128)S(1)} %weight_shares.3, bf16[3,512,512]{2,1,0:T(8,128)(2,1)S(1)} %collective-permute-done.40), kind=kLoop, calls=%fused_computation | loop fusion | flops 1572864 | bytes 7864320 | tf_op jit(solution)/shard_map/broadcast_in_dim | solution.py:831
  (86 shorter events, 29.6 us)
Async XLA Ops:
  3.5 8.1 %collective-permute-start = (bf16[32,2048]{1,0:T(8,128)(2,1)S(1)}, bf16[32,2048]{1,0:T(8,128)(2,1)S(1)}, u32[]{:S(2)}, u32[]{:S(2)}) collective-permute-start(bf16[32,2048]{1,0:T(8,128)(2,1)S(1)} %get-tuple-element.46), channel_id=1, source_target_pairs={{0,1},{1,2},{2,3},{3,0},{4,5},{5,6},{6,7},{7,4},{8,9},{9,10},{10,1... | collective-permute-start | bytes 393224 | tf_op jit(solution)/shard_map/ppermute | solution.py:139
  5.5 7.8 %collective-permute-start.1 = (bf16[32,2048]{1,0:T(8,128)(2,1)S(1)}, bf16[32,2048]{1,0:T(8,128)(2,1)S(1)}, u32[]{:S(2)}, u32[]{:S(2)}) collective-permute-start(bf16[32,2048]{1,0:T(8,128)(2,1)S(1)} %get-tuple-element.46), channel_id=1, source_target_pairs={{0,3},{1,0},{2,1},{3,2},{4,7},{5,4},{6,5},{7,6},{8,11},{9,8},{10,9... | collective-permute-start | bytes 393224 | tf_op jit(solution)/shard_map/ppermute | solution.py:139
  7.7 7.4 %collective-permute-start.2 = (bf16[32,2048]{1,0:T(8,128)(2,1)S(1)}, bf16[32,2048]{1,0:T(8,128)(2,1)S(1)}, u32[]{:S(2)}, u32[]{:S(2)}) collective-permute-start(bf16[32,2048]{1,0:T(8,128)(2,1)S(1)} %get-tuple-element.46), channel_id=1, source_target_pairs={{0,2},{1,3},{2,0},{3,1},{4,6},{5,7},{6,4},{7,5},{8,10},{9,11},{10,... | collective-permute-start | bytes 393224 | tf_op jit(solution)/shard_map/ppermute | solution.py:139
  9.5 9.2 %collective-permute-start.8 = (bf16[32,4096]{1,0:T(8,128)(2,1)S(1)}, bf16[32,4096]{1,0:T(8,128)(2,1)S(1)}, u32[]{:S(2)}, u32[]{:S(2)}) collective-permute-start(bf16[32,4096]{1,0:T(8,128)(2,1)S(1)} %get-tuple-element.48.grad), channel_id=1, source_target_pairs={{0,4},{1,5},{2,6},{3,7},{4,0},{5,1},{6,2},{7,3},{8,12},{9,13},{10,... | collective-permute-start | bytes 786440 | tf_op jit(solution)/shard_map/ppermute | solution.py:771
  11.0 10.6 %collective-permute-start.4 = (bf16[32,2048]{1,0:T(8,128)(2,1)S(1)}, bf16[32,2048]{1,0:T(8,128)(2,1)S(1)}, u32[]{:S(2)}, u32[]{:S(2)}) collective-permute-start(bf16[32,2048]{1,0:T(8,128)(2,1)S(1)} %get-tuple-element.47), channel_id=1, source_target_pairs={{0,4},{1,5},{2,6},{3,7},{4,0},{5,1},{6,2},{7,3},{8,12},{9,13},{10,... | collective-permute-start | bytes 393224 | tf_op jit(solution)/shard_map/ppermute | solution.py:138
  15.2 22.8 %collective-permute-start.3 = (bf16[4,32,2048]{2,1,0:T(8,128)(2,1)S(1)}, bf16[4,32,2048]{2,1,0:T(8,128)(2,1)S(1)}, u32[]{:S(2)}, u32[]{:S(2)}) collective-permute-start(bf16[4,32,2048]{2,1,0:T(8,128)(2,1)S(1)} %pad_maximum_fusion.refs_0_), channel_id=1, source_target_pairs={{0,4},{1,5},{2,6},{3,7},{4,0},{5,1},{6,2},{7,3},{8,12},{9,13},{10,... | collective-permute-start | bytes 1572872 | tf_op jit(solution)/shard_map/ppermute | solution.py:142
  18.8 33.8 %collective-permute-start.10 = (bf16[2,32,4096]{2,1,0:T(8,128)(2,1)S(1)}, bf16[2,32,4096]{2,1,0:T(8,128)(2,1)S(1)}, u32[]{:S(2)}, u32[]{:S(2)}) collective-permute-start(bf16[2,32,4096]{2,1,0:T(8,128)(2,1)S(1)} %pad_maximum_fusion.1.refs_7_.p0), channel_id=1, source_target_pairs={{0,3},{1,0},{2,1},{3,2},{4,7},{5,4},{6,5},{7,6},{8,11},{9,8},{10,9... | collective-permute-start | bytes 1572872 | tf_op jit(solution)/shard_map/ppermute | solution.py:773
  21.6 12.6 %collective-permute-start.5 = (bf16[2,32,2048]{2,1,0:T(8,128)(2,1)S(1)}, bf16[2,32,2048]{2,1,0:T(8,128)(2,1)S(1)}, u32[]{:S(2)}, u32[]{:S(2)}) collective-permute-start(bf16[2,32,2048]{2,1,0:T(8,128)(2,1)S(1)} %pad_maximum_fusion.2.refs_2_), channel_id=1, source_target_pairs={{0,1},{1,2},{2,3},{3,0},{4,5},{5,6},{6,7},{7,4},{8,9},{9,10},{10,1... | collective-permute-start | bytes 786440 | tf_op jit(solution)/shard_map/ppermute | solution.py:140
  22.7 15.3 %collective-permute-start.6 = (bf16[2,32,2048]{2,1,0:T(8,128)(2,1)S(1)}, bf16[2,32,2048]{2,1,0:T(8,128)(2,1)S(1)}, u32[]{:S(2)}, u32[]{:S(2)}) collective-permute-start(bf16[2,32,2048]{2,1,0:T(8,128)(2,1)S(1)} %pad_maximum_fusion.2.refs_2_), channel_id=1, source_target_pairs={{0,3},{1,0},{2,1},{3,2},{4,7},{5,4},{6,5},{7,6},{8,11},{9,8},{10,9... | collective-permute-start | bytes 786440 | tf_op jit(solution)/shard_map/ppermute | solution.py:140
  24.9 13.1 %collective-permute-start.7 = (bf16[2,32,2048]{2,1,0:T(8,128)(2,1)S(1)}, bf16[2,32,2048]{2,1,0:T(8,128)(2,1)S(1)}, u32[]{:S(2)}, u32[]{:S(2)}) collective-permute-start(bf16[2,32,2048]{2,1,0:T(8,128)(2,1)S(1)} %pad_maximum_fusion.2.refs_2_), channel_id=1, source_target_pairs={{0,2},{1,3},{2,0},{3,1},{4,6},{5,7},{6,4},{7,5},{8,10},{9,11},{10,... | collective-permute-start | bytes 786440 | tf_op jit(solution)/shard_map/ppermute | solution.py:140
  34.2 20.3 %collective-permute-start.9 = (bf16[2,32,4096]{2,1,0:T(8,128)(2,1)S(1)}, bf16[2,32,4096]{2,1,0:T(8,128)(2,1)S(1)}, u32[]{:S(2)}, u32[]{:S(2)}) collective-permute-start(bf16[2,32,4096]{2,1,0:T(8,128)(2,1)S(1)} %pad_maximum_fusion.1.refs_7_.p0), channel_id=1, source_target_pairs={{0,1},{1,2},{2,3},{3,0},{4,5},{5,6},{6,7},{7,4},{8,9},{9,10},{10,1... | collective-permute-start | bytes 1572872 | tf_op jit(solution)/shard_map/ppermute | solution.py:773
  38.0 4.6 %copy-start = (bf16[1,4096,3,512]{3,1,2,0:T(8,128)(2,1)S(1)}, bf16[1,4096,3,512]{3,1,2,0:T(8,128)(2,1)}, u32[]{:S(2)}) copy-start(bf16[1,4096,3,512]{3,1,2,0:T(8,128)(2,1)} %param.11) | copy-start | bytes 37748740
  42.6 11.9 %copy-start.1 = (bf16[1,4096,3,512]{3,1,2,0:T(8,128)(2,1)S(1)}, bf16[1,4096,3,512]{3,1,2,0:T(8,128)(2,1)}, u32[]{:S(2)}) copy-start(bf16[1,4096,3,512]{3,1,2,0:T(8,128)(2,1)} %param.11) | copy-start | bytes 37748740
  46.3 10.8 %collective-permute-start.11 = (bf16[2,256,512]{2,1,0:T(8,128)(2,1)S(1)}, bf16[2,256,512]{2,1,0:T(8,128)(2,1)S(1)}, u32[]{:S(2)}, u32[]{:S(2)}) collective-permute-start(bf16[2,256,512]{2,1,0:T(8,128)(2,1)S(1)} %get-tuple-element.50.own_kv), channel_id=1, source_target_pairs={{0,64},{64,0},{1,65},{65,1},{2,66},{66,2},{3,67},{67,3},{4,68},{68... | collective-permute-start | bytes 1572872 | tf_op jit(solution)/shard_map/ppermute | solution.py:775
  49.1 10.7 %collective-permute-start.12 = (bf16[2,32,4096]{2,1,0:T(8,128)(2,1)S(1)}, bf16[2,32,4096]{2,1,0:T(8,128)(2,1)S(1)}, u32[]{:S(2)}, u32[]{:S(2)}) collective-permute-start(bf16[2,32,4096]{2,1,0:T(8,128)(2,1)S(1)} %pad_maximum_fusion.1.refs_7_.p0), channel_id=1, source_target_pairs={{0,2},{1,3},{2,0},{3,1},{4,6},{5,7},{6,4},{7,5},{8,10},{9,11},{10,... | collective-permute-start | bytes 1572872 | tf_op jit(solution)/shard_map/ppermute | solution.py:773
  51.0 10.5 %collective-permute-start.13 = (bf16[256,1024]{1,0:T(8,128)(2,1)S(1)}, bf16[256,1024]{1,0:T(8,128)(2,1)S(1)}, u32[]{:S(2)}, u32[]{:S(2)}) collective-permute-start(bf16[256,1024]{1,0:T(8,128)(2,1)S(1)} %get-tuple-element.51), channel_id=1, source_target_pairs={{0,16},{8,24},{16,32},{24,40},{32,48},{40,56},{48,0},{56,8},{1,17}... | collective-permute-start | bytes 1572872 | tf_op jit(solution)/shard_map/ppermute | solution.py:744
  52.6 4.4 %copy-start.9 = (s32[1,4]{1,0:T(1,128)S(1)}, s32[1,4]{1,0:T(1,128)}, u32[]{:S(2)}) copy-start(s32[1,4]{1,0:T(1,128)} %runs.3) | copy-start | bytes 52
  52.6 9.2 %collective-permute-start.14 = (bf16[256,1024]{1,0:T(8,128)(2,1)S(1)}, bf16[256,1024]{1,0:T(8,128)(2,1)S(1)}, u32[]{:S(2)}, u32[]{:S(2)}) collective-permute-start(bf16[256,1024]{1,0:T(8,128)(2,1)S(1)} %get-tuple-element.52), channel_id=1, source_target_pairs={{0,48},{8,56},{16,0},{24,8},{32,16},{40,24},{48,32},{56,40},{1,49}... | collective-permute-start | bytes 1572872 | tf_op jit(solution)/shard_map/ppermute | solution.py:744
  54.5 7.3 %copy-start.2 = (bf16[1,4096,512]{2,1,0:T(8,128)(2,1)S(1)}, bf16[1,4096,512]{2,1,0:T(8,128)(2,1)}, u32[]{:S(2)}) copy-start(bf16[1,4096,512]{2,1,0:T(8,128)(2,1)} %weight.3) | copy-start | bytes 12582916
  69.3 19.5 %collective-permute-start.19 = (bf16[4,512,512]{2,1,0:T(8,128)(2,1)S(1)}, bf16[4,512,512]{2,1,0:T(8,128)(2,1)S(1)}, u32[]{:S(2)}, u32[]{:S(2)}) collective-permute-start(bf16[4,512,512]{2,1,0:T(8,128)(2,1)S(1)} %get-tuple-element.62), channel_id=1, source_target_pairs={{0,8},{8,0},{16,24},{24,16},{32,40},{40,32},{48,56},{56,48},{1,9},... | collective-permute-start | bytes 6291464 | tf_op jit(solution)/shard_map/ppermute | solution.py:788
  69.4 15.8 %collective-permute-start.18 = (bf16[2,256,512]{2,1,0:T(8,128)(2,1)S(1)}, bf16[2,256,512]{2,1,0:T(8,128)(2,1)S(1)}, u32[]{:S(2)}, u32[]{:S(2)}) collective-permute-start(bf16[2,256,512]{2,1,0:T(8,128)(2,1)S(1)} %get-tuple-element.60), channel_id=1, source_target_pairs={{0,64},{64,0},{1,65},{65,1},{2,66},{66,2},{3,67},{67,3},{4,68},{68... | collective-permute-start | bytes 1572872 | tf_op jit(solution)/shard_map/ppermute | solution.py:784
  70.0 17.0 %collective-permute-start.20 = (bf16[256,1024]{1,0:T(8,128)(2,1)S(1)}, bf16[256,1024]{1,0:T(8,128)(2,1)S(1)}, u32[]{:S(2)}, u32[]{:S(2)}) collective-permute-start(bf16[256,1024]{1,0:T(8,128)(2,1)S(1)} %get-tuple-element.63), channel_id=1, source_target_pairs={{0,32},{8,40},{16,48},{24,56},{32,0},{40,8},{48,16},{56,24},{1,33}... | collective-permute-start | bytes 1572872 | tf_op jit(solution)/shard_map/ppermute | solution.py:744
  75.3 18.2 %collective-permute-start.15 = (bf16[2,32,4096]{2,1,0:T(8,128)(2,1)S(1)}, bf16[2,32,4096]{2,1,0:T(8,128)(2,1)S(1)}, u32[]{:S(2)}, u32[]{:S(2)}) collective-permute-start(bf16[2,32,4096]{2,1,0:T(8,128)(2,1)S(1)} %get-tuple-element.56), channel_id=1, source_target_pairs={{0,3},{1,0},{2,1},{3,2},{4,7},{5,4},{6,5},{7,6},{8,11},{9,8},{10,9... | collective-permute-start | bytes 1572872 | tf_op jit(solution)/shard_map/ppermute | solution.py:786
  80.9 14.6 %collective-permute-start.16 = (bf16[2,32,4096]{2,1,0:T(8,128)(2,1)S(1)}, bf16[2,32,4096]{2,1,0:T(8,128)(2,1)S(1)}, u32[]{:S(2)}, u32[]{:S(2)}) collective-permute-start(bf16[2,32,4096]{2,1,0:T(8,128)(2,1)S(1)} %get-tuple-element.57), channel_id=1, source_target_pairs={{0,1},{1,2},{2,3},{3,0},{4,5},{5,6},{6,7},{7,4},{8,9},{9,10},{10,1... | collective-permute-start | bytes 1572872 | tf_op jit(solution)/shard_map/ppermute | solution.py:786
  85.4 20.5 %collective-permute-start.34 = (bf16[3,256,512]{2,1,0:T(8,128)(2,1)S(1)}, bf16[3,256,512]{2,1,0:T(8,128)(2,1)S(1)}, u32[]{:S(2)}, u32[]{:S(2)}) collective-permute-start(bf16[3,256,512]{2,1,0:T(8,128)(2,1)S(1)} %sum_keys.1.grads.g0), channel_id=1, source_target_pairs={{0,16},{8,24},{16,32},{24,40},{32,48},{40,56},{48,0},{56,8},{1,17}... | collective-permute-start | bytes 2359304 | tf_op jit(solution)/shard_map/ppermute | solution.py:792
  87.0 18.8 %collective-permute-start.35 = (bf16[3,256,512]{2,1,0:T(8,128)(2,1)S(1)}, bf16[3,256,512]{2,1,0:T(8,128)(2,1)S(1)}, u32[]{:S(2)}, u32[]{:S(2)}) collective-permute-start(bf16[3,256,512]{2,1,0:T(8,128)(2,1)S(1)} %sum_keys.1.grads.g0), channel_id=1, source_target_pairs={{0,48},{8,56},{16,0},{24,8},{32,16},{40,24},{48,32},{56,40},{1,49}... | collective-permute-start | bytes 2359304 | tf_op jit(solution)/shard_map/ppermute | solution.py:793
  91.9 15.6 %collective-permute-start.21 = (bf16[4,32,2048]{2,1,0:T(8,128)(2,1)S(1)}, bf16[4,32,2048]{2,1,0:T(8,128)(2,1)S(1)}, u32[]{:S(2)}, u32[]{:S(2)}) collective-permute-start(bf16[4,32,2048]{2,1,0:T(8,128)(2,1)S(1)} %get-tuple-element.65), channel_id=1, source_target_pairs={{0,4},{1,5},{2,6},{3,7},{4,0},{5,1},{6,2},{7,3},{8,12},{9,13},{10,... | collective-permute-start | bytes 1572872 | tf_op jit(solution)/shard_map/ppermute | solution.py:796
  98.6 8.9 %collective-permute-start.22 = (bf16[5,16,2048]{2,1,0:T(8,128)(2,1)S(1)}, bf16[5,16,2048]{2,1,0:T(8,128)(2,1)S(1)}, u32[]{:S(2)}, u32[]{:S(2)}) collective-permute-start(bf16[5,16,2048]{2,1,0:T(8,128)(2,1)S(1)} %get-tuple-element.70), channel_id=1, source_target_pairs={{0,3},{1,0},{2,1},{3,2},{4,7},{5,4},{6,5},{7,6},{8,11},{9,8},{10,9... | collective-permute-start | bytes 983048 | tf_op jit(solution)/shard_map/ppermute | solution.py:798
  107.6 10.4 %collective-permute-start.36 = (bf16[3,128,512]{2,1,0:T(8,128)(2,1)S(1)}, bf16[3,128,512]{2,1,0:T(8,128)(2,1)S(1)}, u32[]{:S(2)}, u32[]{:S(2)}) collective-permute-start(bf16[3,128,512]{2,1,0:T(8,128)(2,1)S(1)} %get-tuple-element.83), channel_id=1, source_target_pairs={{0,16},{8,24},{16,32},{24,40},{32,48},{40,56},{48,0},{56,8},{1,17}... | collective-permute-start | bytes 1179656 | tf_op jit(solution)/shard_map/ppermute | solution.py:801
  107.8 10.2 %collective-permute-start.37 = (bf16[3,128,512]{2,1,0:T(8,128)(2,1)S(1)}, bf16[3,128,512]{2,1,0:T(8,128)(2,1)S(1)}, u32[]{:S(2)}, u32[]{:S(2)}) collective-permute-start(bf16[3,128,512]{2,1,0:T(8,128)(2,1)S(1)} %get-tuple-element.84), channel_id=1, source_target_pairs={{0,48},{8,56},{16,0},{24,8},{32,16},{40,24},{48,32},{56,40},{1,49}... | collective-permute-start | bytes 1179656 | tf_op jit(solution)/shard_map/ppermute | solution.py:801
  110.9 36.4 %collective-permute-start.17 = (bf16[2,32,4096]{2,1,0:T(8,128)(2,1)S(1)}, bf16[2,32,4096]{2,1,0:T(8,128)(2,1)S(1)}, u32[]{:S(2)}, u32[]{:S(2)}) collective-permute-start(bf16[2,32,4096]{2,1,0:T(8,128)(2,1)S(1)} %get-tuple-element.58), channel_id=1, source_target_pairs={{0,2},{1,3},{2,0},{3,1},{4,6},{5,7},{6,4},{7,5},{8,10},{9,11},{10,... | collective-permute-start | bytes 1572872 | tf_op jit(solution)/shard_map/ppermute | solution.py:786
  113.1 21.1 %collective-permute-start.23 = (bf16[5,16,2048]{2,1,0:T(8,128)(2,1)S(1)}, bf16[5,16,2048]{2,1,0:T(8,128)(2,1)S(1)}, u32[]{:S(2)}, u32[]{:S(2)}) collective-permute-start(bf16[5,16,2048]{2,1,0:T(8,128)(2,1)S(1)} %get-tuple-element.71), channel_id=1, source_target_pairs={{0,1},{1,2},{2,3},{3,0},{4,5},{5,6},{6,7},{7,4},{8,9},{9,10},{10,1... | collective-permute-start | bytes 983048 | tf_op jit(solution)/shard_map/ppermute | solution.py:798
  115.5 22.3 %collective-permute-start.24 = (bf16[5,16,2048]{2,1,0:T(8,128)(2,1)S(1)}, bf16[5,16,2048]{2,1,0:T(8,128)(2,1)S(1)}, u32[]{:S(2)}, u32[]{:S(2)}) collective-permute-start(bf16[5,16,2048]{2,1,0:T(8,128)(2,1)S(1)} %get-tuple-element.72), channel_id=1, source_target_pairs={{0,2},{1,3},{2,0},{3,1},{4,6},{5,7},{6,4},{7,5},{8,10},{9,11},{10,... | collective-permute-start | bytes 983048 | tf_op jit(solution)/shard_map/ppermute | solution.py:798
  120.3 23.4 %copy-start.7 = (bf16[1,4096]{1,0:T(2,128)(2,1)S(1)}, bf16[1,4096]{1,0:T(2,128)(2,1)}, u32[]{:S(2)}) copy-start(bf16[1,4096]{1,0:T(2,128)(2,1)} %gain.5) | copy-start | bytes 24580
  120.3 65.2 %collective-permute-start.40 = (bf16[3,512,512]{2,1,0:T(8,128)(2,1)S(1)}, bf16[3,512,512]{2,1,0:T(8,128)(2,1)S(1)}, u32[]{:S(2)}, u32[]{:S(2)}) collective-permute-start(bf16[3,512,512]{2,1,0:T(8,128)(2,1)S(1)} %weight_shares.2.refs_0_), channel_id=1, source_target_pairs={{0,8},{8,0},{16,24},{24,16},{32,40},{40,32},{48,56},{56,48},{1,9},... | collective-permute-start | bytes 4718600 | tf_op jit(solution)/shard_map/ppermute | solution.py:822
  138.0 5.7 %collective-permute-start.27 = (bf16[3,16,2048]{2,1,0:T(8,128)(2,1)S(1)}, bf16[3,16,2048]{2,1,0:T(8,128)(2,1)S(1)}, u32[]{:S(2)}, u32[]{:S(2)}) collective-permute-start(bf16[3,16,2048]{2,1,0:T(8,128)(2,1)S(1)} %get-tuple-element.73.refs_0_), channel_id=1, source_target_pairs={{0,4},{1,5},{2,6},{3,7},{4,0},{5,1},{6,2},{7,3},{8,12},{9,13},{10,... | collective-permute-start | bytes 589832 | tf_op jit(solution)/shard_map/ppermute | solution.py:803
  140.1 12.3 %collective-permute-start.25 = (bf16[32,2048]{1,0:T(8,128)(2,1)S(1)}, bf16[32,2048]{1,0:T(8,128)(2,1)S(1)}, u32[]{:S(2)}, u32[]{:S(2)}) collective-permute-start(bf16[32,2048]{1,0:T(8,128)(2,1)S(1)} %get-tuple-element.74), channel_id=1, source_target_pairs={{0,3},{1,0},{2,1},{3,2},{4,7},{5,4},{6,5},{7,6},{8,11},{9,8},{10,9... | collective-permute-start | bytes 393224 | tf_op jit(solution)/shard_map/ppermute | solution.py:816
  143.8 1.3 collective-permute-start.30
  143.8 16.0 %collective-permute-start.28 = (bf16[32,2048]{1,0:T(8,128)(2,1)S(1)}, bf16[32,2048]{1,0:T(8,128)(2,1)S(1)}, u32[]{:S(2)}, u32[]{:S(2)}) collective-permute-start(bf16[32,2048]{1,0:T(8,128)(2,1)S(1)} %get-tuple-element.80), channel_id=1, source_target_pairs={{0,1},{1,2},{2,3},{3,0},{4,5},{5,6},{6,7},{7,4},{8,9},{9,10},{10,1... | collective-permute-start | bytes 393224 | tf_op jit(solution)/shard_map/ppermute | solution.py:816
  145.0 15.4 %collective-permute-start.29 = (bf16[32,2048]{1,0:T(8,128)(2,1)S(1)}, bf16[32,2048]{1,0:T(8,128)(2,1)S(1)}, u32[]{:S(2)}, u32[]{:S(2)}) collective-permute-start(bf16[32,2048]{1,0:T(8,128)(2,1)S(1)} %get-tuple-element.81), channel_id=1, source_target_pairs={{0,2},{1,3},{2,0},{3,1},{4,6},{5,7},{6,4},{7,5},{8,10},{9,11},{10,... | collective-permute-start | bytes 393224 | tf_op jit(solution)/shard_map/ppermute | solution.py:816
  147.4 5.0 %collective-permute-start.31 = (f32[1,4096]{1,0:T(1,128)S(1)}, f32[1,4096]{1,0:T(1,128)S(1)}, u32[]{:S(2)}, u32[]{:S(2)}) collective-permute-start(f32[1,4096]{1,0:T(1,128)S(1)} %add.15.refs_0_), channel_id=1, source_target_pairs={{0,16},{8,24},{16,32},{24,40},{32,48},{40,56},{48,0},{56,8},{1,17}... | collective-permute-start | bytes 49160 | tf_op jit(solution)/shard_map/ppermute | solution.py:810
  152.4 3.7 %collective-permute-start.32 = (f32[1,4096]{1,0:T(1,128)S(1)}, f32[1,4096]{1,0:T(1,128)S(1)}, u32[]{:S(2)}, u32[]{:S(2)}) collective-permute-start(f32[1,4096]{1,0:T(1,128)S(1)} %add.15.refs_0_), channel_id=1, source_target_pairs={{0,48},{8,56},{16,0},{24,8},{32,16},{40,24},{48,32},{56,40},{1,49}... | collective-permute-start | bytes 49160 | tf_op jit(solution)/shard_map/ppermute | solution.py:810
  152.4 5.2 %collective-permute-start.33 = (f32[1,4096]{1,0:T(1,128)S(1)}, f32[1,4096]{1,0:T(1,128)S(1)}, u32[]{:S(2)}, u32[]{:S(2)}) collective-permute-start(f32[1,4096]{1,0:T(1,128)S(1)} %add.15.refs_0_), channel_id=1, source_target_pairs={{0,32},{8,40},{16,48},{24,56},{32,0},{40,8},{48,16},{56,24},{1,33}... | collective-permute-start | bytes 49160 | tf_op jit(solution)/shard_map/ppermute | solution.py:810
  153.4 8.9 %copy-start.4 = (bf16[1,1,32,4096]{3,2,1,0:T(8,128)(2,1)S(1)}, bf16[1,1,32,4096]{3,2,1,0:T(8,128)(2,1)}, u32[]{:S(2)}) copy-start(bf16[1,1,32,4096]{3,2,1,0:T(8,128)(2,1)} %param.7) | copy-start | bytes 786436
  156.1 22.5 %collective-permute-start.38 = (bf16[512,512]{1,0:T(8,128)(2,1)S(1)}, bf16[512,512]{1,0:T(8,128)(2,1)S(1)}, u32[]{:S(2)}, u32[]{:S(2)}) collective-permute-start(bf16[512,512]{1,0:T(8,128)(2,1)S(1)} %get-tuple-element.68.refs_0_), channel_id=1, source_target_pairs={{0,48},{8,56},{16,0},{24,8},{32,16},{40,24},{48,32},{56,40},{1,49}... | collective-permute-start | bytes 1572872 | tf_op jit(solution)/shard_map/ppermute | solution.py:790
  157.6 24.4 %collective-permute-start.39 = (bf16[512,512]{1,0:T(8,128)(2,1)S(1)}, bf16[512,512]{1,0:T(8,128)(2,1)S(1)}, u32[]{:S(2)}, u32[]{:S(2)}) collective-permute-start(bf16[512,512]{1,0:T(8,128)(2,1)S(1)} %get-tuple-element.85), channel_id=1, source_target_pairs={{0,16},{8,24},{16,32},{24,40},{32,48},{40,56},{48,0},{56,8},{1,17}... | collective-permute-start | bytes 1572872 | tf_op jit(solution)/shard_map/ppermute | solution.py:790
  159.9 24.4 %collective-permute-start.41 = (bf16[512,512]{1,0:T(8,128)(2,1)S(1)}, bf16[512,512]{1,0:T(8,128)(2,1)S(1)}, u32[]{:S(2)}, u32[]{:S(2)}) collective-permute-start(bf16[512,512]{1,0:T(8,128)(2,1)S(1)} %sum_slot.1), channel_id=1, source_target_pairs={{0,32},{8,40},{16,48},{24,56},{32,0},{40,8},{48,16},{56,24},{1,33}... | collective-permute-start | bytes 1572872 | tf_op jit(solution)/shard_map/ppermute | solution.py:807
  160.4 6.4 %collective-permute-start.26 = (bf16[32,4096]{1,0:T(8,128)(2,1)S(1)}, bf16[32,4096]{1,0:T(8,128)(2,1)S(1)}, u32[]{:S(2)}, u32[]{:S(2)}) collective-permute-start(bf16[32,4096]{1,0:T(8,128)(2,1)S(1)} %get-tuple-element.76), channel_id=1, source_target_pairs={{0,4},{1,5},{2,6},{3,7},{4,0},{5,1},{6,2},{7,3},{8,12},{9,13},{10,... | collective-permute-start | bytes 786440 | tf_op jit(solution)/shard_map/ppermute | solution.py:824
  (4 other events, 7.1 us)

commit v9 on v8

--- a/solution.py
+++ b/solution.py
@@ -112,26 +112,58 @@
     return [ref.at[pl.ds(i * KCUT, KCUT)] for i in range(KCUTS)]
 
 
-def norm_kernel(x, gain, cot, n_left, n_right, grad, inv):
+def norm_kernel(x, gain, n_left, n_right, inv):
     x_float = x[...].astype(f32)
     scale = lax.rsqrt(jnp.mean(x_float * x_float, axis=1, keepdims=True) + 1e-05)
     normed = (x_float * scale * gain[...].astype(f32)).astype(bf16)
     n_left[...] = normed[:, :HALF]
     n_right[...] = normed[:, HALF:]
-    grad[...] = (cot[...].astype(f32) * valid_rows()).astype(bf16)
     inv[...] = jnp.broadcast_to(scale, (ROWS, 128))
 
 
-def norm_rows(x, gain, cot):
+def norm_rows(x, gain):
     part = sds((ROWS, HALF), bf16)
     return call(
         norm_kernel,
-        [part, part, sds((ROWS, WIDTH), bf16), sds((ROWS, 128), f32)],
+        [part, part, sds((ROWS, 128), f32)],
         vmem=4,
-        nbytes=4 * ROWS * WIDTH * 2,
-        in_specs=[VMEM] * 3,
+        nbytes=2 * ROWS * WIDTH * 2,
+        in_specs=[VMEM] * 2,
         name="norm_rows",
-    )(x, gain, cot)
+    )(x, gain)
+
+
+def grad_kernel(cot, *refs):
+    refs[-1][...] = (cot[...].astype(f32) * valid_rows()).astype(bf16)
+
+
+def grad_rows_of(cot, after):
+    return call(
+        grad_kernel,
+        sds((ROWS, WIDTH), bf16),
+        vmem=4,
+        nbytes=2 * ROWS * WIDTH * 2,
+        in_specs=[VMEM] + [ANY] * len(after),
+        out_specs=VMEM,
+        name="grad_rows",
+    )(cot, *after)
+
+
+def pair_kernel(own, other, *refs):
+    refs[-1][0] = own[...]
+    refs[-1][1] = other[...]
+
+
+def pair_of(own, other, after):
+    return call(
+        pair_kernel,
+        sds((2,) + own.shape, own.dtype),
+        vmem=4,
+        nbytes=own.size * 8,
+        in_specs=[VMEM] * 2 + [ANY] * len(after),
+        out_specs=VMEM,
+        name="pair",
+    )(own, other, *after)
 
 
 def gather_blocks(left, right):
@@ -179,19 +211,19 @@
     )(own, *came, *after)
 
 
-def sum_left_kernel(own, c1, c2, c3, *refs):
+def sum_left_kernel(own, c1, c2, *refs):
     kept, sent, gain = refs[-3:]
     for part in range(2):
         total = own[part].astype(f32)
-        for came in (c1, c2, c3):
+        for came in (c1, c2):
             total = total + came[part].astype(f32)
         kept[pl.ds(part * 16, 16)] = total
         total = own[2 + part].astype(f32)
-        for came in (c1, c2, c3):
+        for came in (c1, c2):
             total = total + came[2 + part].astype(f32)
         sent[part] = total.astype(bf16)
     left, right = gain_from(own[4])
-    for came in (c1, c2, c3):
+    for came in (c1, c2):
         more_left, more_right = gain_from(came[4])
         left, right = left + more_left, right + more_right
     sent[2] = gain_rows_of(left, right)
@@ -205,7 +237,7 @@
         [sds((ROWS, HALF), f32), sds((3, 16, HALF), bf16), sds((2, HALF), f32)],
         vmem=4,
         nbytes=11 * ROWS * HALF * 2,
-        in_specs=[VMEM] * 4 + [ANY] * len(after),
+        in_specs=[VMEM] * 3 + [ANY] * len(after),
         out_specs=[VMEM] * 3,
         name="sum_left",
     )(own, *came, *after)
@@ -229,6 +261,79 @@
     )(own, came, gain)
 
 
+def pass_left_kernel(back, forth, far_a, far_b, *refs):
+    out_back, out_forth = refs[-2:]
+    out_forth[...] = forth[...]
+    out_back[...] = back[...]
+    for part in range(2):
+        out_forth[part] = (forth[part].astype(f32) + far_a[part].astype(f32)).astype(bf16)
+        total = back[2 + part].astype(f32) + far_b[part].astype(f32)
+        out_back[2 + part] = total.astype(bf16)
+    left, right = gain_from(forth[4])
+    more_left, more_right = gain_from(far_a[2])
+    out_forth[4] = gain_rows_of(left + more_left, right + more_right)
+
+
+def pass_left(back, forth, far_a, far_b, after=()):
+    return call(
+        pass_left_kernel,
+        [sds(back.shape, bf16)] * 2,
+        vmem=6,
+        nbytes=6 * back.size * 2,
+        in_specs=[VMEM] * 4 + [ANY] * len(after),
+        out_specs=[VMEM] * 2,
+        name="pass_left",
+    )(back, forth, far_a, far_b, *after)
+
+
+def pass_out_kernel(back, forth, far_a, far_b, *refs):
+    out_back, out_forth = refs[-2:]
+    half = COLS // 2
+    out_forth[half:] = forth[half:]
+    out_forth[:half] = (forth[:half].astype(f32) + far_a[...].astype(f32)).astype(bf16)
+    out_back[:half] = back[:half]
+    out_back[half:] = (back[half:].astype(f32) + far_b[...].astype(f32)).astype(bf16)
+
+
+def pass_out(back, forth, far_a, far_b, after=()):
+    return call(
+        pass_out_kernel,
+        [sds(back.shape, bf16)] * 2,
+        vmem=6,
+        nbytes=6 * back.size * 2,
+        in_specs=[VMEM] * 4 + [ANY] * len(after),
+        out_specs=[VMEM] * 2,
+        name="pass_out",
+    )(back, forth, far_a, far_b, *after)
+
+
+def sum_out_kernel(own, came, *refs):
+    kept, back, forth, far_a, far_b = refs[-5:]
+    half = COLS // 2
+
+    def total(slot, rows=slice(None)):
+        return own[slot, rows].astype(f32) + came[slot, rows].astype(f32)
+
+    kept[...] = total(0)
+    back[...] = total(1).astype(bf16)
+    forth[...] = total(2).astype(bf16)
+    far_a[...] = total(3, slice(0, half)).astype(bf16)
+    far_b[...] = total(3, slice(half, COLS)).astype(bf16)
+
+
+def sum_out(own, came, after=()):
+    whole_share, half_share = sds((COLS, COLS), bf16), sds((COLS // 2, COLS), bf16)
+    return call(
+        sum_out_kernel,
+        [sds((COLS, COLS), f32), whole_share, whole_share, half_share, half_share],
+        vmem=12,
+        nbytes=own.size * 6,
+        in_specs=[VMEM] * 2 + [ANY] * len(after),
+        out_specs=[VMEM] * 5,
+        name="sum_out",
+    )(own, came, *after)
+
+
 def sum_x_kernel(waits, own, came, *refs):
     kept, sends = refs[waits], refs[waits + 1:]
     kept[...] = own[0].astype(f32) + came[0].astype(f32)
@@ -268,9 +373,27 @@
     )(back, forth, *after)
 
 
-def sum_rest_kernel(kept, c1, c2, c3, *refs):
+def late_kernel(count, *refs):
+    for i in range(count):
+        refs[i - count][...] = refs[i][...]
+
+
+def late(arrays, after):
+    count = len(arrays)
+    return call(
+        functools.partial(late_kernel, count),
+        [sds(v.shape, v.dtype) for v in arrays],
+        vmem=10,
+        nbytes=sum(v.size * 4 for v in arrays),
+        in_specs=[VMEM] * count + [ANY] * len(after),
+        out_specs=[VMEM] * count,
+        name="late",
+    )(*arrays, *after)
+
+
+def sum_rest_kernel(kept, c1, c2, *refs):
     total = kept[...]
-    for came in (c1, c2, c3):
+    for came in (c1, c2):
         total = total + came[...].astype(f32)
     refs[-1][...] = total
 
@@ -281,26 +404,10 @@
         sds(kept.shape, f32),
         vmem=6,
         nbytes=14 * kept.size,
-        in_specs=[VMEM] * 4 + [ANY] * len(after),
+        in_specs=[VMEM] * 3 + [ANY] * len(after),
         out_specs=VMEM,
         name="sum_rest",
     )(kept, *came, *after)
-
-
-def sum_slot_kernel(slot, own, came, *refs):
-    refs[-1][...] = (own[slot].astype(f32) + came[slot].astype(f32)).astype(bf16)
-
-
-def sum_slot(slot, own, came, after):
-    return call(
-        functools.partial(sum_slot_kernel, slot),
-        sds(own.shape[1:], bf16),
-        vmem=8,
-        nbytes=own.size * 2,
-        in_specs=[VMEM] * 2 + [ANY] * len(after),
-        out_specs=VMEM,
-        name="sum_slot",
-    )(own, came, *after)
 
 
 def sum_keys_kernel(q_grad, own, came, *refs):
@@ -482,7 +589,7 @@
 
 
 def back_left_kernel(waits, grads, weight, normed, gain_right, *refs):
-    outs, buffer, sems = refs[waits:waits + 4], refs[-2], refs[-1]
+    outs, far, buffer, sems = refs[waits:waits + 3], refs[-4:-2], refs[-2], refs[-1]
     for cols, rounded, terms in back_products(
         grads, weight, 0, normed, buffer, sems
     ):
@@ -493,6 +600,11 @@
                 out[2 * xbit, :, cols] = rounded[start:start + 16]
                 out[2 * xbit + 1, :, cols] = rounded[start + 16:start + ROWS]
             out[4, :, cols] = gains
+        for xbit, out in enumerate(far):
+            start = (xbit * 4 + 3) * ROWS
+            out[0, :, cols] = rounded[start:start + 16]
+            out[1, :, cols] = rounded[start + 16:start + ROWS]
+        far[0][2, :, cols] = gains
 
 
 def back_dot(kernel, grads, weights, normed, extra, out_shape, after, name):
@@ -518,7 +630,8 @@
 
 
 def back_left(grads, weights, normed, gain_right, after=()):
-    out = [sds((5, 16, HALF), bf16)] * 4
+    out = [sds((5, 16, HALF), bf16)] * 3
+    out += [sds((3, 16, HALF), bf16), sds((2, 16, HALF), bf16)]
     return back_dot(back_left_kernel, grads, weights, normed, [gain_right], out, after, "back_left")
 
 
@@ -766,10 +879,11 @@
     w_parts = jnp.transpose(w_qkv[0], (1, 0, 2))
     spans = (text_gaps, image_runs)
 
-    n_left, n_right, grad_rows, inv = norm_rows(x_rows, gains, cotangent[0, 0])
+    n_left, n_right, inv = norm_rows(x_rows, gains)
     pieces = gather_blocks(n_left, n_right)
+    grad_rows = grad_rows_of(cotangent[0, 0], pieces[2:3])
     grad_other = lax.ppermute(grad_rows, "tp", X_SWAP)
-    grad_pair = jnp.stack([grad_rows, grad_other])
+    grad_pair = pair_of(grad_rows, grad_other, pieces[3:4])
     grad_pairs = [grad_pair] + [lax.ppermute(grad_pair, "tp", z_shift(k)) for k in STEPS[1:]]
     normed_full, own_kv = key_value(pieces, w_parts, [grad_pair])
     other_kv = lax.ppermute(own_kv, "grp", GRP_SWAP)
@@ -777,34 +891,49 @@
     chunks = chunks_over_y(normed_full)
 
     mixed = attend_forward(spans, query, own_kv, other_kv, [])
-    grad_full, grad_mixed = grad_mixed_of(grad_pairs, w_out, [mixed] + chunks[:2])
+    proj = proj_parts(mixed, w_out, [])
+    grad_full, grad_mixed = grad_mixed_of(grad_pairs, w_out, [proj[0]] + chunks[:2])
     q_grad, own_part, other_part = attend_backward(
         spans, query, own_kv, other_kv, mixed, grad_mixed, []
     )
     back = lax.ppermute(other_part, "grp", GRP_SWAP)
-    proj = proj_parts(mixed, w_out, [q_grad])
-    proj_came = [lax.ppermute(proj[i], "tp", z_shift(-STEPS[i])) for i in range(1, 4)]
+    sends = late(proj[1:3], [q_grad])
+    proj_came = [lax.ppermute(v, "tp", z_shift(-k)) for v, k in zip(sends, (1, 3))]
     out_own, out_sent = out_weight_parts(grad_full, mixed, [q_grad])
     out_came = lax.ppermute(out_sent, "seq", CORE_SWAP)
-    out_kept, *out_sends = sum_x(out_own, out_came, sends=2)
-    out_terms = [lax.ppermute(v, "seq", y_shift(-k)) for v, k in zip(out_sends, STEPS[1:3])]
-    own_grads = sum_keys(q_grad, own_part, back, [proj[0]])
+    own_grads = sum_keys(q_grad, own_part, back, sends[:1])
+    (far_sent,) = late(proj[3:], [own_grads])
+    proj_came.append(lax.ppermute(far_sent, "tp", z_shift(2)))
     back_grads = lax.ppermute(own_grads, "seq", y_shift(1))
     next_grads = lax.ppermute(own_grads, "seq", y_shift(3))
 
     right = back_right(own_grads, w_parts, normed_full, [out_came] + chunks[2:])
     right_x = lax.ppermute(right[1], "tp", X_SWAP)
-    left = back_left(own_grads, w_parts, normed_full, right[2], [out_sends[0]] + proj_came[:2])
-    left_came = [lax.ppermute(left[i], "tp", z_shift(-STEPS[i])) for i in range(1, 4)]
-    relayed = halves(back_grads, next_grads, left_came[:1] + [right_x])
+    left = back_left(own_grads, w_parts, normed_full, right[2], proj_came[:2])
+    left_far_a = lax.ppermute(left[3], "tp", z_shift(1))
+    left_far_b = lax.ppermute(left[4], "tp", z_shift(3))
+    out_kept, *out_sends = sum_out(out_own, out_came, [left_far_a])
+    out_far_a = lax.ppermute(out_sends[2], "seq", y_shift(1))
+    out_far_b = lax.ppermute(out_sends[3], "seq", y_shift(3))
+    left_back, left_forth = pass_left(
+        left[1], left[2], left_far_a, left_far_b, [right_x]
+    )
+    left_came = [
+        lax.ppermute(left_forth, "tp", z_shift(1)), lax.ppermute(left_back, "tp", z_shift(3))
+    ]
+    relayed = halves(back_grads, next_grads, [left_far_a, left_far_b, proj_came[2]])
     grads = [own_grads, back_grads, next_grads]
     grads += [lax.ppermute(v, "seq", y_shift(k)) for v, k in zip(relayed, (1, 3))]
-    left_kept, left_sent, gain_kept = sum_left(left[0], left_came)
+    out_back, out_forth = pass_out(
+        out_sends[0], out_sends[1], out_far_a, out_far_b, left_came[:1]
+    )
+    out_terms = [
+        lax.ppermute(out_forth, "seq", y_shift(1)), lax.ppermute(out_back, "seq", y_shift(3))
+    ]
+    left_kept, left_sent, gain_kept = sum_left(left[0], left_came, [right_x])
     left_x = lax.ppermute(left_sent, "tp", X_SWAP)
     gain_sum = sum_gain(gain_kept, left_x, gains)
     gain_sum = gain_sum + lax.ppermute(gain_sum, "seq", CORE_SWAP)
-    out_far = sum_slot(3, out_own, out_came, [gain_sum])
-    out_terms.append(lax.ppermute(out_far, "seq", y_shift(2)))
     gain_grad = gain_sum
     for k in STEPS[1:]:
         gain_grad = gain_grad + lax.ppermute(gain_sum, "seq", y_shift(k))
@@ -818,9 +947,9 @@
         x_rows, grad_rows, gains, inv, (left_kept, left_x), (right_kept, *right_came)
     )
 
-    qkv_mine = weight_shares(1, *shares, f32, [qkv_sent] + out_terms[:2])
+    qkv_mine = weight_shares(1, *shares, f32, [qkv_sent])
     qkv_share = qkv_mine + lax.ppermute(qkv_sent, "seq", CORE_SWAP).astype(f32)
-    proj_kept, proj_sent = sum_z(proj[0], proj_came, right_came[:1])
+    proj_kept, proj_sent = sum_z(proj[0], proj_came)
     proj_x = lax.ppermute(proj_sent, "tp", X_SWAP)
     layer_out = layer_rows(x_rows, proj_kept, proj_x)
     out_share = sum_rest(out_kept, out_terms, right_came[:1])

time: 188 us -> 185 us (0.984)
  waiting for transfers between devices: 82.8 us -> 67.8 us
  starting transfers between devices: 60.9 us -> 70.9 us
    ppermute x3, waiting for transfers between devices: 12.6 us -> 0.01 us  [gather_blocks(): lax.ppermute(right_pair, 'tp', z_shift(k))]
    ppermute x1, waiting for transfers between devices: 1.99 us -> 12.1 us  [per_device(): grad_other = lax.ppermute(grad_rows, 'tp', X_SWAP)]
    ppermute x9, waiting for transfers between devices: 35.4 us -> 25.9 us  [the longest x1 9.66 us: per_device(): proj_came.append(lax.ppermute(far_sent, 'tp', z_shift(2)))]
    ppermute x3, waiting for transfers between devices: 7.49 us -> 0.01 us  [per_device(): gain_grad = gain_grad + lax.ppermute(gain_sum, 'seq', y_shift(k))]
    ppermute x1, starting transfers between devices: 0.58 us -> 6.09 us  [per_device(): back = lax.ppermute(other_part, 'grp', GRP_SWAP)]
    ppermute x1, waiting for transfers between devices: 4.2 us -> 0.01 us  [per_device(): back_grads = lax.ppermute(own_grads, 'seq', y_shift(1))]
    ppermute x3, starting transfers between devices: 0.94 us -> 4.44 us  [per_device(): gain_grad = gain_grad + lax.ppermute(gain_sum, 'seq', y_shift(k))]
    ppermute x3 -> x5, waiting for transfers between devices: 0.01 us -> 3.49 us  [per_device(): lax.ppermute(v, 'tp', z_shift(-k))]
  transfers between devices with their start and end apart: 42 -> 44, of which waited for: 24 -> 16; matrix products, arithmetic and copies ran while one was open for 0% -> 0% of each run, Pallas kernels for 13% -> 14%
where the time goes in v9:
time: 185 us; the launch traced here: 183 us
  starting transfers between devices  70.9 us (38%)
  waiting for transfers between devices  67.8 us (37%)
  Pallas kernels  33.1 us (18%)
  local copies, waits for them, and re-layouts  7.2 us (4%)
  other arithmetic  2.98 us (2%)
    ppermute x1, waiting for transfers between devices, per_device(): grad_other = lax.ppermute(grad_rows, 'tp', X_SWAP)  12.1 us
    ppermute x1, waiting for transfers between devices, per_device(): proj_came.append(lax.ppermute(far_sent, 'tp', z_shift(2)))  9.66 us
    ppermute x1, starting transfers between devices, per_device(): proj_came.append(lax.ppermute(far_sent, 'tp', z_shift(2)))  8.88 us
    ppermute x1, waiting for transfers between devices, per_device(): lax.ppermute(out_forth, 'seq', y_shift(1))  8.14 us
    unnamed x20, local copies, waits for them, and re-layouts  7.2 us
    ppermute x1, waiting for transfers between devices, per_device(): back = lax.ppermute(other_part, 'grp', GRP_SWAP)  7.15 us
    ppermute x3, starting transfers between devices, chunks_over_y(): lax.ppermute(sent, 'seq', y_shift(k))  6.89 us
    ppermute x1, waiting for transfers between devices, per_device(): left_x = lax.ppermute(left_sent, 'tp', X_SWAP)  6.88 us
  transfers between devices with their start and end apart: 44, of which 16 were waited for; matrix products, arithmetic and copies ran while one was open for 0% of the time, Pallas kernels for 14%

profile of v9, /device:TPU:0, one launch (start us, length us, event | category | flops | bytes accessed | tf_op | source)
XLA Modules:
  0.0 183.3 jit_solution(9165801076310361441)
XLA Ops:
  2.5 2.1 %collective-permute-start = (bf16[32,2048]{1,0:T(8,128)(2,1)S(1)}, bf16[32,2048]{1,0:T(8,128)(2,1)S(1)}, u32[]{:S(2)}, u32[]{:S(2)}) collective-permute-start(bf16[32,2048]{1,0:T(8,128)(2,1)S(1)} %get-tuple-element.54), channel_id=1, source_target_pairs={{0,1},{1,2},{2,3},{3,0},{4,5},{5,6},{6,7},{7,4},{8,9},{9,10},{10,1... | collective-permute-start | bytes 393224 | tf_op jit(solution)/shard_map/ppermute | solution.py:171
  4.5 2.2 %collective-permute-start.1 = (bf16[32,2048]{1,0:T(8,128)(2,1)S(1)}, bf16[32,2048]{1,0:T(8,128)(2,1)S(1)}, u32[]{:S(2)}, u32[]{:S(2)}) collective-permute-start(bf16[32,2048]{1,0:T(8,128)(2,1)S(1)} %get-tuple-element.54), channel_id=1, source_target_pairs={{0,3},{1,0},{2,1},{3,2},{4,7},{5,4},{6,5},{7,6},{8,11},{9,8},{10,9... | collective-permute-start | bytes 393224 | tf_op jit(solution)/shard_map/ppermute | solution.py:171
  6.7 1.8 collective-permute-start.2
  8.5 1.5 collective-permute-start.4
  10.2 2.2 %collective-permute-done.1 = bf16[32,2048]{1,0:T(8,128)(2,1)S(1)} collective-permute-done((bf16[32,2048]{1,0:T(8,128)(2,1)S(1)}, bf16[32,2048]{1,0:T(8,128)(2,1)S(1)}, u32[]{:S(2)}, u32[]{:S(2)}) %collective-permute-start.1) | collective-permute-done | bytes 131104 | tf_op jit(solution)/shard_map/ppermute | solution.py:171
  12.3 1.8 collective-permute-done.2
  14.2 1.6 collective-permute-start.3
  18.6 2.1 %collective-permute-start.6 = (bf16[2,32,2048]{2,1,0:T(8,128)(2,1)S(1)}, bf16[2,32,2048]{2,1,0:T(8,128)(2,1)S(1)}, u32[]{:S(2)}, u32[]{:S(2)}) collective-permute-start(bf16[2,32,2048]{2,1,0:T(8,128)(2,1)S(1)} %pad_maximum_fusion.1.refs_0_.refs_2_), channel_id=1, source_target_pairs={{0,3},{1,0},{2,1},{3,2},{4,7},{5,4},{6,5},{7,6},{8,11},{9,8},{10,9... | collective-permute-start | bytes 786440 | tf_op jit(solution)/shard_map/ppermute | solution.py:172
  20.8 12.1 %collective-permute-done.8.other = bf16[32,4096]{1,0:T(8,128)(2,1)S(1)} collective-permute-done((bf16[32,4096]{1,0:T(8,128)(2,1)S(1)}, bf16[32,4096]{1,0:T(8,128)(2,1)S(1)}, u32[]{:S(2)}, u32[]{:S(2)}) %collective-permute-start.8) | collective-permute-done | bytes 262176 | tf_op jit(solution)/shard_map/ppermute | solution.py:885
  33.4 1.6 collective-permute-start.9
  35.0 4.6 %copy-done = bf16[1,4096,3,512]{3,1,2,0:T(8,128)(2,1)S(1)} copy-done((bf16[1,4096,3,512]{3,1,2,0:T(8,128)(2,1)S(1)}, bf16[1,4096,3,512]{3,1,2,0:T(8,128)(2,1)}, u32[]{:S(2)}) %copy-start) | copy-done | bytes 12582936
  39.6 3.7 %key_value.1 = (bf16[256,4096]{1,0:T(8,128)(2,1)S(1)}, bf16[2,256,512]{2,1,0:T(8,128)(2,1)S(1)}) custom-call(bf16[4,32,2048]{2,1,0:T(8,128)(2,1)S(1)} %pad_maximum_fusion.refs_0_, bf16[4,32,2048]{2,1,0:T(8,128)(2,1)S(1)} %collective-permute-done.3.refs_1_, bf16[2,32,2048]{2,1,0:T(8,128)(2,1)S(1)} %pad_maximum_fusion.1.refs_0_.refs_2_, ...), custom_call_target="tpu_custom_call" | custom-call | flops 2147483648 | bytes 12582912 | tf_op jit(solution)/shard_map/key_value/pallas_call | solution.py:476
  43.3 3.1 %collective-permute-start.11 = (bf16[2,256,512]{2,1,0:T(8,128)(2,1)S(1)}, bf16[2,256,512]{2,1,0:T(8,128)(2,1)S(1)}, u32[]{:S(2)}, u32[]{:S(2)}) collective-permute-start(bf16[2,256,512]{2,1,0:T(8,128)(2,1)S(1)} %get-tuple-element.57.own_kv), channel_id=1, source_target_pairs={{0,64},{64,0},{1,65},{65,1},{2,66},{66,2},{3,67},{67,3},{4,68},{68... | collective-permute-start | bytes 1572872 | tf_op jit(solution)/shard_map/ppermute | solution.py:889
  46.9 1.6 collective-permute-start.13
  48.6 2.1 %collective-permute-start.14 = (bf16[256,1024]{1,0:T(8,128)(2,1)S(1)}, bf16[256,1024]{1,0:T(8,128)(2,1)S(1)}, u32[]{:S(2)}, u32[]{:S(2)}) collective-permute-start(bf16[256,1024]{1,0:T(8,128)(2,1)S(1)} %get-tuple-element.62), channel_id=1, source_target_pairs={{0,48},{8,56},{16,0},{24,8},{32,16},{40,24},{48,32},{56,40},{1,49}... | collective-permute-start | bytes 1572872 | tf_op jit(solution)/shard_map/ppermute | solution.py:857
  50.6 1.8 query.1
  52.4 4.0 %collective-permute-done.11.other_kv = bf16[2,256,512]{2,1,0:T(8,128)(2,1)S(1)} collective-permute-done((bf16[2,256,512]{2,1,0:T(8,128)(2,1)S(1)}, bf16[2,256,512]{2,1,0:T(8,128)(2,1)S(1)}, u32[]{:S(2)}, u32[]{:S(2)}) %collective-permute-start.11) | collective-permute-done | bytes 524320 | tf_op jit(solution)/shard_map/ppermute | solution.py:889
  56.4 2.4 %attend_forward.1.left.mixed = bf16[256,512]{1,0:T(8,128)(2,1)S(1)} custom-call(s32[1,5]{1,0:T(1,128)S(1)} %copy-done.8, s32[1,4]{1,0:T(1,128)S(1)} %copy-done.9, bf16[256,512]{1,0:T(8,128)(2,1)S(1)} %query.1, bf16[2,256,512]{2,1,0:T(8,128)(2,1)S(1)} %get-tuple-element.57.own_kv, bf16[2,256,512]{2,1,0:T(8,128)(2,1)S(1)} %collective-permute-done.11.other_kv), custom_call_target="tpu_custom_call" | custom-call | flops 536870912 | bytes 1572864 | tf_op jit(solution)/shard_map/attend_forward/pallas_call | solution.py:756
  58.8 2.2 %proj_parts.1 = (bf16[2,32,4096]{2,1,0:T(8,128)(2,1)S(1)}, bf16[2,32,4096]{2,1,0:T(8,128)(2,1)S(1)}, bf16[2,32,4096]{2,1,0:T(8,128)(2,1)S(1)}, bf16[2,32,4096]{2,1,0:T(8,128)(2,1)S(1)}) custom-call(bf16[256,512]{1,0:T(8,128)(2,1)S(1)} %attend_forward.1.left.mixed, bf16[1,4096,512]{2,1,0:T(8,128)(2,1)S(1)} %copy-done.2), custom_call_target="tpu_custom_call" | custom-call | flops 1073741824 | bytes 6291456 | tf_op jit(solution)/shard_map/proj_parts/pallas_call | solution.py:652
  61.0 1.9 %grad_mixed.1 = (bf16[256,4096]{1,0:T(8,128)(2,1)S(1)}, bf16[256,512]{1,0:T(8,128)(2,1)S(1)}) custom-call(bf16[2,32,4096]{2,1,0:T(8,128)(2,1)S(1)} %pair.1.refs_7_.p0, bf16[2,32,4096]{2,1,0:T(8,128)(2,1)S(1)} %collective-permute-done.9.refs_0_.p1, bf16[2,32,4096]{2,1,0:T(8,128)(2,1)S(1)} %collective-permute-done.10.refs_1_.p2, ...), custom_call_target="tpu_custom_call" | custom-call | flops 1073741824 | bytes 8388608 | tf_op jit(solution)/shard_map/grad_mixed/pallas_call | solution.py:525
  63.0 4.3 %attend_backward.1 = (bf16[256,512]{1,0:T(8,128)(2,1)S(1)}, f32[2,256,512]{2,1,0:T(8,128)S(1)}, bf16[2,256,512]{2,1,0:T(8,128)(2,1)S(1)}) custom-call(s32[1,5]{1,0:T(1,128)S(1)} %copy-done.8, s32[1,4]{1,0:T(1,128)S(1)} %copy-done.9, bf16[256,512]{1,0:T(8,128)(2,1)S(1)} %query.1, bf16[2,256,512]{2,1,0:T(8,128)(2,1)S(1)} %get-tuple-element.57.own_kv, ...), custom_call_target="tpu_custom_call" | custom-call | flops 1073741824 | bytes 3145728 | tf_op jit(solution)/shard_map/attend_backward/pallas_call | solution.py:770
  68.6 6.1 %collective-permute-start.17 = (bf16[2,256,512]{2,1,0:T(8,128)(2,1)S(1)}, bf16[2,256,512]{2,1,0:T(8,128)(2,1)S(1)}, u32[]{:S(2)}, u32[]{:S(2)}) collective-permute-start(bf16[2,256,512]{2,1,0:T(8,128)(2,1)S(1)} %get-tuple-element.69), channel_id=1, source_target_pairs={{0,64},{64,0},{1,65},{65,1},{2,66},{66,2},{3,67},{67,3},{4,68},{68... | collective-permute-start | bytes 1572872 | tf_op jit(solution)/shard_map/ppermute | solution.py:899
  74.7 3.2 %collective-permute-start.21 = (bf16[256,1024]{1,0:T(8,128)(2,1)S(1)}, bf16[256,1024]{1,0:T(8,128)(2,1)S(1)}, u32[]{:S(2)}, u32[]{:S(2)}) collective-permute-start(bf16[256,1024]{1,0:T(8,128)(2,1)S(1)} %get-tuple-element.75), channel_id=1, source_target_pairs={{0,32},{8,40},{16,48},{24,56},{32,0},{40,8},{48,16},{56,24},{1,33}... | collective-permute-start | bytes 1572872 | tf_op jit(solution)/shard_map/ppermute | solution.py:857
  78.1 2.0 %collective-permute-start.16 = (bf16[2,32,4096]{2,1,0:T(8,128)(2,1)S(1)}, bf16[2,32,4096]{2,1,0:T(8,128)(2,1)S(1)}, u32[]{:S(2)}, u32[]{:S(2)}) collective-permute-start(bf16[2,32,4096]{2,1,0:T(8,128)(2,1)S(1)} %get-tuple-element.66), channel_id=1, source_target_pairs={{0,1},{1,2},{2,3},{3,0},{4,5},{5,6},{6,7},{7,4},{8,9},{9,10},{10,1... | collective-permute-start | bytes 1572872 | tf_op jit(solution)/shard_map/ppermute | solution.py:901
  80.1 7.1 %collective-permute-done.17.came = bf16[2,256,512]{2,1,0:T(8,128)(2,1)S(1)} collective-permute-done((bf16[2,256,512]{2,1,0:T(8,128)(2,1)S(1)}, bf16[2,256,512]{2,1,0:T(8,128)(2,1)S(1)}, u32[]{:S(2)}, u32[]{:S(2)}) %collective-permute-start.17) | collective-permute-done | bytes 524320 | tf_op jit(solution)/shard_map/ppermute | solution.py:899
  87.3 1.6 collective-permute-start.35
  90.2 3.0 %collective-permute-start.36 = (bf16[3,256,512]{2,1,0:T(8,128)(2,1)S(1)}, bf16[3,256,512]{2,1,0:T(8,128)(2,1)S(1)}, u32[]{:S(2)}, u32[]{:S(2)}) collective-permute-start(bf16[3,256,512]{2,1,0:T(8,128)(2,1)S(1)} %sum_keys.1.refs_1_.grads.g0), channel_id=1, source_target_pairs={{0,48},{8,56},{16,0},{24,8},{32,16},{40,24},{48,32},{56,40},{1,49}... | collective-permute-start | bytes 2359304 | tf_op jit(solution)/shard_map/ppermute | solution.py:908
  93.3 8.9 %collective-permute-start.18 = (bf16[2,32,4096]{2,1,0:T(8,128)(2,1)S(1)}, bf16[2,32,4096]{2,1,0:T(8,128)(2,1)S(1)}, u32[]{:S(2)}, u32[]{:S(2)}) collective-permute-start(bf16[2,32,4096]{2,1,0:T(8,128)(2,1)S(1)} %late.3), channel_id=1, source_target_pairs={{0,2},{1,3},{2,0},{3,1},{4,6},{5,7},{6,4},{7,5},{8,10},{9,11},{10,... | collective-permute-start | bytes 1572872 | tf_op jit(solution)/shard_map/ppermute | solution.py:906
  102.2 3.1 %back_right.1 = (bf16[4,32,2048]{2,1,0:T(8,128)(2,1)S(1)}, bf16[4,32,2048]{2,1,0:T(8,128)(2,1)S(1)}, f32[1,2048]{1,0:T(1,128)S(1)}) custom-call(bf16[3,256,512]{2,1,0:T(8,128)(2,1)S(1)} %sum_keys.1.refs_1_.grads.g0, bf16[3,4096,512]{2,1,0:T(8,128)(2,1)S(1)} %bitcast.20, bf16[256,4096]{1,0:T(8,128)(2,1)S(1)} %get-tuple-element.56.full.normed, ...), custom_call_target="tpu_custom_call" | custom-call | flops 1610612736 | bytes 8388608 | tf_op jit(solution)/shard_map/back_right/pallas_call | solution.py:611
  105.3 3.1 %back_left.1 = (bf16[5,16,2048]{2,1,0:T(8,128)(2,1)S(1)}, bf16[5,16,2048]{2,1,0:T(8,128)(2,1)S(1)}, bf16[5,16,2048]{2,1,0:T(8,128)(2,1)S(1)}, bf16[3,16,2048]{2,1,0:T(8,128)(2,1)S(1)}, bf16[2,16,2048]{2,1,0:T(8,128)(2,1)S(1)}) custom-call(bf16[3,256,512]{2,1,0:T(8,128)(2,1)S(1)} %sum_keys.1.refs_1_.grads.g0, bf16[3,4096,512]{2,1,0:T(8,128)(2,1)S(1)} %bitcast.21, ...), custom_call_target="tpu_custom_call" | custom-call | flops 1610612736 | bytes 8388608 | tf_op jit(solution)/shard_map/back_left/pallas_call | solution.py:611
  108.9 9.7 %collective-permute-done.18.c3.refs_2_ = bf16[2,32,4096]{2,1,0:T(8,128)(2,1)S(1)} collective-permute-done((bf16[2,32,4096]{2,1,0:T(8,128)(2,1)S(1)}, bf16[2,32,4096]{2,1,0:T(8,128)(2,1)S(1)}, u32[]{:S(2)}, u32[]{:S(2)}) %collective-permute-start.18) | collective-permute-done | bytes 524320 | tf_op jit(solution)/shard_map/ppermute | solution.py:906
  118.6 5.0 %collective-permute-done.23.far_b.refs_1_ = bf16[2,16,2048]{2,1,0:T(8,128)(2,1)S(1)} collective-permute-done((bf16[2,16,2048]{2,1,0:T(8,128)(2,1)S(1)}, bf16[2,16,2048]{2,1,0:T(8,128)(2,1)S(1)}, u32[]{:S(2)}, u32[]{:S(2)}) %collective-permute-start.23) | collective-permute-done | bytes 131104 | tf_op jit(solution)/shard_map/ppermute | solution.py:914
  123.7 3.2 %collective-permute-start.38 = (bf16[3,128,512]{2,1,0:T(8,128)(2,1)S(1)}, bf16[3,128,512]{2,1,0:T(8,128)(2,1)S(1)}, u32[]{:S(2)}, u32[]{:S(2)}) collective-permute-start(bf16[3,128,512]{2,1,0:T(8,128)(2,1)S(1)} %get-tuple-element.94), channel_id=1, source_target_pairs={{0,48},{8,56},{16,0},{24,8},{32,16},{40,24},{48,32},{56,40},{1,49}... | collective-permute-start | bytes 1179656 | tf_op jit(solution)/shard_map/ppermute | solution.py:926
  127.1 3.2 %collective-permute-start.26 = (bf16[5,16,2048]{2,1,0:T(8,128)(2,1)S(1)}, bf16[5,16,2048]{2,1,0:T(8,128)(2,1)S(1)}, u32[]{:S(2)}, u32[]{:S(2)}) collective-permute-start(bf16[5,16,2048]{2,1,0:T(8,128)(2,1)S(1)} %get-tuple-element.84), channel_id=1, source_target_pairs={{0,3},{1,0},{2,1},{3,2},{4,7},{5,4},{6,5},{7,6},{8,11},{9,8},{10,9... | collective-permute-start | bytes 983048 | tf_op jit(solution)/shard_map/ppermute | solution.py:922
  130.3 2.8 %collective-permute-done.37.g3 = bf16[3,128,512]{2,1,0:T(8,128)(2,1)S(1)} collective-permute-done((bf16[3,128,512]{2,1,0:T(8,128)(2,1)S(1)}, bf16[3,128,512]{2,1,0:T(8,128)(2,1)S(1)}, u32[]{:S(2)}, u32[]{:S(2)}) %collective-permute-start.37) | collective-permute-done | bytes 393248 | tf_op jit(solution)/shard_map/ppermute | solution.py:926
  133.1 2.2 %weight_shares.2.refs_0_ = bf16[3,512,512]{2,1,0:T(8,128)(2,1)S(1)} custom-call(bf16[256,4096]{1,0:T(8,128)(2,1)S(1)} %get-tuple-element.56.full.normed, bf16[256,1024]{1,0:T(8,128)(2,1)S(1)} %collective-permute-done.13.refs_1_.c1, bf16[256,1024]{1,0:T(8,128)(2,1)S(1)} %collective-permute-done.14.refs_2_.c2, ...), custom_call_target="tpu_custom_call" | custom-call | flops 1610612736 | bytes 7340032 | tf_op jit(solution)/shard_map/weight_shares/pallas_call | solution.py:827
  136.0 2.1 %collective-permute-start.27 = (bf16[3,16,2048]{2,1,0:T(8,128)(2,1)S(1)}, bf16[3,16,2048]{2,1,0:T(8,128)(2,1)S(1)}, u32[]{:S(2)}, u32[]{:S(2)}) collective-permute-start(bf16[3,16,2048]{2,1,0:T(8,128)(2,1)S(1)} %get-tuple-element.86.refs_0_), channel_id=1, source_target_pairs={{0,4},{1,5},{2,6},{3,7},{4,0},{5,1},{6,2},{7,3},{8,12},{9,13},{10,... | collective-permute-start | bytes 589832 | tf_op jit(solution)/shard_map/ppermute | solution.py:934
  138.6 3.2 %collective-permute-start.41 = (bf16[256,512]{1,0:T(8,128)(2,1)S(1)}, bf16[256,512]{1,0:T(8,128)(2,1)S(1)}, u32[]{:S(2)}, u32[]{:S(2)}) collective-permute-start(bf16[256,512]{1,0:T(8,128)(2,1)S(1)} %get-tuple-element.100), channel_id=1, source_target_pairs={{0,48},{8,56},{16,0},{24,8},{32,16},{40,24},{48,32},{56,40},{1,49}... | collective-permute-start | bytes 786440 | tf_op jit(solution)/shard_map/ppermute | solution.py:917
  141.8 6.9 %collective-permute-done.27.l_came.came = bf16[3,16,2048]{2,1,0:T(8,128)(2,1)S(1)} collective-permute-done((bf16[3,16,2048]{2,1,0:T(8,128)(2,1)S(1)}, bf16[3,16,2048]{2,1,0:T(8,128)(2,1)S(1)}, u32[]{:S(2)}, u32[]{:S(2)}) %collective-permute-start.27) | collective-permute-done | bytes 196640 | tf_op jit(solution)/shard_map/ppermute | solution.py:934
  153.1 1.8 collective-permute-done.28.r1.refs_0_
  154.9 3.0 %collective-permute-start.33 = (f32[1,4096]{1,0:T(1,128)S(1)}, f32[1,4096]{1,0:T(1,128)S(1)}, u32[]{:S(2)}, u32[]{:S(2)}) collective-permute-start(f32[1,4096]{1,0:T(1,128)S(1)} %add.15), channel_id=1, source_target_pairs={{0,48},{8,56},{16,0},{24,8},{32,16},{40,24},{48,32},{56,40},{1,49}... | collective-permute-start | bytes 49160 | tf_op jit(solution)/shard_map/ppermute | solution.py:939
  157.9 1.7 collective-permute-done.29.r2
  159.6 1.5 collective-permute-start.34
  161.0 2.3 %weight_shares.3 = f32[3,512,512]{2,1,0:T(8,128)S(1)} custom-call(bf16[256,4096]{1,0:T(8,128)(2,1)S(1)} %get-tuple-element.56.full.normed, bf16[256,1024]{1,0:T(8,128)(2,1)S(1)} %collective-permute-done.13.refs_1_.c1, bf16[256,1024]{1,0:T(8,128)(2,1)S(1)} %collective-permute-done.14.refs_2_.c2, bf16[256,1024]{1,0:T(8,128)(2,1)S(1)} %collective-permute-done.21.refs_1_.c3, ...), custom_call_target="tpu_custom_call" | custom-call | flops 1610612736 | bytes 7340032 | tf_op jit(solution)/shard_map/weight_shares/pallas_call | solution.py:827
  163.5 2.5 %collective-permute-start.42 = (bf16[512,512]{1,0:T(8,128)(2,1)S(1)}, bf16[512,512]{1,0:T(8,128)(2,1)S(1)}, u32[]{:S(2)}, u32[]{:S(2)}) collective-permute-start(bf16[512,512]{1,0:T(8,128)(2,1)S(1)} %get-tuple-element.101), channel_id=1, source_target_pairs={{0,16},{8,24},{16,32},{24,40},{32,48},{40,56},{48,0},{56,8},{1,17}... | collective-permute-start | bytes 1572872 | tf_op jit(solution)/shard_map/ppermute | solution.py:931
  168.5 8.1 %collective-permute-done.42.c1 = bf16[512,512]{1,0:T(8,128)(2,1)S(1)} collective-permute-done((bf16[512,512]{1,0:T(8,128)(2,1)S(1)}, bf16[512,512]{1,0:T(8,128)(2,1)S(1)}, u32[]{:S(2)}, u32[]{:S(2)}) %collective-permute-start.42) | collective-permute-done | bytes 524320 | tf_op jit(solution)/shard_map/ppermute | solution.py:931
  176.6 3.1 %collective-permute-done.43.c2 = bf16[512,512]{1,0:T(8,128)(2,1)S(1)} collective-permute-done((bf16[512,512]{1,0:T(8,128)(2,1)S(1)}, bf16[512,512]{1,0:T(8,128)(2,1)S(1)}, u32[]{:S(2)}, u32[]{:S(2)}) %collective-permute-start.43) | collective-permute-done | bytes 524320 | tf_op jit(solution)/shard_map/ppermute | solution.py:931
  180.9 2.2 %add_bitcast_fusion = f32[1,512,3,512]{3,1,2,0:T(8,128)} fusion(f32[3,512,512]{2,1,0:T(8,128)S(1)} %weight_shares.3, bf16[3,512,512]{2,1,0:T(8,128)(2,1)S(1)} %collective-permute-done.39), kind=kLoop, calls=%fused_computation | loop fusion | flops 1572864 | bytes 7864320 | tf_op jit(solution)/shard_map/broadcast_in_dim | solution.py:960
  (94 shorter events, 19.0 us)
Async XLA Ops:
  2.5 7.7 %collective-permute-start = (bf16[32,2048]{1,0:T(8,128)(2,1)S(1)}, bf16[32,2048]{1,0:T(8,128)(2,1)S(1)}, u32[]{:S(2)}, u32[]{:S(2)}) collective-permute-start(bf16[32,2048]{1,0:T(8,128)(2,1)S(1)} %get-tuple-element.54), channel_id=1, source_target_pairs={{0,1},{1,2},{2,3},{3,0},{4,5},{5,6},{6,7},{7,4},{8,9},{9,10},{10,1... | collective-permute-start | bytes 393224 | tf_op jit(solution)/shard_map/ppermute | solution.py:171
  4.5 7.8 %collective-permute-start.1 = (bf16[32,2048]{1,0:T(8,128)(2,1)S(1)}, bf16[32,2048]{1,0:T(8,128)(2,1)S(1)}, u32[]{:S(2)}, u32[]{:S(2)}) collective-permute-start(bf16[32,2048]{1,0:T(8,128)(2,1)S(1)} %get-tuple-element.54), channel_id=1, source_target_pairs={{0,3},{1,0},{2,1},{3,2},{4,7},{5,4},{6,5},{7,6},{8,11},{9,8},{10,9... | collective-permute-start | bytes 393224 | tf_op jit(solution)/shard_map/ppermute | solution.py:171
  6.7 7.4 %collective-permute-start.2 = (bf16[32,2048]{1,0:T(8,128)(2,1)S(1)}, bf16[32,2048]{1,0:T(8,128)(2,1)S(1)}, u32[]{:S(2)}, u32[]{:S(2)}) collective-permute-start(bf16[32,2048]{1,0:T(8,128)(2,1)S(1)} %get-tuple-element.54), channel_id=1, source_target_pairs={{0,2},{1,3},{2,0},{3,1},{4,6},{5,7},{6,4},{7,5},{8,10},{9,11},{10,... | collective-permute-start | bytes 393224 | tf_op jit(solution)/shard_map/ppermute | solution.py:171
  8.5 7.3 %collective-permute-start.4 = (bf16[32,2048]{1,0:T(8,128)(2,1)S(1)}, bf16[32,2048]{1,0:T(8,128)(2,1)S(1)}, u32[]{:S(2)}, u32[]{:S(2)}) collective-permute-start(bf16[32,2048]{1,0:T(8,128)(2,1)S(1)} %get-tuple-element.55), channel_id=1, source_target_pairs={{0,4},{1,5},{2,6},{3,7},{4,0},{5,1},{6,2},{7,3},{8,12},{9,13},{10,... | collective-permute-start | bytes 393224 | tf_op jit(solution)/shard_map/ppermute | solution.py:170
  14.2 20.8 %collective-permute-start.3 = (bf16[4,32,2048]{2,1,0:T(8,128)(2,1)S(1)}, bf16[4,32,2048]{2,1,0:T(8,128)(2,1)S(1)}, u32[]{:S(2)}, u32[]{:S(2)}) collective-permute-start(bf16[4,32,2048]{2,1,0:T(8,128)(2,1)S(1)} %pad_maximum_fusion.refs_0_), channel_id=1, source_target_pairs={{0,4},{1,5},{2,6},{3,7},{4,0},{5,1},{6,2},{7,3},{8,12},{9,13},{10,... | collective-permute-start | bytes 1572872 | tf_op jit(solution)/shard_map/ppermute | solution.py:174
  16.8 16.0 %collective-permute-start.8 = (bf16[32,4096]{1,0:T(8,128)(2,1)S(1)}, bf16[32,4096]{1,0:T(8,128)(2,1)S(1)}, u32[]{:S(2)}, u32[]{:S(2)}) collective-permute-start(bf16[32,4096]{1,0:T(8,128)(2,1)S(1)} %grad_rows.1.own.grad), channel_id=1, source_target_pairs={{0,4},{1,5},{2,6},{3,7},{4,0},{5,1},{6,2},{7,3},{8,12},{9,13},{10,... | collective-permute-start | bytes 786440 | tf_op jit(solution)/shard_map/ppermute | solution.py:885
  17.5 15.4 %collective-permute-start.5 = (bf16[2,32,2048]{2,1,0:T(8,128)(2,1)S(1)}, bf16[2,32,2048]{2,1,0:T(8,128)(2,1)S(1)}, u32[]{:S(2)}, u32[]{:S(2)}) collective-permute-start(bf16[2,32,2048]{2,1,0:T(8,128)(2,1)S(1)} %pad_maximum_fusion.1.refs_0_.refs_2_), channel_id=1, source_target_pairs={{0,1},{1,2},{2,3},{3,0},{4,5},{5,6},{6,7},{7,4},{8,9},{9,10},{10,1... | collective-permute-start | bytes 786440 | tf_op jit(solution)/shard_map/ppermute | solution.py:172
  18.6 16.4 %collective-permute-start.6 = (bf16[2,32,2048]{2,1,0:T(8,128)(2,1)S(1)}, bf16[2,32,2048]{2,1,0:T(8,128)(2,1)S(1)}, u32[]{:S(2)}, u32[]{:S(2)}) collective-permute-start(bf16[2,32,2048]{2,1,0:T(8,128)(2,1)S(1)} %pad_maximum_fusion.1.refs_0_.refs_2_), channel_id=1, source_target_pairs={{0,3},{1,0},{2,1},{3,2},{4,7},{5,4},{6,5},{7,6},{8,11},{9,8},{10,9... | collective-permute-start | bytes 786440 | tf_op jit(solution)/shard_map/ppermute | solution.py:172
  20.7 14.3 %collective-permute-start.7 = (bf16[2,32,2048]{2,1,0:T(8,128)(2,1)S(1)}, bf16[2,32,2048]{2,1,0:T(8,128)(2,1)S(1)}, u32[]{:S(2)}, u32[]{:S(2)}) collective-permute-start(bf16[2,32,2048]{2,1,0:T(8,128)(2,1)S(1)} %pad_maximum_fusion.1.refs_0_.refs_2_), channel_id=1, source_target_pairs={{0,2},{1,3},{2,0},{3,1},{4,6},{5,7},{6,4},{7,5},{8,10},{9,11},{10,... | collective-permute-start | bytes 786440 | tf_op jit(solution)/shard_map/ppermute | solution.py:172
  32.9 15.7 %collective-permute-start.10 = (bf16[2,32,4096]{2,1,0:T(8,128)(2,1)S(1)}, bf16[2,32,4096]{2,1,0:T(8,128)(2,1)S(1)}, u32[]{:S(2)}, u32[]{:S(2)}) collective-permute-start(bf16[2,32,4096]{2,1,0:T(8,128)(2,1)S(1)} %pair.1.refs_7_.p0), channel_id=1, source_target_pairs={{0,3},{1,0},{2,1},{3,2},{4,7},{5,4},{6,5},{7,6},{8,11},{9,8},{10,9... | collective-permute-start | bytes 1572872 | tf_op jit(solution)/shard_map/ppermute | solution.py:887
  33.4 17.3 %collective-permute-start.9 = (bf16[2,32,4096]{2,1,0:T(8,128)(2,1)S(1)}, bf16[2,32,4096]{2,1,0:T(8,128)(2,1)S(1)}, u32[]{:S(2)}, u32[]{:S(2)}) collective-permute-start(bf16[2,32,4096]{2,1,0:T(8,128)(2,1)S(1)} %pair.1.refs_7_.p0), channel_id=1, source_target_pairs={{0,1},{1,2},{2,3},{3,0},{4,5},{5,6},{6,7},{7,4},{8,9},{9,10},{10,1... | collective-permute-start | bytes 1572872 | tf_op jit(solution)/shard_map/ppermute | solution.py:887
  39.6 11.0 %copy-start.1 = (bf16[1,4096,3,512]{3,1,2,0:T(8,128)(2,1)S(1)}, bf16[1,4096,3,512]{3,1,2,0:T(8,128)(2,1)}, u32[]{:S(2)}) copy-start(bf16[1,4096,3,512]{3,1,2,0:T(8,128)(2,1)} %param.11) | copy-start | bytes 37748740
  43.3 13.1 %collective-permute-start.11 = (bf16[2,256,512]{2,1,0:T(8,128)(2,1)S(1)}, bf16[2,256,512]{2,1,0:T(8,128)(2,1)S(1)}, u32[]{:S(2)}, u32[]{:S(2)}) collective-permute-start(bf16[2,256,512]{2,1,0:T(8,128)(2,1)S(1)} %get-tuple-element.57.own_kv), channel_id=1, source_target_pairs={{0,64},{64,0},{1,65},{65,1},{2,66},{66,2},{3,67},{67,3},{4,68},{68... | collective-permute-start | bytes 1572872 | tf_op jit(solution)/shard_map/ppermute | solution.py:889
  46.4 14.6 %collective-permute-start.12 = (bf16[2,32,4096]{2,1,0:T(8,128)(2,1)S(1)}, bf16[2,32,4096]{2,1,0:T(8,128)(2,1)S(1)}, u32[]{:S(2)}, u32[]{:S(2)}) collective-permute-start(bf16[2,32,4096]{2,1,0:T(8,128)(2,1)S(1)} %pair.1.refs_7_.p0), channel_id=1, source_target_pairs={{0,2},{1,3},{2,0},{3,1},{4,6},{5,7},{6,4},{7,5},{8,10},{9,11},{10,... | collective-permute-start | bytes 1572872 | tf_op jit(solution)/shard_map/ppermute | solution.py:887
  46.9 14.1 %collective-permute-start.13 = (bf16[256,1024]{1,0:T(8,128)(2,1)S(1)}, bf16[256,1024]{1,0:T(8,128)(2,1)S(1)}, u32[]{:S(2)}, u32[]{:S(2)}) collective-permute-start(bf16[256,1024]{1,0:T(8,128)(2,1)S(1)} %get-tuple-element.61), channel_id=1, source_target_pairs={{0,16},{8,24},{16,32},{24,40},{32,48},{40,56},{48,0},{56,8},{1,17}... | collective-permute-start | bytes 1572872 | tf_op jit(solution)/shard_map/ppermute | solution.py:857
  48.6 12.5 %collective-permute-start.14 = (bf16[256,1024]{1,0:T(8,128)(2,1)S(1)}, bf16[256,1024]{1,0:T(8,128)(2,1)S(1)}, u32[]{:S(2)}, u32[]{:S(2)}) collective-permute-start(bf16[256,1024]{1,0:T(8,128)(2,1)S(1)} %get-tuple-element.62), channel_id=1, source_target_pairs={{0,48},{8,56},{16,0},{24,8},{32,16},{40,24},{48,32},{56,40},{1,49}... | collective-permute-start | bytes 1572872 | tf_op jit(solution)/shard_map/ppermute | solution.py:857
  50.6 8.1 %copy-start.2 = (bf16[1,4096,512]{2,1,0:T(8,128)(2,1)S(1)}, bf16[1,4096,512]{2,1,0:T(8,128)(2,1)}, u32[]{:S(2)}) copy-start(bf16[1,4096,512]{2,1,0:T(8,128)(2,1)} %weight.3) | copy-start | bytes 12582916
  68.5 24.7 %collective-permute-start.20 = (bf16[4,512,512]{2,1,0:T(8,128)(2,1)S(1)}, bf16[4,512,512]{2,1,0:T(8,128)(2,1)S(1)}, u32[]{:S(2)}, u32[]{:S(2)}) collective-permute-start(bf16[4,512,512]{2,1,0:T(8,128)(2,1)S(1)} %get-tuple-element.74), channel_id=1, source_target_pairs={{0,8},{8,0},{16,24},{24,16},{32,40},{40,32},{48,56},{56,48},{1,9},... | collective-permute-start | bytes 6291464 | tf_op jit(solution)/shard_map/ppermute | solution.py:903
  68.6 18.6 %collective-permute-start.17 = (bf16[2,256,512]{2,1,0:T(8,128)(2,1)S(1)}, bf16[2,256,512]{2,1,0:T(8,128)(2,1)S(1)}, u32[]{:S(2)}, u32[]{:S(2)}) collective-permute-start(bf16[2,256,512]{2,1,0:T(8,128)(2,1)S(1)} %get-tuple-element.69), channel_id=1, source_target_pairs={{0,64},{64,0},{1,65},{65,1},{2,66},{66,2},{3,67},{67,3},{4,68},{68... | collective-permute-start | bytes 1572872 | tf_op jit(solution)/shard_map/ppermute | solution.py:899
  74.7 15.5 %collective-permute-start.21 = (bf16[256,1024]{1,0:T(8,128)(2,1)S(1)}, bf16[256,1024]{1,0:T(8,128)(2,1)S(1)}, u32[]{:S(2)}, u32[]{:S(2)}) collective-permute-start(bf16[256,1024]{1,0:T(8,128)(2,1)S(1)} %get-tuple-element.75), channel_id=1, source_target_pairs={{0,32},{8,40},{16,48},{24,56},{32,0},{40,8},{48,16},{56,24},{1,33}... | collective-permute-start | bytes 1572872 | tf_op jit(solution)/shard_map/ppermute | solution.py:857
  78.0 27.3 %collective-permute-start.15 = (bf16[2,32,4096]{2,1,0:T(8,128)(2,1)S(1)}, bf16[2,32,4096]{2,1,0:T(8,128)(2,1)S(1)}, u32[]{:S(2)}, u32[]{:S(2)}) collective-permute-start(bf16[2,32,4096]{2,1,0:T(8,128)(2,1)S(1)} %get-tuple-element.65.refs_0_), channel_id=1, source_target_pairs={{0,3},{1,0},{2,1},{3,2},{4,7},{5,4},{6,5},{7,6},{8,11},{9,8},{10,9... | collective-permute-start | bytes 1572872 | tf_op jit(solution)/shard_map/ppermute | solution.py:901
  78.1 27.2 %collective-permute-start.16 = (bf16[2,32,4096]{2,1,0:T(8,128)(2,1)S(1)}, bf16[2,32,4096]{2,1,0:T(8,128)(2,1)S(1)}, u32[]{:S(2)}, u32[]{:S(2)}) collective-permute-start(bf16[2,32,4096]{2,1,0:T(8,128)(2,1)S(1)} %get-tuple-element.66), channel_id=1, source_target_pairs={{0,1},{1,2},{2,3},{3,0},{4,5},{5,6},{6,7},{7,4},{8,9},{9,10},{10,1... | collective-permute-start | bytes 1572872 | tf_op jit(solution)/shard_map/ppermute | solution.py:901
  87.3 31.2 %collective-permute-start.35 = (bf16[3,256,512]{2,1,0:T(8,128)(2,1)S(1)}, bf16[3,256,512]{2,1,0:T(8,128)(2,1)S(1)}, u32[]{:S(2)}, u32[]{:S(2)}) collective-permute-start(bf16[3,256,512]{2,1,0:T(8,128)(2,1)S(1)} %sum_keys.1.refs_1_.grads.g0), channel_id=1, source_target_pairs={{0,16},{8,24},{16,32},{24,40},{32,48},{40,56},{48,0},{56,8},{1,17}... | collective-permute-start | bytes 2359304 | tf_op jit(solution)/shard_map/ppermute | solution.py:907
  90.2 28.3 %collective-permute-start.36 = (bf16[3,256,512]{2,1,0:T(8,128)(2,1)S(1)}, bf16[3,256,512]{2,1,0:T(8,128)(2,1)S(1)}, u32[]{:S(2)}, u32[]{:S(2)}) collective-permute-start(bf16[3,256,512]{2,1,0:T(8,128)(2,1)S(1)} %sum_keys.1.refs_1_.grads.g0), channel_id=1, source_target_pairs={{0,48},{8,56},{16,0},{24,8},{32,16},{40,24},{48,32},{56,40},{1,49}... | collective-permute-start | bytes 2359304 | tf_op jit(solution)/shard_map/ppermute | solution.py:908
  93.3 25.3 %collective-permute-start.18 = (bf16[2,32,4096]{2,1,0:T(8,128)(2,1)S(1)}, bf16[2,32,4096]{2,1,0:T(8,128)(2,1)S(1)}, u32[]{:S(2)}, u32[]{:S(2)}) collective-permute-start(bf16[2,32,4096]{2,1,0:T(8,128)(2,1)S(1)} %late.3), channel_id=1, source_target_pairs={{0,2},{1,3},{2,0},{3,1},{4,6},{5,7},{6,4},{7,5},{8,10},{9,11},{10,... | collective-permute-start | bytes 1572872 | tf_op jit(solution)/shard_map/ppermute | solution.py:906
  108.4 15.1 %collective-permute-start.22 = (bf16[3,16,2048]{2,1,0:T(8,128)(2,1)S(1)}, bf16[3,16,2048]{2,1,0:T(8,128)(2,1)S(1)}, u32[]{:S(2)}, u32[]{:S(2)}) collective-permute-start(bf16[3,16,2048]{2,1,0:T(8,128)(2,1)S(1)} %get-tuple-element.80), channel_id=1, source_target_pairs={{0,1},{1,2},{2,3},{3,0},{4,5},{5,6},{6,7},{7,4},{8,9},{9,10},{10,1... | collective-permute-start | bytes 589832 | tf_op jit(solution)/shard_map/ppermute | solution.py:913
  108.9 18.0 %collective-permute-start.24 = (bf16[4,32,2048]{2,1,0:T(8,128)(2,1)S(1)}, bf16[4,32,2048]{2,1,0:T(8,128)(2,1)S(1)}, u32[]{:S(2)}, u32[]{:S(2)}) collective-permute-start(bf16[4,32,2048]{2,1,0:T(8,128)(2,1)S(1)} %get-tuple-element.82), channel_id=1, source_target_pairs={{0,4},{1,5},{2,6},{3,7},{4,0},{5,1},{6,2},{7,3},{8,12},{9,13},{10,... | collective-permute-start | bytes 1572872 | tf_op jit(solution)/shard_map/ppermute | solution.py:911
  118.5 5.0 %collective-permute-start.23 = (bf16[2,16,2048]{2,1,0:T(8,128)(2,1)S(1)}, bf16[2,16,2048]{2,1,0:T(8,128)(2,1)S(1)}, u32[]{:S(2)}, u32[]{:S(2)}) collective-permute-start(bf16[2,16,2048]{2,1,0:T(8,128)(2,1)S(1)} %get-tuple-element.81), channel_id=1, source_target_pairs={{0,3},{1,0},{2,1},{3,2},{4,7},{5,4},{6,5},{7,6},{8,11},{9,8},{10,9... | collective-permute-start | bytes 393224 | tf_op jit(solution)/shard_map/ppermute | solution.py:914
  123.6 9.5 %collective-permute-start.37 = (bf16[3,128,512]{2,1,0:T(8,128)(2,1)S(1)}, bf16[3,128,512]{2,1,0:T(8,128)(2,1)S(1)}, u32[]{:S(2)}, u32[]{:S(2)}) collective-permute-start(bf16[3,128,512]{2,1,0:T(8,128)(2,1)S(1)} %get-tuple-element.93), channel_id=1, source_target_pairs={{0,16},{8,24},{16,32},{24,40},{32,48},{40,56},{48,0},{56,8},{1,17}... | collective-permute-start | bytes 1179656 | tf_op jit(solution)/shard_map/ppermute | solution.py:926
  123.7 9.4 %collective-permute-start.38 = (bf16[3,128,512]{2,1,0:T(8,128)(2,1)S(1)}, bf16[3,128,512]{2,1,0:T(8,128)(2,1)S(1)}, u32[]{:S(2)}, u32[]{:S(2)}) collective-permute-start(bf16[3,128,512]{2,1,0:T(8,128)(2,1)S(1)} %get-tuple-element.94), channel_id=1, source_target_pairs={{0,48},{8,56},{16,0},{24,8},{32,16},{40,24},{48,32},{56,40},{1,49}... | collective-permute-start | bytes 1179656 | tf_op jit(solution)/shard_map/ppermute | solution.py:926
  127.0 8.8 %collective-permute-start.25 = (bf16[5,16,2048]{2,1,0:T(8,128)(2,1)S(1)}, bf16[5,16,2048]{2,1,0:T(8,128)(2,1)S(1)}, u32[]{:S(2)}, u32[]{:S(2)}) collective-permute-start(bf16[5,16,2048]{2,1,0:T(8,128)(2,1)S(1)} %get-tuple-element.83), channel_id=1, source_target_pairs={{0,1},{1,2},{2,3},{3,0},{4,5},{5,6},{6,7},{7,4},{8,9},{9,10},{10,1... | collective-permute-start | bytes 983048 | tf_op jit(solution)/shard_map/ppermute | solution.py:922
  127.1 8.7 %collective-permute-start.26 = (bf16[5,16,2048]{2,1,0:T(8,128)(2,1)S(1)}, bf16[5,16,2048]{2,1,0:T(8,128)(2,1)S(1)}, u32[]{:S(2)}, u32[]{:S(2)}) collective-permute-start(bf16[5,16,2048]{2,1,0:T(8,128)(2,1)S(1)} %get-tuple-element.84), channel_id=1, source_target_pairs={{0,3},{1,0},{2,1},{3,2},{4,7},{5,4},{6,5},{7,6},{8,11},{9,8},{10,9... | collective-permute-start | bytes 983048 | tf_op jit(solution)/shard_map/ppermute | solution.py:922
  135.4 45.5 %collective-permute-start.39 = (bf16[3,512,512]{2,1,0:T(8,128)(2,1)S(1)}, bf16[3,512,512]{2,1,0:T(8,128)(2,1)S(1)}, u32[]{:S(2)}, u32[]{:S(2)}) collective-permute-start(bf16[3,512,512]{2,1,0:T(8,128)(2,1)S(1)} %weight_shares.2.refs_0_), channel_id=1, source_target_pairs={{0,8},{8,0},{16,24},{24,16},{32,40},{40,32},{48,56},{56,48},{1,9},... | collective-permute-start | bytes 4718600 | tf_op jit(solution)/shard_map/ppermute | solution.py:951
  135.7 13.2 %collective-permute-start.19 = (bf16[32,4096]{1,0:T(8,128)(2,1)S(1)}, bf16[32,4096]{1,0:T(8,128)(2,1)S(1)}, u32[]{:S(2)}, u32[]{:S(2)}) collective-permute-start(bf16[32,4096]{1,0:T(8,128)(2,1)S(1)} %get-tuple-element.71), channel_id=1, source_target_pairs={{0,4},{1,5},{2,6},{3,7},{4,0},{5,1},{6,2},{7,3},{8,12},{9,13},{10,... | collective-permute-start | bytes 786440 | tf_op jit(solution)/shard_map/ppermute | solution.py:953
  136.0 12.7 %collective-permute-start.27 = (bf16[3,16,2048]{2,1,0:T(8,128)(2,1)S(1)}, bf16[3,16,2048]{2,1,0:T(8,128)(2,1)S(1)}, u32[]{:S(2)}, u32[]{:S(2)}) collective-permute-start(bf16[3,16,2048]{2,1,0:T(8,128)(2,1)S(1)} %get-tuple-element.86.refs_0_), channel_id=1, source_target_pairs={{0,4},{1,5},{2,6},{3,7},{4,0},{5,1},{6,2},{7,3},{8,12},{9,13},{10,... | collective-permute-start | bytes 589832 | tf_op jit(solution)/shard_map/ppermute | solution.py:934
  138.0 10.7 %copy-start.7 = (bf16[1,4096]{1,0:T(2,128)(2,1)S(1)}, bf16[1,4096]{1,0:T(2,128)(2,1)}, u32[]{:S(2)}) copy-start(bf16[1,4096]{1,0:T(2,128)(2,1)} %gain.5) | copy-start | bytes 24580
  138.0 13.0 %copy-start.4 = (bf16[1,1,32,4096]{3,2,1,0:T(8,128)(2,1)S(1)}, bf16[1,1,32,4096]{3,2,1,0:T(8,128)(2,1)}, u32[]{:S(2)}) copy-start(bf16[1,1,32,4096]{3,2,1,0:T(8,128)(2,1)} %param.7) | copy-start | bytes 786436
  138.5 13.4 %collective-permute-start.40 = (bf16[256,512]{1,0:T(8,128)(2,1)S(1)}, bf16[256,512]{1,0:T(8,128)(2,1)S(1)}, u32[]{:S(2)}, u32[]{:S(2)}) collective-permute-start(bf16[256,512]{1,0:T(8,128)(2,1)S(1)} %get-tuple-element.99), channel_id=1, source_target_pairs={{0,16},{8,24},{16,32},{24,40},{32,48},{40,56},{48,0},{56,8},{1,17}... | collective-permute-start | bytes 786440 | tf_op jit(solution)/shard_map/ppermute | solution.py:916
  138.6 14.5 %collective-permute-start.41 = (bf16[256,512]{1,0:T(8,128)(2,1)S(1)}, bf16[256,512]{1,0:T(8,128)(2,1)S(1)}, u32[]{:S(2)}, u32[]{:S(2)}) collective-permute-start(bf16[256,512]{1,0:T(8,128)(2,1)S(1)} %get-tuple-element.100), channel_id=1, source_target_pairs={{0,48},{8,56},{16,0},{24,8},{32,16},{40,24},{48,32},{56,40},{1,49}... | collective-permute-start | bytes 786440 | tf_op jit(solution)/shard_map/ppermute | solution.py:917
  148.7 1.3 collective-permute-start.31
  149.0 6.0 %collective-permute-start.28 = (bf16[32,2048]{1,0:T(8,128)(2,1)S(1)}, bf16[32,2048]{1,0:T(8,128)(2,1)S(1)}, u32[]{:S(2)}, u32[]{:S(2)}) collective-permute-start(bf16[32,2048]{1,0:T(8,128)(2,1)S(1)} %get-tuple-element.89), channel_id=1, source_target_pairs={{0,3},{1,0},{2,1},{3,2},{4,7},{5,4},{6,5},{7,6},{8,11},{9,8},{10,9... | collective-permute-start | bytes 393224 | tf_op jit(solution)/shard_map/ppermute | solution.py:945
  150.0 9.6 %collective-permute-start.29 = (bf16[32,2048]{1,0:T(8,128)(2,1)S(1)}, bf16[32,2048]{1,0:T(8,128)(2,1)S(1)}, u32[]{:S(2)}, u32[]{:S(2)}) collective-permute-start(bf16[32,2048]{1,0:T(8,128)(2,1)S(1)} %get-tuple-element.90), channel_id=1, source_target_pairs={{0,1},{1,2},{2,3},{3,0},{4,5},{5,6},{6,7},{7,4},{8,9},{9,10},{10,1... | collective-permute-start | bytes 393224 | tf_op jit(solution)/shard_map/ppermute | solution.py:945
  151.9 11.6 %collective-permute-start.30 = (bf16[32,2048]{1,0:T(8,128)(2,1)S(1)}, bf16[32,2048]{1,0:T(8,128)(2,1)S(1)}, u32[]{:S(2)}, u32[]{:S(2)}) collective-permute-start(bf16[32,2048]{1,0:T(8,128)(2,1)S(1)} %get-tuple-element.91), channel_id=1, source_target_pairs={{0,2},{1,3},{2,0},{3,1},{4,6},{5,7},{6,4},{7,5},{8,10},{9,11},{10,... | collective-permute-start | bytes 393224 | tf_op jit(solution)/shard_map/ppermute | solution.py:945
  153.1 13.9 %collective-permute-start.32 = (f32[1,4096]{1,0:T(1,128)S(1)}, f32[1,4096]{1,0:T(1,128)S(1)}, u32[]{:S(2)}, u32[]{:S(2)}) collective-permute-start(f32[1,4096]{1,0:T(1,128)S(1)} %add.15), channel_id=1, source_target_pairs={{0,16},{8,24},{16,32},{24,40},{32,48},{40,56},{48,0},{56,8},{1,17}... | collective-permute-start | bytes 49160 | tf_op jit(solution)/shard_map/ppermute | solution.py:939
  154.9 12.9 %collective-permute-start.33 = (f32[1,4096]{1,0:T(1,128)S(1)}, f32[1,4096]{1,0:T(1,128)S(1)}, u32[]{:S(2)}, u32[]{:S(2)}) collective-permute-start(f32[1,4096]{1,0:T(1,128)S(1)} %add.15), channel_id=1, source_target_pairs={{0,48},{8,56},{16,0},{24,8},{32,16},{40,24},{48,32},{56,40},{1,49}... | collective-permute-start | bytes 49160 | tf_op jit(solution)/shard_map/ppermute | solution.py:939
  159.6 8.3 %collective-permute-start.34 = (f32[1,4096]{1,0:T(1,128)S(1)}, f32[1,4096]{1,0:T(1,128)S(1)}, u32[]{:S(2)}, u32[]{:S(2)}) collective-permute-start(f32[1,4096]{1,0:T(1,128)S(1)} %add.15), channel_id=1, source_target_pairs={{0,32},{8,40},{16,48},{24,56},{32,0},{40,8},{48,16},{56,24},{1,33}... | collective-permute-start | bytes 49160 | tf_op jit(solution)/shard_map/ppermute | solution.py:939
  163.5 13.2 %collective-permute-start.42 = (bf16[512,512]{1,0:T(8,128)(2,1)S(1)}, bf16[512,512]{1,0:T(8,128)(2,1)S(1)}, u32[]{:S(2)}, u32[]{:S(2)}) collective-permute-start(bf16[512,512]{1,0:T(8,128)(2,1)S(1)} %get-tuple-element.101), channel_id=1, source_target_pairs={{0,16},{8,24},{16,32},{24,40},{32,48},{40,56},{48,0},{56,8},{1,17}... | collective-permute-start | bytes 1572872 | tf_op jit(solution)/shard_map/ppermute | solution.py:931
  167.1 12.7 %collective-permute-start.43 = (bf16[512,512]{1,0:T(8,128)(2,1)S(1)}, bf16[512,512]{1,0:T(8,128)(2,1)S(1)}, u32[]{:S(2)}, u32[]{:S(2)}) collective-permute-start(bf16[512,512]{1,0:T(8,128)(2,1)S(1)} %get-tuple-element.102), channel_id=1, source_target_pairs={{0,48},{8,56},{16,0},{24,8},{32,16},{40,24},{48,32},{56,40},{1,49}... | collective-permute-start | bytes 1572872 | tf_op jit(solution)/shard_map/ppermute | solution.py:931
  (6 other events, 22.8 us)

commit v10 on v9

--- a/solution.py
+++ b/solution.py
@@ -112,58 +112,42 @@
     return [ref.at[pl.ds(i * KCUT, KCUT)] for i in range(KCUTS)]
 
 
-def norm_kernel(x, gain, n_left, n_right, inv):
+def touch_kernel(weight, pair, *refs):
+    refs[-1][...] = pair[...]
+
+
+def touch(pair, weight):
+    return call(
+        touch_kernel,
+        sds(pair.shape, pair.dtype),
+        vmem=4,
+        nbytes=pair.size * 4,
+        in_specs=[ANY, VMEM],
+        out_specs=VMEM,
+        name="touch",
+    )(weight, pair)
+
+
+def norm_kernel(x, gain, cot, n_left, n_right, grad, inv):
     x_float = x[...].astype(f32)
     scale = lax.rsqrt(jnp.mean(x_float * x_float, axis=1, keepdims=True) + 1e-05)
     normed = (x_float * scale * gain[...].astype(f32)).astype(bf16)
     n_left[...] = normed[:, :HALF]
     n_right[...] = normed[:, HALF:]
+    grad[...] = (cot[...].astype(f32) * valid_rows()).astype(bf16)
     inv[...] = jnp.broadcast_to(scale, (ROWS, 128))
 
 
-def norm_rows(x, gain):
+def norm_rows(x, gain, cot):
     part = sds((ROWS, HALF), bf16)
     return call(
         norm_kernel,
-        [part, part, sds((ROWS, 128), f32)],
+        [part, part, sds((ROWS, WIDTH), bf16), sds((ROWS, 128), f32)],
         vmem=4,
-        nbytes=2 * ROWS * WIDTH * 2,
-        in_specs=[VMEM] * 2,
+        nbytes=4 * ROWS * WIDTH * 2,
+        in_specs=[VMEM] * 3,
         name="norm_rows",
-    )(x, gain)
-
-
-def grad_kernel(cot, *refs):
-    refs[-1][...] = (cot[...].astype(f32) * valid_rows()).astype(bf16)
-
-
-def grad_rows_of(cot, after):
-    return call(
-        grad_kernel,
-        sds((ROWS, WIDTH), bf16),
-        vmem=4,
-        nbytes=2 * ROWS * WIDTH * 2,
-        in_specs=[VMEM] + [ANY] * len(after),
-        out_specs=VMEM,
-        name="grad_rows",
-    )(cot, *after)
-
-
-def pair_kernel(own, other, *refs):
-    refs[-1][0] = own[...]
-    refs[-1][1] = other[...]
-
-
-def pair_of(own, other, after):
-    return call(
-        pair_kernel,
-        sds((2,) + own.shape, own.dtype),
-        vmem=4,
-        nbytes=own.size * 8,
-        in_specs=[VMEM] * 2 + [ANY] * len(after),
-        out_specs=VMEM,
-        name="pair",
-    )(own, other, *after)
+    )(x, gain, cot)
 
 
 def gather_blocks(left, right):
@@ -879,11 +863,10 @@
     w_parts = jnp.transpose(w_qkv[0], (1, 0, 2))
     spans = (text_gaps, image_runs)
 
-    n_left, n_right, inv = norm_rows(x_rows, gains)
+    n_left, n_right, grad_rows, inv = norm_rows(x_rows, gains, cotangent[0, 0])
     pieces = gather_blocks(n_left, n_right)
-    grad_rows = grad_rows_of(cotangent[0, 0], pieces[2:3])
     grad_other = lax.ppermute(grad_rows, "tp", X_SWAP)
-    grad_pair = pair_of(grad_rows, grad_other, pieces[3:4])
+    grad_pair = touch(jnp.stack([grad_rows, grad_other]), w_parts)
     grad_pairs = [grad_pair] + [lax.ppermute(grad_pair, "tp", z_shift(k)) for k in STEPS[1:]]
     normed_full, own_kv = key_value(pieces, w_parts, [grad_pair])
     other_kv = lax.ppermute(own_kv, "grp", GRP_SWAP)
@@ -897,13 +880,11 @@
         spans, query, own_kv, other_kv, mixed, grad_mixed, []
     )
     back = lax.ppermute(other_part, "grp", GRP_SWAP)
-    sends = late(proj[1:3], [q_grad])
-    proj_came = [lax.ppermute(v, "tp", z_shift(-k)) for v, k in zip(sends, (1, 3))]
+    sends = late(proj[1:], [q_grad])
+    proj_came = [lax.ppermute(v, "tp", z_shift(-k)) for v, k in zip(sends, STEPS[1:])]
     out_own, out_sent = out_weight_parts(grad_full, mixed, [q_grad])
     out_came = lax.ppermute(out_sent, "seq", CORE_SWAP)
     own_grads = sum_keys(q_grad, own_part, back, sends[:1])
-    (far_sent,) = late(proj[3:], [own_grads])
-    proj_came.append(lax.ppermute(far_sent, "tp", z_shift(2)))
     back_grads = lax.ppermute(own_grads, "seq", y_shift(1))
     next_grads = lax.ppermute(own_grads, "seq", y_shift(3))
 
@@ -912,37 +893,39 @@
     left = back_left(own_grads, w_parts, normed_full, right[2], proj_came[:2])
     left_far_a = lax.ppermute(left[3], "tp", z_shift(1))
     left_far_b = lax.ppermute(left[4], "tp", z_shift(3))
-    out_kept, *out_sends = sum_out(out_own, out_came, [left_far_a])
-    out_far_a = lax.ppermute(out_sends[2], "seq", y_shift(1))
-    out_far_b = lax.ppermute(out_sends[3], "seq", y_shift(3))
-    left_back, left_forth = pass_left(
-        left[1], left[2], left_far_a, left_far_b, [right_x]
-    )
+    left_back, left_forth = pass_left(left[1], left[2], left_far_a, left_far_b, proj_came[2:])
     left_came = [
         lax.ppermute(left_forth, "tp", z_shift(1)), lax.ppermute(left_back, "tp", z_shift(3))
     ]
-    relayed = halves(back_grads, next_grads, [left_far_a, left_far_b, proj_came[2]])
-    grads = [own_grads, back_grads, next_grads]
-    grads += [lax.ppermute(v, "seq", y_shift(k)) for v, k in zip(relayed, (1, 3))]
+    out_kept, *out_sends = sum_out(
+        out_own, out_came, [left_back, back_grads, next_grads, right_x]
+    )
+    out_far_a = lax.ppermute(out_sends[2], "seq", y_shift(1))
+    out_far_b = lax.ppermute(out_sends[3], "seq", y_shift(3))
     out_back, out_forth = pass_out(
-        out_sends[0], out_sends[1], out_far_a, out_far_b, left_came[:1]
+        out_sends[0], out_sends[1], out_far_a, out_far_b
     )
     out_terms = [
         lax.ppermute(out_forth, "seq", y_shift(1)), lax.ppermute(out_back, "seq", y_shift(3))
     ]
-    left_kept, left_sent, gain_kept = sum_left(left[0], left_came, [right_x])
+    left_kept, left_sent, gain_kept = sum_left(left[0], left_came, [out_back])
     left_x = lax.ppermute(left_sent, "tp", X_SWAP)
-    gain_sum = sum_gain(gain_kept, left_x, gains)
-    gain_sum = gain_sum + lax.ppermute(gain_sum, "seq", CORE_SWAP)
+    gain_tp = sum_gain(gain_kept, left_x, gains)
+    gain_sum = gain_tp + lax.ppermute(gain_tp, "seq", CORE_SWAP)
     gain_grad = gain_sum
     for k in STEPS[1:]:
         gain_grad = gain_grad + lax.ppermute(gain_sum, "seq", y_shift(k))
-    shares = (normed_full, chunks, grads)
-    qkv_sent = weight_shares(0, *shares, bf16)
     right_kept, *right_sends = sum_x(
         right[0], right_x, [left_sent]
     )
+    relayed = halves(
+        back_grads, next_grads, [gain_tp, right_sends[0]] + out_terms
+    )
+    grads = [own_grads, back_grads, next_grads]
+    grads += [lax.ppermute(v, "seq", y_shift(k)) for v, k in zip(relayed, (1, 3))]
     right_came = [lax.ppermute(v, "tp", z_shift(-k)) for v, k in zip(right_sends, STEPS[1:])]
+    shares = (normed_full, chunks, grads)
+    qkv_sent = weight_shares(0, *shares, bf16, right_came + [gain_sum])
     tokens_grad = token_rows(
         x_rows, grad_rows, gains, inv, (left_kept, left_x), (right_kept, *right_came)
     )

time: 185 us -> 168 us (0.908)
  waiting for transfers between devices: 67.8 us -> 43.7 us
  starting transfers between devices: 70.9 us -> 76.2 us
    ppermute x5 -> x6, starting transfers between devices: 5.21 us -> 18.9 us  [per_device(): lax.ppermute(v, 'tp', z_shift(-k))]
    ppermute x1, waiting for transfers between devices: 12.1 us -> 0.01 us  [per_device(): grad_other = lax.ppermute(grad_rows, 'tp', X_SWAP)]
    ppermute x2 -> x1, waiting for transfers between devices: 9.87 us -> 0.01 us  [per_device(): gain_sum = gain_tp + lax.ppermute(gain_tp, 'seq', CORE_SWAP)]
    ppermute x5 -> x6, waiting for transfers between devices: 3.49 us -> 13.1 us  [per_device(): lax.ppermute(v, 'tp', z_shift(-k))]
    ppermute x2 -> x1, starting transfers between devices: 8.97 us -> 0.01 us  [per_device(): gain_sum = gain_tp + lax.ppermute(gain_tp, 'seq', CORE_SWAP)]
    ppermute x3, starting transfers between devices: 3.33 us -> 10.3 us  [gather_blocks(): lax.ppermute(right_pair, 'tp', z_shift(k))]
    ppermute x1, waiting for transfers between devices: 8.14 us -> 2.24 us  [per_device(): lax.ppermute(out_forth, 'seq', y_shift(1))]
    ppermute x1, starting transfers between devices: 6.09 us -> 1.87 us  [per_device(): back = lax.ppermute(other_part, 'grp', GRP_SWAP)]
where the time goes in v10:
time: 168 us; the launch traced here: 165 us
  starting transfers between devices  76.2 us (45%)
  waiting for transfers between devices  43.7 us (26%)
  Pallas kernels  33.1 us (20%)
  local copies, waits for them, and re-layouts  7.76 us (5%)
  other arithmetic  3.03 us (2%)
    ppermute x6, starting transfers between devices, per_device(): lax.ppermute(v, 'tp', z_shift(-k))  18.9 us
    ppermute x6, waiting for transfers between devices, per_device(): lax.ppermute(v, 'tp', z_shift(-k))  13.1 us
    ppermute x3, starting transfers between devices, gather_blocks(): lax.ppermute(right_pair, 'tp', z_shift(k))  10.3 us
    unnamed x20, local copies, waits for them, and re-layouts  7.76 us
    ppermute x1, waiting for transfers between devices, per_device(): back = lax.ppermute(other_part, 'grp', GRP_SWAP)  7.37 us
    ppermute x3, starting transfers between devices, chunks_over_y(): lax.ppermute(sent, 'seq', y_shift(k))  6.9 us
    pallas_call x2, Pallas kernels, back_dot(): call(functools.partial(kernel, len(after)), out_shape, vmem=20, flops=2 *...  6.2 us
    ppermute x3, starting transfers between devices, gather_blocks(): lax.ppermute(left, 'tp', z_shift(k))  5.9 us
  transfers between devices with their start and end apart: 44, of which 16 were waited for; matrix products, arithmetic and copies ran while one was open for 0% of the time, Pallas kernels for 14%

profile of v10, /device:TPU:0, one launch (start us, length us, event | category | flops | bytes accessed | tf_op | source)
XLA Modules:
  0.0 165.0 jit_solution(5255864619902832565)
XLA Ops:
  3.5 1.7 %collective-permute-start.4 = (bf16[32,2048]{1,0:T(8,128)(2,1)S(1)}, bf16[32,2048]{1,0:T(8,128)(2,1)S(1)}, u32[]{:S(2)}, u32[]{:S(2)}) collective-permute-start(bf16[32,2048]{1,0:T(8,128)(2,1)S(1)} %get-tuple-element.57), channel_id=1, source_target_pairs={{0,4},{1,5},{2,6},{3,7},{4,0},{5,1},{6,2},{7,3},{8,12},{9,13},{10,... | collective-permute-start | bytes 393224 | tf_op jit(solution)/shard_map/ppermute | solution.py:154
  5.1 3.9 %collective-permute-start.2 = (bf16[32,2048]{1,0:T(8,128)(2,1)S(1)}, bf16[32,2048]{1,0:T(8,128)(2,1)S(1)}, u32[]{:S(2)}, u32[]{:S(2)}) collective-permute-start(bf16[32,2048]{1,0:T(8,128)(2,1)S(1)} %get-tuple-element.56), channel_id=1, source_target_pairs={{0,2},{1,3},{2,0},{3,1},{4,6},{5,7},{6,4},{7,5},{8,10},{9,11},{10,... | collective-permute-start | bytes 393224 | tf_op jit(solution)/shard_map/ppermute | solution.py:155
  9.7 1.3 collective-permute-start
  11.6 1.3 collective-permute-start.7
  12.9 4.2 %collective-permute-start.6 = (bf16[2,32,2048]{2,1,0:T(8,128)(2,1)S(1)}, bf16[2,32,2048]{2,1,0:T(8,128)(2,1)S(1)}, u32[]{:S(2)}, u32[]{:S(2)}) collective-permute-start(bf16[2,32,2048]{2,1,0:T(8,128)(2,1)S(1)} %pad_maximum_fusion.2.refs_2_), channel_id=1, source_target_pairs={{0,3},{1,0},{2,1},{3,2},{4,7},{5,4},{6,5},{7,6},{8,11},{9,8},{10,9... | collective-permute-start | bytes 786440 | tf_op jit(solution)/shard_map/ppermute | solution.py:156
  17.2 4.9 %collective-permute-start.5 = (bf16[2,32,2048]{2,1,0:T(8,128)(2,1)S(1)}, bf16[2,32,2048]{2,1,0:T(8,128)(2,1)S(1)}, u32[]{:S(2)}, u32[]{:S(2)}) collective-permute-start(bf16[2,32,2048]{2,1,0:T(8,128)(2,1)S(1)} %pad_maximum_fusion.2.refs_2_), channel_id=1, source_target_pairs={{0,1},{1,2},{2,3},{3,0},{4,5},{5,6},{6,7},{7,4},{8,9},{9,10},{10,1... | collective-permute-start | bytes 786440 | tf_op jit(solution)/shard_map/ppermute | solution.py:156
  22.8 4.6 %copy-done = bf16[1,4096,3,512]{3,1,2,0:T(8,128)(2,1)S(1)} copy-done((bf16[1,4096,3,512]{3,1,2,0:T(8,128)(2,1)S(1)}, bf16[1,4096,3,512]{3,1,2,0:T(8,128)(2,1)}, u32[]{:S(2)}) %copy-start) | copy-done | bytes 12582936
  29.5 1.9 %collective-permute-done.3.refs_1_ = bf16[4,32,2048]{2,1,0:T(8,128)(2,1)S(1)} collective-permute-done((bf16[4,32,2048]{2,1,0:T(8,128)(2,1)S(1)}, bf16[4,32,2048]{2,1,0:T(8,128)(2,1)S(1)}, u32[]{:S(2)}, u32[]{:S(2)}) %collective-permute-start.3) | collective-permute-done | bytes 524320 | tf_op jit(solution)/shard_map/ppermute | solution.py:158
  32.0 3.7 %key_value.1 = (bf16[256,4096]{1,0:T(8,128)(2,1)S(1)}, bf16[2,256,512]{2,1,0:T(8,128)(2,1)S(1)}) custom-call(bf16[4,32,2048]{2,1,0:T(8,128)(2,1)S(1)} %pad_maximum_fusion.refs_0_, bf16[4,32,2048]{2,1,0:T(8,128)(2,1)S(1)} %collective-permute-done.3.refs_1_, bf16[2,32,2048]{2,1,0:T(8,128)(2,1)S(1)} %pad_maximum_fusion.2.refs_2_, ...), custom_call_target="tpu_custom_call" | custom-call | flops 2147483648 | bytes 12582912 | tf_op jit(solution)/shard_map/key_value/pallas_call | solution.py:460
  35.7 3.2 %collective-permute-start.11 = (bf16[2,256,512]{2,1,0:T(8,128)(2,1)S(1)}, bf16[2,256,512]{2,1,0:T(8,128)(2,1)S(1)}, u32[]{:S(2)}, u32[]{:S(2)}) collective-permute-start(bf16[2,256,512]{2,1,0:T(8,128)(2,1)S(1)} %get-tuple-element.60.own_kv), channel_id=1, source_target_pairs={{0,64},{64,0},{1,65},{65,1},{2,66},{66,2},{3,67},{67,3},{4,68},{68... | collective-permute-start | bytes 1572872 | tf_op jit(solution)/shard_map/ppermute | solution.py:872
  38.9 2.3 %collective-permute-start.12 = (bf16[2,32,4096]{2,1,0:T(8,128)(2,1)S(1)}, bf16[2,32,4096]{2,1,0:T(8,128)(2,1)S(1)}, u32[]{:S(2)}, u32[]{:S(2)}) collective-permute-start(bf16[2,32,4096]{2,1,0:T(8,128)(2,1)S(1)} %touch.1.refs_7_.p0), channel_id=1, source_target_pairs={{0,2},{1,3},{2,0},{3,1},{4,6},{5,7},{6,4},{7,5},{8,10},{9,11},{10,... | collective-permute-start | bytes 1572872 | tf_op jit(solution)/shard_map/ppermute | solution.py:870
  41.3 1.6 collective-permute-start.13
  42.9 2.1 %collective-permute-start.14 = (bf16[256,1024]{1,0:T(8,128)(2,1)S(1)}, bf16[256,1024]{1,0:T(8,128)(2,1)S(1)}, u32[]{:S(2)}, u32[]{:S(2)}) collective-permute-start(bf16[256,1024]{1,0:T(8,128)(2,1)S(1)} %get-tuple-element.66), channel_id=1, source_target_pairs={{0,48},{8,56},{16,0},{24,8},{32,16},{40,24},{48,32},{56,40},{1,49}... | collective-permute-start | bytes 1572872 | tf_op jit(solution)/shard_map/ppermute | solution.py:841
  45.0 1.8 %query.1 = bf16[256,512]{1,0:T(8,128)(2,1)S(1)} custom-call(bf16[256,4096]{1,0:T(8,128)(2,1)S(1)} %get-tuple-element.59.full.normed, bf16[3,4096,512]{2,1,0:T(8,128)(2,1)S(1)} %bitcast.22, bf16[2,32,4096]{2,1,0:T(8,128)(2,1)S(1)} %collective-permute-done.9.refs_0_.p1, bf16[2,32,4096]{2,1,0:T(8,128)(2,1)S(1)} %collective-permute-done.10.refs_1_.p2), custom_call_target="tpu_custom_call" | custom-call | flops 1073741824 | bytes 6291456 | tf_op jit(solution)/shard_map/query/pallas_call | solution.py:486
  46.8 2.4 %attend_forward.1.left.mixed = bf16[256,512]{1,0:T(8,128)(2,1)S(1)} custom-call(s32[1,5]{1,0:T(1,128)S(1)} %copy-done.8, s32[1,4]{1,0:T(1,128)S(1)} %copy-done.9, bf16[256,512]{1,0:T(8,128)(2,1)S(1)} %query.1, bf16[2,256,512]{2,1,0:T(8,128)(2,1)S(1)} %get-tuple-element.60.own_kv, bf16[2,256,512]{2,1,0:T(8,128)(2,1)S(1)} %collective-permute-done.11.other_kv), custom_call_target="tpu_custom_call" | custom-call | flops 536870912 | bytes 1572864 | tf_op jit(solution)/shard_map/attend_forward/pallas_call | solution.py:740
  49.2 2.2 %proj_parts.1 = (bf16[2,32,4096]{2,1,0:T(8,128)(2,1)S(1)}, bf16[2,32,4096]{2,1,0:T(8,128)(2,1)S(1)}, bf16[2,32,4096]{2,1,0:T(8,128)(2,1)S(1)}, bf16[2,32,4096]{2,1,0:T(8,128)(2,1)S(1)}) custom-call(bf16[256,512]{1,0:T(8,128)(2,1)S(1)} %attend_forward.1.left.mixed, bf16[1,4096,512]{2,1,0:T(8,128)(2,1)S(1)} %copy-done.2), custom_call_target="tpu_custom_call" | custom-call | flops 1073741824 | bytes 6291456 | tf_op jit(solution)/shard_map/proj_parts/pallas_call | solution.py:636
  52.5 1.9 %grad_mixed.1 = (bf16[256,4096]{1,0:T(8,128)(2,1)S(1)}, bf16[256,512]{1,0:T(8,128)(2,1)S(1)}) custom-call(bf16[2,32,4096]{2,1,0:T(8,128)(2,1)S(1)} %touch.1.refs_7_.p0, bf16[2,32,4096]{2,1,0:T(8,128)(2,1)S(1)} %collective-permute-done.9.refs_0_.p1, bf16[2,32,4096]{2,1,0:T(8,128)(2,1)S(1)} %collective-permute-done.10.refs_1_.p2, ...), custom_call_target="tpu_custom_call" | custom-call | flops 1073741824 | bytes 8388608 | tf_op jit(solution)/shard_map/grad_mixed/pallas_call | solution.py:509
  54.4 4.3 %attend_backward.1 = (bf16[256,512]{1,0:T(8,128)(2,1)S(1)}, f32[2,256,512]{2,1,0:T(8,128)S(1)}, bf16[2,256,512]{2,1,0:T(8,128)(2,1)S(1)}) custom-call(s32[1,5]{1,0:T(1,128)S(1)} %copy-done.8, s32[1,4]{1,0:T(1,128)S(1)} %copy-done.9, bf16[256,512]{1,0:T(8,128)(2,1)S(1)} %query.1, bf16[2,256,512]{2,1,0:T(8,128)(2,1)S(1)} %get-tuple-element.60.own_kv, ...), custom_call_target="tpu_custom_call" | custom-call | flops 1073741824 | bytes 3145728 | tf_op jit(solution)/shard_map/attend_backward/pallas_call | solution.py:754
  58.7 1.3 out_weight_parts.1
  60.1 1.9 %collective-permute-start.19 = (bf16[2,256,512]{2,1,0:T(8,128)(2,1)S(1)}, bf16[2,256,512]{2,1,0:T(8,128)(2,1)S(1)}, u32[]{:S(2)}, u32[]{:S(2)}) collective-permute-start(bf16[2,256,512]{2,1,0:T(8,128)(2,1)S(1)} %get-tuple-element.76), channel_id=1, source_target_pairs={{0,64},{64,0},{1,65},{65,1},{2,66},{66,2},{3,67},{67,3},{4,68},{68... | collective-permute-start | bytes 1572872 | tf_op jit(solution)/shard_map/ppermute | solution.py:882
  61.9 3.2 %collective-permute-start.21 = (bf16[256,1024]{1,0:T(8,128)(2,1)S(1)}, bf16[256,1024]{1,0:T(8,128)(2,1)S(1)}, u32[]{:S(2)}, u32[]{:S(2)}) collective-permute-start(bf16[256,1024]{1,0:T(8,128)(2,1)S(1)} %get-tuple-element.79), channel_id=1, source_target_pairs={{0,32},{8,40},{16,48},{24,56},{32,0},{40,8},{48,16},{56,24},{1,33}... | collective-permute-start | bytes 1572872 | tf_op jit(solution)/shard_map/ppermute | solution.py:841
  65.3 3.2 %collective-permute-start.15 = (bf16[2,32,4096]{2,1,0:T(8,128)(2,1)S(1)}, bf16[2,32,4096]{2,1,0:T(8,128)(2,1)S(1)}, u32[]{:S(2)}, u32[]{:S(2)}) collective-permute-start(bf16[2,32,4096]{2,1,0:T(8,128)(2,1)S(1)} %get-tuple-element.69.refs_0_), channel_id=1, source_target_pairs={{0,3},{1,0},{2,1},{3,2},{4,7},{5,4},{6,5},{7,6},{8,11},{9,8},{10,9... | collective-permute-start | bytes 1572872 | tf_op jit(solution)/shard_map/ppermute | solution.py:884
  68.5 7.4 %collective-permute-done.19.came = bf16[2,256,512]{2,1,0:T(8,128)(2,1)S(1)} collective-permute-done((bf16[2,256,512]{2,1,0:T(8,128)(2,1)S(1)}, bf16[2,256,512]{2,1,0:T(8,128)(2,1)S(1)}, u32[]{:S(2)}, u32[]{:S(2)}) %collective-permute-start.19) | collective-permute-done | bytes 524320 | tf_op jit(solution)/shard_map/ppermute | solution.py:882
  76.0 3.0 %collective-permute-start.27 = (bf16[3,256,512]{2,1,0:T(8,128)(2,1)S(1)}, bf16[3,256,512]{2,1,0:T(8,128)(2,1)S(1)}, u32[]{:S(2)}, u32[]{:S(2)}) collective-permute-start(bf16[3,256,512]{2,1,0:T(8,128)(2,1)S(1)} %sum_keys.1.grads.g0), channel_id=1, source_target_pairs={{0,48},{8,56},{16,0},{24,8},{32,16},{40,24},{48,32},{56,40},{1,49}... | collective-permute-start | bytes 2359304 | tf_op jit(solution)/shard_map/ppermute | solution.py:889
  79.0 11.4 %collective-permute-start.17 = (bf16[2,32,4096]{2,1,0:T(8,128)(2,1)S(1)}, bf16[2,32,4096]{2,1,0:T(8,128)(2,1)S(1)}, u32[]{:S(2)}, u32[]{:S(2)}) collective-permute-start(bf16[2,32,4096]{2,1,0:T(8,128)(2,1)S(1)} %get-tuple-element.71), channel_id=1, source_target_pairs={{0,2},{1,3},{2,0},{3,1},{4,6},{5,7},{6,4},{7,5},{8,10},{9,11},{10,... | collective-permute-start | bytes 1572872 | tf_op jit(solution)/shard_map/ppermute | solution.py:884
  90.5 3.1 %back_right.1 = (bf16[4,32,2048]{2,1,0:T(8,128)(2,1)S(1)}, bf16[4,32,2048]{2,1,0:T(8,128)(2,1)S(1)}, f32[1,2048]{1,0:T(1,128)S(1)}) custom-call(bf16[3,256,512]{2,1,0:T(8,128)(2,1)S(1)} %sum_keys.1.grads.g0, bf16[3,4096,512]{2,1,0:T(8,128)(2,1)S(1)} %bitcast.23, bf16[256,4096]{1,0:T(8,128)(2,1)S(1)} %get-tuple-element.59.full.normed, ...), custom_call_target="tpu_custom_call" | custom-call | flops 1610612736 | bytes 8388608 | tf_op jit(solution)/shard_map/back_right/pallas_call | solution.py:595
  94.3 3.1 %back_left.1 = (bf16[5,16,2048]{2,1,0:T(8,128)(2,1)S(1)}, bf16[5,16,2048]{2,1,0:T(8,128)(2,1)S(1)}, bf16[5,16,2048]{2,1,0:T(8,128)(2,1)S(1)}, bf16[3,16,2048]{2,1,0:T(8,128)(2,1)S(1)}, bf16[2,16,2048]{2,1,0:T(8,128)(2,1)S(1)}) custom-call(bf16[3,256,512]{2,1,0:T(8,128)(2,1)S(1)} %sum_keys.1.grads.g0, bf16[3,4096,512]{2,1,0:T(8,128)(2,1)S(1)} %bitcast.24, ...), custom_call_target="tpu_custom_call" | custom-call | flops 1610612736 | bytes 8388608 | tf_op jit(solution)/shard_map/back_left/pallas_call | solution.py:595
  97.5 6.8 %collective-permute-done.17.c3.refs_0_ = bf16[2,32,4096]{2,1,0:T(8,128)(2,1)S(1)} collective-permute-done((bf16[2,32,4096]{2,1,0:T(8,128)(2,1)S(1)}, bf16[2,32,4096]{2,1,0:T(8,128)(2,1)S(1)}, u32[]{:S(2)}, u32[]{:S(2)}) %collective-permute-start.17) | collective-permute-done | bytes 524320 | tf_op jit(solution)/shard_map/ppermute | solution.py:884
  104.3 4.9 %collective-permute-done.23.far_b = bf16[2,16,2048]{2,1,0:T(8,128)(2,1)S(1)} collective-permute-done((bf16[2,16,2048]{2,1,0:T(8,128)(2,1)S(1)}, bf16[2,16,2048]{2,1,0:T(8,128)(2,1)S(1)}, u32[]{:S(2)}, u32[]{:S(2)}) %collective-permute-start.23) | collective-permute-done | bytes 131104 | tf_op jit(solution)/shard_map/ppermute | solution.py:895
  109.8 1.3 collective-permute-start.29
  111.1 2.0 %collective-permute-start.30 = (bf16[256,512]{1,0:T(8,128)(2,1)S(1)}, bf16[256,512]{1,0:T(8,128)(2,1)S(1)}, u32[]{:S(2)}, u32[]{:S(2)}) collective-permute-start(bf16[256,512]{1,0:T(8,128)(2,1)S(1)} %get-tuple-element.93), channel_id=1, source_target_pairs={{0,48},{8,56},{16,0},{24,8},{32,16},{40,24},{48,32},{56,40},{1,49}... | collective-permute-start | bytes 786440 | tf_op jit(solution)/shard_map/ppermute | solution.py:904
  113.1 1.3 collective-permute-start.25
  115.2 2.4 %collective-permute-done.29.far_a = bf16[256,512]{1,0:T(8,128)(2,1)S(1)} collective-permute-done((bf16[256,512]{1,0:T(8,128)(2,1)S(1)}, bf16[256,512]{1,0:T(8,128)(2,1)S(1)}, u32[]{:S(2)}, u32[]{:S(2)}) %collective-permute-start.29) | collective-permute-done | bytes 262176 | tf_op jit(solution)/shard_map/ppermute | solution.py:903
  118.6 1.5 collective-permute-start.39
  120.0 1.8 %collective-permute-start.40 = (bf16[512,512]{1,0:T(8,128)(2,1)S(1)}, bf16[512,512]{1,0:T(8,128)(2,1)S(1)}, u32[]{:S(2)}, u32[]{:S(2)}) collective-permute-start(bf16[512,512]{1,0:T(8,128)(2,1)S(1)} %get-tuple-element.94.refs_0_), channel_id=1, source_target_pairs={{0,48},{8,56},{16,0},{24,8},{32,16},{40,24},{48,32},{56,40},{1,49}... | collective-permute-start | bytes 1572872 | tf_op jit(solution)/shard_map/ppermute | solution.py:909
  123.5 5.1 %collective-permute-done.31.l_came.came = bf16[3,16,2048]{2,1,0:T(8,128)(2,1)S(1)} collective-permute-done((bf16[3,16,2048]{2,1,0:T(8,128)(2,1)S(1)}, bf16[3,16,2048]{2,1,0:T(8,128)(2,1)S(1)}, u32[]{:S(2)}, u32[]{:S(2)}) %collective-permute-start.31) | collective-permute-done | bytes 196640 | tf_op jit(solution)/shard_map/ppermute | solution.py:912
  128.6 2.2 %collective-permute-done.39.refs_2_.c1 = bf16[512,512]{1,0:T(8,128)(2,1)S(1)} collective-permute-done((bf16[512,512]{1,0:T(8,128)(2,1)S(1)}, bf16[512,512]{1,0:T(8,128)(2,1)S(1)}, u32[]{:S(2)}, u32[]{:S(2)}) %collective-permute-start.39) | collective-permute-done | bytes 524320 | tf_op jit(solution)/shard_map/ppermute | solution.py:909
  132.1 2.4 %collective-permute-start.42 = (bf16[3,128,512]{2,1,0:T(8,128)(2,1)S(1)}, bf16[3,128,512]{2,1,0:T(8,128)(2,1)S(1)}, u32[]{:S(2)}, u32[]{:S(2)}) collective-permute-start(bf16[3,128,512]{2,1,0:T(8,128)(2,1)S(1)} %get-tuple-element.105), channel_id=1, source_target_pairs={{0,48},{8,56},{16,0},{24,8},{32,16},{40,24},{48,32},{56,40},{1,49}... | collective-permute-start | bytes 1179656 | tf_op jit(solution)/shard_map/ppermute | solution.py:925
  135.4 1.9 %collective-permute-start.34 = (bf16[32,2048]{1,0:T(8,128)(2,1)S(1)}, bf16[32,2048]{1,0:T(8,128)(2,1)S(1)}, u32[]{:S(2)}, u32[]{:S(2)}) collective-permute-start(bf16[32,2048]{1,0:T(8,128)(2,1)S(1)} %get-tuple-element.101), channel_id=1, source_target_pairs={{0,2},{1,3},{2,0},{3,1},{4,6},{5,7},{6,4},{7,5},{8,10},{9,11},{10,... | collective-permute-start | bytes 393224 | tf_op jit(solution)/shard_map/ppermute | solution.py:926
  137.4 1.3 collective-permute-start.32
  138.7 5.7 %collective-permute-done.33.r2.refs_1_ = bf16[32,2048]{1,0:T(8,128)(2,1)S(1)} collective-permute-done((bf16[32,2048]{1,0:T(8,128)(2,1)S(1)}, bf16[32,2048]{1,0:T(8,128)(2,1)S(1)}, u32[]{:S(2)}, u32[]{:S(2)}) %collective-permute-start.33) | collective-permute-done | bytes 131104 | tf_op jit(solution)/shard_map/ppermute | solution.py:926
  145.1 2.3 %weight_shares.2.refs_0_ = bf16[3,512,512]{2,1,0:T(8,128)(2,1)S(1)} custom-call(bf16[256,4096]{1,0:T(8,128)(2,1)S(1)} %get-tuple-element.59.full.normed, bf16[256,1024]{1,0:T(8,128)(2,1)S(1)} %collective-permute-done.13.refs_1_.c1, bf16[256,1024]{1,0:T(8,128)(2,1)S(1)} %collective-permute-done.14.refs_2_.c2, ...), custom_call_target="tpu_custom_call" | custom-call | flops 1610612736 | bytes 7340032 | tf_op jit(solution)/shard_map/weight_shares/pallas_call | solution.py:811
  147.9 1.7 %collective-permute-start.18 = (bf16[32,4096]{1,0:T(8,128)(2,1)S(1)}, bf16[32,4096]{1,0:T(8,128)(2,1)S(1)}, u32[]{:S(2)}, u32[]{:S(2)}) collective-permute-start(bf16[32,4096]{1,0:T(8,128)(2,1)S(1)} %get-tuple-element.73), channel_id=1, source_target_pairs={{0,4},{1,5},{2,6},{3,7},{4,0},{5,1},{6,2},{7,3},{8,12},{9,13},{10,... | collective-permute-start | bytes 786440 | tf_op jit(solution)/shard_map/ppermute | solution.py:936
  149.6 1.4 collective-permute-start.38
  151.6 1.5 collective-permute-start.36
  153.0 3.6 %collective-permute-done.18.came = bf16[32,4096]{1,0:T(8,128)(2,1)S(1)} collective-permute-done((bf16[32,4096]{1,0:T(8,128)(2,1)S(1)}, bf16[32,4096]{1,0:T(8,128)(2,1)S(1)}, u32[]{:S(2)}, u32[]{:S(2)}) %collective-permute-start.18) | collective-permute-done | bytes 262176 | tf_op jit(solution)/shard_map/ppermute | solution.py:936
  160.3 2.2 %weight_shares.3 = f32[3,512,512]{2,1,0:T(8,128)S(1)} custom-call(bf16[256,4096]{1,0:T(8,128)(2,1)S(1)} %get-tuple-element.59.full.normed, bf16[256,1024]{1,0:T(8,128)(2,1)S(1)} %collective-permute-done.13.refs_1_.c1, bf16[256,1024]{1,0:T(8,128)(2,1)S(1)} %collective-permute-done.14.refs_2_.c2, bf16[256,1024]{1,0:T(8,128)(2,1)S(1)} %collective-permute-done.21.refs_1_.c3, ...), custom_call_target="tpu_custom_call" | custom-call | flops 1610612736 | bytes 7340032 | tf_op jit(solution)/shard_map/weight_shares/pallas_call | solution.py:811
  162.5 2.2 %add_bitcast_fusion = f32[1,512,3,512]{3,1,2,0:T(8,128)} fusion(f32[3,512,512]{2,1,0:T(8,128)S(1)} %weight_shares.3, bf16[3,512,512]{2,1,0:T(8,128)(2,1)S(1)} %collective-permute-done.43), kind=kLoop, calls=%fused_computation | loop fusion | flops 1572864 | bytes 7864320 | tf_op jit(solution)/shard_map/broadcast_in_dim | solution.py:943
  (93 shorter events, 21.4 us)
Async XLA Ops:
  3.5 8.1 %collective-permute-start.4 = (bf16[32,2048]{1,0:T(8,128)(2,1)S(1)}, bf16[32,2048]{1,0:T(8,128)(2,1)S(1)}, u32[]{:S(2)}, u32[]{:S(2)}) collective-permute-start(bf16[32,2048]{1,0:T(8,128)(2,1)S(1)} %get-tuple-element.57), channel_id=1, source_target_pairs={{0,4},{1,5},{2,6},{3,7},{4,0},{5,1},{6,2},{7,3},{8,12},{9,13},{10,... | collective-permute-start | bytes 393224 | tf_op jit(solution)/shard_map/ppermute | solution.py:154
  5.1 7.7 %collective-permute-start.2 = (bf16[32,2048]{1,0:T(8,128)(2,1)S(1)}, bf16[32,2048]{1,0:T(8,128)(2,1)S(1)}, u32[]{:S(2)}, u32[]{:S(2)}) collective-permute-start(bf16[32,2048]{1,0:T(8,128)(2,1)S(1)} %get-tuple-element.56), channel_id=1, source_target_pairs={{0,2},{1,3},{2,0},{3,1},{4,6},{5,7},{6,4},{7,5},{8,10},{9,11},{10,... | collective-permute-start | bytes 393224 | tf_op jit(solution)/shard_map/ppermute | solution.py:155
  9.0 8.2 %collective-permute-start.1 = (bf16[32,2048]{1,0:T(8,128)(2,1)S(1)}, bf16[32,2048]{1,0:T(8,128)(2,1)S(1)}, u32[]{:S(2)}, u32[]{:S(2)}) collective-permute-start(bf16[32,2048]{1,0:T(8,128)(2,1)S(1)} %get-tuple-element.56), channel_id=1, source_target_pairs={{0,3},{1,0},{2,1},{3,2},{4,7},{5,4},{6,5},{7,6},{8,11},{9,8},{10,9... | collective-permute-start | bytes 393224 | tf_op jit(solution)/shard_map/ppermute | solution.py:155
  9.7 12.4 %collective-permute-start = (bf16[32,2048]{1,0:T(8,128)(2,1)S(1)}, bf16[32,2048]{1,0:T(8,128)(2,1)S(1)}, u32[]{:S(2)}, u32[]{:S(2)}) collective-permute-start(bf16[32,2048]{1,0:T(8,128)(2,1)S(1)} %get-tuple-element.56), channel_id=1, source_target_pairs={{0,1},{1,2},{2,3},{3,0},{4,5},{5,6},{6,7},{7,4},{8,9},{9,10},{10,1... | collective-permute-start | bytes 393224 | tf_op jit(solution)/shard_map/ppermute | solution.py:155
  11.0 11.7 %collective-permute-start.8 = (bf16[32,4096]{1,0:T(8,128)(2,1)S(1)}, bf16[32,4096]{1,0:T(8,128)(2,1)S(1)}, u32[]{:S(2)}, u32[]{:S(2)}) collective-permute-start(bf16[32,4096]{1,0:T(8,128)(2,1)S(1)} %get-tuple-element.58.grad), channel_id=1, source_target_pairs={{0,4},{1,5},{2,6},{3,7},{4,0},{5,1},{6,2},{7,3},{8,12},{9,13},{10,... | collective-permute-start | bytes 786440 | tf_op jit(solution)/shard_map/ppermute | solution.py:868
  11.6 16.9 %collective-permute-start.7 = (bf16[2,32,2048]{2,1,0:T(8,128)(2,1)S(1)}, bf16[2,32,2048]{2,1,0:T(8,128)(2,1)S(1)}, u32[]{:S(2)}, u32[]{:S(2)}) collective-permute-start(bf16[2,32,2048]{2,1,0:T(8,128)(2,1)S(1)} %pad_maximum_fusion.2.refs_2_), channel_id=1, source_target_pairs={{0,2},{1,3},{2,0},{3,1},{4,6},{5,7},{6,4},{7,5},{8,10},{9,11},{10,... | collective-permute-start | bytes 786440 | tf_op jit(solution)/shard_map/ppermute | solution.py:156
  12.9 16.7 %collective-permute-start.6 = (bf16[2,32,2048]{2,1,0:T(8,128)(2,1)S(1)}, bf16[2,32,2048]{2,1,0:T(8,128)(2,1)S(1)}, u32[]{:S(2)}, u32[]{:S(2)}) collective-permute-start(bf16[2,32,2048]{2,1,0:T(8,128)(2,1)S(1)} %pad_maximum_fusion.2.refs_2_), channel_id=1, source_target_pairs={{0,3},{1,0},{2,1},{3,2},{4,7},{5,4},{6,5},{7,6},{8,11},{9,8},{10,9... | collective-permute-start | bytes 786440 | tf_op jit(solution)/shard_map/ppermute | solution.py:156
  17.2 12.3 %collective-permute-start.5 = (bf16[2,32,2048]{2,1,0:T(8,128)(2,1)S(1)}, bf16[2,32,2048]{2,1,0:T(8,128)(2,1)S(1)}, u32[]{:S(2)}, u32[]{:S(2)}) collective-permute-start(bf16[2,32,2048]{2,1,0:T(8,128)(2,1)S(1)} %pad_maximum_fusion.2.refs_2_), channel_id=1, source_target_pairs={{0,1},{1,2},{2,3},{3,0},{4,5},{5,6},{6,7},{7,4},{8,9},{9,10},{10,1... | collective-permute-start | bytes 786440 | tf_op jit(solution)/shard_map/ppermute | solution.py:156
  22.2 9.3 %collective-permute-start.3 = (bf16[4,32,2048]{2,1,0:T(8,128)(2,1)S(1)}, bf16[4,32,2048]{2,1,0:T(8,128)(2,1)S(1)}, u32[]{:S(2)}, u32[]{:S(2)}) collective-permute-start(bf16[4,32,2048]{2,1,0:T(8,128)(2,1)S(1)} %pad_maximum_fusion.refs_0_), channel_id=1, source_target_pairs={{0,4},{1,5},{2,6},{3,7},{4,0},{5,1},{6,2},{7,3},{8,12},{9,13},{10,... | collective-permute-start | bytes 1572872 | tf_op jit(solution)/shard_map/ppermute | solution.py:158
  22.8 4.6 %copy-start = (bf16[1,4096,3,512]{3,1,2,0:T(8,128)(2,1)S(1)}, bf16[1,4096,3,512]{3,1,2,0:T(8,128)(2,1)}, u32[]{:S(2)}) copy-start(bf16[1,4096,3,512]{3,1,2,0:T(8,128)(2,1)} %param.11) | copy-start | bytes 37748740
  27.4 4.6 %copy-start.1 = (bf16[1,4096,3,512]{3,1,2,0:T(8,128)(2,1)S(1)}, bf16[1,4096,3,512]{3,1,2,0:T(8,128)(2,1)}, u32[]{:S(2)}) copy-start(bf16[1,4096,3,512]{3,1,2,0:T(8,128)(2,1)} %param.11) | copy-start | bytes 37748740
  27.4 15.5 %collective-permute-start.10 = (bf16[2,32,4096]{2,1,0:T(8,128)(2,1)S(1)}, bf16[2,32,4096]{2,1,0:T(8,128)(2,1)S(1)}, u32[]{:S(2)}, u32[]{:S(2)}) collective-permute-start(bf16[2,32,4096]{2,1,0:T(8,128)(2,1)S(1)} %touch.1.refs_7_.p0), channel_id=1, source_target_pairs={{0,3},{1,0},{2,1},{3,2},{4,7},{5,4},{6,5},{7,6},{8,11},{9,8},{10,9... | collective-permute-start | bytes 1572872 | tf_op jit(solution)/shard_map/ppermute | solution.py:870
  28.5 16.5 %collective-permute-start.9 = (bf16[2,32,4096]{2,1,0:T(8,128)(2,1)S(1)}, bf16[2,32,4096]{2,1,0:T(8,128)(2,1)S(1)}, u32[]{:S(2)}, u32[]{:S(2)}) collective-permute-start(bf16[2,32,4096]{2,1,0:T(8,128)(2,1)S(1)} %touch.1.refs_7_.p0), channel_id=1, source_target_pairs={{0,1},{1,2},{2,3},{3,0},{4,5},{5,6},{6,7},{7,4},{8,9},{9,10},{10,1... | collective-permute-start | bytes 1572872 | tf_op jit(solution)/shard_map/ppermute | solution.py:870
  35.7 11.1 %collective-permute-start.11 = (bf16[2,256,512]{2,1,0:T(8,128)(2,1)S(1)}, bf16[2,256,512]{2,1,0:T(8,128)(2,1)S(1)}, u32[]{:S(2)}, u32[]{:S(2)}) collective-permute-start(bf16[2,256,512]{2,1,0:T(8,128)(2,1)S(1)} %get-tuple-element.60.own_kv), channel_id=1, source_target_pairs={{0,64},{64,0},{1,65},{65,1},{2,66},{66,2},{3,67},{67,3},{4,68},{68... | collective-permute-start | bytes 1572872 | tf_op jit(solution)/shard_map/ppermute | solution.py:872
  38.9 12.5 %collective-permute-start.12 = (bf16[2,32,4096]{2,1,0:T(8,128)(2,1)S(1)}, bf16[2,32,4096]{2,1,0:T(8,128)(2,1)S(1)}, u32[]{:S(2)}, u32[]{:S(2)}) collective-permute-start(bf16[2,32,4096]{2,1,0:T(8,128)(2,1)S(1)} %touch.1.refs_7_.p0), channel_id=1, source_target_pairs={{0,2},{1,3},{2,0},{3,1},{4,6},{5,7},{6,4},{7,5},{8,10},{9,11},{10,... | collective-permute-start | bytes 1572872 | tf_op jit(solution)/shard_map/ppermute | solution.py:870
  41.3 10.5 %collective-permute-start.13 = (bf16[256,1024]{1,0:T(8,128)(2,1)S(1)}, bf16[256,1024]{1,0:T(8,128)(2,1)S(1)}, u32[]{:S(2)}, u32[]{:S(2)}) collective-permute-start(bf16[256,1024]{1,0:T(8,128)(2,1)S(1)} %get-tuple-element.65), channel_id=1, source_target_pairs={{0,16},{8,24},{16,32},{24,40},{32,48},{40,56},{48,0},{56,8},{1,17}... | collective-permute-start | bytes 1572872 | tf_op jit(solution)/shard_map/ppermute | solution.py:841
  42.9 9.5 %collective-permute-start.14 = (bf16[256,1024]{1,0:T(8,128)(2,1)S(1)}, bf16[256,1024]{1,0:T(8,128)(2,1)S(1)}, u32[]{:S(2)}, u32[]{:S(2)}) collective-permute-start(bf16[256,1024]{1,0:T(8,128)(2,1)S(1)} %get-tuple-element.66), channel_id=1, source_target_pairs={{0,48},{8,56},{16,0},{24,8},{32,16},{40,24},{48,32},{56,40},{1,49}... | collective-permute-start | bytes 1572872 | tf_op jit(solution)/shard_map/ppermute | solution.py:841
  60.0 19.0 %collective-permute-start.20 = (bf16[4,512,512]{2,1,0:T(8,128)(2,1)S(1)}, bf16[4,512,512]{2,1,0:T(8,128)(2,1)S(1)}, u32[]{:S(2)}, u32[]{:S(2)}) collective-permute-start(bf16[4,512,512]{2,1,0:T(8,128)(2,1)S(1)} %get-tuple-element.78), channel_id=1, source_target_pairs={{0,8},{8,0},{16,24},{24,16},{32,40},{40,32},{48,56},{56,48},{1,9},... | collective-permute-start | bytes 6291464 | tf_op jit(solution)/shard_map/ppermute | solution.py:886
  60.1 15.8 %collective-permute-start.19 = (bf16[2,256,512]{2,1,0:T(8,128)(2,1)S(1)}, bf16[2,256,512]{2,1,0:T(8,128)(2,1)S(1)}, u32[]{:S(2)}, u32[]{:S(2)}) collective-permute-start(bf16[2,256,512]{2,1,0:T(8,128)(2,1)S(1)} %get-tuple-element.76), channel_id=1, source_target_pairs={{0,64},{64,0},{1,65},{65,1},{2,66},{66,2},{3,67},{67,3},{4,68},{68... | collective-permute-start | bytes 1572872 | tf_op jit(solution)/shard_map/ppermute | solution.py:882
  61.9 17.1 %collective-permute-start.21 = (bf16[256,1024]{1,0:T(8,128)(2,1)S(1)}, bf16[256,1024]{1,0:T(8,128)(2,1)S(1)}, u32[]{:S(2)}, u32[]{:S(2)}) collective-permute-start(bf16[256,1024]{1,0:T(8,128)(2,1)S(1)} %get-tuple-element.79), channel_id=1, source_target_pairs={{0,32},{8,40},{16,48},{24,56},{32,0},{40,8},{48,16},{56,24},{1,33}... | collective-permute-start | bytes 1572872 | tf_op jit(solution)/shard_map/ppermute | solution.py:841
  65.2 28.3 %collective-permute-start.16 = (bf16[2,32,4096]{2,1,0:T(8,128)(2,1)S(1)}, bf16[2,32,4096]{2,1,0:T(8,128)(2,1)S(1)}, u32[]{:S(2)}, u32[]{:S(2)}) collective-permute-start(bf16[2,32,4096]{2,1,0:T(8,128)(2,1)S(1)} %get-tuple-element.70), channel_id=1, source_target_pairs={{0,1},{1,2},{2,3},{3,0},{4,5},{5,6},{6,7},{7,4},{8,9},{9,10},{10,1... | collective-permute-start | bytes 1572872 | tf_op jit(solution)/shard_map/ppermute | solution.py:884
  65.3 28.9 %collective-permute-start.15 = (bf16[2,32,4096]{2,1,0:T(8,128)(2,1)S(1)}, bf16[2,32,4096]{2,1,0:T(8,128)(2,1)S(1)}, u32[]{:S(2)}, u32[]{:S(2)}) collective-permute-start(bf16[2,32,4096]{2,1,0:T(8,128)(2,1)S(1)} %get-tuple-element.69.refs_0_), channel_id=1, source_target_pairs={{0,3},{1,0},{2,1},{3,2},{4,7},{5,4},{6,5},{7,6},{8,11},{9,8},{10,9... | collective-permute-start | bytes 1572872 | tf_op jit(solution)/shard_map/ppermute | solution.py:884
  76.0 33.3 %collective-permute-start.27 = (bf16[3,256,512]{2,1,0:T(8,128)(2,1)S(1)}, bf16[3,256,512]{2,1,0:T(8,128)(2,1)S(1)}, u32[]{:S(2)}, u32[]{:S(2)}) collective-permute-start(bf16[3,256,512]{2,1,0:T(8,128)(2,1)S(1)} %sum_keys.1.grads.g0), channel_id=1, source_target_pairs={{0,48},{8,56},{16,0},{24,8},{32,16},{40,24},{48,32},{56,40},{1,49}... | collective-permute-start | bytes 2359304 | tf_op jit(solution)/shard_map/ppermute | solution.py:889
  79.0 30.3 %collective-permute-start.26 = (bf16[3,256,512]{2,1,0:T(8,128)(2,1)S(1)}, bf16[3,256,512]{2,1,0:T(8,128)(2,1)S(1)}, u32[]{:S(2)}, u32[]{:S(2)}) collective-permute-start(bf16[3,256,512]{2,1,0:T(8,128)(2,1)S(1)} %sum_keys.1.grads.g0), channel_id=1, source_target_pairs={{0,16},{8,24},{16,32},{24,40},{32,48},{40,56},{48,0},{56,8},{1,17}... | collective-permute-start | bytes 2359304 | tf_op jit(solution)/shard_map/ppermute | solution.py:888
  79.0 25.2 %collective-permute-start.17 = (bf16[2,32,4096]{2,1,0:T(8,128)(2,1)S(1)}, bf16[2,32,4096]{2,1,0:T(8,128)(2,1)S(1)}, u32[]{:S(2)}, u32[]{:S(2)}) collective-permute-start(bf16[2,32,4096]{2,1,0:T(8,128)(2,1)S(1)} %get-tuple-element.71), channel_id=1, source_target_pairs={{0,2},{1,3},{2,0},{3,1},{4,6},{5,7},{6,4},{7,5},{8,10},{9,11},{10,... | collective-permute-start | bytes 1572872 | tf_op jit(solution)/shard_map/ppermute | solution.py:884
  93.6 15.8 %collective-permute-start.28 = (bf16[4,32,2048]{2,1,0:T(8,128)(2,1)S(1)}, bf16[4,32,2048]{2,1,0:T(8,128)(2,1)S(1)}, u32[]{:S(2)}, u32[]{:S(2)}) collective-permute-start(bf16[4,32,2048]{2,1,0:T(8,128)(2,1)S(1)} %get-tuple-element.89), channel_id=1, source_target_pairs={{0,4},{1,5},{2,6},{3,7},{4,0},{5,1},{6,2},{7,3},{8,12},{9,13},{10,... | collective-permute-start | bytes 1572872 | tf_op jit(solution)/shard_map/ppermute | solution.py:892
  97.4 11.8 %collective-permute-start.22 = (bf16[3,16,2048]{2,1,0:T(8,128)(2,1)S(1)}, bf16[3,16,2048]{2,1,0:T(8,128)(2,1)S(1)}, u32[]{:S(2)}, u32[]{:S(2)}) collective-permute-start(bf16[3,16,2048]{2,1,0:T(8,128)(2,1)S(1)} %get-tuple-element.84), channel_id=1, source_target_pairs={{0,1},{1,2},{2,3},{3,0},{4,5},{5,6},{6,7},{7,4},{8,9},{9,10},{10,1... | collective-permute-start | bytes 589832 | tf_op jit(solution)/shard_map/ppermute | solution.py:894
  104.2 5.0 %collective-permute-start.23 = (bf16[2,16,2048]{2,1,0:T(8,128)(2,1)S(1)}, bf16[2,16,2048]{2,1,0:T(8,128)(2,1)S(1)}, u32[]{:S(2)}, u32[]{:S(2)}) collective-permute-start(bf16[2,16,2048]{2,1,0:T(8,128)(2,1)S(1)} %get-tuple-element.85), channel_id=1, source_target_pairs={{0,3},{1,0},{2,1},{3,2},{4,7},{5,4},{6,5},{7,6},{8,11},{9,8},{10,9... | collective-permute-start | bytes 393224 | tf_op jit(solution)/shard_map/ppermute | solution.py:895
  109.8 7.8 %collective-permute-start.29 = (bf16[256,512]{1,0:T(8,128)(2,1)S(1)}, bf16[256,512]{1,0:T(8,128)(2,1)S(1)}, u32[]{:S(2)}, u32[]{:S(2)}) collective-permute-start(bf16[256,512]{1,0:T(8,128)(2,1)S(1)} %get-tuple-element.92), channel_id=1, source_target_pairs={{0,16},{8,24},{16,32},{24,40},{32,48},{40,56},{48,0},{56,8},{1,17}... | collective-permute-start | bytes 786440 | tf_op jit(solution)/shard_map/ppermute | solution.py:903
  111.1 7.3 %collective-permute-start.30 = (bf16[256,512]{1,0:T(8,128)(2,1)S(1)}, bf16[256,512]{1,0:T(8,128)(2,1)S(1)}, u32[]{:S(2)}, u32[]{:S(2)}) collective-permute-start(bf16[256,512]{1,0:T(8,128)(2,1)S(1)} %get-tuple-element.93), channel_id=1, source_target_pairs={{0,48},{8,56},{16,0},{24,8},{32,16},{40,24},{48,32},{56,40},{1,49}... | collective-permute-start | bytes 786440 | tf_op jit(solution)/shard_map/ppermute | solution.py:904
  113.1 9.6 %collective-permute-start.25 = (bf16[5,16,2048]{2,1,0:T(8,128)(2,1)S(1)}, bf16[5,16,2048]{2,1,0:T(8,128)(2,1)S(1)}, u32[]{:S(2)}, u32[]{:S(2)}) collective-permute-start(bf16[5,16,2048]{2,1,0:T(8,128)(2,1)S(1)} %get-tuple-element.87.refs_0_), channel_id=1, source_target_pairs={{0,3},{1,0},{2,1},{3,2},{4,7},{5,4},{6,5},{7,6},{8,11},{9,8},{10,9... | collective-permute-start | bytes 983048 | tf_op jit(solution)/shard_map/ppermute | solution.py:898
  114.4 8.3 %collective-permute-start.24 = (bf16[5,16,2048]{2,1,0:T(8,128)(2,1)S(1)}, bf16[5,16,2048]{2,1,0:T(8,128)(2,1)S(1)}, u32[]{:S(2)}, u32[]{:S(2)}) collective-permute-start(bf16[5,16,2048]{2,1,0:T(8,128)(2,1)S(1)} %get-tuple-element.86), channel_id=1, source_target_pairs={{0,1},{1,2},{2,3},{3,0},{4,5},{5,6},{6,7},{7,4},{8,9},{9,10},{10,1... | collective-permute-start | bytes 983048 | tf_op jit(solution)/shard_map/ppermute | solution.py:898
  118.4 10.2 %copy-start.7 = (bf16[1,4096]{1,0:T(2,128)(2,1)S(1)}, bf16[1,4096]{1,0:T(2,128)(2,1)}, u32[]{:S(2)}) copy-start(bf16[1,4096]{1,0:T(2,128)(2,1)} %gain.5) | copy-start | bytes 24580
  118.6 12.3 %collective-permute-start.39 = (bf16[512,512]{1,0:T(8,128)(2,1)S(1)}, bf16[512,512]{1,0:T(8,128)(2,1)S(1)}, u32[]{:S(2)}, u32[]{:S(2)}) collective-permute-start(bf16[512,512]{1,0:T(8,128)(2,1)S(1)} %get-tuple-element.103), channel_id=1, source_target_pairs={{0,16},{8,24},{16,32},{24,40},{32,48},{40,56},{48,0},{56,8},{1,17}... | collective-permute-start | bytes 1572872 | tf_op jit(solution)/shard_map/ppermute | solution.py:909
  120.0 11.0 %collective-permute-start.40 = (bf16[512,512]{1,0:T(8,128)(2,1)S(1)}, bf16[512,512]{1,0:T(8,128)(2,1)S(1)}, u32[]{:S(2)}, u32[]{:S(2)}) collective-permute-start(bf16[512,512]{1,0:T(8,128)(2,1)S(1)} %get-tuple-element.94.refs_0_), channel_id=1, source_target_pairs={{0,48},{8,56},{16,0},{24,8},{32,16},{40,24},{48,32},{56,40},{1,49}... | collective-permute-start | bytes 1572872 | tf_op jit(solution)/shard_map/ppermute | solution.py:909
  122.8 5.7 %collective-permute-start.31 = (bf16[3,16,2048]{2,1,0:T(8,128)(2,1)S(1)}, bf16[3,16,2048]{2,1,0:T(8,128)(2,1)S(1)}, u32[]{:S(2)}, u32[]{:S(2)}) collective-permute-start(bf16[3,16,2048]{2,1,0:T(8,128)(2,1)S(1)} %get-tuple-element.96.refs_0_), channel_id=1, source_target_pairs={{0,4},{1,5},{2,6},{3,7},{4,0},{5,1},{6,2},{7,3},{8,12},{9,13},{10,... | collective-permute-start | bytes 589832 | tf_op jit(solution)/shard_map/ppermute | solution.py:912
  131.1 14.0 %collective-permute-start.41 = (bf16[3,128,512]{2,1,0:T(8,128)(2,1)S(1)}, bf16[3,128,512]{2,1,0:T(8,128)(2,1)S(1)}, u32[]{:S(2)}, u32[]{:S(2)}) collective-permute-start(bf16[3,128,512]{2,1,0:T(8,128)(2,1)S(1)} %get-tuple-element.104), channel_id=1, source_target_pairs={{0,16},{8,24},{16,32},{24,40},{32,48},{40,56},{48,0},{56,8},{1,17}... | collective-permute-start | bytes 1179656 | tf_op jit(solution)/shard_map/ppermute | solution.py:925
  132.1 13.0 %collective-permute-start.42 = (bf16[3,128,512]{2,1,0:T(8,128)(2,1)S(1)}, bf16[3,128,512]{2,1,0:T(8,128)(2,1)S(1)}, u32[]{:S(2)}, u32[]{:S(2)}) collective-permute-start(bf16[3,128,512]{2,1,0:T(8,128)(2,1)S(1)} %get-tuple-element.105), channel_id=1, source_target_pairs={{0,48},{8,56},{16,0},{24,8},{32,16},{40,24},{48,32},{56,40},{1,49}... | collective-permute-start | bytes 1179656 | tf_op jit(solution)/shard_map/ppermute | solution.py:925
  134.5 2.8 %collective-permute-start.35 = (f32[1,4096]{1,0:T(1,128)S(1)}, f32[1,4096]{1,0:T(1,128)S(1)}, u32[]{:S(2)}, u32[]{:S(2)}) collective-permute-start(f32[1,4096]{1,0:T(1,128)S(1)} %sum_gain.1.refs_0_), channel_id=1, source_target_pairs={{0,8},{8,0},{16,24},{24,16},{32,40},{40,32},{48,56},{56,48},{1,9},... | collective-permute-start | bytes 49160 | tf_op jit(solution)/shard_map/ppermute | solution.py:914
  134.5 9.9 %collective-permute-start.33 = (bf16[32,2048]{1,0:T(8,128)(2,1)S(1)}, bf16[32,2048]{1,0:T(8,128)(2,1)S(1)}, u32[]{:S(2)}, u32[]{:S(2)}) collective-permute-start(bf16[32,2048]{1,0:T(8,128)(2,1)S(1)} %get-tuple-element.100), channel_id=1, source_target_pairs={{0,1},{1,2},{2,3},{3,0},{4,5},{5,6},{6,7},{7,4},{8,9},{9,10},{10,1... | collective-permute-start | bytes 393224 | tf_op jit(solution)/shard_map/ppermute | solution.py:926
  135.4 9.0 %collective-permute-start.34 = (bf16[32,2048]{1,0:T(8,128)(2,1)S(1)}, bf16[32,2048]{1,0:T(8,128)(2,1)S(1)}, u32[]{:S(2)}, u32[]{:S(2)}) collective-permute-start(bf16[32,2048]{1,0:T(8,128)(2,1)S(1)} %get-tuple-element.101), channel_id=1, source_target_pairs={{0,2},{1,3},{2,0},{3,1},{4,6},{5,7},{6,4},{7,5},{8,10},{9,11},{10,... | collective-permute-start | bytes 393224 | tf_op jit(solution)/shard_map/ppermute | solution.py:926
  137.4 7.7 %collective-permute-start.32 = (bf16[32,2048]{1,0:T(8,128)(2,1)S(1)}, bf16[32,2048]{1,0:T(8,128)(2,1)S(1)}, u32[]{:S(2)}, u32[]{:S(2)}) collective-permute-start(bf16[32,2048]{1,0:T(8,128)(2,1)S(1)} %get-tuple-element.99.refs_1_), channel_id=1, source_target_pairs={{0,3},{1,0},{2,1},{3,2},{4,7},{5,4},{6,5},{7,6},{8,11},{9,8},{10,9... | collective-permute-start | bytes 393224 | tf_op jit(solution)/shard_map/ppermute | solution.py:926
  147.3 9.3 %copy-start.4 = (bf16[1,1,32,4096]{3,2,1,0:T(8,128)(2,1)S(1)}, bf16[1,1,32,4096]{3,2,1,0:T(8,128)(2,1)}, u32[]{:S(2)}) copy-start(bf16[1,1,32,4096]{3,2,1,0:T(8,128)(2,1)} %param.7) | copy-start | bytes 786436
  147.3 15.2 %collective-permute-start.43 = (bf16[3,512,512]{2,1,0:T(8,128)(2,1)S(1)}, bf16[3,512,512]{2,1,0:T(8,128)(2,1)S(1)}, u32[]{:S(2)}, u32[]{:S(2)}) collective-permute-start(bf16[3,512,512]{2,1,0:T(8,128)(2,1)S(1)} %weight_shares.2.refs_0_), channel_id=1, source_target_pairs={{0,8},{8,0},{16,24},{24,16},{32,40},{40,32},{48,56},{56,48},{1,9},... | collective-permute-start | bytes 4718600 | tf_op jit(solution)/shard_map/ppermute | solution.py:934
  147.9 8.8 %collective-permute-start.18 = (bf16[32,4096]{1,0:T(8,128)(2,1)S(1)}, bf16[32,4096]{1,0:T(8,128)(2,1)S(1)}, u32[]{:S(2)}, u32[]{:S(2)}) collective-permute-start(bf16[32,4096]{1,0:T(8,128)(2,1)S(1)} %get-tuple-element.73), channel_id=1, source_target_pairs={{0,4},{1,5},{2,6},{3,7},{4,0},{5,1},{6,2},{7,3},{8,12},{9,13},{10,... | collective-permute-start | bytes 786440 | tf_op jit(solution)/shard_map/ppermute | solution.py:936
  149.6 8.9 %collective-permute-start.38 = (f32[1,4096]{1,0:T(1,128)S(1)}, f32[1,4096]{1,0:T(1,128)S(1)}, u32[]{:S(2)}, u32[]{:S(2)}) collective-permute-start(f32[1,4096]{1,0:T(1,128)S(1)} %add.15.refs_3_), channel_id=1, source_target_pairs={{0,32},{8,40},{16,48},{24,56},{32,0},{40,8},{48,16},{56,24},{1,33}... | collective-permute-start | bytes 49160 | tf_op jit(solution)/shard_map/ppermute | solution.py:917
  151.0 7.5 %collective-permute-start.37 = (f32[1,4096]{1,0:T(1,128)S(1)}, f32[1,4096]{1,0:T(1,128)S(1)}, u32[]{:S(2)}, u32[]{:S(2)}) collective-permute-start(f32[1,4096]{1,0:T(1,128)S(1)} %add.15.refs_3_), channel_id=1, source_target_pairs={{0,48},{8,56},{16,0},{24,8},{32,16},{40,24},{48,32},{56,40},{1,49}... | collective-permute-start | bytes 49160 | tf_op jit(solution)/shard_map/ppermute | solution.py:917
  151.6 7.0 %collective-permute-start.36 = (f32[1,4096]{1,0:T(1,128)S(1)}, f32[1,4096]{1,0:T(1,128)S(1)}, u32[]{:S(2)}, u32[]{:S(2)}) collective-permute-start(f32[1,4096]{1,0:T(1,128)S(1)} %add.15.refs_3_), channel_id=1, source_target_pairs={{0,16},{8,24},{16,32},{24,40},{32,48},{40,56},{48,0},{56,8},{1,17}... | collective-permute-start | bytes 49160 | tf_op jit(solution)/shard_map/ppermute | solution.py:917
  (6 other events, 14.6 us)
